TPU v7x, 32 devices: a whole 2x2x4 slice. The times are simulated.
32 devices in a mesh: expert: 4 (over y, x), shard: 4 (over z), dp: 2 (over core).
Axes of the slice: x: 2, y: 2, z: 4, core: 2. Of those that a mesh axis runs over, the one named last changes fastest.
Arguments:
- tokens: bfloat16 [8, 2560, 1024], P(('expert', 'dp'), 'shard'), may hold values from -6 to 6
- teacher: bfloat16 [8, 2560, 1024], P(('expert', 'dp'), 'shard'), may hold values from -6 to 6
- seg_ids: int32 [8, 2560], P(('expert', 'dp')), may hold values from 0 to 12, as said below
- parents: int32 [8, 13], P(('expert', 'dp')), may hold values from 0 to 12, as said below
- depth: int32 [8, 2560], P(('expert', 'dp')), may hold values from 0 to 1279, as said below
- valid: int32 [8, 2560], P(('expert', 'dp')), may hold values from 0 to 1, as said below
- routes: int32 [8, 2560, 2], P(('expert', 'dp')), may hold values from 0 to 3, all different within a row; in each aligned block of 2560 rows (0 to 2559, 2560 to 5119, ..., all dimensions but the last counted through in order) at most 1600 rows name the same one
- norm1_gain: float32 [1024], replicated, may hold values from 0.5 to 1.5
- w_query: bfloat16 [1024, 1024], P(None, 'shard'), may hold values from -0.1875 to 0.1875
- w_key: bfloat16 [1024, 1024], P(None, 'shard'), may hold values from -0.1875 to 0.1875
- w_value: bfloat16 [1024, 1024], P(None, 'shard'), may hold values from -0.1875 to 0.1875
- w_out: bfloat16 [1024, 1024], P('shard'), may hold values from -3 to 3
- rel_bias: float32 [32, 16], P(None, 'shard'), may hold values from -4 to 4
- norm2_gain: float32 [1024], replicated, may hold values from 0.5 to 1.5
- router: float32 [1024, 4], replicated, may hold values from -0.12 to 0.12
- w_gate: bfloat16 [4, 1024, 2816], P('expert', None, 'shard'), may hold values from -0.1875 to 0.1875
- w_up: bfloat16 [4, 1024, 2816], P('expert', None, 'shard'), may hold values from -0.1875 to 0.1875
- w_down: bfloat16 [4, 2816, 1024], P('expert', 'shard'), may hold values from -0.21875 to 0.21875
Outputs:
- output: bfloat16 [8, 2560, 1024], P(('expert', 'dp'), 'shard')
- loss: float32 [], replicated
- grad_tokens: float32 [8, 2560, 1024], P(('expert', 'dp'), 'shard')
- grad_norm1: float32 [1024], replicated
- grad_query: float32 [1024, 1024], P(None, 'shard')
- grad_key: float32 [1024, 1024], P(None, 'shard')
- grad_value: float32 [1024, 1024], P(None, 'shard')
- grad_out: float32 [1024, 1024], P('shard')
- grad_bias: float32 [32, 16], P(None, 'shard')
- grad_norm2: float32 [1024], replicated
- grad_router: float32 [1024, 4], replicated
- grad_gate: float32 [4, 1024, 2816], P('expert', None, 'shard')
- grad_up: float32 [4, 1024, 2816], P('expert', None, 'shard')
- grad_down: float32 [4, 2816, 1024], P('expert', 'shard')
Inputs may be any that keep to these rules, and one draw needn't show every extreme that they name: `seg_ids`: each tree is a trunk of 1024 positions, then 4 times a branch of 128 positions followed by its 2 leaves of 128 positions; each segment's positions form one run and carry one label. `parents`: for each segment label the label of the segment it grows from; the trunk names itself. Within a segment depth rises by one a position; a segment's first position has the number of valid positions of its ancestors. Each segment's valid positions come first and are 1 to all of its positions; the rest are padding. `routes`: among the 2560 tokens of one tree, no expert is named by more than 1600 tokens.
All inputs are finite; a program needn't handle non-finite values.
Results may differ from a plain program's by a relative error of at most 0.014.
Values may be sent and summed in bfloat16 or wider, within the bound.
A program may use at most 256 MiB of HBM per device.

v0:
```python
import math

import jax
import jax.numpy as jnp
from jax import lax
from jax.sharding import PartitionSpec as P

MAX_DIST = 128


EPSILON = 1e-06
MASKED_SCORE = -1e30
SCORE_SCALE = 0.125
HIGHEST_PRECISION = lax.Precision.HIGHEST


def gather_rows(values):
    return lax.all_gather(values, "shard", axis=0, tiled=True)


def reduce_rows(values):
    return lax.psum_scatter(values, "shard", scatter_dimension=0, tiled=True)


def bucket_index(distance, bucket_count):
    half_count = bucket_count // 2
    counted = jnp.zeros_like(distance)
    for number in range(1, bucket_count - half_count):
        border = math.ceil(
            half_count * (MAX_DIST / half_count) ** (number / (bucket_count - half_count))
        )
        counted = counted + (distance >= border).astype(jnp.int32)
    return jnp.where(distance < half_count, distance, half_count + counted)


def routing_tables(route_rows, experts, capacity):
    length, top_count = route_rows.shape
    flat_routes = route_rows.reshape(-1)
    onehot_rows = (flat_routes[:, None] == jnp.arange(experts, dtype=jnp.int32)[None, :]).astype(
        jnp.int32
    )
    earlier = jnp.cumsum(onehot_rows, axis=0) - onehot_rows
    slots = jnp.sum(earlier * onehot_rows, axis=1)
    target = flat_routes * capacity + slots
    source = (
        jnp.zeros((experts * capacity,), jnp.int32)
        .at[target]
        .set(jnp.arange(length * top_count, dtype=jnp.int32) + 1)
    )
    return (target, source)


def gelu_tanh(values):
    return jax.nn.gelu(values, approximate=True)


def expert_forward(row_values, gate_w, up_w, down_w):
    gate_pre = jnp.einsum("grd,gdf->grf", row_values, gate_w, preferred_element_type=jnp.float32)
    up_pre = jnp.einsum("grd,gdf->grf", row_values, up_w, preferred_element_type=jnp.float32)
    inner_low = (gelu_tanh(gate_pre) * up_pre).astype(jnp.bfloat16)
    return jnp.einsum("grf,gfd->grd", inner_low, down_w, preferred_element_type=jnp.float32)


def expert_backward(row_values, grad_values, gate_w, up_w, down_w):
    gate_pre = jnp.einsum("grd,gdf->grf", row_values, gate_w, preferred_element_type=jnp.float32)
    up_pre = jnp.einsum("grd,gdf->grf", row_values, up_w, preferred_element_type=jnp.float32)
    activated, gelu_back = jax.vjp(gelu_tanh, gate_pre)
    inner_low = (activated * up_pre).astype(jnp.bfloat16)
    down_grad = jnp.einsum(
        "grf,grd->gfd", inner_low, grad_values, preferred_element_type=jnp.float32
    )
    grad_inner = jnp.einsum("grd,gfd->grf", grad_values, down_w, preferred_element_type=jnp.float32)
    grad_gate_pre = gelu_back(grad_inner * up_pre)[0].astype(jnp.bfloat16)
    grad_up_pre = (grad_inner * activated).astype(jnp.bfloat16)
    gate_grad = jnp.einsum(
        "grd,grf->gdf", row_values, grad_gate_pre, preferred_element_type=jnp.float32
    )
    up_grad = jnp.einsum(
        "grd,grf->gdf", row_values, grad_up_pre, preferred_element_type=jnp.float32
    )
    rows_grad = jnp.einsum(
        "grf,gdf->grd", grad_gate_pre, gate_w, preferred_element_type=jnp.float32
    )
    rows_grad = rows_grad + jnp.einsum(
        "grf,gdf->grd", grad_up_pre, up_w, preferred_element_type=jnp.float32
    )
    return (rows_grad, gate_grad, up_grad, down_grad)


def on_device(
    tokens,
    teacher,
    seg_ids,
    parents,
    depth,
    valid,
    routes,
    norm1_gain,
    w_query,
    w_key,
    w_value,
    w_out,
    rel_bias,
    norm2_gain,
    router,
    w_gate,
    w_up,
    w_down,
):
    shard_index = lax.axis_index("shard")
    experts = lax.axis_size("expert") * w_gate.shape[0]
    token_rows = tokens[0].astype(jnp.float32)
    local_rows, width = token_rows.shape
    length = seg_ids.shape[1]
    top_count = routes.shape[2]
    capacity = 5 * length * top_count // (4 * experts)
    heads_here = rel_bias.shape[1]
    head_width = w_query.shape[1] // heads_here
    bucket_count = rel_bias.shape[0]
    segment = seg_ids[0]
    depths = depth[0]
    validity = valid[0]
    route_rows = routes[0]
    segment_labels = jnp.arange(parents.shape[1], dtype=jnp.int32)

    def parent_of(members):
        return jnp.sum(
            jnp.where(members[:, None] == segment_labels[None, :], parents[0][None, :], 0), axis=1
        )

    first_up = parent_of(segment)
    second_up = parent_of(first_up)
    row_start = shard_index * local_rows
    valid_local = lax.dynamic_slice_in_dim(validity, row_start, local_rows, 0).astype(jnp.float32)
    route_local = lax.dynamic_slice_in_dim(route_rows, row_start, local_rows, 0)
    scale_one = lax.rsqrt(jnp.mean(token_rows * token_rows, axis=1, keepdims=True) + EPSILON)
    base_one = token_rows * scale_one
    normed_one = (base_one * norm1_gain).astype(jnp.bfloat16)
    normed_all = gather_rows(normed_one)

    def project(matrix):
        projected = jnp.dot(normed_all, matrix, preferred_element_type=jnp.float32)
        return projected.astype(jnp.bfloat16).reshape(length, heads_here, head_width)

    query_rows = project(w_query)
    key_rows = project(w_key)
    value_rows = project(w_value)
    block_rows = min(512, length)
    blocks = length // block_rows
    key_allow = validity > 0

    def split_blocks(values):
        return values.reshape((blocks, block_rows) + values.shape[1:])

    def score_block(query_block, query_depth, query_seg, query_up, query_top):
        raw_scores = (
            jnp.einsum("qhd,khd->hqk", query_block, key_rows, preferred_element_type=jnp.float32)
            * SCORE_SCALE
        )
        distance = jnp.maximum(query_depth[:, None] - depths[None, :], 0)
        bucket = bucket_index(distance, bucket_count)
        bias_rows = jnp.zeros(raw_scores.shape, jnp.float32)
        for number in range(bucket_count):
            bias_rows = bias_rows + jnp.where(
                (bucket == number)[None], rel_bias[number][:, None, None], 0.0
            )
        raw_scores = raw_scores + bias_rows
        allowed = (
            key_allow[None, :]
            & (depths[None, :] <= query_depth[:, None])
            & (
                (segment[None, :] == query_seg[:, None])
                | (segment[None, :] == query_up[:, None])
                | (segment[None, :] == query_top[:, None])
            )
        )
        return (jnp.where(allowed[None], raw_scores, MASKED_SCORE), bucket)

    block_inputs = (
        split_blocks(query_rows),
        split_blocks(depths),
        split_blocks(segment),
        split_blocks(first_up),
        split_blocks(second_up),
    )

    def forward_block(running, pieces):
        scores, bucket = score_block(*pieces)
        highest = jnp.max(scores, axis=2, keepdims=True)
        shifted = jnp.exp(scores - highest)
        totals = jnp.sum(shifted, axis=2, keepdims=True)
        probs_low = (shifted / totals).astype(jnp.bfloat16)
        result = jnp.einsum(
            "hqk,khd->qhd", probs_low, value_rows, preferred_element_type=jnp.float32
        )
        return (running, (result, highest[:, :, 0] + jnp.log(totals[:, :, 0])))

    unused, (attended, log_totals) = lax.scan(forward_block, 0, block_inputs)
    attended_low = attended.reshape(length, heads_here * head_width).astype(jnp.bfloat16)
    update = reduce_rows(jnp.dot(attended_low, w_out, preferred_element_type=jnp.float32))
    hidden = token_rows + update
    scale_two = lax.rsqrt(jnp.mean(hidden * hidden, axis=1, keepdims=True) + EPSILON)
    base_two = hidden * scale_two
    normed_two = (base_two * norm2_gain).astype(jnp.bfloat16)
    normed_wide = normed_two.astype(jnp.float32)
    expert_ids = jnp.arange(experts, dtype=jnp.int32)
    route_match = route_local[:, :, None] == expert_ids[None, None, :]
    logits = jnp.dot(normed_wide, router, precision=HIGHEST_PRECISION)
    chosen = jnp.sum(jnp.where(route_match, logits[:, None, :], 0.0), axis=2)
    gates = jax.nn.softmax(chosen, axis=1)
    target, source = routing_tables(route_rows, experts, capacity)
    filled = (source > 0)[:, None]
    slot_entry = jnp.maximum(source - 1, 0)
    slot_token = slot_entry // top_count
    normed_full = gather_rows(normed_two)
    send_rows = jnp.where(
        filled, jnp.take(normed_full, slot_token, axis=0), jnp.zeros((), jnp.bfloat16)
    ).reshape(experts, capacity, width)
    received = lax.all_to_all(send_rows, "expert", split_axis=0, concat_axis=0, tiled=True)
    produced = expert_forward(received.reshape(1, -1, width), w_gate, w_up, w_down)
    expert_out = produced.reshape(received.shape[0], received.shape[1], width)
    returned = lax.all_to_all(
        expert_out.astype(jnp.bfloat16), "expert", split_axis=0, concat_axis=0, tiled=True
    ).astype(expert_out.dtype)
    picked = jnp.take(returned.reshape(experts * capacity, width), target, axis=0).reshape(
        length, top_count, width
    )
    expert_local = lax.psum_scatter(
        picked.astype(jnp.bfloat16), "shard", scatter_dimension=0, tiled=True
    ).astype(jnp.float32)
    combined = jnp.sum(gates[:, :, None] * expert_local, axis=1)
    output_rows = hidden + combined
    valid_total = lax.psum(jnp.sum(validity), ("expert", "dp"))
    valid_count = jnp.asarray(valid_total).astype(jnp.float32)
    factor = length * lax.axis_size("expert") * lax.axis_size("dp") / valid_count
    error = output_rows - teacher[0].astype(jnp.float32)
    error_sum = jnp.sum(valid_local[:, None] * error * error)
    grad_output = valid_local[:, None] * error * factor
    grad_gates = jnp.sum(grad_output[:, None, :] * expert_local, axis=2)
    grad_send_local = (gates[:, :, None] * grad_output[:, None, :]).astype(jnp.bfloat16)
    grad_send_all = gather_rows(grad_send_local).reshape(length * top_count, width)
    send_grads = jnp.where(
        filled, jnp.take(grad_send_all, slot_entry, axis=0), jnp.zeros((), jnp.bfloat16)
    ).reshape(experts, capacity, width)
    received_grads = lax.all_to_all(send_grads, "expert", split_axis=0, concat_axis=0, tiled=True)
    rows_grad, gate_part, up_part, down_part = expert_backward(
        received.reshape(1, -1, width), received_grads.reshape(1, -1, width), w_gate, w_up, w_down
    )
    rows_grad = rows_grad.reshape(received.shape)
    grad_back = lax.all_to_all(
        rows_grad.astype(jnp.bfloat16), "expert", split_axis=0, concat_axis=0, tiled=True
    ).astype(rows_grad.dtype)
    expert_back = jnp.take(grad_back.reshape(experts * capacity, width), target, axis=0).reshape(
        length, top_count, width
    )
    expert_back_local = lax.psum_scatter(
        jnp.sum(expert_back, axis=1).astype(jnp.bfloat16), "shard", scatter_dimension=0, tiled=True
    ).astype(jnp.float32)
    gate_grad, up_grad, down_grad = (
        lax.psum(gate_part.astype(jnp.bfloat16), "dp").astype(jnp.float32),
        lax.psum(up_part.astype(jnp.bfloat16), "dp").astype(jnp.float32),
        lax.psum(down_part.astype(jnp.bfloat16), "dp").astype(jnp.float32),
    )
    weighted = jnp.sum(gates * grad_gates, axis=1, keepdims=True)
    grad_chosen = gates * (grad_gates - weighted)
    grad_logits = jnp.sum(jnp.where(route_match, grad_chosen[:, :, None], 0.0), axis=1)
    router_grad = jnp.einsum("rd,re->de", normed_wide, grad_logits, precision=HIGHEST_PRECISION)
    grad_normed_two = jnp.einsum("re,de->rd", grad_logits, router, precision=HIGHEST_PRECISION)
    grad_normed_two = grad_normed_two + expert_back_local
    grad_base_two = grad_normed_two * norm2_gain
    norm2_grad = jnp.sum(grad_normed_two * base_two, axis=0)
    grad_hidden = grad_output + scale_two * (
        grad_base_two - base_two * jnp.mean(grad_base_two * base_two, axis=1, keepdims=True)
    )
    grad_update = gather_rows(grad_hidden.astype(jnp.bfloat16))
    out_grad = jnp.einsum(
        "la,ld->ad", attended_low, grad_update, preferred_element_type=jnp.float32
    )
    grad_attended = jnp.einsum("ld,ad->la", grad_update, w_out, preferred_element_type=jnp.float32)
    grad_attended = grad_attended.astype(jnp.bfloat16).reshape(length, heads_here, head_width)

    def backward_block(running, pieces):
        key_grad, value_grad, bias_total = running
        query_block, query_depth, query_seg, query_up, query_top, grad_block, log_block = pieces
        scores, bucket = score_block(query_block, query_depth, query_seg, query_up, query_top)
        probs = jnp.exp(scores - log_block[:, :, None])
        probs_low = probs.astype(jnp.bfloat16)
        grad_probs = jnp.einsum(
            "qhd,khd->hqk", grad_block, value_rows, preferred_element_type=jnp.float32
        )
        centre = jnp.sum(probs * grad_probs, axis=2, keepdims=True)
        grad_scores = (probs * (grad_probs - centre)).astype(jnp.bfloat16)
        query_grad = (
            jnp.einsum("hqk,khd->qhd", grad_scores, key_rows, preferred_element_type=jnp.float32)
            * SCORE_SCALE
        ).astype(jnp.bfloat16)
        key_grad = (
            key_grad
            + jnp.einsum(
                "hqk,qhd->khd", grad_scores, query_block, preferred_element_type=jnp.float32
            )
            * SCORE_SCALE
        )
        value_grad = value_grad + jnp.einsum(
            "hqk,qhd->khd", probs_low, grad_block, preferred_element_type=jnp.float32
        )
        score_wide = grad_scores.astype(jnp.float32)
        bias_step = jnp.stack(
            [
                jnp.sum(jnp.where((bucket == number)[None], score_wide, 0.0), axis=(1, 2))
                for number in range(bucket_count)
            ]
        )
        return ((key_grad, value_grad, bias_total + bias_step), query_grad)

    start_grads = (
        jnp.zeros((length, heads_here, head_width), jnp.float32),
        jnp.zeros((length, heads_here, head_width), jnp.float32),
        jnp.zeros((bucket_count, heads_here), jnp.float32),
    )
    (key_grad, value_grad, bias_grad), query_grads = lax.scan(
        backward_block, start_grads, block_inputs + (split_blocks(grad_attended), log_totals)
    )
    grad_queries = query_grads.reshape(length, heads_here * head_width)
    grad_keys = key_grad.astype(jnp.bfloat16).reshape(length, heads_here * head_width)
    grad_values = value_grad.astype(jnp.bfloat16).reshape(length, heads_here * head_width)
    query_wgrad = jnp.einsum(
        "ld,la->da", normed_all, grad_queries, preferred_element_type=jnp.float32
    )
    key_wgrad = jnp.einsum("ld,la->da", normed_all, grad_keys, preferred_element_type=jnp.float32)
    value_wgrad = jnp.einsum(
        "ld,la->da", normed_all, grad_values, preferred_element_type=jnp.float32
    )
    grad_normed_all = jnp.einsum(
        "la,da->ld", grad_queries, w_query, preferred_element_type=jnp.float32
    )
    grad_normed_all = grad_normed_all + jnp.einsum(
        "la,da->ld", grad_keys, w_key, preferred_element_type=jnp.float32
    )
    grad_normed_all = grad_normed_all + jnp.einsum(
        "la,da->ld", grad_values, w_value, preferred_element_type=jnp.float32
    )
    grad_normed_one = reduce_rows(grad_normed_all)
    grad_base_one = grad_normed_one * norm1_gain
    norm1_grad = jnp.sum(grad_normed_one * base_one, axis=0)
    grad_tokens = grad_hidden + scale_one * (
        grad_base_one - base_one * jnp.mean(grad_base_one * base_one, axis=1, keepdims=True)
    )
    query_wgrad, key_wgrad, value_wgrad, out_grad, bias_grad = (
        lax.psum(query_wgrad.astype(jnp.bfloat16), ("expert", "dp")).astype(jnp.float32),
        lax.psum(key_wgrad.astype(jnp.bfloat16), ("expert", "dp")).astype(jnp.float32),
        lax.psum(value_wgrad.astype(jnp.bfloat16), ("expert", "dp")).astype(jnp.float32),
        lax.psum(out_grad.astype(jnp.bfloat16), ("expert", "dp")).astype(jnp.float32),
        lax.psum(bias_grad.astype(jnp.bfloat16), ("expert", "dp")).astype(jnp.float32),
    )
    router_grad, norm1_grad, norm2_grad, error_total = lax.psum(
        (router_grad, norm1_grad, norm2_grad, error_sum), ("expert", "shard", "dp")
    )
    loss = error_total / (width * valid_count)
    return (
        output_rows.astype(jnp.bfloat16)[None],
        loss,
        grad_tokens[None],
        norm1_grad,
        query_wgrad,
        key_wgrad,
        value_wgrad,
        out_grad,
        bias_grad,
        norm2_grad,
        router_grad,
        gate_grad,
        up_grad,
        down_grad,
    )


def solution(mesh):
    in_specs = (
        P(("expert", "dp"), "shard", None),
        P(("expert", "dp"), "shard", None),
        P(("expert", "dp"), None),
        P(("expert", "dp"), None),
        P(("expert", "dp"), None),
        P(("expert", "dp"), None),
        P(("expert", "dp"), None, None),
        P(),
        P(None, "shard"),
        P(None, "shard"),
        P(None, "shard"),
        P("shard", None),
        P(None, "shard"),
        P(),
        P(),
        P("expert", None, "shard"),
        P("expert", None, "shard"),
        P("expert", "shard", None),
    )
    out_specs = (
        P(("expert", "dp"), "shard", None),
        P(),
        P(("expert", "dp"), "shard", None),
        P(),
        P(None, "shard"),
        P(None, "shard"),
        P(None, "shard"),
        P("shard", None),
        P(None, "shard"),
        P(),
        P(),
        P("expert", None, "shard"),
        P("expert", None, "shard"),
        P("expert", "shard", None),
    )
    return jax.shard_map(
        on_device, mesh=mesh, in_specs=in_specs, out_specs=out_specs, check_vma=False
    )
```

profile of v0, /device:TPU:0, one launch (start us, length us, event | category | flops | bytes accessed | tf_op | source)
XLA Modules:
  0.0 4848.8 jit_solution(2193163747899021596)
XLA Ops:
  13.0 100.3 %all-gather.5.cloned.1.call-done = bf16[2560,1024]{1,0:T(8,128)(2,1)} async-done(((bf16[640,1024]{1,0:T(8,128)(2,1)}), bf16[2560,1024]{1,0:T(8,128)(2,1)}) %all-gather.5.cloned.1.call-update) | async-done | bytes 5242896 | tf_op jit(solution)/shard_map/all_gather | solution.py:18
  134.7 780.1 %while.29 = (s32[]{:T(128)}, bf16[5,512,4,64]{1,3,2,0:T(8,128)(2,1)}, f32[5,4,512]{2,1,0:T(4,128)}, pred[2560]{0:T(1024)(128)(4,1)S(1)}, s32[1,2560]{1,0:T(1,128...) while((s32[]{:T(128)}, ...), condition=%wide.region_6.7_spmd, body=%wide.region_3.6_spmd.sunk | while | flops 1836316672 | bytes 158663328 | solution.py:198
  146.9 41.1 or_and_fusion.4
  188.0 91.7 %fusion.219 = (f32[4,512]{1,0:T(4,128)S(1)}, f32[4,512,2560]{2,1,0:T(8,128)}) fusion(f32[4]{0:T(128)S(1)} %get-tuple-element.1027, pred[512,2560]{1,0:T(8,128)(4,1)} %get-tuple-element.1032, f32[4]{0:T(128)S(1)} %get-tuple-element.1033, pred[512,2560]{1,0:T(8,128)(4,1)} %get-tuple-element.1034, f32[4]{0:T(128)S(1)} %get-tuple-element.1035, ...), kind=kOutput, calls=%fused_computation.406.clone.2 | convolution fusion | flops 1022359552 | bytes 65806852 | tf_op jit(solution)/shard_map/while/body/eval_jaxpr/qhd,khd->hqk/dot_general | solution.py:157
  300.5 41.1 or_and_fusion.4
  341.7 91.7 %fusion.219 = (f32[4,512]{1,0:T(4,128)S(1)}, f32[4,512,2560]{2,1,0:T(8,128)}) fusion(f32[4]{0:T(128)S(1)} %get-tuple-element.1027, pred[512,2560]{1,0:T(8,128)(4,1)} %get-tuple-element.1032, f32[4]{0:T(128)S(1)} %get-tuple-element.1033, pred[512,2560]{1,0:T(8,128)(4,1)} %get-tuple-element.1034, f32[4]{0:T(128)S(1)} %get-tuple-element.1035, ...), kind=kOutput, calls=%fused_computation.406.clone.2 | convolution fusion | flops 1022359552 | bytes 65806852 | tf_op jit(solution)/shard_map/while/body/eval_jaxpr/qhd,khd->hqk/dot_general | solution.py:157
  454.1 41.1 or_and_fusion.4
  495.3 91.7 %fusion.219 = (f32[4,512]{1,0:T(4,128)S(1)}, f32[4,512,2560]{2,1,0:T(8,128)}) fusion(f32[4]{0:T(128)S(1)} %get-tuple-element.1027, pred[512,2560]{1,0:T(8,128)(4,1)} %get-tuple-element.1032, f32[4]{0:T(128)S(1)} %get-tuple-element.1033, pred[512,2560]{1,0:T(8,128)(4,1)} %get-tuple-element.1034, f32[4]{0:T(128)S(1)} %get-tuple-element.1035, ...), kind=kOutput, calls=%fused_computation.406.clone.2 | convolution fusion | flops 1022359552 | bytes 65806852 | tf_op jit(solution)/shard_map/while/body/eval_jaxpr/qhd,khd->hqk/dot_general | solution.py:157
  607.8 41.1 or_and_fusion.4
  648.9 91.7 %fusion.219 = (f32[4,512]{1,0:T(4,128)S(1)}, f32[4,512,2560]{2,1,0:T(8,128)}) fusion(f32[4]{0:T(128)S(1)} %get-tuple-element.1027, pred[512,2560]{1,0:T(8,128)(4,1)} %get-tuple-element.1032, f32[4]{0:T(128)S(1)} %get-tuple-element.1033, pred[512,2560]{1,0:T(8,128)(4,1)} %get-tuple-element.1034, f32[4]{0:T(128)S(1)} %get-tuple-element.1035, ...), kind=kOutput, calls=%fused_computation.406.clone.2 | convolution fusion | flops 1022359552 | bytes 65806852 | tf_op jit(solution)/shard_map/while/body/eval_jaxpr/qhd,khd->hqk/dot_general | solution.py:157
  761.4 41.1 or_and_fusion.4
  802.6 91.7 %fusion.219 = (f32[4,512]{1,0:T(4,128)S(1)}, f32[4,512,2560]{2,1,0:T(8,128)}) fusion(f32[4]{0:T(128)S(1)} %get-tuple-element.1027, pred[512,2560]{1,0:T(8,128)(4,1)} %get-tuple-element.1032, f32[4]{0:T(128)S(1)} %get-tuple-element.1033, pred[512,2560]{1,0:T(8,128)(4,1)} %get-tuple-element.1034, f32[4]{0:T(128)S(1)} %get-tuple-element.1035, ...), kind=kOutput, calls=%fused_computation.406.clone.2 | convolution fusion | flops 1022359552 | bytes 65806852 | tf_op jit(solution)/shard_map/while/body/eval_jaxpr/qhd,khd->hqk/dot_general | solution.py:157
  924.5 176.5 %reduce-scatter.4.cloned.1.call-done = f32[640,1024]{1,0:T(8,128)} async-done(((f32[2560,1024]{1,0:T(8,128)}), f32[640,1024]{1,0:T(8,128)}) %reduce-scatter.4.cloned.1.call-update) | async-done | bytes 2621456 | tf_op jit(solution)/shard_map/reduce_scatter | solution.py:22
  1130.9 74.3 %all-gather.7.cloned.1.call-done = bf16[2560,1024]{1,0:T(8,128)(2,1)} async-done(((bf16[640,1024]{1,0:T(8,128)(2,1)}), bf16[2560,1024]{1,0:T(8,128)(2,1)}) %all-gather.7.cloned.1.call-update) | async-done | bytes 5242896 | tf_op jit(solution)/shard_map/all_gather | solution.py:18
  1244.1 147.2 %all_to_all.20 = bf16[4,1600,1024]{2,1,0:T(8,128)(2,1)S(1)} all-to-all(bf16[4,1600,1024]{2,1,0:T(8,128)(2,1)S(1)} %select_select_fusion.1), channel_id=1, replica_groups=mesh['expert'=4,'shard'=4,'dp'=2] {'expert'}, dimensions={0} | all-to-all | bytes 26214400 | tf_op jit(solution)/shard_map/all_to_all | solution.py:219
  1482.6 141.5 %all-to-all-done.1 = bf16[4,1600,1024]{2,1,0:T(8,128)(2,1)} async-done(((bf16[4,1600,1024]{2,1,0:T(8,128)(2,1)}), bf16[4,1600,1024]{2,1,0:T(8,128)(2,1)}, u32[]{:S(2)}, u32[]{:S(2)}) %all-to-all-start.1) | async-done | bytes 13107232 | tf_op jit(solution)/shard_map/all_to_all | solution.py:222
  1697.8 341.2 %all-reduce.8.cloned.1.call-done = bf16[2560,2,1024]{2,1,0:T(2,128)(2,1)} async-done(((bf16[2560,2,1024]{2,1,0:T(2,128)(2,1)}), bf16[2560,2,1024]{2,1,0:T(2,128)(2,1)}) %all-reduce.8.cloned.1.call-update) | async-done | bytes 10485776
  2062.2 182.9 %all-gather.9.cloned.1.call-done = bf16[2560,2,1024]{2,1,0:T(2,128)(2,1)} async-done(((bf16[640,2,1024]{2,1,0:T(2,128)(2,1)}), bf16[2560,2,1024]{2,1,0:T(2,128)(2,1)}) %all-gather.9.cloned.1.call-update) | async-done | bytes 10485776 | tf_op jit(solution)/shard_map/all_gather | solution.py:18
  2261.1 33.6 gather_fusion.1
  2302.1 148.2 %all_to_all.21 = bf16[4,1600,1024]{2,1,0:T(8,128)(2,1)} all-to-all(bf16[4,1600,1024]{2,1,0:T(8,128)(2,1)S(1)} %select_select_fusion), channel_id=1, replica_groups=mesh['expert'=4,'shard'=4,'dp'=2] {'expert'}, dimensions={0} | all-to-all | bytes 26214400 | tf_op jit(solution)/shard_map/all_to_all | solution.py:245
  2450.3 36.8 multiply_convert_fusion.1
  2522.6 147.3 %all_to_all.22 = bf16[4,1600,1024]{2,1,0:T(8,128)(2,1)S(1)} all-to-all(bf16[4,1600,1024]{2,1,0:T(8,128)(2,1)} %bitcast.493), channel_id=1, replica_groups=mesh['expert'=4,'shard'=4,'dp'=2] {'expert'}, dimensions={0} | all-to-all | bytes 26214400 | tf_op jit(solution)/shard_map/all_to_all | solution.py:250
  2679.2 36.1 gather_fusion.3
  2802.3 72.3 %reduce-scatter.6.cloned.1.call-done = bf16[640,1024]{1,0:T(8,128)(2,1)} async-done(((bf16[2560,1024]{1,0:T(8,128)(2,1)}), bf16[640,1024]{1,0:T(8,128)(2,1)}) %reduce-scatter.6.cloned.1.call-update) | async-done | bytes 1310736 | tf_op jit(solution)/shard_map/reduce_scatter | solution.py:256
  2919.1 66.1 %all-gather.11.cloned.1.call-done = bf16[2560,1024]{1,0:T(8,128)(2,1)} async-done(((bf16[640,1024]{1,0:T(8,128)(2,1)}), bf16[2560,1024]{1,0:T(8,128)(2,1)}) %all-gather.11.cloned.1.call-update) | async-done | bytes 5242896 | tf_op jit(solution)/shard_map/all_gather | solution.py:18
  2995.7 1529.1 %while.30 = (s32[]{:T(128)}, f32[2560,4,64]{0,2,1:T(8,128)}, f32[2560,4,64]{0,2,1:T(8,128)}, f32[32,4]{0,1:T(4,128)}, bf16[5,512,4,64]{1,3,2,0:T(8,128)(2,1)}, /...) while((s32[]{:T(128)}, f32[2560,4,64]{0,2,1:T(8,128)}, ...), condition=%wide.region_62.64_spmd.clone, body=%wide.region_28.63_spmd.clone.sunk | while | flops 4204394752 | bytes 443175776 | solution.py:321
  3009.1 38.6 or_and_fusion.5
  3047.8 98.0 %multiply_reduce_fusion.6 = (f32[4,512]{1,0:T(4,128)S(1)}, f32[4,512,2560]{2,1,0:T(8,128)}) fusion(f32[4,512,2560]{2,1,0:T(8,128)} %fusion.231, f32[4,512]{1,0:T(4,128)S(1)} %dynamic-slice_bitcast_fusion.3, f32[4]{0:T(128)S(1)} %get-tuple-element.1138, pred[512,2560]{1,0:T(8,128)(4,1)} %get-tuple-element.1120, f32[4]{0:T(128)S(1)} %get-tuple-element.1139, ...), kind=kOutput, calls=%fused_computation.167.clone.2 | convolution fusion | flops 1032845312 | bytes 86786560 | tf_op jit(solution)/shard_map/while/body/eval_jaxpr/qhd,khd->hqk/dot_general | solution.py:157
  3145.8 78.7 %fusion.232 = (f32[4]{0:T(128)S(1)}, f32[4]{0:T(128)S(1)}, f32[4]{0:T(128)S(1)}, f32[4]{0:T(128)S(1)}, f32[4]{0:T(128)S(1)}, /*index=5*/f32[4]{0:T(128)S(1)}, f3...) fusion(pred[512,2560]{1,0:T(8,128)(4,1)} %get-tuple-element.112, ...), kind=kLoop, calls=%fused_computation.165.clone.1 | loop fusion | flops 209715184 | bytes 76030240 | tf_op jit(solution)/shard_map/while/body/eval_jaxpr/reduce_sum | solution.py:310
  3236.9 43.8 fusion.235
  3312.5 38.6 or_and_fusion.5
  3351.2 98.0 %multiply_reduce_fusion.6 = (f32[4,512]{1,0:T(4,128)S(1)}, f32[4,512,2560]{2,1,0:T(8,128)}) fusion(f32[4,512,2560]{2,1,0:T(8,128)} %fusion.231, f32[4,512]{1,0:T(4,128)S(1)} %dynamic-slice_bitcast_fusion.3, f32[4]{0:T(128)S(1)} %get-tuple-element.1138, pred[512,2560]{1,0:T(8,128)(4,1)} %get-tuple-element.1120, f32[4]{0:T(128)S(1)} %get-tuple-element.1139, ...), kind=kOutput, calls=%fused_computation.167.clone.2 | convolution fusion | flops 1032845312 | bytes 86786560 | tf_op jit(solution)/shard_map/while/body/eval_jaxpr/qhd,khd->hqk/dot_general | solution.py:157
  3449.2 78.7 %fusion.232 = (f32[4]{0:T(128)S(1)}, f32[4]{0:T(128)S(1)}, f32[4]{0:T(128)S(1)}, f32[4]{0:T(128)S(1)}, f32[4]{0:T(128)S(1)}, /*index=5*/f32[4]{0:T(128)S(1)}, f3...) fusion(pred[512,2560]{1,0:T(8,128)(4,1)} %get-tuple-element.112, ...), kind=kLoop, calls=%fused_computation.165.clone.1 | loop fusion | flops 209715184 | bytes 76030240 | tf_op jit(solution)/shard_map/while/body/eval_jaxpr/reduce_sum | solution.py:310
  3541.0 43.8 fusion.235
  3616.7 38.6 or_and_fusion.5
  3655.4 98.0 %multiply_reduce_fusion.6 = (f32[4,512]{1,0:T(4,128)S(1)}, f32[4,512,2560]{2,1,0:T(8,128)}) fusion(f32[4,512,2560]{2,1,0:T(8,128)} %fusion.231, f32[4,512]{1,0:T(4,128)S(1)} %dynamic-slice_bitcast_fusion.3, f32[4]{0:T(128)S(1)} %get-tuple-element.1138, pred[512,2560]{1,0:T(8,128)(4,1)} %get-tuple-element.1120, f32[4]{0:T(128)S(1)} %get-tuple-element.1139, ...), kind=kOutput, calls=%fused_computation.167.clone.2 | convolution fusion | flops 1032845312 | bytes 86786560 | tf_op jit(solution)/shard_map/while/body/eval_jaxpr/qhd,khd->hqk/dot_general | solution.py:157
  3753.4 78.7 %fusion.232 = (f32[4]{0:T(128)S(1)}, f32[4]{0:T(128)S(1)}, f32[4]{0:T(128)S(1)}, f32[4]{0:T(128)S(1)}, f32[4]{0:T(128)S(1)}, /*index=5*/f32[4]{0:T(128)S(1)}, f3...) fusion(pred[512,2560]{1,0:T(8,128)(4,1)} %get-tuple-element.112, ...), kind=kLoop, calls=%fused_computation.165.clone.1 | loop fusion | flops 209715184 | bytes 76030240 | tf_op jit(solution)/shard_map/while/body/eval_jaxpr/reduce_sum | solution.py:310
  3845.2 43.8 fusion.235
  3920.8 38.6 or_and_fusion.5
  3959.5 98.0 %multiply_reduce_fusion.6 = (f32[4,512]{1,0:T(4,128)S(1)}, f32[4,512,2560]{2,1,0:T(8,128)}) fusion(f32[4,512,2560]{2,1,0:T(8,128)} %fusion.231, f32[4,512]{1,0:T(4,128)S(1)} %dynamic-slice_bitcast_fusion.3, f32[4]{0:T(128)S(1)} %get-tuple-element.1138, pred[512,2560]{1,0:T(8,128)(4,1)} %get-tuple-element.1120, f32[4]{0:T(128)S(1)} %get-tuple-element.1139, ...), kind=kOutput, calls=%fused_computation.167.clone.2 | convolution fusion | flops 1032845312 | bytes 86786560 | tf_op jit(solution)/shard_map/while/body/eval_jaxpr/qhd,khd->hqk/dot_general | solution.py:157
  4057.6 78.7 %fusion.232 = (f32[4]{0:T(128)S(1)}, f32[4]{0:T(128)S(1)}, f32[4]{0:T(128)S(1)}, f32[4]{0:T(128)S(1)}, f32[4]{0:T(128)S(1)}, /*index=5*/f32[4]{0:T(128)S(1)}, f3...) fusion(pred[512,2560]{1,0:T(8,128)(4,1)} %get-tuple-element.112, ...), kind=kLoop, calls=%fused_computation.165.clone.1 | loop fusion | flops 209715184 | bytes 76030240 | tf_op jit(solution)/shard_map/while/body/eval_jaxpr/reduce_sum | solution.py:310
  4149.4 43.8 fusion.235
  4225.0 38.6 or_and_fusion.5
  4263.7 98.0 %multiply_reduce_fusion.6 = (f32[4,512]{1,0:T(4,128)S(1)}, f32[4,512,2560]{2,1,0:T(8,128)}) fusion(f32[4,512,2560]{2,1,0:T(8,128)} %fusion.231, f32[4,512]{1,0:T(4,128)S(1)} %dynamic-slice_bitcast_fusion.3, f32[4]{0:T(128)S(1)} %get-tuple-element.1138, pred[512,2560]{1,0:T(8,128)(4,1)} %get-tuple-element.1120, f32[4]{0:T(128)S(1)} %get-tuple-element.1139, ...), kind=kOutput, calls=%fused_computation.167.clone.2 | convolution fusion | flops 1032845312 | bytes 86786560 | tf_op jit(solution)/shard_map/while/body/eval_jaxpr/qhd,khd->hqk/dot_general | solution.py:157
  4361.8 78.7 %fusion.232 = (f32[4]{0:T(128)S(1)}, f32[4]{0:T(128)S(1)}, f32[4]{0:T(128)S(1)}, f32[4]{0:T(128)S(1)}, f32[4]{0:T(128)S(1)}, /*index=5*/f32[4]{0:T(128)S(1)}, f3...) fusion(pred[512,2560]{1,0:T(8,128)(4,1)} %get-tuple-element.112, ...), kind=kLoop, calls=%fused_computation.165.clone.1 | loop fusion | flops 209715184 | bytes 76030240 | tf_op jit(solution)/shard_map/while/body/eval_jaxpr/reduce_sum | solution.py:310
  4453.6 43.8 fusion.235
  4619.2 171.3 %reduce-scatter.8.cloned.1.call-done = f32[640,1024]{1,0:T(8,128)} async-done(((f32[2560,1024]{1,0:T(8,128)}), f32[640,1024]{1,0:T(8,128)}) %reduce-scatter.8.cloned.1.call-update) | async-done | bytes 2621456 | tf_op jit(solution)/shard_map/reduce_scatter | solution.py:22
  4793.2 42.0 all-reduce.1
  (944 shorter events, 930.1 us)
Async XLA Ops:
  7.2 1451.6 %copy-start = (bf16[1,704,1024]{2,1,0:T(8,128)(2,1)S(1)}, bf16[1,704,1024]{2,1,0:T(8,128)(2,1)}, u32[]{:S(2)}) copy-start(bf16[1,704,1024]{2,1,0:T(8,128)(2,1)} %param.41) | copy-start | bytes 4325380
  7.3 106.1 %copy-start.57 = (bf16[1024,256]{1,0:T(8,128)(2,1)S(1)}, bf16[1024,256]{1,0:T(8,128)(2,1)}, u32[]{:S(2)}) copy-start(bf16[1024,256]{1,0:T(8,128)(2,1)} %param.32) | copy-start | bytes 1572868
  7.3 106.1 %all-gather.5.cloned.1.call-start = ((), (), s32[]{:S(2)}) async-start(), calls=%async_computation.7 | async-start | bytes 6553600 | tf_op jit(solution)/shard_map/all_gather | solution.py:18
  12.4 1088.5 %reduce-scatter.4.cloned.1.call-start = ((), (), s32[]{:S(2)}) async-start(), calls=%async_computation.8 | async-start | bytes 13107200 | tf_op jit(solution)/shard_map/reduce_scatter | solution.py:22
  924.3 176.6 %copy-start.22 = (bf16[1,640,1024]{2,1,0:T(8,128)(2,1)S(1)}, bf16[1,640,1024]{2,1,0:T(8,128)(2,1)}, u32[]{:S(2)}) copy-start(bf16[1,640,1024]{2,1,0:T(8,128)(2,1)} %param.24) | copy-start | bytes 3932164
  924.4 180.2 %copy-start.108 = (f32[1024]{0:T(1024)S(1)}, f32[1024]{0:T(1024)}, u32[]{:S(2)}) copy-start(f32[1024]{0:T(1024)} %param.37) | copy-start | bytes 12292
  924.4 181.6 %copy-start.70 = (s32[1,2560,2]{1,2,0:T(2,128)S(1)}, s32[1,2560,2]{1,2,0:T(2,128)}, u32[]{:S(2)}) copy-start(s32[1,2560,2]{1,2,0:T(2,128)} %param.30) | copy-start | bytes 61444
  924.4 280.8 %all-gather.7.cloned.1.call-start = ((), (), s32[]{:S(2)}) async-start(), calls=%async_computation.9 | async-start | bytes 6553600 | tf_op jit(solution)/shard_map/all_gather | solution.py:18
  1130.0 106.6 %copy-start.64 = (s32[6400]{0:T(1024)}, s32[6400]{0:T(1024)S(1)}, u32[]{:S(2)}) copy-start(s32[6400]{0:T(1024)S(1)} %scatter_custom_fusion) | copy-start | bytes 76804
  1130.8 105.8 %copy-start.98 = (pred[4,1600]{1,0:T(4,128)(4,1)}, pred[4,1600]{1,0:T(4,128)(4,1)S(1)}, u32[]{:S(2)}) copy-start(pred[4,1600]{1,0:T(4,128)(4,1)S(1)} %broadcast_in_dim.1260) | copy-start | bytes 19204
  1244.1 152.0 %copy-start.116 = (bf16[1,1024,704]{1,2,0:T(8,128)(2,1)S(1)}, bf16[1,1024,704]{1,2,0:T(8,128)(2,1)}, u32[]{:S(2)}) copy-start(bf16[1,1024,704]{1,2,0:T(8,128)(2,1)} %param.39) | copy-start | bytes 4325380
  1476.1 148.1 %all-to-all-start.1 = ((bf16[4,1600,1024]{2,1,0:T(8,128)(2,1)}), bf16[4,1600,1024]{2,1,0:T(8,128)(2,1)}, u32[]{:S(2)}, u32[]{:S(2)}) async-start(bf16[4,1600,1024]{2,1,0:T(8,128)(2,1)} %convolution_convert_fusion), calls=%async_computation.2 | async-start | bytes 26214400 | tf_op jit(solution)/shard_map/all_to_all | solution.py:222
  1482.5 556.4 %all-reduce.8.cloned.1.call-start = ((), (), s32[]{:S(2)}) async-start(), calls=%async_computation.14 | async-start | bytes 20971520
  1482.6 173.7 %copy-start.104 = (pred[5120]{0:T(1024)(128)(4,1)}, pred[5120]{0:T(1024)(128)(4,1)S(1)}, u32[]{:S(2)}) copy-start(pred[5120]{0:T(1024)(128)(4,1)S(1)} %compare_and_fusion.1) | copy-start | bytes 15364
  1482.6 173.7 %copy-start.66 = (s32[5120]{0:T(1024)}, s32[5120]{0:T(1024)S(1)}, u32[]{:S(2)}) copy-start(s32[5120]{0:T(1024)S(1)} %broadcast_clamp_fusion) | copy-start | bytes 61444
  1682.9 562.2 %all-gather.9.cloned.1.call-start = ((), (), s32[]{:S(2)}) async-start(), calls=%async_computation.10 | async-start | bytes 13107200 | tf_op jit(solution)/shard_map/all_gather | solution.py:18
  1694.5 357.8 %copy-start.106 = (f32[640]{0:T(1024)}, f32[640]{0:T(1024)S(1)}, u32[]{:S(2)}) copy-start(f32[640]{0:T(1024)S(1)} %convert_reduce_fusion) | copy-start | bytes 7684
  1696.3 353.0 %copy-start.37 = (bf16[1,640,1024]{2,1,0:T(8,128)(2,1)S(1)}, bf16[1,640,1024]{2,1,0:T(8,128)(2,1)}, u32[]{:S(2)}) copy-start(bf16[1,640,1024]{2,1,0:T(8,128)(2,1)} %param.25) | copy-start | bytes 3932164
  2062.0 812.7 %reduce-scatter.6.cloned.1.call-start = ((), (), s32[]{:S(2)}) async-start(), calls=%async_computation.11 | async-start | bytes 6553600 | tf_op jit(solution)/shard_map/reduce_scatter | solution.py:256
  2784.0 201.2 %all-gather.11.cloned.1.call-start = ((), (), s32[]{:S(2)}) async-start(), calls=%async_computation.12 | async-start | bytes 6553600 | tf_op jit(solution)/shard_map/all_gather | solution.py:18
  2886.5 1679.6 %all-reduce.12.cloned.1.call-start = ((), (), s32[]{:S(2)}) async-start(), calls=%async_computation.16 | async-start | bytes 8650752 | tf_op jit(solution)/shard_map/psum | solution.py:260
  2919.0 1691.8 %all-reduce.10.cloned.1.call-start = ((), (), s32[]{:S(2)}) async-start(), calls=%async_computation.15 | async-start | bytes 4194304 | tf_op jit(solution)/shard_map/psum | solution.py:350
  3047.7 98.1 %copy-start.3 = (pred[512,2560]{1,0:T(8,128)(4,1)}, pred[512,2560]{1,0:T(8,128)(4,1)S(1)}, u32[]{:S(2)}) copy-start(pred[512,2560]{1,0:T(8,128)(4,1)S(1)} %get-tuple-element.1160) | copy-start | bytes 3932164 | tf_op jit(solution)/shard_map/while
  3047.7 98.1 %copy-start.5 = (pred[512,2560]{1,0:T(8,128)(4,1)}, pred[512,2560]{1,0:T(8,128)(4,1)S(1)}, u32[]{:S(2)}) copy-start(pred[512,2560]{1,0:T(8,128)(4,1)S(1)} %get-tuple-element.1158) | copy-start | bytes 3932164 | tf_op jit(solution)/shard_map/while
  3047.7 98.1 %copy-start.7 = (pred[512,2560]{1,0:T(8,128)(4,1)}, pred[512,2560]{1,0:T(8,128)(4,1)S(1)}, u32[]{:S(2)}) copy-start(pred[512,2560]{1,0:T(8,128)(4,1)S(1)} %get-tuple-element.1156) | copy-start | bytes 3932164 | tf_op jit(solution)/shard_map/while
  3655.3 98.1 %copy-start.3 = (pred[512,2560]{1,0:T(8,128)(4,1)}, pred[512,2560]{1,0:T(8,128)(4,1)S(1)}, u32[]{:S(2)}) copy-start(pred[512,2560]{1,0:T(8,128)(4,1)S(1)} %get-tuple-element.1160) | copy-start | bytes 3932164 | tf_op jit(solution)/shard_map/while
  3655.3 98.1 %copy-start.5 = (pred[512,2560]{1,0:T(8,128)(4,1)}, pred[512,2560]{1,0:T(8,128)(4,1)S(1)}, u32[]{:S(2)}) copy-start(pred[512,2560]{1,0:T(8,128)(4,1)S(1)} %get-tuple-element.1158) | copy-start | bytes 3932164 | tf_op jit(solution)/shard_map/while
  3655.3 98.1 %copy-start.7 = (pred[512,2560]{1,0:T(8,128)(4,1)}, pred[512,2560]{1,0:T(8,128)(4,1)S(1)}, u32[]{:S(2)}) copy-start(pred[512,2560]{1,0:T(8,128)(4,1)S(1)} %get-tuple-element.1156) | copy-start | bytes 3932164 | tf_op jit(solution)/shard_map/while
  3655.3 98.1 %copy-start.9 = (pred[512,2560]{1,0:T(8,128)(4,1)}, pred[512,2560]{1,0:T(8,128)(4,1)S(1)}, u32[]{:S(2)}) copy-start(pred[512,2560]{1,0:T(8,128)(4,1)S(1)} %get-tuple-element.1154) | copy-start | bytes 3932164 | tf_op jit(solution)/shard_map/while
  3655.3 98.1 %copy-start.11 = (pred[512,2560]{1,0:T(8,128)(4,1)}, pred[512,2560]{1,0:T(8,128)(4,1)S(1)}, u32[]{:S(2)}) copy-start(pred[512,2560]{1,0:T(8,128)(4,1)S(1)} %get-tuple-element.1152) | copy-start | bytes 3932164 | tf_op jit(solution)/shard_map/while
  3655.3 98.1 %copy-start.12 = (pred[512,2560]{1,0:T(8,128)(4,1)}, pred[512,2560]{1,0:T(8,128)(4,1)S(1)}, u32[]{:S(2)}) copy-start(pred[512,2560]{1,0:T(8,128)(4,1)S(1)} %get-tuple-element.1150) | copy-start | bytes 3932164 | tf_op jit(solution)/shard_map/while
  3959.5 98.1 %copy-start.3 = (pred[512,2560]{1,0:T(8,128)(4,1)}, pred[512,2560]{1,0:T(8,128)(4,1)S(1)}, u32[]{:S(2)}) copy-start(pred[512,2560]{1,0:T(8,128)(4,1)S(1)} %get-tuple-element.1160) | copy-start | bytes 3932164 | tf_op jit(solution)/shard_map/while
  3959.5 98.1 %copy-start.5 = (pred[512,2560]{1,0:T(8,128)(4,1)}, pred[512,2560]{1,0:T(8,128)(4,1)S(1)}, u32[]{:S(2)}) copy-start(pred[512,2560]{1,0:T(8,128)(4,1)S(1)} %get-tuple-element.1158) | copy-start | bytes 3932164 | tf_op jit(solution)/shard_map/while
  3959.5 98.1 %copy-start.7 = (pred[512,2560]{1,0:T(8,128)(4,1)}, pred[512,2560]{1,0:T(8,128)(4,1)S(1)}, u32[]{:S(2)}) copy-start(pred[512,2560]{1,0:T(8,128)(4,1)S(1)} %get-tuple-element.1156) | copy-start | bytes 3932164 | tf_op jit(solution)/shard_map/while
  3959.5 98.1 %copy-start.9 = (pred[512,2560]{1,0:T(8,128)(4,1)}, pred[512,2560]{1,0:T(8,128)(4,1)S(1)}, u32[]{:S(2)}) copy-start(pred[512,2560]{1,0:T(8,128)(4,1)S(1)} %get-tuple-element.1154) | copy-start | bytes 3932164 | tf_op jit(solution)/shard_map/while
  3959.5 98.1 %copy-start.11 = (pred[512,2560]{1,0:T(8,128)(4,1)}, pred[512,2560]{1,0:T(8,128)(4,1)S(1)}, u32[]{:S(2)}) copy-start(pred[512,2560]{1,0:T(8,128)(4,1)S(1)} %get-tuple-element.1152) | copy-start | bytes 3932164 | tf_op jit(solution)/shard_map/while
  3959.5 98.1 %copy-start.12 = (pred[512,2560]{1,0:T(8,128)(4,1)}, pred[512,2560]{1,0:T(8,128)(4,1)S(1)}, u32[]{:S(2)}) copy-start(pred[512,2560]{1,0:T(8,128)(4,1)S(1)} %get-tuple-element.1150) | copy-start | bytes 3932164 | tf_op jit(solution)/shard_map/while
  4263.6 98.1 %copy-start.3 = (pred[512,2560]{1,0:T(8,128)(4,1)}, pred[512,2560]{1,0:T(8,128)(4,1)S(1)}, u32[]{:S(2)}) copy-start(pred[512,2560]{1,0:T(8,128)(4,1)S(1)} %get-tuple-element.1160) | copy-start | bytes 3932164 | tf_op jit(solution)/shard_map/while
  4263.7 98.1 %copy-start.5 = (pred[512,2560]{1,0:T(8,128)(4,1)}, pred[512,2560]{1,0:T(8,128)(4,1)S(1)}, u32[]{:S(2)}) copy-start(pred[512,2560]{1,0:T(8,128)(4,1)S(1)} %get-tuple-element.1158) | copy-start | bytes 3932164 | tf_op jit(solution)/shard_map/while
  4263.7 98.1 %copy-start.7 = (pred[512,2560]{1,0:T(8,128)(4,1)}, pred[512,2560]{1,0:T(8,128)(4,1)S(1)}, u32[]{:S(2)}) copy-start(pred[512,2560]{1,0:T(8,128)(4,1)S(1)} %get-tuple-element.1156) | copy-start | bytes 3932164 | tf_op jit(solution)/shard_map/while
  4263.7 98.1 %copy-start.9 = (pred[512,2560]{1,0:T(8,128)(4,1)}, pred[512,2560]{1,0:T(8,128)(4,1)S(1)}, u32[]{:S(2)}) copy-start(pred[512,2560]{1,0:T(8,128)(4,1)S(1)} %get-tuple-element.1154) | copy-start | bytes 3932164 | tf_op jit(solution)/shard_map/while
  4263.7 98.1 %copy-start.11 = (pred[512,2560]{1,0:T(8,128)(4,1)}, pred[512,2560]{1,0:T(8,128)(4,1)S(1)}, u32[]{:S(2)}) copy-start(pred[512,2560]{1,0:T(8,128)(4,1)S(1)} %get-tuple-element.1152) | copy-start | bytes 3932164 | tf_op jit(solution)/shard_map/while
  4263.7 98.1 %copy-start.12 = (pred[512,2560]{1,0:T(8,128)(4,1)}, pred[512,2560]{1,0:T(8,128)(4,1)S(1)}, u32[]{:S(2)}) copy-start(pred[512,2560]{1,0:T(8,128)(4,1)S(1)} %get-tuple-element.1150) | copy-start | bytes 3932164 | tf_op jit(solution)/shard_map/while
  4551.0 239.5 %reduce-scatter.8.cloned.1.call-start = ((), (), s32[]{:S(2)}) async-start(), calls=%async_computation.13 | async-start | bytes 13107200 | tf_op jit(solution)/shard_map/reduce_scatter | solution.py:22
  4571.5 219.0 %copy-start.23 = (bf16[1,640,1024]{2,1,0:T(8,128)(2,1)S(1)}, bf16[1,640,1024]{2,1,0:T(8,128)(2,1)}, u32[]{:S(2)}) copy-start(bf16[1,640,1024]{2,1,0:T(8,128)(2,1)} %param.24) | copy-start | bytes 3932164
  4571.5 219.0 %copy-start.91 = (f32[640]{0:T(1024)S(1)}, f32[640]{0:T(1024)}, u32[]{:S(2)}) copy-start(f32[640]{0:T(1024)} %copy-done.90) | copy-start | bytes 7684
  4571.5 219.0 %copy-start.110 = (f32[1024]{0:T(1024)S(1)}, f32[1024]{0:T(1024)}, u32[]{:S(2)}) copy-start(f32[1024]{0:T(1024)} %param.31) | copy-start | bytes 12292
  4573.5 219.7 %copy-start.112 = (f32[1024]{0:T(1024)S(1)}, f32[1024]{0:T(1024)}, u32[]{:S(2)}) copy-start(f32[1024]{0:T(1024)} %get-tuple-element.438) | copy-start | bytes 12292
  (226 other events, 4301.7 us)
Sparse Core Ops, SparseCore 0:
  12.6 100.7 all-gather.4
  924.5 176.3 reduce-scatter.3
  1106.1 99.0 all-gather.6
  1683.0 355.9 all-reduce.7
  2062.1 182.8 all-gather.8
  2784.1 90.4 reduce-scatter.5
  2886.6 98.5 all-gather.10
  2988.0 27.2 all-reduce.11
  4551.2 59.6 all-reduce.9
  4613.2 177.3 reduce-scatter.7
where the time goes:
time: 4860 us; the launch traced here: 4850 us
  matrix products  1410 us (29%)
  waiting for transfers between devices  1350 us (28%)
  other arithmetic  1210 us (25%)
  blocking collectives  506 us (10%)
  local copies, waits for them, and re-layouts  315 us (6%)
    dot_general x10, matrix products, score_block(): jnp.einsum('qhd,khd->hqk', query_block, key_rows, preferred_element_type=...  948 us
    reduce_sum x10, other arithmetic, backward_block(): jnp.sum(jnp.where((bucket == number)[None], score_wide, 0.0), axis=(1, 2))  612 us
    all_gather x4, waiting for transfers between devices, gather_rows(): return lax.all_gather(values, 'shard', axis=0, tiled=True)  424 us
    and x10, other arithmetic, score_block(): key_allow[None, :] & (depths[None, :] <= query_depth[:, None])  399 us
    reduce_scatter x2, waiting for transfers between devices, reduce_rows(): return lax.psum_scatter(values, 'shard', scatter_dimension=0, tiled=True)  348 us
    unnamed x11, waiting for transfers between devices  341 us
    all_to_all x1, blocking collectives, on_device(): lax.all_to_all(send_grads, 'expert', split_axis=0, concat_axis=0, tiled=T...  148 us
    all_to_all x1, blocking collectives, on_device(): lax.all_to_all(rows_grad.astype(jnp.bfloat16), 'expert', split_axis=0, co...  147 us
  transfers between devices with their start and end apart: 11, of which 10 were waited for; matrix products, arithmetic and copies ran while one was open for 34% of the time, Pallas kernels for 0%

commit v1 on v0

v1 whole, which is shorter than its diff:
```python
import functools
import math

import jax
import jax.numpy as jnp
from jax import lax
from jax.experimental import pallas as pl
from jax.experimental.pallas import tpu as pltpu
from jax.sharding import PartitionSpec as P

TRUNK, SEGMENT, NBRANCH, NLEAF = 1024, 128, 4, 2
TILE = 128
TRUNK_TILES = TRUNK // TILE
HEAD_DIM = 64
MASKED = -1e30
DIAG, SUB, FAR, NONE, BRANCH_NEAR, LEAF_NEAR, LEAF_BRANCH = 0, 1, 2, 3, 4, 6, 14
CLASSES = 18
LIMIT_AT, OFFSET_AT = 0, 32


def head_rows(block, heads):
    lane = lax.broadcasted_iota(jnp.int32, block.shape, 1) // HEAD_DIM
    return jnp.concatenate(
        [jnp.where(lane == h, block, jnp.zeros((), block.dtype)) for h in range(heads)], axis=0
    )


def fill_bias(info, table, bias, heads):
    rows = lax.broadcasted_iota(jnp.int32, (TILE, TILE), 0)
    lanes = lax.broadcasted_iota(jnp.int32, (TILE, TILE), 1)

    def one(number, carry):
        place = jnp.clip(info[OFFSET_AT + number] + lanes - rows, 0, TILE - 1)
        hidden = ((number == DIAG) & (rows > lanes)) | (number == NONE)
        for h in range(heads):
            line = jnp.broadcast_to(table[h : h + 1, :], (TILE, TILE))
            values = jnp.take_along_axis(line, place, axis=1)
            bias[number, :, h * TILE : (h + 1) * TILE] = jnp.where(hidden, MASKED, values)
        return carry

    lax.fori_loop(0, CLASSES, one, 0)


def tile_plan(i, info):
    last = info[LIMIT_AT + 20]
    trunk = i < TRUNK_TILES
    place = jnp.maximum(i - TRUNK_TILES, 0)
    branch = place // (1 + NLEAF)
    leaf = (place % (1 + NLEAF)) > 0
    branch_tile = TRUNK_TILES + branch * (1 + NLEAF)
    near = jnp.where(trunk, i, last)
    tiles = jnp.minimum(near, last) + 1
    near_class = jnp.where(trunk, DIAG, jnp.where(leaf, LEAF_NEAR + branch, BRANCH_NEAR))
    next_class = jnp.where(trunk, SUB, jnp.where(leaf, LEAF_NEAR + NBRANCH + branch, BRANCH_NEAR + 1))
    trunk_steps = (tiles + 1) // 2
    steps = trunk_steps + jnp.where(trunk, 0, 1)
    tail = (
        (jnp.where(leaf, branch_tile, i), jnp.where(leaf, LEAF_BRANCH + branch, DIAG)),
        (i, jnp.where(leaf, DIAG, NONE)),
    )

    def tile_of(step, half):
        kt = step * 2 + half
        in_trunk = step < trunk_steps
        kind = jnp.where(
            kt == near, near_class, jnp.where(kt == near - 1, next_class, jnp.where(kt < near, FAR, NONE))
        )
        return jnp.where(in_trunk, kt, tail[half][0]), jnp.where(in_trunk, kind, tail[half][1])

    return steps, tile_of


def masked_scores(scores, half, tile, kind, info, bias, heads):
    rows = lax.broadcasted_iota(jnp.int32, (TILE, TILE), 0)
    shade = jnp.where(rows < info[LIMIT_AT + tile], 0.0, MASKED)
    shade = jnp.concatenate([shade] * heads, axis=1)
    return scores[half * TILE : (half + 1) * TILE] + bias[kind] + shade


def rows_at(ref, tile):
    return ref[pl.ds(pl.multiple_of(tile * TILE, TILE), TILE), :]


def lanes_at(ref, first, count, tile):
    return ref[first : first + count, pl.ds(pl.multiple_of(tile * TILE, TILE), TILE)]


def forward_kernel(info, table, q, k, v_t, out, log_total, bias, score, total_out, *, heads):
    i = pl.program_id(0)

    @pl.when(i == 0)
    def _():
        fill_bias(info, table, bias, heads)

    steps, tile_of = tile_plan(i, info)
    queries = head_rows(q[...] * jnp.bfloat16(0.125), heads)
    width = heads * TILE

    def first(step, highest):
        (ta, ka), (tb, kb) = tile_of(step, 0), tile_of(step, 1)
        keys = jnp.concatenate([rows_at(k, ta), rows_at(k, tb)], axis=0)
        raw = lax.dot_general(keys, queries, (((1,), (1,)), ((), ())), preferred_element_type=jnp.float32)
        both = jnp.concatenate(
            [masked_scores(raw, 0, ta, ka, info, bias, heads), masked_scores(raw, 1, tb, kb, info, bias, heads)],
            axis=0,
        )
        score[pl.ds(pl.multiple_of(step * 2 * TILE, 2 * TILE), 2 * TILE), :] = both
        return jnp.maximum(highest, jnp.max(both.reshape(2 * TILE // 8, 8, width), axis=0))

    highest = lax.fori_loop(0, steps, first, jnp.full((8, width), MASKED, jnp.float32))
    highest = jnp.max(highest, axis=0, keepdims=True)
    total_out[...] = jnp.zeros_like(total_out)
    pairs = heads // 2

    def second(step, total):
        (ta, _), (tb, _) = tile_of(step, 0), tile_of(step, 1)
        part = jnp.exp(score[pl.ds(pl.multiple_of(step * 2 * TILE, 2 * TILE), 2 * TILE), :] - highest)
        low = part.astype(jnp.bfloat16)
        for p in range(pairs):
            values = jnp.concatenate(
                [lanes_at(v_t, p * TILE, TILE, ta), lanes_at(v_t, p * TILE, TILE, tb)], axis=1
            )
            total_out[p] += jnp.dot(
                values, low[:, p * 2 * TILE : (p + 1) * 2 * TILE], preferred_element_type=jnp.float32
            )
        return total + jnp.sum(part.reshape(2 * TILE // 8, 8, width), axis=0)

    total = lax.fori_loop(0, steps, second, jnp.zeros((8, width), jnp.float32))
    total = jnp.sum(total, axis=0, keepdims=True)
    inverse = 1.0 / total
    for h in range(heads):
        p, odd = h // 2, h % 2
        block = total_out[p, odd * HEAD_DIM : (odd + 1) * HEAD_DIM, odd * TILE : (odd + 1) * TILE]
        out[h * HEAD_DIM : (h + 1) * HEAD_DIM, :] = (
            block * inverse[:, h * TILE : (h + 1) * TILE]
        ).astype(jnp.bfloat16)
    log_total[0] = highest + jnp.log(total)


def attention_forward(info, table, q, k, v_t):
    length, columns = q.shape
    heads = columns // HEAD_DIM
    tiles = length // TILE
    width = heads * TILE
    whole = lambda shape: pl.BlockSpec(shape, lambda i, info: (0,) * len(shape))
    return pl.pallas_call(
        functools.partial(forward_kernel, heads=heads),
        grid_spec=pltpu.PrefetchScalarGridSpec(
            num_scalar_prefetch=1,
            grid=(tiles,),
            in_specs=[
                whole(table.shape),
                pl.BlockSpec((TILE, columns), lambda i, info: (i, 0)),
                whole(k.shape),
                whole(v_t.shape),
            ],
            out_specs=[
                pl.BlockSpec((columns, TILE), lambda i, info: (0, i)),
                pl.BlockSpec((1, 1, width), lambda i, info: (i, 0, 0)),
            ],
            scratch_shapes=[
                pltpu.VMEM((CLASSES, TILE, width), jnp.float32),
                pltpu.VMEM((10 * TILE, width), jnp.float32),
                pltpu.VMEM((heads // 2, TILE, 2 * TILE), jnp.float32),
            ],
        ),
        out_shape=[
            jax.ShapeDtypeStruct((columns, length), jnp.bfloat16),
            jax.ShapeDtypeStruct((tiles, 1, width), jnp.float32),
        ],
        compiler_params=pltpu.CompilerParams(
            dimension_semantics=("arbitrary",), vmem_limit_bytes=50 << 20
        ),
        name="attention_forward",
    )(info, table, q, k, v_t)


def backward_kernel(
    info, table, q, k, k_t, v, grad, attended_t, log_total,
    grad_q, grad_k, grad_v, ahead, behind,
    bias, by_class, total_q, total_k, total_v, *, heads, tiles,
):
    i = pl.program_id(0)
    width = heads * TILE

    @pl.when(i == 0)
    def _():
        fill_bias(info, table, bias, heads)
        by_class[...] = jnp.zeros_like(by_class)
        total_k[...] = jnp.zeros_like(total_k)
        total_v[...] = jnp.zeros_like(total_v)

    steps, tile_of = tile_plan(i, info)
    queries = head_rows(q[...] * jnp.bfloat16(0.125), heads)
    grads = head_rows(grad[...], heads)
    product = jnp.transpose(grad[...].astype(jnp.float32)) * attended_t[...].astype(jnp.float32)
    centre = jnp.concatenate(
        [
            jnp.sum(product[h * HEAD_DIM : (h + 1) * HEAD_DIM], axis=0, keepdims=True)
            for h in range(heads)
        ],
        axis=1,
    )
    logs = log_total[0]
    total_q[...] = jnp.zeros_like(total_q)
    pairs = heads // 2

    def one(step, carry):
        (ta, ka), (tb, kb) = tile_of(step, 0), tile_of(step, 1)
        keys = jnp.concatenate([rows_at(k, ta), rows_at(k, tb)], axis=0)
        values = jnp.concatenate([rows_at(v, ta), rows_at(v, tb)], axis=0)
        raw = lax.dot_general(keys, queries, (((1,), (1,)), ((), ())), preferred_element_type=jnp.float32)
        both = jnp.concatenate(
            [masked_scores(raw, 0, ta, ka, info, bias, heads), masked_scores(raw, 1, tb, kb, info, bias, heads)],
            axis=0,
        )
        probs = jnp.exp(both - logs)
        grad_probs = lax.dot_general(
            values, grads, (((1,), (1,)), ((), ())), preferred_element_type=jnp.float32
        )
        grad_scores = probs * (grad_probs - centre)
        by_class[ka] += grad_scores[:TILE]
        by_class[kb] += grad_scores[TILE:]
        low = grad_scores.astype(jnp.bfloat16)
        value_part = jnp.dot(probs.astype(jnp.bfloat16), grads, preferred_element_type=jnp.float32)
        key_part = jnp.dot(low, queries, preferred_element_type=jnp.float32)
        for half, tile in ((0, ta), (1, tb)):
            at = pl.ds(pl.multiple_of(tile * TILE, TILE), TILE)
            total_v[at, :] += value_part[half * TILE : (half + 1) * TILE]
            total_k[at, :] += key_part[half * TILE : (half + 1) * TILE]
        for p in range(pairs):
            keys_t = jnp.concatenate(
                [lanes_at(k_t, p * TILE, TILE, ta), lanes_at(k_t, p * TILE, TILE, tb)], axis=1
            )
            total_q[p] += jnp.dot(
                keys_t, low[:, p * 2 * TILE : (p + 1) * 2 * TILE], preferred_element_type=jnp.float32
            )
        return carry

    lax.fori_loop(0, steps, one, 0)
    for h in range(heads):
        p, odd = h // 2, h % 2
        block = total_q[p, odd * HEAD_DIM : (odd + 1) * HEAD_DIM, odd * TILE : (odd + 1) * TILE]
        grad_q[h * HEAD_DIM : (h + 1) * HEAD_DIM, :] = (block * 0.125).astype(jnp.bfloat16)

    @pl.when(i == tiles - 1)
    def _():
        grad_k[...] = total_k[...].astype(jnp.bfloat16)
        grad_v[...] = total_v[...].astype(jnp.bfloat16)
        rows = lax.broadcasted_iota(jnp.int32, (TILE, TILE), 0)
        lanes = lax.broadcasted_iota(jnp.int32, (TILE, TILE), 1)

        def reduce(number, carry):
            for h in range(heads):
                block = by_class[number, :, h * TILE : (h + 1) * TILE]
                turned = jnp.take_along_axis(block, (rows + lanes) % TILE, axis=1)
                forward = jnp.sum(jnp.where(rows + lanes < TILE, turned, 0.0), axis=0, keepdims=True)
                wrapped = jnp.sum(jnp.where(rows + lanes < TILE, 0.0, turned), axis=0, keepdims=True)
                ahead[number, :, h * TILE : (h + 1) * TILE] = forward
                behind[number, :, h * TILE : (h + 1) * TILE] = wrapped
            return carry

        lax.fori_loop(0, CLASSES, reduce, 0)


def attention_backward(info, table, q, k, k_t, v, grad, attended_t, log_total):
    length, columns = q.shape
    heads = columns // HEAD_DIM
    tiles = length // TILE
    width = heads * TILE
    whole = lambda shape: pl.BlockSpec(shape, lambda i, info: (0,) * len(shape))
    rows = pl.BlockSpec((TILE, columns), lambda i, info: (i, 0))
    lanes = pl.BlockSpec((columns, TILE), lambda i, info: (0, i))
    return pl.pallas_call(
        functools.partial(backward_kernel, heads=heads, tiles=tiles),
        grid_spec=pltpu.PrefetchScalarGridSpec(
            num_scalar_prefetch=1,
            grid=(tiles,),
            in_specs=[
                whole(table.shape), rows, whole(k.shape), whole(k_t.shape), whole(v.shape), rows, lanes,
                pl.BlockSpec((1, 1, width), lambda i, info: (i, 0, 0)),
            ],
            out_specs=[
                lanes, whole(k.shape), whole(v.shape),
                whole((CLASSES, 1, width)), whole((CLASSES, 1, width)),
            ],
            scratch_shapes=[
                pltpu.VMEM((CLASSES, TILE, width), jnp.float32),
                pltpu.VMEM((CLASSES, TILE, width), jnp.float32),
                pltpu.VMEM((heads // 2, TILE, 2 * TILE), jnp.float32),
                pltpu.VMEM((length, columns), jnp.float32),
                pltpu.VMEM((length, columns), jnp.float32),
            ],
        ),
        out_shape=[
            jax.ShapeDtypeStruct((columns, length), jnp.bfloat16),
            jax.ShapeDtypeStruct((length, columns), jnp.bfloat16),
            jax.ShapeDtypeStruct((length, columns), jnp.bfloat16),
            jax.ShapeDtypeStruct((CLASSES, 1, width), jnp.float32),
            jax.ShapeDtypeStruct((CLASSES, 1, width), jnp.float32),
        ],
        compiler_params=pltpu.CompilerParams(
            dimension_semantics=("arbitrary",), vmem_limit_bytes=56 << 20
        ),
        name="attention_backward",
    )(info, table, q, k, k_t, v, grad, attended_t, log_total)


def bucket_index(distance, bucket_count, max_dist=128):
    half_count = bucket_count // 2
    counted = jnp.zeros_like(distance)
    for number in range(1, bucket_count - half_count):
        border = math.ceil(half_count * (max_dist / half_count) ** (number / (bucket_count - half_count)))
        counted = counted + (distance >= border).astype(jnp.int32)
    return jnp.where(distance < half_count, distance, half_count + counted)


def attention_info(validity):
    trunk = jnp.sum(validity[:TRUNK])
    lengths = jnp.sum(validity[TRUNK:].reshape(NBRANCH, 1 + NLEAF, SEGMENT), axis=2)
    last = (trunk - 1) // TILE
    limits = jnp.concatenate([trunk - TILE * jnp.arange(TRUNK_TILES), lengths.reshape(-1)])
    left = trunk - last * TILE
    branch = lengths[:, 0]
    offsets = jnp.concatenate(
        [
            jnp.array([0, TILE, 4096, 0]),
            jnp.stack([left, left + TILE]),
            left + branch,
            left + branch + TILE,
            branch,
        ]
    )
    info = jnp.zeros((64,), jnp.int32)
    info = info.at[:20].set(limits).at[20].set(last).at[OFFSET_AT : OFFSET_AT + CLASSES].set(offsets)
    return info, offsets


def bias_table(rel_bias):
    places = bucket_index(jnp.arange(TILE, dtype=jnp.int32), rel_bias.shape[0])
    pick = (places[:, None] == jnp.arange(rel_bias.shape[0])[None, :]).astype(jnp.float32)
    shifted = rel_bias - rel_bias[-1:]
    return jnp.einsum("db,bh->hd", pick, shifted, precision=lax.Precision.HIGHEST)


def bias_gradient(ahead, behind, offsets, bucket_count):
    heads = ahead.shape[2] // TILE
    lane = jnp.arange(TILE, dtype=jnp.int32)[None, :]
    distance = jnp.stack([offsets[:, None] + lane, offsets[:, None] + lane - TILE], axis=0)
    bucket = bucket_index(jnp.maximum(distance, 0), bucket_count)
    pick = (bucket[..., None] == jnp.arange(bucket_count)).astype(jnp.float32)
    sums = jnp.stack([ahead, behind], axis=0).reshape(2, CLASSES, heads, TILE)
    return jnp.einsum("sclb,schl->bh", pick, sums, precision=lax.Precision.HIGHEST)


EPSILON = 1e-06
SLOT_TILE = 256


def compact_kernel(bounds, slots, scale, rows, out):
    block = pl.program_id(0)

    @pl.when(block == 0)
    def _():
        out[...] = jnp.zeros_like(out)

    values = rows[0]
    if scale is not None:
        values = (scale[0] * values.astype(jnp.float32)).astype(jnp.bfloat16)
    count = values.shape[0]
    places = lax.broadcasted_iota(jnp.int32, (SLOT_TILE, count), 0)

    def one(tile, carry):
        pick = (slots[0] - tile * SLOT_TILE == places).astype(jnp.float32).astype(jnp.bfloat16)
        at = pl.ds(pl.multiple_of(tile * SLOT_TILE, SLOT_TILE), SLOT_TILE)
        part = jnp.dot(pick, values, preferred_element_type=jnp.float32)
        out[at, :] += part.astype(jnp.bfloat16)
        return carry

    lax.fori_loop(bounds[block] // SLOT_TILE, pl.cdiv(bounds[block + 1], SLOT_TILE), one, 0)


def compact(bounds, slots, rows, scale=None):
    blocks, count, width = rows.shape
    padded = pl.cdiv(blocks * count, SLOT_TILE) * SLOT_TILE
    specs = [
        pl.BlockSpec((1, 1, count), lambda b, bounds: (b, 0, 0)),
        pl.BlockSpec((1, count, 1), lambda b, bounds: (b, 0, 0)),
        pl.BlockSpec((1, count, width), lambda b, bounds: (b, 0, 0)),
    ]
    body = compact_kernel
    operands = (slots.reshape(blocks, 1, count), scale, rows)
    if scale is None:
        body = lambda bounds, slots, rows, out: compact_kernel(bounds, slots, None, rows, out)
        specs = [specs[0], specs[2]]
        operands = (operands[0], rows)
    return pl.pallas_call(
        body,
        grid_spec=pltpu.PrefetchScalarGridSpec(
            num_scalar_prefetch=1,
            grid=(blocks,),
            in_specs=specs,
            out_specs=pl.BlockSpec(
                (padded, width), lambda b, bounds: (0, 0), pipeline_mode=pl.Buffered(1)
            ),
        ),
        out_shape=jax.ShapeDtypeStruct((padded, width), jnp.bfloat16),
        compiler_params=pltpu.CompilerParams(vmem_limit_bytes=48 << 20),
        name="compact",
    )(bounds, *operands)


def expand_kernel(bounds, slots, rows, out):
    block = pl.program_id(0)
    count = out.shape[1]
    out[0] = jnp.zeros(out.shape[1:], out.dtype)
    places = lax.broadcasted_iota(jnp.int32, (count, SLOT_TILE), 1)

    def one(tile, carry):
        pick = (slots[0] - tile * SLOT_TILE == places).astype(jnp.float32).astype(jnp.bfloat16)
        at = pl.ds(pl.multiple_of(tile * SLOT_TILE, SLOT_TILE), SLOT_TILE)
        part = jnp.dot(pick, rows[at, :].astype(jnp.bfloat16), preferred_element_type=jnp.float32)
        out[0] += part.astype(jnp.bfloat16)
        return carry

    lax.fori_loop(bounds[block] // SLOT_TILE, pl.cdiv(bounds[block + 1], SLOT_TILE), one, 0)


def expand(bounds, slots, rows):
    blocks, count = slots.shape
    padded, width = rows.shape
    return pl.pallas_call(
        expand_kernel,
        grid_spec=pltpu.PrefetchScalarGridSpec(
            num_scalar_prefetch=1,
            grid=(blocks,),
            in_specs=[
                pl.BlockSpec((1, count, 1), lambda b, bounds: (b, 0, 0)),
                pl.BlockSpec((padded, width), lambda b, bounds: (0, 0), pipeline_mode=pl.Buffered(1)),
            ],
            out_specs=pl.BlockSpec((1, count, width), lambda b, bounds: (b, 0, 0)),
        ),
        out_shape=jax.ShapeDtypeStruct((blocks, count, width), jnp.bfloat16),
        compiler_params=pltpu.CompilerParams(vmem_limit_bytes=48 << 20),
        name="expand",
    )(bounds, slots.reshape(blocks, count, 1), rows)


GELU_IN = math.sqrt(2.0 / math.pi)
GELU_CUBE = 0.044715


def gelu_parts(pre):
    square = pre * pre
    bent = jnp.tanh(GELU_IN * pre * (1.0 + GELU_CUBE * square))
    half = 0.5 * (1.0 + bent)
    return pre * half, half, bent, square


def expert_forward_kernel(bounds, rows, gate_w, up_w, down_w, total):
    step = pl.program_id(0)
    columns = gate_w.shape[-1]
    width = rows.shape[1]

    def one(tile, carry):
        at = pl.ds(pl.multiple_of(tile * SLOT_TILE, SLOT_TILE), SLOT_TILE)
        values = rows[at, :]
        gate_pre = jnp.dot(values, gate_w[...].reshape(width, columns), preferred_element_type=jnp.float32)
        up_pre = jnp.dot(values, up_w[...].reshape(width, columns), preferred_element_type=jnp.float32)
        inner = (gelu_parts(gate_pre)[0] * up_pre).astype(jnp.bfloat16)
        part = jnp.dot(inner, down_w[...].reshape(columns, width), preferred_element_type=jnp.float32)

        @pl.when(step == 0)
        def _():
            total[at, :] = part

        @pl.when(step > 0)
        def _():
            total[at, :] += part

        return carry

    lax.fori_loop(0, pl.cdiv(bounds[bounds.shape[0] - 1], SLOT_TILE), one, 0)


def weight_spec(array):
    halves, shards, rows, columns = array.shape
    return pl.BlockSpec((halves, 1, rows, columns), lambda s, bounds: (0, s, 0, 0))


def expert_forward(bounds, rows, gate_w, up_w, down_w):
    padded, width = rows.shape
    whole = pl.BlockSpec((padded, width), lambda s, bounds: (0, 0), pipeline_mode=pl.Buffered(1))
    return pl.pallas_call(
        expert_forward_kernel,
        grid_spec=pltpu.PrefetchScalarGridSpec(
            num_scalar_prefetch=1,
            grid=(gate_w.shape[1],),
            in_specs=[whole, weight_spec(gate_w), weight_spec(up_w), weight_spec(down_w)],
            out_specs=whole,
        ),
        out_shape=jax.ShapeDtypeStruct((padded, width), jnp.float32),
        compiler_params=pltpu.CompilerParams(vmem_limit_bytes=56 << 20),
        name="expert_forward",
    )(bounds, rows, gate_w, up_w, down_w)


def expert_backward_kernel(
    bounds, rows, grads, gate_w, up_w, down_w,
    gate_out, up_out, down_out, total,
    gate_total, up_total, down_total,
):
    step = pl.program_id(0)
    columns = gate_w.shape[-1]
    width = rows.shape[1]
    gate_total[...] = jnp.zeros_like(gate_total)
    up_total[...] = jnp.zeros_like(up_total)
    down_total[...] = jnp.zeros_like(down_total)
    first = (((0,), (0,)), ((), ()))
    last = (((1,), (1,)), ((), ()))

    def one(tile, carry):
        at = pl.ds(pl.multiple_of(tile * SLOT_TILE, SLOT_TILE), SLOT_TILE)
        values, upstream = rows[at, :], grads[at, :]
        gate_m = gate_w[...].reshape(width, columns)
        up_m = up_w[...].reshape(width, columns)
        down_m = down_w[...].reshape(columns, width)
        gate_pre = jnp.dot(values, gate_m, preferred_element_type=jnp.float32)
        up_pre = jnp.dot(values, up_m, preferred_element_type=jnp.float32)
        grad_inner = lax.dot_general(upstream, down_m, last, preferred_element_type=jnp.float32)
        active, half, bent, square = gelu_parts(gate_pre)
        slope = half + (0.5 * GELU_IN) * gate_pre * (1.0 - bent * bent) * (1.0 + 3.0 * GELU_CUBE * square)
        inner = (active * up_pre).astype(jnp.bfloat16)
        grad_gate = (grad_inner * up_pre * slope).astype(jnp.bfloat16)
        grad_up = (grad_inner * active).astype(jnp.bfloat16)
        down_total[...] += lax.dot_general(inner, upstream, first, preferred_element_type=jnp.float32)
        gate_total[...] += lax.dot_general(values, grad_gate, first, preferred_element_type=jnp.float32)
        up_total[...] += lax.dot_general(values, grad_up, first, preferred_element_type=jnp.float32)
        part = lax.dot_general(grad_gate, gate_m, last, preferred_element_type=jnp.float32)
        part = part + lax.dot_general(grad_up, up_m, last, preferred_element_type=jnp.float32)

        @pl.when(step == 0)
        def _():
            total[at, :] = part

        @pl.when(step > 0)
        def _():
            total[at, :] += part

        return carry

    lax.fori_loop(0, pl.cdiv(bounds[bounds.shape[0] - 1], SLOT_TILE), one, 0)
    gate_out[0] = gate_total[...].astype(jnp.bfloat16)
    up_out[0] = up_total[...].astype(jnp.bfloat16)
    down_out[0] = down_total[...].astype(jnp.bfloat16)


def expert_backward(bounds, rows, grads, gate_w, up_w, down_w):
    padded, width = rows.shape
    shards, columns = gate_w.shape[1], gate_w.shape[3]
    whole = pl.BlockSpec((padded, width), lambda s, bounds: (0, 0), pipeline_mode=pl.Buffered(1))
    wide = pl.BlockSpec((1, width, columns), lambda s, bounds: (s, 0, 0))
    tall = pl.BlockSpec((1, columns, width), lambda s, bounds: (s, 0, 0))
    return pl.pallas_call(
        expert_backward_kernel,
        grid_spec=pltpu.PrefetchScalarGridSpec(
            num_scalar_prefetch=1,
            grid=(shards,),
            in_specs=[whole, whole, weight_spec(gate_w), weight_spec(up_w), weight_spec(down_w)],
            out_specs=[wide, wide, tall, whole],
            scratch_shapes=[
                pltpu.VMEM((width, columns), jnp.float32),
                pltpu.VMEM((width, columns), jnp.float32),
                pltpu.VMEM((columns, width), jnp.float32),
            ],
        ),
        out_shape=[
            jax.ShapeDtypeStruct((shards, width, columns), jnp.bfloat16),
            jax.ShapeDtypeStruct((shards, width, columns), jnp.bfloat16),
            jax.ShapeDtypeStruct((shards, columns, width), jnp.bfloat16),
            jax.ShapeDtypeStruct((padded, width), jnp.float32),
        ],
        compiler_params=pltpu.CompilerParams(vmem_limit_bytes=60 << 20),
        name="expert_backward",
    )(bounds, rows, grads, gate_w, up_w, down_w)


def split_float(values):
    high = values.astype(jnp.bfloat16)
    rest = values - high.astype(jnp.float32)
    middle = rest.astype(jnp.bfloat16)
    low = (rest - middle.astype(jnp.float32)).astype(jnp.bfloat16)
    return jnp.concatenate([high, middle, low], axis=1)


def join_float(products, count):
    return products[:, 2 * count :] + products[:, count : 2 * count] + products[:, :count]


def gather_weight(weight):
    cores = lax.axis_size("dp")
    half = weight.shape[0] // cores
    mine = lax.dynamic_slice_in_dim(weight, lax.axis_index("dp") * half, half, 0)
    return lax.all_gather(lax.all_gather(mine, "shard", axis=0), "dp", axis=0)


def scatter_weight_grad(parts):
    cores = lax.axis_size("dp")
    shards, rows, columns = parts.shape
    parts = parts.reshape(shards, cores, rows // cores, columns)
    mine = lax.psum_scatter(parts, "dp", scatter_dimension=1, tiled=False)
    mine = lax.psum_scatter(mine, "shard", scatter_dimension=0, tiled=False)
    return lax.all_gather(mine, "dp", axis=0, tiled=True).astype(jnp.float32)


def on_device(
    tokens, teacher, seg_ids, parents, depth, valid, routes, norm1_gain, w_query, w_key, w_value,
    w_out, rel_bias, norm2_gain, router, w_gate, w_up, w_down,
):
    shard_index = lax.axis_index("shard")
    expert_index = lax.axis_index("expert")
    shards = lax.axis_size("shard")
    columns = lax.axis_size("expert")
    experts = columns * w_gate.shape[0]
    token_rows = tokens[0].astype(jnp.float32)
    local_rows, width = token_rows.shape
    length = seg_ids.shape[1]
    heads_here = rel_bias.shape[1]
    bucket_count = rel_bias.shape[0]
    validity = valid[0]
    route_rows = routes[0]
    head_columns = w_query.shape[1]

    row_start = shard_index * local_rows
    valid_local = lax.dynamic_slice_in_dim(validity, row_start, local_rows, 0).astype(jnp.float32)
    route_local = lax.dynamic_slice_in_dim(route_rows, row_start, local_rows, 0)

    scale_one = lax.rsqrt(jnp.mean(token_rows * token_rows, axis=1, keepdims=True) + EPSILON)
    base_one = token_rows * scale_one
    normed_one = (base_one * norm1_gain).astype(jnp.bfloat16)
    normed_all = lax.all_gather(normed_one, "shard", axis=0, tiled=True)
    out_all = lax.all_gather(w_out, "shard", axis=0, tiled=True)
    gate_all = gather_weight(w_gate[0])
    up_all = gather_weight(w_up[0])
    down_all = gather_weight(w_down[0])
    valid_total = lax.psum(jnp.sum(validity), ("expert", "dp")).astype(jnp.float32)

    route_all = lax.all_gather(route_local, "expert", axis=0)
    taken = jnp.any(route_all == expert_index, axis=2)
    order = jnp.cumsum(taken.reshape(-1).astype(jnp.int32))
    slots = jnp.where(taken, order.reshape(taken.shape) - 1, -1)
    bounds = jnp.concatenate([jnp.zeros((1,), jnp.int32), order[local_rows - 1 :: local_rows]])

    info, offsets = attention_info(validity)
    table = bias_table(rel_bias)
    weights = jnp.concatenate([w_query, w_key, w_value], axis=1)
    projected = jnp.dot(normed_all, weights, preferred_element_type=jnp.float32).astype(jnp.bfloat16)
    query_rows, key_rows, value_rows = jnp.split(projected, 3, axis=1)
    attended_t, log_totals = attention_forward(info, table, query_rows, key_rows, value_rows.T)

    pieces = attended_t.reshape(head_columns, shards, local_rows).transpose(1, 0, 2)
    pieces = lax.all_to_all(pieces, "shard", split_axis=0, concat_axis=0, tiled=True)
    attended_here = pieces.reshape(shards * head_columns, local_rows)
    update = lax.dot_general(
        attended_here, out_all, (((0,), (0,)), ((), ())), preferred_element_type=jnp.float32
    )
    hidden = token_rows + update
    scale_two = lax.rsqrt(jnp.mean(hidden * hidden, axis=1, keepdims=True) + EPSILON)
    base_two = hidden * scale_two
    normed_two = (base_two * norm2_gain).astype(jnp.bfloat16)

    expert_ids = jnp.arange(experts, dtype=jnp.int32)
    router_pieces = split_float(router)

    def gates_of(rows, named):
        logits = join_float(jnp.dot(rows, router_pieces, preferred_element_type=jnp.float32), experts)
        match = named[:, :, None] == expert_ids[None, None, :]
        chosen = jnp.sum(jnp.where(match, logits[:, None, :], 0.0), axis=2)
        return jax.nn.softmax(chosen, axis=1), match

    gates, route_match = gates_of(normed_two, route_local)
    normed_layer = lax.all_gather(normed_two, "expert", axis=0)
    route_flat = route_all.reshape(columns * local_rows, -1)
    gates_layer, _ = gates_of(normed_layer.reshape(columns * local_rows, width), route_flat)
    gate_here = jnp.sum(jnp.where(route_flat == expert_index, gates_layer, 0.0), axis=1)
    gate_here = gate_here.reshape(columns, local_rows, 1)
    expert_rows = compact(bounds, slots, normed_layer)
    produced = expert_forward(bounds, expert_rows, gate_all, up_all, down_all)
    produced_layer = expand(bounds, slots, produced)
    shares = (gate_here * produced_layer.astype(jnp.float32)).astype(jnp.bfloat16)
    combined = lax.psum_scatter(shares, "expert", scatter_dimension=0, tiled=False).astype(jnp.float32)

    output_rows = hidden + combined
    factor = length * columns * lax.axis_size("dp") / valid_total
    error = output_rows - teacher[0].astype(jnp.float32)
    error_sum = jnp.sum(valid_local[:, None] * error * error)
    grad_output = valid_local[:, None] * error * factor
    grad_layer = lax.all_gather(grad_output.astype(jnp.bfloat16), "expert", axis=0)
    gate_grads = jnp.sum(grad_layer.astype(jnp.float32) * produced_layer.astype(jnp.float32), axis=2)
    gate_grads = lax.all_to_all(gate_grads, "expert", split_axis=0, concat_axis=0, tiled=True)
    grad_rows = compact(bounds, slots, grad_layer, gate_here)
    gate_part, up_part, down_part, rows_grad = expert_backward(
        bounds, expert_rows, grad_rows, gate_all, up_all, down_all
    )
    expert_back = lax.psum_scatter(
        expand(bounds, slots, rows_grad), "expert", scatter_dimension=0, tiled=False
    ).astype(jnp.float32)
    gate_grad = scatter_weight_grad(gate_part)
    up_grad = scatter_weight_grad(up_part)
    down_grad = scatter_weight_grad(down_part)

    grad_gates = jnp.sum(jnp.where(route_match, gate_grads.T[:, None, :], 0.0), axis=2)
    weighted = jnp.sum(gates * grad_gates, axis=1, keepdims=True)
    grad_chosen = gates * (grad_gates - weighted)
    grad_logits = jnp.sum(jnp.where(route_match, grad_chosen[:, :, None], 0.0), axis=1)
    router_grad = join_float(
        lax.dot_general(
            normed_two, split_float(grad_logits), (((0,), (0,)), ((), ())),
            preferred_element_type=jnp.float32,
        ),
        experts,
    )
    grad_normed_two = expert_back
    for number in range(experts):
        grad_normed_two = grad_normed_two + grad_logits[:, number : number + 1] * router[:, number][None]
    grad_base_two = grad_normed_two * norm2_gain
    norm2_grad = jnp.sum(grad_normed_two * base_two, axis=0)
    grad_hidden = grad_output + scale_two * (
        grad_base_two - base_two * jnp.mean(grad_base_two * base_two, axis=1, keepdims=True)
    )
    grad_update = grad_hidden.astype(jnp.bfloat16)
    out_grad = jnp.dot(attended_here, grad_update, preferred_element_type=jnp.float32)
    grad_heads = lax.dot_general(
        grad_update, out_all, (((1,), (1,)), ((), ())), preferred_element_type=jnp.float32
    ).astype(jnp.bfloat16)
    grad_heads = grad_heads.reshape(local_rows, shards, head_columns).transpose(1, 0, 2)
    grad_attended = lax.all_to_all(
        grad_heads, "shard", split_axis=0, concat_axis=0, tiled=True
    ).reshape(length, head_columns)

    grad_queries_t, grad_keys, grad_values, ahead, behind = attention_backward(
        info, table, query_rows, key_rows, key_rows.T, value_rows, grad_attended, attended_t, log_totals
    )
    bias_grad = bias_gradient(ahead, behind, offsets, bucket_count)
    across = (((0,), (0,)), ((), ()))
    grad_three = jnp.concatenate([grad_queries_t.T, grad_keys, grad_values], axis=1)
    three_wgrad = lax.dot_general(normed_all, grad_three, across, preferred_element_type=jnp.float32)
    grad_normed_all = lax.dot_general(
        grad_three, weights, (((1,), (1,)), ((), ())), preferred_element_type=jnp.float32
    )
    grad_normed_one = lax.psum_scatter(
        grad_normed_all.astype(jnp.bfloat16), "shard", scatter_dimension=0, tiled=True
    ).astype(jnp.float32)
    grad_base_one = grad_normed_one * norm1_gain
    norm1_grad = jnp.sum(grad_normed_one * base_one, axis=0)
    grad_tokens = grad_hidden + scale_one * (
        grad_base_one - base_one * jnp.mean(grad_base_one * base_one, axis=1, keepdims=True)
    )
    out_grad = lax.psum_scatter(
        out_grad.astype(jnp.bfloat16), "shard", scatter_dimension=0, tiled=True
    )
    three_wgrad, out_grad, bias_grad = lax.psum(
        (three_wgrad.astype(jnp.bfloat16), out_grad, bias_grad.astype(jnp.bfloat16)), ("expert", "dp")
    )
    three_wgrad, out_grad, bias_grad = (
        value.astype(jnp.float32) for value in (three_wgrad, out_grad, bias_grad)
    )
    query_wgrad, key_wgrad, value_wgrad = jnp.split(three_wgrad, 3, axis=1)
    router_grad, norm1_grad, norm2_grad, error_total = lax.psum(
        (router_grad, norm1_grad, norm2_grad, error_sum), ("expert", "shard", "dp")
    )
    loss = error_total / (width * valid_total)
    return (
        output_rows.astype(jnp.bfloat16)[None],
        loss,
        grad_tokens[None],
        norm1_grad,
        query_wgrad,
        key_wgrad,
        value_wgrad,
        out_grad,
        bias_grad,
        norm2_grad,
        router_grad,
        gate_grad[None],
        up_grad[None],
        down_grad[None],
    )


def solution(mesh):
    in_specs = (
        P(("expert", "dp"), "shard", None),
        P(("expert", "dp"), "shard", None),
        P(("expert", "dp"), None),
        P(("expert", "dp"), None),
        P(("expert", "dp"), None),
        P(("expert", "dp"), None),
        P(("expert", "dp"), None, None),
        P(),
        P(None, "shard"),
        P(None, "shard"),
        P(None, "shard"),
        P("shard", None),
        P(None, "shard"),
        P(),
        P(),
        P("expert", None, "shard"),
        P("expert", None, "shard"),
        P("expert", "shard", None),
    )
    out_specs = (
        P(("expert", "dp"), "shard", None),
        P(),
        P(("expert", "dp"), "shard", None),
        P(),
        P(None, "shard"),
        P(None, "shard"),
        P(None, "shard"),
        P("shard", None),
        P(None, "shard"),
        P(),
        P(),
        P("expert", None, "shard"),
        P("expert", None, "shard"),
        P("expert", "shard", None),
    )
    return jax.shard_map(
        on_device, mesh=mesh, in_specs=in_specs, out_specs=out_specs, check_vma=False
    )
```

time: 4860 us -> 1430 us (0.29)
  matrix products: 1410 us -> 40.2 us
  other arithmetic: 1210 us -> 49.7 us
  waiting for transfers between devices: 1350 us -> 870 us
  blocking collectives: 506 us -> 92.2 us
  local copies, waits for them, and re-layouts: 315 us -> 71.7 us
  Pallas kernels: 0 us -> 225 us
    dot_general x59 -> x11, matrix products: 1410 us -> 40.2 us  [the longest x1 8.83 us: on_device(): lax.dot_general(normed_all, grad_three, across, preferred_element_type=jn...]
    reduce_sum x25 -> x9, other arithmetic: 711 us -> 7.25 us  [the longest x1 5.6 us: on_device(): jnp.sum(grad_layer.astype(jnp.float32) * produced_layer.astype(jnp.float3...]
    all_to_all x3 -> x0, blocking collectives: 443 us -> none  [the longest x1 148 us: on_device(): lax.all_to_all(send_grads, 'expert', split_axis=0, concat_axis=0, tiled=T...]
    and x12 -> x0, other arithmetic: 399 us -> none  [the longest x10 399 us: score_block(): key_allow[None, :] & (depths[None, :] <= query_depth[:, None])]
    unnamed x11 -> x26, waiting for transfers between devices: 341 us -> 76.2 us
    pallas_call x0 -> x8, Pallas kernels: none -> 225 us  [the longest x1 73.7 us: expert_backward(): pl.pallas_call(expert_backward_kernel, grid_spec=pltpu.PrefetchScalarGrid...]
    reduce_scatter x3 -> x8, waiting for transfers between devices: 420 us -> 248 us  [the longest x3 117 us: scatter_weight_grad(): mine = lax.psum_scatter(mine, 'shard', scatter_dimension=0, tiled=False)]
    gather x4 -> x0, local copies, waits for them, and re-layouts: 133 us -> none  [the longest x1 36.1 us: on_device(): jnp.take(grad_back.reshape(experts * capacity, width), target, axis=0)]
  transfers between devices with their start and end apart: 11 -> 27, of which waited for: 10 -> 24; matrix products, arithmetic and copies ran while one was open for 34% -> 10% of each run, Pallas kernels for 0% -> 6%
where the time goes in v1:
time: 1430 us; the launch traced here: 1410 us
  waiting for transfers between devices  870 us (61%)
  Pallas kernels  225 us (16%)
  blocking collectives  92.2 us (6%)
  local copies, waits for them, and re-layouts  71.7 us (5%)
  other arithmetic  49.7 us (3%)
  starting transfers between devices  44.7 us (3%)
  matrix products  40.2 us (3%)
  between operations  19.2 us (1%)
    all_gather x6, waiting for transfers between devices, gather_weight(): return lax.all_gather(lax.all_gather(mine, 'shard', axis=0), 'dp', axis=0)  135 us
    reduce_scatter x3, waiting for transfers between devices, scatter_weight_grad(): mine = lax.psum_scatter(mine, 'shard', scatter_dimension=0, tiled=False)  117 us
    all_gather x1, waiting for transfers between devices, on_device(): normed_all = lax.all_gather(normed_one, 'shard', axis=0, tiled=True)  98.2 us
    reduce_scatter x1, waiting for transfers between devices, on_device(): lax.psum_scatter(grad_normed_all.astype(jnp.bfloat16), 'shard', scatter_d...  93.8 us
    unnamed x26, waiting for transfers between devices  76.2 us
    pallas_call x1, Pallas kernels, expert_backward(): pl.pallas_call(expert_backward_kernel, grid_spec=pltpu.PrefetchScalarGrid...  73.7 us
    all_to_all x1, waiting for transfers between devices, on_device(): lax.all_to_all(pieces, 'shard', split_axis=0, concat_axis=0, tiled=True)  65 us
    all_to_all x1, waiting for transfers between devices, on_device(): lax.all_to_all(grad_heads, 'shard', split_axis=0, concat_axis=0, tiled=True)  61.3 us
  transfers between devices with their start and end apart: 27, of which 24 were waited for; matrix products, arithmetic and copies ran while one was open for 10% of the time, Pallas kernels for 6%

profile of v1, /device:TPU:0, one launch (start us, length us, event | category | flops | bytes accessed | tf_op | source)
XLA Modules:
  0.0 1412.7 jit_solution(17959412185683713843)
XLA Ops:
  15.1 57.0 %all-gather.26.cloned.1.call-done = bf16[4,512,704]{1,2,0:T(8,128)(2,1)} async-done(((bf16[1,512,704]{1,2,0:T(8,128)(2,1)}), bf16[4,512,704]{1,2,0:T(8,128)(2,1)}) %all-gather.26.cloned.1.call-update) | async-done | bytes 2883600 | tf_op jit(solution)/shard_map/all_gather | solution.py:604
  75.4 56.7 %all-gather.28.cloned.1.call-done = bf16[4,512,704]{1,2,0:T(8,128)(2,1)} async-done(((bf16[1,512,704]{1,2,0:T(8,128)(2,1)}), bf16[4,512,704]{1,2,0:T(8,128)(2,1)}) %all-gather.28.cloned.1.call-update) | async-done | bytes 2883600 | tf_op jit(solution)/shard_map/all_gather | solution.py:604
  132.8 98.2 %all-gather.22.cloned.1.call-done = bf16[2560,1024]{1,0:T(8,128)(2,1)} async-done(((bf16[640,1024]{1,0:T(8,128)(2,1)}), bf16[2560,1024]{1,0:T(8,128)(2,1)}) %all-gather.22.cloned.1.call-update) | async-done | bytes 5242896 | tf_op jit(solution)/shard_map/all_gather | solution.py:641
  231.1 7.1 convolution_convert_fusion.1
  243.6 33.8 %attention_forward.1 = (bf16[256,2560]{1,0:T(8,128)(2,1)S(1)}, f32[20,1,512]{2,1,0:T(1,128)S(1)}) custom-call(s32[64]{0:T(128)S(1)} %constant_dynamic-update-slice_fusion.3.info, f32[4,128]{1,0:T(4,128)S(1)} %fusion.28.table, bf16[2560,256]{1,0:T(8,128)(2,1)S(1)} %get-tuple-element.101.q, bf16[2560,256]{1,0:T(8,128)(2,1)S(1)} %get-tuple-element.100.k, ...), custom_call_target="tpu_custom_call" | custom-call | tf_op jit(solution)/shard_map/attention_forward/pallas_call | solution.py:146
  283.3 65.0 %all-to-all-done = bf16[4,256,640]{2,1,0:T(8,128)(2,1)S(1)} async-done(((bf16[4,256,640]{2,1,0:T(8,128)(2,1)}), bf16[4,256,640]{2,1,0:T(8,128)(2,1)S(1)}, u32[]{:S(2)}, u32[]{:S(2)}) %all-to-all-start) | async-done | bytes 1310752 | tf_op jit(solution)/shard_map/all_to_all | solution.py:662
  355.0 6.6 all-gather.30.cloned.1.call-done
  361.8 14.9 %all_gather.63 = s32[4,640,2]{1,2,0:T(2,128)S(1)} all-gather(s32[1,640,2]{1,2,0:T(2,128)S(1)} %constant_dynamic-slice_fusion.3), channel_id=1, replica_groups=mesh['expert'=4,'shard'=4,'dp'=2] {'expert'}, dimensions={0}, use_global_device_ids=true | all-gather | bytes 25600 | tf_op jit(solution)/shard_map/all_gather | solution.py:648
  380.5 8.4 copy.151
  388.9 10.3 all-gather.36.cloned.1.call-done
  399.2 8.4 copy.152
  407.6 56.7 %all-gather.32.cloned.1.call-done = bf16[2560,1024]{1,0:T(8,128)(2,1)} async-done(((bf16[640,1024]{1,0:T(8,128)(2,1)}), bf16[2560,1024]{1,0:T(8,128)(2,1)}) %all-gather.32.cloned.1.call-update) | async-done | bytes 5242896 | tf_op jit(solution)/shard_map/all_gather | solution.py:682
  464.3 4.0 fusion.53
  473.5 7.1 compact.2.rows
  483.1 32.4 %expert_forward.1.rows = f32[2560,1024]{1,0:T(8,128)} custom-call(s32[5]{0:T(128)} %copy-done.7, bf16[2560,1024]{1,0:T(8,128)(2,1)} %copy-done.2, bf16[2,4,512,704]{3,2,1,0:T(8,128)(2,1)} %bitcast.116, bf16[2,4,512,704]{3,2,1,0:T(8,128)(2,1)} %bitcast.118, bf16[2,4,352,1024]{3,2,1,0:T(8,128)(2,1)} %bitcast.121), custom_call_target="tpu_custom_call" | custom-call | tf_op jit(solution)/shard_map/expert_forward/pallas_call | solution.py:494
  515.6 9.8 expand.2
  525.4 5.7 fusion
  531.8 22.1 %psum.57 = s32[]{:T(128)} all-reduce(s32[]{:T(128)} %reduce_sum.182), channel_id=1, replica_groups=mesh['expert'=4,'shard'=4,'dp'=2] {'expert','dp'}, use_global_device_ids=true, to_apply=%region_15.16 | all-reduce | flops 1 | bytes 8 | tf_op jit(solution)/shard_map/psum | solution.py:646
  554.7 52.2 %reduce-scatter.31.cloned.1.call-done = bf16[1,640,1024]{2,1,0:T(8,128)(2,1)} async-done(((bf16[4,640,1024]{2,1,0:T(8,128)(2,1)}), bf16[1,640,1024]{2,1,0:T(8,128)(2,1)}) %reduce-scatter.31.cloned.1.call-update) | async-done | bytes 1310736
  611.4 60.8 %all-gather.40.cloned.1.call-done = bf16[2560,1024]{1,0:T(8,128)(2,1)} async-done(((bf16[640,1024]{1,0:T(8,128)(2,1)}), bf16[2560,1024]{1,0:T(8,128)(2,1)}) %all-gather.40.cloned.1.call-update) | async-done | bytes 5242896 | tf_op jit(solution)/shard_map/all_gather | solution.py:698
  672.2 9.7 compact.3.grads
  681.8 73.7 %expert_backward.1 = (bf16[4,1024,704]{2,1,0:T(8,128)(2,1)}, bf16[4,1024,704]{2,1,0:T(8,128)(2,1)}, bf16[4,704,1024]{2,1,0:T(8,128)(2,1)}, f32[2560,1024]{1,0:T(8,128)}) custom-call(s32[5]{0:T(128)} %copy-done.7, bf16[2560,1024]{1,0:T(8,128)(2,1)} %copy-done.2, bf16[2560,1024]{1,0:T(8,128)(2,1)} %compact.3.grads, bf16[2,4,512,704]{3,2,1,0:T(8,128)(2,1)} %bitcast.117, ...), custom_call_target="tpu_custom_call" | custom-call | tf_op jit(solution)/shard_map/expert_backward/pallas_call | solution.py:564
  755.6 9.8 expand.3
  765.5 8.4 copy.160
  774.0 8.3 copy.161
  782.4 5.8 copy.162
  789.9 5.6 fusion.1
  796.1 34.5 %all-to-all-start.1 = ((f32[4,1,640]{2,1,0:T(1,128)}), f32[4,1,640]{2,1,0:T(1,128)S(1)}, u32[]{:S(2)}, u32[]{:S(2)}) async-start(f32[4,1,640]{2,1,0:T(1,128)} %copy.154), calls=%async_computation.1 | async-start | bytes 20480 | tf_op jit(solution)/shard_map/all_to_all | solution.py:700
  831.1 4.2 all-to-all-done.1
  835.5 22.9 %reduce-scatter.33.cloned.1.call-done = bf16[1,640,1024]{2,1,0:T(8,128)(2,1)} async-done(((bf16[4,640,1024]{2,1,0:T(8,128)(2,1)}), bf16[1,640,1024]{2,1,0:T(8,128)(2,1)}) %reduce-scatter.33.cloned.1.call-update) | async-done | bytes 1310736
  858.4 5.7 multiply_reduce_fusion
  874.5 17.3 %reduce-scatter.23.cloned.1.call-done = bf16[4,1,512,704]{2,3,0,1:T(8,128)(2,1)} async-done(((bf16[4,2,512,704]{2,3,0,1:T(8,128)(2,1)}), bf16[4,1,512,704]{2,3,0,1:T(8,128)(2,1)}) %reduce-scatter.23.cloned.1.call-update) | async-done | bytes 2883600 | tf_op jit(solution)/shard_map/reduce_scatter | solution.py:611
  891.9 17.2 %reduce-scatter.27.cloned.1.call-done = bf16[4,1,352,1024]{3,2,0,1:T(8,128)(2,1)} async-done(((bf16[4,2,352,1024]{3,2,0,1:T(8,128)(2,1)}), bf16[4,1,352,1024]{3,2,0,1:T(8,128)(2,1)}) %reduce-scatter.27.cloned.1.call-update) | async-done | bytes 2883600 | tf_op jit(solution)/shard_map/reduce_scatter | solution.py:611
  913.5 4.9 all-to-all-start.2
  920.2 61.3 %all-to-all-done.2 = bf16[4,640,256]{2,1,0:T(8,128)(2,1)} async-done(((bf16[4,640,256]{2,1,0:T(8,128)(2,1)}), bf16[4,640,256]{2,1,0:T(8,128)(2,1)}, u32[]{:S(2)}, u32[]{:S(2)}) %all-to-all-start.2) | async-done | bytes 1310752 | tf_op jit(solution)/shard_map/all_to_all | solution.py:737
  981.5 48.9 %attention_backward.1 = (bf16[256,2560]{1,0:T(8,128)(2,1)}, bf16[2560,256]{1,0:T(8,128)(2,1)}, bf16[2560,256]{1,0:T(8,128)(2,1)}, f32[18,1,512]{2,1,0:T(1,128)}, f32[18,1,512]{2,1,0:T(1,128)}) custom-call(s32[64]{0:T(128)} %copy-done.11, f32[4,128]{1,0:T(4,128)} %copy-done.10, bf16[2560,256]{1,0:T(8,128)(2,1)} %copy-done.4, bf16[2560,256]{1,0:T(8,128)(2,1)} %copy-done.3, ...), custom_call_target="tpu_custom_call" | custom-call | tf_op jit(solution)/shard_map/attention_backward/pallas_call | solution.py:274
  1032.0 8.8 convolution_convert_fusion.3
  1041.7 58.0 %reduce-scatter.25.cloned.1.call-done = bf16[1,512,704]{1,2,0:T(8,128)(2,1)} async-done(((bf16[4,512,704]{1,2,0:T(8,128)(2,1)}), bf16[1,512,704]{1,2,0:T(8,128)(2,1)}) %reduce-scatter.25.cloned.1.call-update) | async-done | bytes 720912 | tf_op jit(solution)/shard_map/reduce_scatter | solution.py:612
  1099.7 58.3 %reduce-scatter.29.cloned.1.call-done = bf16[1,352,1024]{2,1,0:T(8,128)(2,1)} async-done(((bf16[4,352,1024]{2,1,0:T(8,128)(2,1)}), bf16[1,352,1024]{2,1,0:T(8,128)(2,1)}) %reduce-scatter.29.cloned.1.call-update) | async-done | bytes 720912 | tf_op jit(solution)/shard_map/reduce_scatter | solution.py:612
  1158.1 8.8 convolution_convert_fusion
  1168.5 13.8 psum.61
  1182.8 40.5 %all-reduce.7.cloned.1.call-done = (bf16[1024,768]{1,0:T(8,128)(2,1)}, bf16[256,1024]{1,0:T(8,128)(2,1)}) async-done(((bf16[1024,768]{1,0:T(8,128)(2,1)}, bf16[256,1024]{1,0:T(8,128)(2,1)}), (bf16[1024,768]{1,0:T(8,128)(2,1)}, bf16[256,1024]{1,0:T(8,128)(2,1)})) %all-reduce.7.cloned.1.call-update) | async-done | bytes 2097168 | tf_op jit(solution)/shard_map/psum | solution.py:762
  1227.3 6.4 all-gather.42.cloned.1.call-done
  1237.1 9.1 all-gather.44.cloned.1.call-done
  1249.4 9.1 all-gather.46.cloned.1.call-done
  1261.8 93.8 %reduce-scatter.15.cloned.1.call-done = bf16[640,1024]{1,0:T(8,128)(2,1)} async-done(((bf16[2560,1024]{1,0:T(8,128)(2,1)}), bf16[640,1024]{1,0:T(8,128)(2,1)}) %reduce-scatter.15.cloned.1.call-update) | async-done | bytes 1310736 | tf_op jit(solution)/shard_map/reduce_scatter | solution.py:751
  1357.9 41.5 %all-reduce.3 = (f32[]{:T(128)}, f32[1024]{0:T(1024)}, f32[1024]{0:T(1024)}, f32[1024,4]{0,1:T(4,128)}) all-reduce(f32[]{:T(128)} %get-tuple-element.76, f32[1024]{0:T(1024)S(1)} %get-tuple-element.74, f32[1024]{0:T(1024)S(1)} %get-tuple-element.72, ...), channel_id=1, replica_groups=mesh['expert'=4,'shard'=4,'dp'=2] {'expert','shard','dp'}, use_global_device_ids=true, to_apply=%region_13.14 | all-reduce | flops 6145 | bytes 49160 | tf_op jit(solution)/shard_map/psum | solution.py:769
  1400.1 4.3 fusion.9
  (245 shorter events, 85.8 us)
Async XLA Ops:
  7.2 64.9 %all-gather.26.cloned.1.call-start = ((), (), s32[]{:S(2)}) async-start(), calls=%async_computation.15 | async-start | bytes 3604480 | tf_op jit(solution)/shard_map/all_gather | solution.py:604
  9.5 122.6 %all-gather.28.cloned.1.call-start = ((), (), s32[]{:S(2)}) async-start(), calls=%async_computation.16 | async-start | bytes 3604480 | tf_op jit(solution)/shard_map/all_gather | solution.py:604
  11.6 219.5 %all-gather.22.cloned.1.call-start = ((), (), s32[]{:S(2)}) async-start(), calls=%async_computation.13 | async-start | bytes 6553600 | tf_op jit(solution)/shard_map/all_gather | solution.py:641
  13.5 269.8 %all-gather.24.cloned.1.call-start = ((), (), s32[]{:S(2)}) async-start(), calls=%async_computation.14 | async-start | bytes 2621440 | tf_op jit(solution)/shard_map/all_gather | solution.py:642
  14.0 58.2 %copy-start.34 = (s32[1,2560]{1,0:T(1,128)S(1)}, s32[1,2560]{1,0:T(1,128)}, u32[]{:S(2)}) copy-start(s32[1,2560]{1,0:T(1,128)} %param.27) | copy-start | bytes 30724
  14.0 61.3 %copy-start.42 = (s32[4]{0:T(128)S(1)}, s32[4]{0:T(128)}, u32[]{:S(2)}) copy-start(s32[4]{0:T(128)} %constant.202.clone) | copy-start | bytes 52
  14.1 347.6 %all-gather.30.cloned.1.call-start = ((), (), s32[]{:S(2)}) async-start(), calls=%async_computation.17 | async-start | bytes 3604480 | tf_op jit(solution)/shard_map/all_gather | solution.py:604
  15.1 365.4 %all-gather.34.cloned.1.call-start = ((), (), s32[]{:S(2)}) async-start(), calls=%async_computation.27 | async-start | bytes 8650752 | tf_op jit(solution)/shard_map/all_gather | solution.py:604
  72.1 60.2 %copy-start.41 = (f32[32,4]{0,1:T(4,128)S(1)}, f32[32,4]{0,1:T(4,128)}, u32[]{:S(2)}) copy-start(f32[32,4]{0,1:T(4,128)} %param.34) | copy-start | bytes 1540
  72.1 60.4 %copy-start.28 = (bf16[1024,256]{1,0:T(8,128)(2,1)S(1)}, bf16[1024,256]{1,0:T(8,128)(2,1)}, u32[]{:S(2)}) copy-start(bf16[1024,256]{1,0:T(8,128)(2,1)} %param.30) | copy-start | bytes 1572868
  72.1 60.4 %copy-start.29 = (bf16[1024,256]{1,0:T(8,128)(2,1)S(1)}, bf16[1024,256]{1,0:T(8,128)(2,1)}, u32[]{:S(2)}) copy-start(bf16[1024,256]{1,0:T(8,128)(2,1)} %param.31) | copy-start | bytes 1572868
  72.1 60.4 %copy-start.30 = (bf16[1024,256]{1,0:T(8,128)(2,1)S(1)}, bf16[1024,256]{1,0:T(8,128)(2,1)}, u32[]{:S(2)}) copy-start(bf16[1024,256]{1,0:T(8,128)(2,1)} %param.32) | copy-start | bytes 1572868
  72.1 327.1 %all-gather.36.cloned.1.call-start = ((), (), s32[]{:S(2)}) async-start(), calls=%async_computation.28 | async-start | bytes 8650752 | tf_op jit(solution)/shard_map/all_gather | solution.py:604
  75.4 57.2 %copy-start.39 = (s32[18]{0:T(128)}, s32[18]{0:T(128)S(1)}, u32[]{:S(2)}) copy-start(s32[18]{0:T(128)S(1)} %concatenate.33) | copy-start | bytes 220
  132.3 111.3 %copy-start.11 = (s32[64]{0:T(128)}, s32[64]{0:T(128)S(1)}, u32[]{:S(2)}) copy-start(s32[64]{0:T(128)S(1)} %constant_dynamic-update-slice_fusion.3.info) | copy-start | bytes 772
  132.6 98.5 %copy-start.32 = (bf16[1024,768]{1,0:T(8,128)(2,1)}, bf16[1024,768]{1,0:T(8,128)(2,1)S(1)}, u32[]{:S(2)}) copy-start(bf16[1024,768]{1,0:T(8,128)(2,1)S(1)} %constant_dynamic-update-slice_fusion) | copy-start | bytes 4718596
  132.8 110.8 %copy-start.10 = (f32[4,128]{1,0:T(4,128)}, f32[4,128]{1,0:T(4,128)S(1)}, u32[]{:S(2)}) copy-start(f32[4,128]{1,0:T(4,128)S(1)} %fusion.28.table) | copy-start | bytes 6148
  240.3 37.1 %copy-start.3 = (bf16[2560,256]{1,0:T(8,128)(2,1)}, bf16[2560,256]{1,0:T(8,128)(2,1)S(1)}, u32[]{:S(2)}) copy-start(bf16[2560,256]{1,0:T(8,128)(2,1)S(1)} %get-tuple-element.100.k) | copy-start | bytes 3932164
  240.3 37.1 %copy-start.4 = (bf16[2560,256]{1,0:T(8,128)(2,1)}, bf16[2560,256]{1,0:T(8,128)(2,1)S(1)}, u32[]{:S(2)}) copy-start(bf16[2560,256]{1,0:T(8,128)(2,1)S(1)} %get-tuple-element.101.q) | copy-start | bytes 3932164
  278.5 69.8 %copy-start.15 = (bf16[1,640,1024]{2,1,0:T(8,128)(2,1)S(1)}, bf16[1,640,1024]{2,1,0:T(8,128)(2,1)}, u32[]{:S(2)}) copy-start(bf16[1,640,1024]{2,1,0:T(8,128)(2,1)} %param.25) | copy-start | bytes 3932164
  279.6 68.6 %all-to-all-start = ((bf16[4,256,640]{2,1,0:T(8,128)(2,1)}), bf16[4,256,640]{2,1,0:T(8,128)(2,1)S(1)}, u32[]{:S(2)}, u32[]{:S(2)}) async-start(bf16[4,256,640]{2,1,0:T(8,128)(2,1)} %bitcast.113), calls=%async_computation | async-start | bytes 2621440 | tf_op jit(solution)/shard_map/all_to_all | solution.py:662
  283.2 181.1 %all-gather.32.cloned.1.call-start = ((), (), s32[]{:S(2)}) async-start(), calls=%async_computation.26 | async-start | bytes 6553600 | tf_op jit(solution)/shard_map/all_gather | solution.py:682
  354.9 21.7 %copy-start.33 = (f32[1024,4]{0,1:T(4,128)S(1)}, f32[1024,4]{0,1:T(4,128)}, u32[]{:S(2)}) copy-start(f32[1024,4]{0,1:T(4,128)} %param.36) | copy-start | bytes 49156
  354.9 128.2 %all-gather.38.cloned.1.call-start = ((), (), s32[]{:S(2)}) async-start(), calls=%async_computation.29 | async-start | bytes 8650752 | tf_op jit(solution)/shard_map/all_gather | solution.py:604
  361.7 245.2 %reduce-scatter.31.cloned.1.call-start = ((), (), s32[]{:S(2)}) async-start(), calls=%async_computation.34 | async-start | bytes 6553600
  483.1 32.4 %copy-start.8 = (s32[5]{0:T(128)S(1)}, s32[5]{0:T(128)}, u32[]{:S(2)}) copy-start(s32[5]{0:T(128)} %copy-done.7) | copy-start | bytes 64
  531.1 75.8 %copy-start.18 = (bf16[1,640,1024]{2,1,0:T(8,128)(2,1)S(1)}, bf16[1,640,1024]{2,1,0:T(8,128)(2,1)}, u32[]{:S(2)}) copy-start(bf16[1,640,1024]{2,1,0:T(8,128)(2,1)} %param.26) | copy-start | bytes 3932164
  531.1 141.1 %all-gather.40.cloned.1.call-start = ((), (), s32[]{:S(2)}) async-start(), calls=%async_computation.30 | async-start | bytes 6553600 | tf_op jit(solution)/shard_map/all_gather | solution.py:698
  610.6 247.7 %reduce-scatter.33.cloned.1.call-start = ((), (), s32[]{:S(2)}) async-start(), calls=%async_computation.35 | async-start | bytes 6553600
  681.8 73.7 %copy-start.9 = (s32[5]{0:T(128)S(1)}, s32[5]{0:T(128)}, u32[]{:S(2)}) copy-start(s32[5]{0:T(128)} %copy-done.7) | copy-start | bytes 64
  765.4 109.1 %reduce-scatter.19.cloned.1.call-start = ((), (), s32[]{:S(2)}) async-start(), calls=%async_computation.20 | async-start | bytes 8650752 | tf_op jit(solution)/shard_map/reduce_scatter | solution.py:611
  773.9 117.9 %reduce-scatter.23.cloned.1.call-start = ((), (), s32[]{:S(2)}) async-start(), calls=%async_computation.22 | async-start | bytes 8650752 | tf_op jit(solution)/shard_map/reduce_scatter | solution.py:611
  782.3 126.7 %reduce-scatter.27.cloned.1.call-start = ((), (), s32[]{:S(2)}) async-start(), calls=%async_computation.24 | async-start | bytes 8650752 | tf_op jit(solution)/shard_map/reduce_scatter | solution.py:611
  789.9 68.5 %copy-start.19 = (bf16[1,640,1024]{2,1,0:T(8,128)(2,1)S(1)}, bf16[1,640,1024]{2,1,0:T(8,128)(2,1)}, u32[]{:S(2)}) copy-start(bf16[1,640,1024]{2,1,0:T(8,128)(2,1)} %param.26) | copy-start | bytes 3932164
  796.1 39.2 %all-to-all-start.1 = ((f32[4,1,640]{2,1,0:T(1,128)}), f32[4,1,640]{2,1,0:T(1,128)S(1)}, u32[]{:S(2)}, u32[]{:S(2)}) async-start(f32[4,1,640]{2,1,0:T(1,128)} %copy.154), calls=%async_computation.1 | async-start | bytes 20480 | tf_op jit(solution)/shard_map/all_to_all | solution.py:700
  830.6 210.3 %reduce-scatter.17.cloned.1.call-start = ((), (), s32[]{:S(2)}) async-start(), calls=%async_computation.19 | async-start | bytes 2621440 | tf_op jit(solution)/shard_map/reduce_scatter | solution.py:759
  871.8 169.6 %reduce-scatter.21.cloned.1.call-start = ((), (), s32[]{:S(2)}) async-start(), calls=%async_computation.21 | async-start | bytes 3604480 | tf_op jit(solution)/shard_map/reduce_scatter | solution.py:612
  874.5 225.1 %reduce-scatter.25.cloned.1.call-start = ((), (), s32[]{:S(2)}) async-start(), calls=%async_computation.23 | async-start | bytes 3604480 | tf_op jit(solution)/shard_map/reduce_scatter | solution.py:612
  891.8 17.3 %copy-start.43 = (bf16[1024,1024]{1,0:T(8,128)(2,1)S(1)}, bf16[1024,1024]{1,0:T(8,128)(2,1)}, u32[]{:S(2)}) copy-start(bf16[1024,1024]{1,0:T(8,128)(2,1)} %all-gather.24.cloned.1.call-done) | copy-start | bytes 6291460
  891.8 266.2 %reduce-scatter.29.cloned.1.call-start = ((), (), s32[]{:S(2)}) async-start(), calls=%async_computation.25 | async-start | bytes 3604480 | tf_op jit(solution)/shard_map/reduce_scatter | solution.py:612
  913.5 68.0 %all-to-all-start.2 = ((bf16[4,640,256]{2,1,0:T(8,128)(2,1)}), bf16[4,640,256]{2,1,0:T(8,128)(2,1)}, u32[]{:S(2)}, u32[]{:S(2)}) async-start(bf16[4,640,256]{2,1,0:T(8,128)(2,1)} %bitcast.128), calls=%async_computation.2 | async-start | bytes 2621440 | tf_op jit(solution)/shard_map/all_to_all | solution.py:737
  918.4 304.9 %all-reduce.7.cloned.1.call-start = ((), (), s32[]{:S(2)}) async-start(), calls=%async_computation.36 | async-start | bytes 4194304 | tf_op jit(solution)/shard_map/psum | solution.py:762
  1040.9 192.9 %all-gather.42.cloned.1.call-start = ((), (), s32[]{:S(2)}) async-start(), calls=%async_computation.31 | async-start | bytes 2162688 | tf_op jit(solution)/shard_map/all_gather | solution.py:613
  1041.6 204.5 %all-gather.44.cloned.1.call-start = ((), (), s32[]{:S(2)}) async-start(), calls=%async_computation.32 | async-start | bytes 2162688 | tf_op jit(solution)/shard_map/all_gather | solution.py:613
  1099.7 158.8 %all-gather.46.cloned.1.call-start = ((), (), s32[]{:S(2)}) async-start(), calls=%async_computation.33 | async-start | bytes 2162688 | tf_op jit(solution)/shard_map/all_gather | solution.py:613
  1158.0 197.6 %reduce-scatter.15.cloned.1.call-start = ((), (), s32[]{:S(2)}) async-start(), calls=%async_computation.18 | async-start | bytes 6553600 | tf_op jit(solution)/shard_map/reduce_scatter | solution.py:751
  1249.4 106.2 %copy-start.16 = (bf16[1,640,1024]{2,1,0:T(8,128)(2,1)S(1)}, bf16[1,640,1024]{2,1,0:T(8,128)(2,1)}, u32[]{:S(2)}) copy-start(bf16[1,640,1024]{2,1,0:T(8,128)(2,1)} %param.25) | copy-start | bytes 3932164
  1249.4 106.2 %copy-start.36 = (f32[1024]{0:T(1024)S(1)}, f32[1024]{0:T(1024)}, u32[]{:S(2)}) copy-start(f32[1024]{0:T(1024)} %param.29) | copy-start | bytes 12292
  (25 other events, 92.5 us)
Sparse Core Ops, SparseCore 0:
  10.2 61.8 all-gather.25
  74.2 57.8 all-gather.27
  134.3 96.7 all-gather.21
  232.5 44.3 all-gather.23
  278.8 82.7 all-gather.29
  363.0 17.3 all-gather.33
  382.0 17.1 all-gather.35
  401.6 62.5 all-gather.31
  465.8 15.9 all-gather.37
  531.2 75.6 reduce-scatter.30
  610.7 61.4 all-gather.39
  765.5 92.7 reduce-scatter.32
  860.6 13.7 reduce-scatter.18
  876.7 15.0 reduce-scatter.22
  894.0 15.0 reduce-scatter.26
  911.9 68.5 reduce-scatter.16
  982.6 58.7 reduce-scatter.20
  1043.6 56.0 reduce-scatter.24
  1101.9 56.0 reduce-scatter.28
  1161.7 61.5 all-reduce.6
  1224.9 8.8 all-gather.41
  1235.3 10.7 all-gather.43
  1247.7 10.7 all-gather.45
  1260.6 94.9 reduce-scatter.14

commit v2 on v1

v2 whole, which is shorter than its diff:
```python
import functools
import math

import jax
import jax.numpy as jnp
from jax import lax
from jax.experimental import pallas as pl
from jax.experimental.pallas import tpu as pltpu
from jax.sharding import PartitionSpec as P

TRUNK, SEGMENT, NBRANCH, NLEAF = 1024, 128, 4, 2
TILE = 128
TRUNK_TILES = TRUNK // TILE
HEAD_DIM = 64
MASKED = -1e30
DIAG, SUB, FAR, NONE, BRANCH_NEAR, LEAF_NEAR, LEAF_BRANCH = 0, 1, 2, 3, 4, 6, 14
CLASSES = 18
LIMIT_AT, OFFSET_AT = 0, 32


def head_rows(block, heads):
    lane = lax.broadcasted_iota(jnp.int32, block.shape, 1) // HEAD_DIM
    return jnp.concatenate(
        [jnp.where(lane == h, block, jnp.zeros((), block.dtype)) for h in range(heads)], axis=0
    )


def fill_bias(info, table, bias, heads):
    rows = lax.broadcasted_iota(jnp.int32, (TILE, TILE), 0)
    lanes = lax.broadcasted_iota(jnp.int32, (TILE, TILE), 1)

    def one(number, carry):
        place = jnp.clip(info[OFFSET_AT + number] + lanes - rows, 0, TILE - 1)
        hidden = ((number == DIAG) & (rows > lanes)) | (number == NONE)
        for h in range(heads):
            line = jnp.broadcast_to(table[h : h + 1, :], (TILE, TILE))
            values = jnp.take_along_axis(line, place, axis=1)
            bias[number, :, h * TILE : (h + 1) * TILE] = jnp.where(hidden, MASKED, values)
        return carry

    lax.fori_loop(0, CLASSES, one, 0)


def tile_plan(i, info):
    last = info[LIMIT_AT + 20]
    trunk = i < TRUNK_TILES
    place = jnp.maximum(i - TRUNK_TILES, 0)
    branch = place // (1 + NLEAF)
    leaf = (place % (1 + NLEAF)) > 0
    branch_tile = TRUNK_TILES + branch * (1 + NLEAF)
    near = jnp.where(trunk, i, last)
    near_class = jnp.where(trunk, DIAG, jnp.where(leaf, LEAF_NEAR + branch, BRANCH_NEAR))
    next_class = jnp.where(trunk, SUB, jnp.where(leaf, LEAF_NEAR + NBRANCH + branch, BRANCH_NEAR + 1))
    trunk_steps = TRUNK_TILES // 2
    tail = (
        (jnp.where(leaf, branch_tile, i), jnp.where(leaf, LEAF_BRANCH + branch, DIAG)),
        (i, jnp.where(leaf, DIAG, NONE)),
    )

    def tile_of(step, half):
        kt = step * 2 + half
        in_trunk = trunk | (step < trunk_steps)
        kind = jnp.where(
            kt == near, near_class, jnp.where(kt == near - 1, next_class, jnp.where(kt < near, FAR, NONE))
        )
        return jnp.where(in_trunk, kt, tail[half][0]), jnp.where(in_trunk, kind, tail[half][1])

    return tile_of


def by_steps(i, run):
    for count in range(1, TRUNK_TILES // 2 + 1):

        @pl.when((i < TRUNK_TILES) & (i // 2 == count - 1))
        def _(count=count):
            run(count)

    @pl.when(i >= TRUNK_TILES)
    def _():
        run(TRUNK_TILES // 2 + 1)


def masked_scores(scores, half, tile, kind, info, bias, heads):
    rows = lax.broadcasted_iota(jnp.int32, (TILE, TILE), 0)
    shade = jnp.where(rows < info[LIMIT_AT + tile], 0.0, MASKED)
    shade = jnp.concatenate([shade] * heads, axis=1)
    return scores[half * TILE : (half + 1) * TILE] + bias[kind] + shade


def rows_at(ref, tile):
    return ref[pl.ds(pl.multiple_of(tile * TILE, TILE), TILE), :]


def lanes_at(ref, first, count, tile):
    return ref[first : first + count, pl.ds(pl.multiple_of(tile * TILE, TILE), TILE)]


def forward_kernel(info, table, q, k, v_t, out, log_total, bias, score, total_out, *, heads):
    i = pl.program_id(0)

    @pl.when(i == 0)
    def _():
        fill_bias(info, table, bias, heads)

    tile_of = tile_plan(i, info)
    queries = head_rows(q[...] * jnp.bfloat16(0.125), heads)
    width = heads * TILE

    def first(step, highest):
        (ta, ka), (tb, kb) = tile_of(step, 0), tile_of(step, 1)
        keys = jnp.concatenate([rows_at(k, ta), rows_at(k, tb)], axis=0)
        raw = lax.dot_general(keys, queries, (((1,), (1,)), ((), ())), preferred_element_type=jnp.float32)
        both = jnp.concatenate(
            [masked_scores(raw, 0, ta, ka, info, bias, heads), masked_scores(raw, 1, tb, kb, info, bias, heads)],
            axis=0,
        )
        score[step * 2 * TILE : (step + 1) * 2 * TILE, :] = both
        return jnp.maximum(highest, jnp.max(both.reshape(2 * TILE // 8, 8, width), axis=0))

    pairs = heads // 2

    def run(steps):
        highest = jnp.full((8, width), MASKED, jnp.float32)
        for step in range(steps):
            highest = first(step, highest)
        highest = jnp.max(highest, axis=0, keepdims=True)
        total = jnp.zeros((8, width), jnp.float32)
        for step in range(steps):
            (ta, _), (tb, _) = tile_of(step, 0), tile_of(step, 1)
            part = jnp.exp(score[step * 2 * TILE : (step + 1) * 2 * TILE, :] - highest)
            low = part.astype(jnp.bfloat16)
            for p in range(pairs):
                values = jnp.concatenate(
                    [lanes_at(v_t, p * TILE, TILE, ta), lanes_at(v_t, p * TILE, TILE, tb)], axis=1
                )
                product = jnp.dot(
                    values, low[:, p * 2 * TILE : (p + 1) * 2 * TILE], preferred_element_type=jnp.float32
                )
                if step == 0:
                    total_out[p] = product
                else:
                    total_out[p] += product
            total = total + jnp.sum(part.reshape(2 * TILE // 8, 8, width), axis=0)
        total = jnp.sum(total, axis=0, keepdims=True)
        inverse = 1.0 / total
        for h in range(heads):
            p, odd = h // 2, h % 2
            block = total_out[p, odd * HEAD_DIM : (odd + 1) * HEAD_DIM, odd * TILE : (odd + 1) * TILE]
            out[h * HEAD_DIM : (h + 1) * HEAD_DIM, :] = (
                block * inverse[:, h * TILE : (h + 1) * TILE]
            ).astype(jnp.bfloat16)
        log_total[0] = highest + jnp.log(total)

    by_steps(i, run)


def attention_forward(info, table, q, k, v_t):
    length, columns = q.shape
    heads = columns // HEAD_DIM
    tiles = length // TILE
    width = heads * TILE
    whole = lambda shape: pl.BlockSpec(shape, lambda i, info: (0,) * len(shape))
    return pl.pallas_call(
        functools.partial(forward_kernel, heads=heads),
        grid_spec=pltpu.PrefetchScalarGridSpec(
            num_scalar_prefetch=1,
            grid=(tiles,),
            in_specs=[
                whole(table.shape),
                pl.BlockSpec((TILE, columns), lambda i, info: (i, 0)),
                whole(k.shape),
                whole(v_t.shape),
            ],
            out_specs=[
                pl.BlockSpec((columns, TILE), lambda i, info: (0, i)),
                pl.BlockSpec((1, 1, width), lambda i, info: (i, 0, 0)),
            ],
            scratch_shapes=[
                pltpu.VMEM((CLASSES, TILE, width), jnp.float32),
                pltpu.VMEM((10 * TILE, width), jnp.float32),
                pltpu.VMEM((heads // 2, TILE, 2 * TILE), jnp.float32),
            ],
        ),
        out_shape=[
            jax.ShapeDtypeStruct((columns, length), jnp.bfloat16),
            jax.ShapeDtypeStruct((tiles, 1, width), jnp.float32),
        ],
        compiler_params=pltpu.CompilerParams(
            dimension_semantics=("arbitrary",), vmem_limit_bytes=50 << 20
        ),
        cost_estimate=pl.CostEstimate(flops=4 * 10**10, bytes_accessed=10**7, transcendentals=0),
        name="attention_forward",
    )(info, table, q, k, v_t)


def backward_kernel(
    info, table, q, k, k_t, v, grad, attended_t, log_total,
    grad_q, grad_k, grad_v, ahead, behind,
    bias, by_class, total_q, total_k, total_v, *, heads, tiles,
):
    i = pl.program_id(0)
    width = heads * TILE

    @pl.when(i == 0)
    def _():
        fill_bias(info, table, bias, heads)
        by_class[...] = jnp.zeros_like(by_class)
        total_k[...] = jnp.zeros_like(total_k)
        total_v[...] = jnp.zeros_like(total_v)

    tile_of = tile_plan(i, info)
    queries = head_rows(q[...] * jnp.bfloat16(0.125), heads)
    grads = head_rows(grad[...], heads)
    product = jnp.transpose(grad[...].astype(jnp.float32)) * attended_t[...].astype(jnp.float32)
    centre = jnp.concatenate(
        [
            jnp.sum(product[h * HEAD_DIM : (h + 1) * HEAD_DIM], axis=0, keepdims=True)
            for h in range(heads)
        ],
        axis=1,
    )
    logs = log_total[0]
    total_q[...] = jnp.zeros_like(total_q)
    pairs = heads // 2

    def one(step):
        (ta, ka), (tb, kb) = tile_of(step, 0), tile_of(step, 1)
        keys = jnp.concatenate([rows_at(k, ta), rows_at(k, tb)], axis=0)
        values = jnp.concatenate([rows_at(v, ta), rows_at(v, tb)], axis=0)
        raw = lax.dot_general(keys, queries, (((1,), (1,)), ((), ())), preferred_element_type=jnp.float32)
        both = jnp.concatenate(
            [masked_scores(raw, 0, ta, ka, info, bias, heads), masked_scores(raw, 1, tb, kb, info, bias, heads)],
            axis=0,
        )
        probs = jnp.exp(both - logs)
        grad_probs = lax.dot_general(
            values, grads, (((1,), (1,)), ((), ())), preferred_element_type=jnp.float32
        )
        grad_scores = probs * (grad_probs - centre)
        by_class[ka] += grad_scores[:TILE]
        by_class[kb] += grad_scores[TILE:]
        low = grad_scores.astype(jnp.bfloat16)
        value_part = jnp.dot(probs.astype(jnp.bfloat16), grads, preferred_element_type=jnp.float32)
        key_part = jnp.dot(low, queries, preferred_element_type=jnp.float32)
        for half, tile in ((0, ta), (1, tb)):
            at = pl.ds(pl.multiple_of(tile * TILE, TILE), TILE)
            total_v[at, :] += value_part[half * TILE : (half + 1) * TILE]
            total_k[at, :] += key_part[half * TILE : (half + 1) * TILE]
        for p in range(pairs):
            keys_t = jnp.concatenate(
                [lanes_at(k_t, p * TILE, TILE, ta), lanes_at(k_t, p * TILE, TILE, tb)], axis=1
            )
            total_q[p] += jnp.dot(
                keys_t, low[:, p * 2 * TILE : (p + 1) * 2 * TILE], preferred_element_type=jnp.float32
            )

    def run(steps):
        for step in range(steps):
            one(step)

    by_steps(i, run)
    for h in range(heads):
        p, odd = h // 2, h % 2
        block = total_q[p, odd * HEAD_DIM : (odd + 1) * HEAD_DIM, odd * TILE : (odd + 1) * TILE]
        grad_q[h * HEAD_DIM : (h + 1) * HEAD_DIM, :] = (block * 0.125).astype(jnp.bfloat16)

    @pl.when(i == tiles - 1)
    def _():
        grad_k[...] = total_k[...].astype(jnp.bfloat16)
        grad_v[...] = total_v[...].astype(jnp.bfloat16)
        rows = lax.broadcasted_iota(jnp.int32, (TILE, TILE), 0)
        lanes = lax.broadcasted_iota(jnp.int32, (TILE, TILE), 1)

        def reduce(number, carry):
            for h in range(heads):
                block = by_class[number, :, h * TILE : (h + 1) * TILE]
                turned = jnp.take_along_axis(block, (rows + lanes) % TILE, axis=1)
                forward = jnp.sum(jnp.where(rows + lanes < TILE, turned, 0.0), axis=0, keepdims=True)
                wrapped = jnp.sum(jnp.where(rows + lanes < TILE, 0.0, turned), axis=0, keepdims=True)
                ahead[number, :, h * TILE : (h + 1) * TILE] = forward
                behind[number, :, h * TILE : (h + 1) * TILE] = wrapped
            return carry

        lax.fori_loop(0, CLASSES, reduce, 0)


def attention_backward(info, table, q, k, k_t, v, grad, attended_t, log_total):
    length, columns = q.shape
    heads = columns // HEAD_DIM
    tiles = length // TILE
    width = heads * TILE
    whole = lambda shape: pl.BlockSpec(shape, lambda i, info: (0,) * len(shape))
    rows = pl.BlockSpec((TILE, columns), lambda i, info: (i, 0))
    lanes = pl.BlockSpec((columns, TILE), lambda i, info: (0, i))
    return pl.pallas_call(
        functools.partial(backward_kernel, heads=heads, tiles=tiles),
        grid_spec=pltpu.PrefetchScalarGridSpec(
            num_scalar_prefetch=1,
            grid=(tiles,),
            in_specs=[
                whole(table.shape), rows, whole(k.shape), whole(k_t.shape), whole(v.shape), rows, lanes,
                pl.BlockSpec((1, 1, width), lambda i, info: (i, 0, 0)),
            ],
            out_specs=[
                lanes, whole(k.shape), whole(v.shape),
                whole((CLASSES, 1, width)), whole((CLASSES, 1, width)),
            ],
            scratch_shapes=[
                pltpu.VMEM((CLASSES, TILE, width), jnp.float32),
                pltpu.VMEM((CLASSES, TILE, width), jnp.float32),
                pltpu.VMEM((heads // 2, TILE, 2 * TILE), jnp.float32),
                pltpu.VMEM((length, columns), jnp.float32),
                pltpu.VMEM((length, columns), jnp.float32),
            ],
        ),
        out_shape=[
            jax.ShapeDtypeStruct((columns, length), jnp.bfloat16),
            jax.ShapeDtypeStruct((length, columns), jnp.bfloat16),
            jax.ShapeDtypeStruct((length, columns), jnp.bfloat16),
            jax.ShapeDtypeStruct((CLASSES, 1, width), jnp.float32),
            jax.ShapeDtypeStruct((CLASSES, 1, width), jnp.float32),
        ],
        compiler_params=pltpu.CompilerParams(
            dimension_semantics=("arbitrary",), vmem_limit_bytes=56 << 20
        ),
        cost_estimate=pl.CostEstimate(flops=6 * 10**10, bytes_accessed=10**7, transcendentals=0),
        name="attention_backward",
    )(info, table, q, k, k_t, v, grad, attended_t, log_total)


def bucket_index(distance, bucket_count, max_dist=128):
    half_count = bucket_count // 2
    counted = jnp.zeros_like(distance)
    for number in range(1, bucket_count - half_count):
        border = math.ceil(half_count * (max_dist / half_count) ** (number / (bucket_count - half_count)))
        counted = counted + (distance >= border).astype(jnp.int32)
    return jnp.where(distance < half_count, distance, half_count + counted)


def attention_info(validity):
    trunk = jnp.sum(validity[:TRUNK])
    lengths = jnp.sum(validity[TRUNK:].reshape(NBRANCH, 1 + NLEAF, SEGMENT), axis=2)
    last = (trunk - 1) // TILE
    limits = jnp.concatenate([trunk - TILE * jnp.arange(TRUNK_TILES), lengths.reshape(-1)])
    left = trunk - last * TILE
    branch = lengths[:, 0]
    offsets = jnp.concatenate(
        [
            jnp.array([0, TILE, 4096, 0]),
            jnp.stack([left, left + TILE]),
            left + branch,
            left + branch + TILE,
            branch,
        ]
    )
    info = jnp.zeros((64,), jnp.int32)
    info = info.at[:20].set(limits).at[20].set(last).at[OFFSET_AT : OFFSET_AT + CLASSES].set(offsets)
    return info


def bias_table(rel_bias):
    places = bucket_index(jnp.arange(TILE, dtype=jnp.int32), rel_bias.shape[0])
    pick = (places[:, None] == jnp.arange(rel_bias.shape[0])[None, :]).astype(jnp.float32)
    shifted = rel_bias - rel_bias[-1:]
    return jnp.einsum("db,bh->hd", pick, shifted, precision=lax.Precision.HIGHEST)


def bias_gradient(ahead, behind, offsets, bucket_count):
    heads = ahead.shape[2] // TILE
    lane = jnp.arange(TILE, dtype=jnp.int32)[None, :]
    distance = jnp.stack([offsets[:, None] + lane, offsets[:, None] + lane - TILE], axis=0)
    bucket = bucket_index(jnp.maximum(distance, 0), bucket_count)
    pick = (bucket[..., None] == jnp.arange(bucket_count)).astype(jnp.float32)
    sums = jnp.stack([ahead, behind], axis=0).reshape(2, CLASSES, heads, TILE)
    return jnp.einsum("sclb,schl->bh", pick, sums, precision=lax.Precision.HIGHEST)


EPSILON = 1e-06
SLOT_TILE = 256


def slot_pick(slots, tile, count, axis):
    shape = (SLOT_TILE, count) if axis == 0 else (count, SLOT_TILE)
    places = lax.broadcasted_iota(jnp.int32, shape, axis)
    return (slots - tile * SLOT_TILE == places).astype(jnp.float32).astype(jnp.bfloat16)


def fill_slots(scalars, block, slots, values, out):
    def one(tile, carry):
        at = pl.ds(pl.multiple_of(tile * SLOT_TILE, SLOT_TILE), SLOT_TILE)
        pick = slot_pick(slots, tile, values.shape[0], 0)
        out[at, :] += jnp.dot(pick, values, preferred_element_type=jnp.float32).astype(jnp.bfloat16)
        return carry

    lax.fori_loop(scalars[block] // SLOT_TILE, pl.cdiv(scalars[block + 1], SLOT_TILE), one, 0)


def compact_rows_kernel(scalars, router, slots, named, *refs, blocks, experts):
    stacks, (out, gate) = refs[:-2], refs[-2:]
    rows = [(stack, number) for stack in stacks for number in range(stack.shape[0])]
    out[...] = jnp.zeros_like(out)
    me = scalars[blocks + 1]
    for b, (stack, number) in enumerate(rows):
        values = stack[number]
        fill_slots(scalars, b, slots[b], values, out)
        products = jnp.dot(values, router[...], preferred_element_type=jnp.float32)
        lane = lax.broadcasted_iota(jnp.int32, products.shape, 1)
        lane = jnp.where(lane < 3 * experts, lane % experts, -1)
        choices = [named[b, :, k : k + 1] for k in range(named.shape[2])]
        logits = [
            jnp.sum(jnp.where(lane == choice, products, 0.0), axis=1, keepdims=True) for choice in choices
        ]
        highest = functools.reduce(jnp.maximum, logits)
        powers = [jnp.exp(logit - highest) for logit in logits]
        mine = sum(jnp.where(choice == me, power, 0.0) for choice, power in zip(choices, powers))
        gate[b] = mine / sum(powers)


def whole_calls(kernel, operands, out_shape, name, limit):
    specs = [pl.BlockSpec(memory_space=pltpu.SMEM)]
    specs += [pl.BlockSpec(memory_space=pltpu.VMEM) for _ in operands[1:]]
    return pl.pallas_call(
        kernel,
        in_specs=specs,
        out_specs=jax.tree.map(lambda _: pl.BlockSpec(memory_space=pltpu.VMEM), out_shape),
        out_shape=out_shape,
        compiler_params=pltpu.CompilerParams(vmem_limit_bytes=limit << 20),
        cost_estimate=pl.CostEstimate(flops=10**10, bytes_accessed=3 * 10**7, transcendentals=0),
        name=name,
    )(*operands)


def slot_room(rows):
    return pl.cdiv(rows, SLOT_TILE) * SLOT_TILE


def compact_rows(scalars, router, slots, named, rows, experts):
    (blocks, count), width = slots.shape, rows[0].shape[2]
    return whole_calls(
        functools.partial(compact_rows_kernel, blocks=blocks, experts=experts),
        (scalars, router, slots.reshape(blocks, 1, count), named, *rows),
        [
            jax.ShapeDtypeStruct((slot_room(blocks * count), width), jnp.bfloat16),
            jax.ShapeDtypeStruct((blocks, count, 1), jnp.float32),
        ],
        "compact_rows",
        48,
    )


def compact_grads_kernel(scalars, slots, gate, produced, *refs, blocks):
    stacks, (out, gate_grad) = refs[:-2], refs[-2:]
    rows = [(stack, number) for stack in stacks for number in range(stack.shape[0])]
    out[...] = jnp.zeros_like(out)
    for b, (stack, number) in enumerate(rows):
        wide = stack[number].astype(jnp.float32)
        gate_grad[b] = jnp.sum(wide * produced[b].astype(jnp.float32), axis=1, keepdims=True)
        fill_slots(scalars, b, slots[b], (gate[b] * wide).astype(jnp.bfloat16), out)


def compact_grads(scalars, slots, gate, produced, rows):
    (blocks, count), width = slots.shape, rows[0].shape[2]
    return whole_calls(
        functools.partial(compact_grads_kernel, blocks=blocks),
        (scalars, slots.reshape(blocks, 1, count), gate, produced, *rows),
        [
            jax.ShapeDtypeStruct((slot_room(blocks * count), width), jnp.bfloat16),
            jax.ShapeDtypeStruct((blocks, count, 1), jnp.float32),
        ],
        "compact_grads",
        56,
    )


def expand_kernel(scalars, slots, *refs, blocks, gated):
    gate = refs[0] if gated else None
    rows, outs = (refs[1], refs[2:]) if gated else (refs[0], refs[1:])
    for b in range(blocks):
        out = outs[b]
        count = out.shape[0]
        out[...] = jnp.zeros_like(out)

        def one(tile, carry):
            at = pl.ds(pl.multiple_of(tile * SLOT_TILE, SLOT_TILE), SLOT_TILE)
            pick = slot_pick(slots[b], tile, count, 1)
            part = jnp.dot(pick, rows[at, :].astype(jnp.bfloat16), preferred_element_type=jnp.float32)
            out[...] += part.astype(jnp.bfloat16)
            return carry

        lax.fori_loop(scalars[b] // SLOT_TILE, pl.cdiv(scalars[b + 1], SLOT_TILE), one, 0)
        if gated:
            outs[blocks][b] = out[...]
            out[...] = (gate[b] * out[...].astype(jnp.float32)).astype(jnp.bfloat16)


def expand(scalars, slots, rows, gate=None):
    blocks, count = slots.shape
    width = rows.shape[1]
    shapes = [jax.ShapeDtypeStruct((count, width), jnp.bfloat16)] * blocks
    if gate is not None:
        shapes = shapes + [jax.ShapeDtypeStruct((blocks, count, width), jnp.bfloat16)]
    operands = (scalars, slots.reshape(blocks, count, 1)) + (() if gate is None else (gate,)) + (rows,)
    outs = whole_calls(
        functools.partial(expand_kernel, blocks=blocks, gated=gate is not None),
        operands, shapes, "expand", 56,
    )
    return outs if gate is None else (outs[:blocks], outs[blocks])


GELU_IN = math.sqrt(2.0 / math.pi)
GELU_CUBE = 0.044715


def gelu_parts(pre):
    square = pre * pre
    bent = jnp.tanh(GELU_IN * pre * (1.0 + GELU_CUBE * square))
    half = 0.5 * (1.0 + bent)
    return pre * half, half, bent, square


LAST = (((1,), (1,)), ((), ()))
FIRST = (((0,), (0,)), ((), ()))


def weight_sources(sources, z):
    if len(sources) == 1:
        return [[(None, sources[0].at[number])] for number in range(sources[0].shape[0])]
    own, up_one, down_one, up_two, down_two, far = sources
    low, high = z == 0, z == 3
    return [
        [(None, own)],
        [(z < 3, down_one), (high, up_one)],
        [(low, down_two), ((z == 1) | (z == 2), up_one), (high, up_two)],
        [(low | high, far), (z == 1, down_two), (z == 2, up_two)],
    ]


def weight_copies(step, sources, theirs, room, sem, act):
    def copy(slot, half, view):
        rows = view.shape[1]
        for matrix in range(3):
            act(
                pltpu.make_async_copy(
                    view.at[matrix],
                    room.at[slot, matrix, pl.ds(half * rows, rows)],
                    sem.at[slot, half * 3 + matrix],
                )
            )

    for number, choices in enumerate(sources):
        for condition, view in choices:
            here = step == number if condition is None else (step == number) & condition
            pl.when(here)(functools.partial(copy, number % 2, 0, view))
        pl.when(step == number)(functools.partial(copy, number % 2, 1, theirs.at[number]))


def next_weights(sources, theirs, room, sem):
    step, steps = pl.program_id(0), len(sources)

    @pl.when(step == 0)
    def _():
        weight_copies(step, sources, theirs, room, sem, lambda copy: copy.start())

    @pl.when(step + 1 < steps)
    def _():
        weight_copies(step + 1, sources, theirs, room, sem, lambda copy: copy.start())

    weight_copies(step, sources, theirs, room, sem, lambda copy: copy.wait())
    return step % 2


def expert_forward_kernel(scalars, rows, theirs, *refs):
    mine, (total, room, sem) = refs[:-3], refs[-3:]
    step = pl.program_id(0)
    slot = next_weights(weight_sources(mine, scalars[1]), theirs, room, sem)

    def one(tile, carry):
        at = pl.ds(pl.multiple_of(tile * SLOT_TILE, SLOT_TILE), SLOT_TILE)
        values = rows[at, :]
        gate_pre = lax.dot_general(values, room[slot, 0], LAST, preferred_element_type=jnp.float32)
        up_pre = lax.dot_general(values, room[slot, 1], LAST, preferred_element_type=jnp.float32)
        inner = (gelu_parts(gate_pre)[0] * up_pre).astype(jnp.bfloat16)
        part = jnp.dot(inner, room[slot, 2], preferred_element_type=jnp.float32)

        @pl.when(step == 0)
        def _():
            total[at, :] = part

        @pl.when(step > 0)
        def _():
            total[at, :] += part

        return carry

    lax.fori_loop(0, pl.cdiv(scalars[0], SLOT_TILE), one, 0)


def expert_cost(rows, weights, shards, units):
    return pl.CostEstimate(
        flops=2 * units * rows * shards * weights.shape[-2] * 2 * weights.shape[-1],
        bytes_accessed=4 * weights.size,
        transcendentals=0,
    )


def expert_scratch(weights):
    half, width = weights.shape[-2:]
    return [pltpu.VMEM((2, 3, 2 * half, width), jnp.bfloat16), pltpu.SemaphoreType.DMA((2, 6))]


def expert_forward(scalars, rows, mine, theirs):
    padded, width = rows.shape
    shards = theirs.shape[0]
    whole = pl.BlockSpec((padded, width), lambda s, scalars: (0, 0), pipeline_mode=pl.Buffered(1))
    return pl.pallas_call(
        expert_forward_kernel,
        grid_spec=pltpu.PrefetchScalarGridSpec(
            num_scalar_prefetch=1,
            grid=(shards,),
            in_specs=[whole] + [pl.BlockSpec(memory_space=pl.ANY)] * (1 + len(mine)),
            out_specs=whole,
            scratch_shapes=expert_scratch(theirs),
        ),
        out_shape=jax.ShapeDtypeStruct((padded, width), jnp.float32),
        compiler_params=pltpu.CompilerParams(vmem_limit_bytes=56 << 20),
        cost_estimate=expert_cost(padded, theirs, shards, 3),
        name="expert_forward",
    )(scalars, rows, theirs, *mine)


def expert_backward_kernel(scalars, rows, grads, theirs, *refs):
    mine, rest = refs[:-8], refs[-8:]
    mine_out, theirs_out, total, gate_total, up_total, down_total, room, sem = rest
    step = pl.program_id(0)
    slot = next_weights(weight_sources(mine, scalars[1]), theirs, room, sem)
    gate_total[...] = jnp.zeros_like(gate_total)
    up_total[...] = jnp.zeros_like(up_total)
    down_total[...] = jnp.zeros_like(down_total)

    def one(tile, carry):
        at = pl.ds(pl.multiple_of(tile * SLOT_TILE, SLOT_TILE), SLOT_TILE)
        values, upstream = rows[at, :], grads[at, :]
        gate_pre = lax.dot_general(values, room[slot, 0], LAST, preferred_element_type=jnp.float32)
        up_pre = lax.dot_general(values, room[slot, 1], LAST, preferred_element_type=jnp.float32)
        grad_inner = lax.dot_general(upstream, room[slot, 2], LAST, preferred_element_type=jnp.float32)
        active, half, bent, square = gelu_parts(gate_pre)
        slope = half + (0.5 * GELU_IN) * gate_pre * (1.0 - bent * bent) * (1.0 + 3.0 * GELU_CUBE * square)
        inner = (active * up_pre).astype(jnp.bfloat16)
        grad_gate = (grad_inner * up_pre * slope).astype(jnp.bfloat16)
        grad_up = (grad_inner * active).astype(jnp.bfloat16)
        down_total[...] += lax.dot_general(inner, upstream, FIRST, preferred_element_type=jnp.float32)
        gate_total[...] += lax.dot_general(grad_gate, values, FIRST, preferred_element_type=jnp.float32)
        up_total[...] += lax.dot_general(grad_up, values, FIRST, preferred_element_type=jnp.float32)
        part = jnp.dot(grad_gate, room[slot, 0], preferred_element_type=jnp.float32)
        part = part + jnp.dot(grad_up, room[slot, 1], preferred_element_type=jnp.float32)

        @pl.when(step == 0)
        def _():
            total[at, :] = part

        @pl.when(step > 0)
        def _():
            total[at, :] += part

        return carry

    lax.fori_loop(0, pl.cdiv(scalars[0], SLOT_TILE), one, 0)
    half = mine_out.shape[2]
    for number, sums in enumerate((gate_total, up_total, down_total)):
        mine_out[0, number] = sums[:half].astype(jnp.bfloat16)
        theirs_out[0, number] = sums[half:].astype(jnp.bfloat16)


def expert_backward(scalars, rows, grads, mine, theirs):
    padded, width = rows.shape
    shards, _, half, _ = theirs.shape
    whole = pl.BlockSpec((padded, width), lambda s, scalars: (0, 0), pipeline_mode=pl.Buffered(1))
    out = pl.BlockSpec((1, 3, half, width), lambda s, scalars: (scalars[2 + s], 0, 0, 0))
    shape = jax.ShapeDtypeStruct((shards, 3, half, width), jnp.bfloat16)
    return pl.pallas_call(
        expert_backward_kernel,
        grid_spec=pltpu.PrefetchScalarGridSpec(
            num_scalar_prefetch=1,
            grid=(shards,),
            in_specs=[whole, whole] + [pl.BlockSpec(memory_space=pl.ANY)] * (1 + len(mine)),
            out_specs=[out, out, whole],
            scratch_shapes=[pltpu.VMEM((2 * half, width), jnp.float32)] * 3 + expert_scratch(theirs),
        ),
        out_shape=[shape, shape, jax.ShapeDtypeStruct((padded, width), jnp.float32)],
        compiler_params=pltpu.CompilerParams(vmem_limit_bytes=60 << 20),
        cost_estimate=expert_cost(padded, theirs, shards, 8),
        name="expert_backward",
    )(scalars, rows, grads, theirs, *mine)


def project_kernel(scalars, weights, *refs, parts):
    mine, others = refs[:parts], refs[parts : 2 * parts]
    rows_out, q, k, k_t, v, v_t = refs[2 * parts :]
    count = mine[0].shape[0]
    columns = q.shape[1]
    active = scalars[parts] > 0
    for part in range(parts):
        at = pl.ds(pl.multiple_of(scalars[part] * count, count), count)
        rows = jnp.where(active, mine[part][...], others[part][...])
        rows_out[at, :] = rows
        low = jnp.dot(rows, weights[...], preferred_element_type=jnp.float32).astype(jnp.bfloat16)
        q[at, :] = low[:, :columns]
        k[at, :] = low[:, columns : 2 * columns]
        v[at, :] = low[:, 2 * columns :]
        k_t[:, at] = jnp.transpose(low[:, columns : 2 * columns])
        v_t[:, at] = jnp.transpose(low[:, 2 * columns :])


def project(scalars, weights, mine, others):
    parts, (count, width) = len(mine), mine[0].shape
    length, columns = parts * count, weights.shape[1] // 3
    tall = jax.ShapeDtypeStruct((length, columns), jnp.bfloat16)
    wide = jax.ShapeDtypeStruct((columns, length), jnp.bfloat16)
    return whole_calls(
        functools.partial(project_kernel, parts=parts),
        (scalars, weights, *mine, *others),
        [jax.ShapeDtypeStruct((length, width), jnp.bfloat16), tall, tall, wide, tall, wide],
        "project",
        56,
    )


def split_float(values):
    high = values.astype(jnp.bfloat16)
    rest = values - high.astype(jnp.float32)
    middle = rest.astype(jnp.bfloat16)
    low = (rest - middle.astype(jnp.float32)).astype(jnp.bfloat16)
    return jnp.concatenate([high, middle, low], axis=1)


def join_float(products, count):
    return products[:, 2 * count :] + products[:, count : 2 * count] + products[:, :count]


def swap(array, axis, bit):
    size = lax.axis_size(axis)
    return lax.ppermute(array, axis, [(i, i ^ bit) for i in range(size)])


def sum_over(array, axes):
    for axis in axes:
        bit = 1
        while bit < lax.axis_size(axis):
            array = array + swap(array, axis, bit)
            bit *= 2
    return array


def ring_layer():
    return lax.axis_size("expert") == 4


def layer_member(number):
    return lax.axis_index("expert") ^ number if ring_layer() else number


def layer_gather(rows):
    columns = lax.axis_size("expert")
    if not ring_layer():
        stacked = lax.all_gather(rows, "expert", axis=0)
        return [stacked[number] for number in range(columns)]
    half = rows.shape[0] // 2
    top, bottom = rows[:half], rows[half:]
    x_top, y_bottom = swap(top, "expert", 1), swap(bottom, "expert", 2)
    x_bottom, y_top = swap(bottom, "expert", 1), swap(top, "expert", 2)
    far_top, far_bottom = swap(x_top, "expert", 2), swap(y_bottom, "expert", 1)
    return [top, bottom, x_top, x_bottom, y_top, y_bottom, far_top, far_bottom]


def layer_scatter(parts):
    if not ring_layer():
        return lax.psum_scatter(
            jnp.stack(parts), "expert", scatter_dimension=0, tiled=False
        ).astype(jnp.float32)
    top, bottom, x_top, x_bottom, y_top, y_bottom, far_top, far_bottom = parts
    far_top, far_bottom = swap(far_top, "expert", 1), swap(far_bottom, "expert", 2)
    x_top, y_bottom = swap(x_top, "expert", 1), swap(y_bottom, "expert", 2)
    y_top = swap(y_top + far_top, "expert", 2)
    x_bottom = swap(x_bottom + far_bottom, "expert", 1)
    wide = lambda array: array.astype(jnp.float32)
    return jnp.concatenate(
        [wide(top) + wide(x_top) + wide(y_top), wide(bottom) + wide(x_bottom) + wide(y_bottom)], axis=0
    )


def layer_small(array):
    columns = lax.axis_size("expert")
    if not ring_layer():
        return lax.all_gather(array, "expert", axis=0)
    return jnp.stack([array] + [swap(array, "expert", number) for number in range(1, columns)])


def layer_trade(array):
    if not ring_layer():
        return lax.all_to_all(array, "expert", split_axis=0, concat_axis=0, tiled=True)
    return jnp.stack([array[0]] + [swap(array[n], "expert", n) for n in range(1, array.shape[0])])


def layer_blocks(array, rows):
    half = rows // 2
    return [
        lax.dynamic_slice_in_dim(array, layer_member(number) * rows + side * half, half, 0)
        for number in range(array.shape[0] // rows)
        for side in range(2)
    ]


def layer_place(pieces):
    if not ring_layer():
        return jnp.concatenate(pieces, axis=0)
    half = pieces[0].shape[0]
    out = jnp.zeros((half * len(pieces),) + pieces[0].shape[1:], pieces[0].dtype)
    for place, piece in enumerate(pieces):
        at = layer_member(place // 2) * 2 * half + (place % 2) * half
        out = lax.dynamic_update_slice_in_dim(out, piece, at, 0)
    return out


PLACE = ("shard", "dp")


def split_trees():
    return lax.axis_size("shard") == 4 and lax.axis_size("dp") == 2 and ring_layer()


def move(array, pairs):
    index = lambda place: place[0] * 2 + place[1]
    return lax.ppermute(array, PLACE, [(index(a), index(b)) for a, b in pairs])


def mirrored(pairs):
    flip = lambda place: (3 - place[0], 1 - place[1])
    return pairs + [(flip(a), flip(b)) for a, b in pairs]


def heads_place(group, tree):
    return (2 * tree + group // 2, group % 2)


def my_place():
    z, core = lax.axis_index("shard"), lax.axis_index("dp")
    return z, core, z // 2, 2 * (z % 2) + core


WEIGHT_PAIRS = [((group, tree), heads_place(group, tree)) for group in range(4) for tree in range(2)]


def weights_to_groups(array):
    return move(array, WEIGHT_PAIRS)


def groups_to_weights(array):
    return move(array, [(b, a) for a, b in WEIGHT_PAIRS])


def of_tree(array):
    z, core, tree, group = my_place()
    return jnp.where(core == tree, array, swap(array, "dp", 1))


def tree_gather(own):
    z, core, tree, group = my_place()
    first = move(own, mirrored([((1, 0), (0, 0)), ((2, 0), (1, 0)), ((3, 0), (2, 0))]))
    back = move(own, mirrored([((0, 0), (1, 0))]))
    second = move(first, mirrored([((1, 0), (0, 0)), ((2, 0), (1, 0))]))
    third = move(second, mirrored([((1, 0), (0, 0))]))
    end = (z == 0) | (z == 3)
    step = jnp.where(tree == 0, 1, -1)
    blocks = [own, first, second, jnp.where(end, third, back)]
    places = [z, z + step, z + 2 * step, jnp.where(end, z + 3 * step, z - step)]
    scalars = jnp.stack(places + [core == tree]).astype(jnp.int32)
    return scalars, blocks, [swap(block, "dp", 1) for block in blocks]


def tree_scatter(rows_of):
    z, core, tree, group = my_place()
    active, end = core == tree, (z == 0) | (z == 3)

    def chip_sum(place):
        part = rows_of(jnp.where(tree == 0, place, 3 - place))
        return part + swap(part, "dp", 1)

    far, next_far, next_near, near = chip_sum(3), chip_sum(2), chip_sum(1), chip_sum(0)
    one = move(jnp.where(end, far, near), mirrored([((0, 0), (1, 0)), ((1, 0), (0, 0))]))
    two = move(
        jnp.where(end, next_far, far + one), mirrored([((0, 0), (1, 0)), ((1, 0), (2, 0))])
    )
    three = move(
        jnp.where(active, jnp.where(end, next_near, next_far + two), two),
        mirrored([((0, 0), (1, 0)), ((1, 0), (2, 0)), ((2, 0), (3, 0))]),
    )
    wide = lambda array: array.astype(jnp.float32)
    at_end, in_middle = wide(near) + wide(one), wide(next_near) + wide(three)
    return jnp.where(active, jnp.where(end, at_end, in_middle), wide(three))


def gather_out_weight(weight):
    if not (split_trees()):
        return lax.all_gather(weight, "shard", axis=0, tiled=True)
    z = lax.axis_index("shard")
    rows, width = weight.shape
    quarter = rows // 4
    mine = lax.dynamic_slice_in_dim(weight, lax.axis_index("expert") * quarter, quarter, 0)
    stack = jnp.zeros((rows, width), weight.dtype)
    for number in range(4):
        piece = swap(mine, "shard", number) if number else mine
        stack = lax.dynamic_update_slice_in_dim(stack, piece, (z ^ number) * quarter, 0)
    stack = layer_place(layer_gather(stack)).reshape(4, 4, quarter, width)
    return stack.transpose(1, 0, 2, 3).reshape(4 * rows, width)


def hop(array, pairs):
    return lax.ppermute(array, "shard", pairs)


def weight_hop_one(own):
    if not split_trees():
        return (lax.all_gather(own, "shard", axis=0),)
    return hop(own, [(0, 1), (1, 2), (2, 3)]), hop(own, [(1, 0), (2, 1), (3, 2)])


def weight_hop_two(arrays):
    if not split_trees():
        return arrays
    return hop(arrays[0], [(1, 2), (2, 3)]), hop(arrays[1], [(2, 1), (1, 0)])


def weight_shards():
    z = lax.axis_index("shard")
    if not split_trees():
        return jnp.arange(lax.axis_size("shard"), dtype=jnp.int32)
    places = [
        z,
        jnp.where(z == 3, 2, z + 1),
        jnp.where(z == 0, 2, jnp.where(z == 3, 1, z - 1)),
        jnp.where(z < 2, 3, 0),
    ]
    return jnp.stack(places).astype(jnp.int32)


def greet(devices):
    barrier = pltpu.get_barrier_semaphore()
    for device in devices:
        pl.semaphore_signal(barrier, inc=1, device_id=device, device_id_type=pl.DeviceIdType.MESH)
    pl.semaphore_wait(barrier, len(devices))


def send_to(source, target, sems, number, device):
    return pltpu.make_async_remote_copy(
        src_ref=source,
        dst_ref=target,
        send_sem=sems.at[0, number],
        recv_sem=sems.at[1, number],
        device_id=device,
        device_id_type=pl.DeviceIdType.MESH,
    )


def meet_kernel(rows, own, up_one, down_one, up_two, down_two, layer, theirs, far, sems):
    column, z = lax.axis_index("expert"), lax.axis_index("shard")
    beside, above = {"expert": column ^ 1}, {"expert": column ^ 2}
    next_z, twin = {"shard": z ^ 1}, {"dp": lax.axis_index("dp") ^ 1}
    greet([beside, above, next_z, twin])
    x_top = send_to(rows.at[0], layer.at[0], sems, 0, beside)
    y_bottom = send_to(rows.at[1], layer.at[3], sems, 1, above)
    x_bottom = send_to(rows.at[1], layer.at[1], sems, 2, beside)
    y_top = send_to(rows.at[0], layer.at[2], sems, 3, above)
    for copy in (x_top, y_bottom, x_bottom, y_top):
        copy.start()

    hop_down = send_to(down_two, far, sems, 6, next_z)
    hop_up = send_to(up_two, far, sems, 6, next_z)
    pl.when(z == 1)(hop_down.start)
    pl.when(z == 2)(hop_up.start)
    places = weight_sources((own, up_one, down_one, up_two, down_two, far), z)
    ends = (z == 0) | (z == 3)
    for place, choices in enumerate(places):
        for condition, view in choices:
            if view is far:
                continue
            copy = send_to(view, theirs.at[place], sems, 7 + place, twin)
            if condition is None:
                copy.start()
            else:
                pl.when(condition)(copy.start)

    x_top.wait_recv()
    far_top = send_to(layer.at[0], layer.at[4], sems, 4, above)
    far_top.start()
    y_bottom.wait_recv()
    far_bottom = send_to(layer.at[3], layer.at[5], sems, 5, beside)
    far_bottom.start()
    last = send_to(far, theirs.at[3], sems, 10, twin)

    @pl.when(ends)
    def _():
        hop_down.wait_recv()
        last.start()

    @pl.when(jnp.logical_not(ends))
    def _():
        hop_down.wait_send()

    for copy in (x_top, y_bottom):
        copy.wait_send()
    for copy in (x_bottom, y_top, far_top, far_bottom):
        copy.wait()
    for place in range(4):
        send_to(own, theirs.at[place], sems, 7 + place, twin).wait()


def meet(rows, own, one, two):
    half = rows.shape[0] // 2
    halves = rows.reshape(2, half, rows.shape[1])
    anywhere = pl.BlockSpec(memory_space=pl.ANY)
    layer, theirs, far = pl.pallas_call(
        meet_kernel,
        in_specs=[anywhere] * 6,
        out_specs=[anywhere] * 3,
        out_shape=[
            jax.ShapeDtypeStruct((6,) + halves.shape[1:], rows.dtype),
            jax.ShapeDtypeStruct((4,) + own.shape, own.dtype),
            jax.ShapeDtypeStruct(own.shape, own.dtype),
        ],
        scratch_shapes=[pltpu.SemaphoreType.DMA((2, 11))],
        compiler_params=pltpu.CompilerParams(collective_id=1, has_side_effects=True),
        cost_estimate=pl.CostEstimate(flops=5 * 10**10, bytes_accessed=10**7, transcendentals=0),
        name="meet",
    )(halves, own, *one, *two)
    return [halves, layer], theirs, (own, *one, *two, far)


def reduce_attention_grads(three, out):
    width = out.shape[1]
    if not (split_trees()):
        if split_trees():
            three = groups_to_weights(three)
        out = lax.psum_scatter(out, "shard", scatter_dimension=0, tiled=True)
        three = lax.psum(three, ("expert", "dp"))
        return three.astype(jnp.float32), lax.psum(out, ("expert", "dp")).astype(jnp.float32)
    z = lax.axis_index("shard")
    quarter = width // 4
    part = quarter // 4
    columns = three.shape[1]
    out = out.reshape(4, 4, part, width).transpose(1, 0, 2, 3).reshape(width, width)
    both = jnp.concatenate([three, out], axis=1)
    both = layer_scatter(layer_blocks(both, quarter)).astype(jnp.bfloat16)
    three = groups_to_weights(both[:, :columns])
    out = both[:, columns:]
    pieces = [lax.dynamic_slice_in_dim(out, (z ^ number) * part, part, 0) for number in range(4)]
    pieces = [pieces[0]] + [swap(pieces[number], "shard", number) for number in range(1, 4)]
    out = sum(piece.astype(jnp.float32) for piece in pieces).astype(jnp.bfloat16)
    both = jnp.concatenate([three, out.reshape(quarter, width // 4)], axis=1)
    both = both + swap(both, "dp", 1)
    both = layer_place(layer_gather(both))
    out = both[:, columns:].reshape(4 * part, width)
    return both[:, :columns].astype(jnp.float32), out.astype(jnp.float32)


def trade_pairs(turn):
    return [
        (heads_place(group, tree), ((group + turn) % 4, tree)) for group in range(4) for tree in range(2)
    ]


def heads_to_rows(attended_t, shards):
    columns, length = attended_t.shape
    rows = length // shards
    if not split_trees():
        pieces = attended_t.reshape(columns, shards, rows).transpose(1, 0, 2)
        pieces = lax.all_to_all(pieces, "shard", split_axis=0, concat_axis=0, tiled=True)
        return pieces.reshape(shards * columns, rows)
    z, core, tree, group = my_place()
    out = jnp.zeros((shards * columns, rows), attended_t.dtype)
    for turn in range(4):
        piece = lax.dynamic_slice_in_dim(attended_t, (group + turn) % 4 * rows, rows, 1)
        piece = move(piece, trade_pairs(turn))
        out = lax.dynamic_update_slice_in_dim(out, piece, (z - turn) % 4 * columns, 0)
    return out


def rows_to_heads(grads, shards):
    rows, width = grads.shape
    columns = width // shards
    if not split_trees():
        pieces = grads.reshape(rows, shards, columns).transpose(1, 0, 2)
        pieces = lax.all_to_all(pieces, "shard", split_axis=0, concat_axis=0, tiled=True)
        return pieces.reshape(shards * rows, columns)
    z, core, tree, group = my_place()
    out = jnp.zeros((shards * rows, columns), grads.dtype)
    for turn in range(4):
        piece = lax.dynamic_slice_in_dim(grads, (z - turn) % 4 * columns, columns, 1)
        piece = move(piece, [(b, a) for a, b in trade_pairs(turn)])
        out = lax.dynamic_update_slice_in_dim(out, piece, (group + turn) % 4 * rows, 0)
    return out


def on_device(
    tokens, teacher, seg_ids, parents, depth, valid, routes, norm1_gain, w_query, w_key, w_value,
    w_out, rel_bias, norm2_gain, router, w_gate, w_up, w_down,
):
    shard_index = lax.axis_index("shard")
    expert_index = lax.axis_index("expert")
    shards = lax.axis_size("shard")
    columns = lax.axis_size("expert")
    experts = columns * w_gate.shape[0]
    token_rows = tokens[0].astype(jnp.float32)
    local_rows, width = token_rows.shape
    length = seg_ids.shape[1]
    bucket_count = rel_bias.shape[0]
    validity = valid[0]
    route_rows = routes[0]

    row_start = shard_index * local_rows
    valid_local = lax.dynamic_slice_in_dim(validity, row_start, local_rows, 0).astype(jnp.float32)
    route_local = lax.dynamic_slice_in_dim(route_rows, row_start, local_rows, 0)

    scale_one = lax.rsqrt(jnp.mean(token_rows * token_rows, axis=1, keepdims=True) + EPSILON)
    base_one = token_rows * scale_one
    normed_one = (base_one * norm1_gain).astype(jnp.bfloat16)
    expert_w = jnp.stack([w_gate[0].T, w_up[0].T, w_down[0]])
    half = expert_w.shape[1] // lax.axis_size("dp")
    expert_w = lax.dynamic_slice_in_dim(expert_w, lax.axis_index("dp") * half, half, 1)
    out_all = gather_out_weight(w_out)
    info = attention_info(validity)
    weights = jnp.concatenate([w_query, w_key, w_value], axis=1)
    bias_here = rel_bias
    if split_trees():
        info, bias_here = of_tree(info), weights_to_groups(rel_bias)
        if ring_layer():
            quarter = width // columns
            mine = lax.dynamic_slice_in_dim(weights, expert_index * quarter, quarter, 0)
            mine, normed_one = lax.optimization_barrier((weights_to_groups(mine), normed_one))
            weights = layer_place(layer_gather(mine))
        else:
            weights = weights_to_groups(weights)
        places, mine, others = tree_gather(normed_one)
        mine[3], expert_w = lax.optimization_barrier((mine[3], expert_w))
        weights_one = weight_hop_one(expert_w)
        weights, out_all = lax.optimization_barrier((weights, out_all))
        normed_all, query_rows, key_rows, key_t, value_rows, value_t = project(
            places, weights, mine, others
        )
    else:
        normed_all = lax.all_gather(normed_one, "shard", axis=0, tiled=True)
        projected = jnp.dot(normed_all, weights, preferred_element_type=jnp.float32).astype(jnp.bfloat16)
        query_rows, key_rows, value_rows = jnp.split(projected, 3, axis=1)
        key_t, value_t = key_rows.T, value_rows.T
        weights_one = weight_hop_one(expert_w)
    tree_count = sum_over(jnp.broadcast_to(jnp.sum(validity), (8, 128)), ("dp", "expert"))
    valid_total = tree_count[0, 0].astype(jnp.float32)

    top_count = route_local.shape[1]
    route_layer = layer_small(route_local.T)
    taken = jnp.any(route_layer == expert_index, axis=1)
    order = jnp.cumsum(taken.reshape(-1).astype(jnp.int32))
    slots = jnp.where(taken, order.reshape(taken.shape) - 1, -1)
    half_blocks = 2 * columns if ring_layer() else columns
    block_rows = columns * local_rows // half_blocks
    slots = slots.reshape(half_blocks, block_rows)
    named = route_layer.transpose(0, 2, 1).reshape(half_blocks, block_rows, top_count)
    scalars = jnp.concatenate(
        [jnp.zeros((1,), jnp.int32), order[block_rows - 1 :: block_rows], expert_index[None].astype(jnp.int32)]
    )

    table = bias_table(bias_here)
    attended_t, log_totals = attention_forward(info, table, query_rows, key_rows, value_t)

    attended_t, *weights_one = lax.optimization_barrier((attended_t, *weights_one))
    attended_here = heads_to_rows(attended_t, shards)
    weights_two = weight_hop_two(weights_one)
    update = lax.dot_general(
        attended_here, out_all, (((0,), (0,)), ((), ())), preferred_element_type=jnp.float32
    )
    hidden = token_rows + update

    scale_two = lax.rsqrt(jnp.mean(hidden * hidden, axis=1, keepdims=True) + EPSILON)
    base_two = hidden * scale_two
    normed_two = (base_two * norm2_gain).astype(jnp.bfloat16)

    expert_ids = jnp.arange(experts, dtype=jnp.int32)
    router_pieces = split_float(router)

    def gates_of(rows, named):
        logits = join_float(jnp.dot(rows, router_pieces, preferred_element_type=jnp.float32), experts)
        match = named[:, :, None] == expert_ids[None, None, :]
        chosen = jnp.sum(jnp.where(match, logits[:, None, :], 0.0), axis=2)
        return jax.nn.softmax(chosen, axis=1), match

    gates, route_match = gates_of(normed_two, route_local)
    if split_trees():
        normed_layer, theirs_w, mine_w = meet(normed_two, expert_w, weights_one, weights_two)
    else:
        normed_layer = [block[None] for block in layer_gather(normed_two)]
        mine_w = weights_one
        theirs_w = swap(weights_one[0], "dp", 1)
    expert_scalars = jnp.concatenate(
        [order[-1:], shard_index[None].astype(jnp.int32), weight_shards()]
    )
    router_wide = jnp.pad(router_pieces, ((0, 0), (0, TILE - router_pieces.shape[1])))
    expert_rows, gate_here = compact_rows(scalars, router_wide, slots, named, normed_layer, experts)
    produced = expert_forward(expert_scalars, expert_rows, mine_w, theirs_w)
    shares, produced_layer = expand(scalars, slots, produced, gate_here)
    combined = layer_scatter(shares)

    output_rows = hidden + combined
    factor = length * columns * lax.axis_size("dp") / valid_total
    error = output_rows - teacher[0].astype(jnp.float32)
    error_sum = jnp.sum(valid_local[:, None] * error * error)
    grad_output = valid_local[:, None] * error * factor
    grad_layer = [block[None] for block in layer_gather(grad_output.astype(jnp.bfloat16))]
    grad_rows, gate_grads = compact_grads(scalars, slots, gate_here, produced_layer, grad_layer)
    gate_grads = layer_trade(gate_grads.reshape(columns, local_rows))
    mine_part, theirs_part, rows_grad = expert_backward(
        expert_scalars, expert_rows, grad_rows, mine_w, theirs_w
    )
    expanded = expand(scalars, slots, rows_grad)
    *expanded, mine_part, theirs_part = lax.optimization_barrier((*expanded, mine_part, theirs_part))
    expert_back = layer_scatter(expanded)
    weight_part = mine_part + swap(theirs_part, "dp", 1)
    weight_part = lax.psum_scatter(weight_part, "shard", scatter_dimension=0, tiled=False)

    members = jnp.stack([jnp.asarray(layer_member(number), jnp.int32) for number in range(columns)])
    grad_gates = jnp.sum(
        jnp.where(route_local[:, :, None] == members[None, None, :], gate_grads.T[:, None, :], 0.0), axis=2
    )
    weighted = jnp.sum(gates * grad_gates, axis=1, keepdims=True)
    grad_chosen = gates * (grad_gates - weighted)
    grad_logits = jnp.sum(jnp.where(route_match, grad_chosen[:, :, None], 0.0), axis=1)
    router_grad = join_float(
        lax.dot_general(
            normed_two, split_float(grad_logits), (((0,), (0,)), ((), ())),
            preferred_element_type=jnp.float32,
        ),
        experts,
    )
    grad_normed_two = expert_back
    for number in range(experts):
        grad_normed_two = grad_normed_two + grad_logits[:, number : number + 1] * router[:, number][None]
    grad_base_two = grad_normed_two * norm2_gain
    norm2_grad = jnp.sum(grad_normed_two * base_two, axis=0)
    grad_hidden = grad_output + scale_two * (
        grad_base_two - base_two * jnp.mean(grad_base_two * base_two, axis=1, keepdims=True)
    )
    grad_update = grad_hidden.astype(jnp.bfloat16)
    out_grad = jnp.dot(attended_here, grad_update, preferred_element_type=jnp.float32)
    grad_heads = lax.dot_general(
        grad_update, out_all, (((1,), (1,)), ((), ())), preferred_element_type=jnp.float32
    ).astype(jnp.bfloat16)
    grad_attended = rows_to_heads(grad_heads, shards)

    grad_queries_t, grad_keys, grad_values, ahead, behind = attention_backward(
        info, table, query_rows, key_rows, key_t, value_rows, grad_attended, attended_t, log_totals
    )
    bias_grad = bias_gradient(ahead, behind, info[OFFSET_AT : OFFSET_AT + CLASSES], bucket_count)
    across = (((0,), (0,)), ((), ()))
    grad_three = jnp.concatenate([grad_queries_t.T, grad_keys, grad_values], axis=1)
    three_wgrad = lax.dot_general(normed_all, grad_three, across, preferred_element_type=jnp.float32)
    norm1_grad = jnp.sum(three_wgrad * weights.astype(jnp.float32), axis=1) / norm1_gain
    def normed_part(block):
        part = lax.dynamic_slice_in_dim(grad_three, block * local_rows, local_rows, 0)
        part = lax.dot_general(
            part, weights, (((1,), (1,)), ((), ())), preferred_element_type=jnp.float32
        )
        return part.astype(jnp.bfloat16)

    if split_trees():
        grad_normed_one = tree_scatter(normed_part)
    else:
        grad_normed_all = jnp.concatenate([normed_part(block) for block in range(shards)], axis=0)
        grad_normed_one = lax.psum_scatter(
            grad_normed_all, "shard", scatter_dimension=0, tiled=True
        ).astype(jnp.float32)
    grad_base_one = grad_normed_one * norm1_gain
    grad_tokens = grad_hidden + scale_one * (
        grad_base_one - base_one * jnp.mean(grad_base_one * base_one, axis=1, keepdims=True)
    )
    three_wgrad, out_grad = reduce_attention_grads(
        three_wgrad.astype(jnp.bfloat16), out_grad.astype(jnp.bfloat16)
    )
    query_wgrad, key_wgrad, value_wgrad = jnp.split(three_wgrad, 3, axis=1)
    heads_here = bias_grad.shape[1]
    group = my_place()[3] if split_trees() else shard_index
    bias_all = lax.dynamic_update_slice_in_dim(
        jnp.zeros((bucket_count, heads_here * shards), jnp.float32), bias_grad, group * heads_here, 1
    )
    bias_line = jnp.pad(bias_all.reshape(-1), (0, width - bias_all.size))
    small = jnp.concatenate(
        [router_grad.T, norm2_grad[None], norm1_grad[None], bias_line[None], jnp.full((1, width), error_sum)],
        axis=0,
    )
    small = sum_over(small, ("dp", "expert", "shard"))
    router_grad, norm2_grad, norm1_grad = small[:experts].T, small[experts], small[experts + 1]
    bias_all = small[experts + 2, : bias_all.size].reshape(bias_all.shape)
    bias_grad = lax.dynamic_slice_in_dim(bias_all, shard_index * heads_here, heads_here, 1)
    error_total = small[experts + 3, 0]
    loss = error_total / (width * valid_total)

    other_part = swap(weight_part, "dp", 1)
    first_core = lax.axis_index("dp") == 0
    weight_grad = jnp.concatenate(
        [jnp.where(first_core, weight_part, other_part), jnp.where(first_core, other_part, weight_part)],
        axis=1,
    ).astype(jnp.float32)
    gate_grad, up_grad, down_grad = weight_grad[0].T[None], weight_grad[1].T[None], weight_grad[2][None]
    return (
        output_rows.astype(jnp.bfloat16)[None],
        loss,
        grad_tokens[None],
        norm1_grad,
        query_wgrad,
        key_wgrad,
        value_wgrad,
        out_grad,
        bias_grad,
        norm2_grad,
        router_grad,
        gate_grad,
        up_grad,
        down_grad,
    )


def solution(mesh):
    in_specs = (
        P(("expert", "dp"), "shard", None),
        P(("expert", "dp"), "shard", None),
        P(("expert", "dp"), None),
        P(("expert", "dp"), None),
        P(("expert", "dp"), None),
        P(("expert", "dp"), None),
        P(("expert", "dp"), None, None),
        P(),
        P(None, "shard"),
        P(None, "shard"),
        P(None, "shard"),
        P("shard", None),
        P(None, "shard"),
        P(),
        P(),
        P("expert", None, "shard"),
        P("expert", None, "shard"),
        P("expert", "shard", None),
    )
    out_specs = (
        P(("expert", "dp"), "shard", None),
        P(),
        P(("expert", "dp"), "shard", None),
        P(),
        P(None, "shard"),
        P(None, "shard"),
        P(None, "shard"),
        P("shard", None),
        P(None, "shard"),
        P(),
        P(),
        P("expert", None, "shard"),
        P("expert", None, "shard"),
        P("expert", "shard", None),
    )
    return jax.shard_map(
        on_device, mesh=mesh, in_specs=in_specs, out_specs=out_specs, check_vma=False
    )
```

time: 1430 us -> 1050 us (0.73)
  waiting for transfers between devices: 870 us -> 250 us
  starting transfers between devices: 44.7 us -> 293 us
  blocking collectives: 92.2 us -> 0 us
  Pallas kernels: 225 us -> 292 us
  other arithmetic: 49.7 us -> 84.4 us
    all_gather x13 -> x0, waiting for transfers between devices: 375 us -> none  [the longest x6 135 us: gather_weight(): return lax.all_gather(lax.all_gather(mine, 'shard', axis=0), 'dp', axis=0)]
    ppermute x0 -> x96, starting transfers between devices: none -> 293 us  [the longest x74 193 us: swap(): return lax.ppermute(array, axis, [(i, i ^ bit) for i in range(size)])]
    ppermute x0 -> x96, waiting for transfers between devices: none -> 250 us  [the longest x74 165 us: swap(): return lax.ppermute(array, axis, [(i, i ^ bit) for i in range(size)])]
    reduce_scatter x8 -> x1, waiting for transfers between devices: 248 us -> 0.01 us  [on_device(): lax.psum_scatter(weight_part, 'shard', scatter_dimension=0, tiled=False)]
    all_to_all x3 -> x0, waiting for transfers between devices: 130 us -> none  [the longest x1 65 us: on_device(): lax.all_to_all(pieces, 'shard', split_axis=0, concat_axis=0, tiled=True)]
    pallas_call x4 -> x6, Pallas kernels: 36.4 us -> 123 us  [the longest x5 64.1 us: whole_calls(): pl.pallas_call(kernel, in_specs=specs, out_specs=jax.tree.map(lambda _: p...]
    psum x3 -> x0, blocking collectives: 77.4 us -> none  [the longest x1 41.5 us: on_device(): lax.psum((router_grad, norm1_grad, norm2_grad, error_sum), ('expert', 'sh...]
    unnamed x26 -> x1, waiting for transfers between devices: 76.2 us -> 0.02 us
  transfers between devices with their start and end apart: 27 -> 97, of which waited for: 24 -> 32; matrix products, arithmetic and copies ran while one was open for 10% -> 15% of each run, Pallas kernels for 6% -> 9%
where the time goes in v2:
time: 1050 us; the launch traced here: 1040 us
  starting transfers between devices  293 us (28%)
  Pallas kernels  292 us (28%)
  waiting for transfers between devices  250 us (24%)
  other arithmetic  84.4 us (8%)
  local copies, waits for them, and re-layouts  70.8 us (7%)
  matrix products  26.9 us (3%)
  between operations  20.4 us (2%)
    ppermute x74, starting transfers between devices, swap(): return lax.ppermute(array, axis, [(i, i ^ bit) for i in range(size)])  193 us
    ppermute x74, waiting for transfers between devices, swap(): return lax.ppermute(array, axis, [(i, i ^ bit) for i in range(size)])  165 us
    ppermute x18, starting transfers between devices, move(): return lax.ppermute(array, PLACE, [(index(a), index(b)) for a, b in pairs])  85.7 us
    ppermute x18, waiting for transfers between devices, move(): return lax.ppermute(array, PLACE, [(index(a), index(b)) for a, b in pairs])  84.6 us
    pallas_call x5, Pallas kernels, whole_calls(): pl.pallas_call(kernel, in_specs=specs, out_specs=jax.tree.map(lambda _: p...  64.1 us
    pallas_call x1, Pallas kernels, expert_backward(): pl.pallas_call(expert_backward_kernel, grid_spec=pltpu.PrefetchScalarGrid...  59.7 us
    pallas_call x1, Pallas kernels, meet(): pl.pallas_call(meet_kernel, in_specs=[anywhere] * 6, out_specs=[anywhere]...  58.6 us
    pallas_call x1, Pallas kernels, attention_backward(): pl.pallas_call(functools.partial(backward_kernel, heads=heads, tiles=tile...  53.1 us
  transfers between devices with their start and end apart: 97, of which 32 were waited for; matrix products, arithmetic and copies ran while one was open for 15% of the time, Pallas kernels for 9%

profile of v2, /device:TPU:0, one launch (start us, length us, event | category | flops | bytes accessed | tf_op | source)
XLA Modules:
  0.0 1037.3 jit_solution(8169343156682619936)
XLA Ops:
  8.6 3.9 collective-permute-start.34
  22.8 10.7 %collective-permute-start = (s32[64]{0:T(128)S(1)}, s32[64]{0:T(128)S(1)}, u32[]{:S(2)}, u32[]{:S(2)}) collective-permute-start(s32[64]{0:T(128)S(1)} %constant_dynamic-update-slice_fusion.38), channel_id=1, source_target_pairs={{0,1},{1,0},{2,3},{3,2},{4,5},{5,4},{6,7},{7,6},{8,9},{9,8},{10,11... | collective-permute-start | bytes 776 | tf_op jit(solution)/shard_map/ppermute | solution.py:742
  35.2 13.0 %collective-permute-done.18.refs_1_ = bf16[640,1024]{1,0:T(8,128)(2,1)} collective-permute-done((bf16[640,1024]{1,0:T(8,128)(2,1)}, bf16[640,1024]{1,0:T(8,128)(2,1)}, u32[]{:S(2)}, u32[]{:S(2)}) %collective-permute-start.18) | collective-permute-done | bytes 1310752 | tf_op jit(solution)/shard_map/ppermute | solution.py:833
  53.6 16.4 %collective-permute-start.9 = (bf16[64,1024]{1,0:T(8,128)(2,1)S(1)}, bf16[64,1024]{1,0:T(8,128)(2,1)S(1)}, u32[]{:S(2)}, u32[]{:S(2)}) collective-permute-start(bf16[64,1024]{1,0:T(8,128)(2,1)S(1)} %get-tuple-element.260), channel_id=1, source_target_pairs={{0,2},{2,0},{4,6},{6,4},{1,3},{3,1},{5,7},{7,5},{8,10},{10,8},{12,... | collective-permute-start | bytes 393224 | tf_op jit(solution)/shard_map/ppermute | solution.py:742
  91.8 4.2 collective-permute-done.12
  112.5 5.2 collective-permute-done.16
  118.6 5.6 collective-permute-done.17
  124.9 4.9 collective-permute-done.7
  135.5 9.1 collective-permute-start.26
  148.6 12.3 %project.1 = (bf16[2560,1024]{1,0:T(8,128)(2,1)}, bf16[2560,256]{1,0:T(8,128)(2,1)}, bf16[2560,256]{1,0:T(8,128)(2,1)}, bf16[256,2560]{1,0:T(8,128)(2,1)}, bf16[...) custom-call(s32[5]{0:T(128)} %stack.108.scalars, bf16[1024,768]{1,0:T(8,128)(2,1)} %copy-done.32, ...), custom_call_target="tpu_custom_call" | custom-call | flops 10000000000 | bytes 30000000 | tf_op jit(solution)/shard_map/project/pallas_call | solution.py:422
  163.5 28.2 %attention_forward.1 = (bf16[256,2560]{1,0:T(8,128)(2,1)S(1)}, f32[20,1,512]{2,1,0:T(1,128)S(1)}) custom-call(s32[64]{0:T(128)S(1)} %broadcast_select_fusion.4.info, f32[4,128]{1,0:T(4,128)S(1)} %fusion.45.table, bf16[2560,256]{1,0:T(8,128)(2,1)S(1)} %copy-done.8, bf16[2560,256]{1,0:T(8,128)(2,1)S(1)} %copy-done.9, bf16[256,2560]{1,0:T(8,128)(2,1)} %get-tuple-element.115.v_t), custom_call_target="tpu_custom_call" | custom-call | flops 40000000000 | bytes 10000000 | tf_op jit(solution)/shard_map/attention_forward/pallas_call | solution.py:163
  196.8 9.7 collective-permute-start.29
  209.1 46.0 %collective-permute-start.31 = (bf16[256,640]{1,0:T(8,128)(2,1)S(1)}, bf16[256,640]{1,0:T(8,128)(2,1)S(1)}, u32[]{:S(2)}, u32[]{:S(2)}) collective-permute-start(bf16[256,640]{1,0:T(8,128)(2,1)S(1)} %get-tuple-element.288), channel_id=1, source_target_pairs={{0,6},{4,7},{1,0},{5,1},{2,2},{6,3},{3,4},{7,5},{8,14},{12,15},{9,... | collective-permute-start | bytes 983048 | tf_op jit(solution)/shard_map/ppermute | solution.py:833
  256.4 7.2 collective-permute-done.31
  269.1 58.6 %meet.1 = (bf16[6,320,1024]{2,1,0:T(8,128)(2,1)}, bf16[4,3,352,1024]{3,2,1,0:T(8,128)(2,1)}, bf16[3,352,1024]{2,1,0:T(8,128)(2,1)}) custom-call(bf16[2,320,1024]{2,1,0:T(8,128)(2,1)} %bitcast.131, bf16[3,352,1024]{2,1,0:T(8,128)(2,1)} %fusion.18.own.refs_0_, bf16[3,352,1024]{2,1,0:T(8,128)(2,1)} %collective-permute-done.26.up_one.refs_1_, ...), custom_call_target="tpu_custom_call" | custom-call | flops 49999998976 | bytes 10000000 | tf_op jit(solution)/shard_map/meet/pallas_call | solution.py:1021
  327.7 12.6 %compact_rows.1 = (bf16[2560,1024]{1,0:T(8,128)(2,1)}, f32[8,320,1]{2,1,0:T(8,128)S(1)}) custom-call(s32[10]{0:T(128)S(1)} %pad_add_fusion.2.scalars, bf16[1024,128]{1,0:T(8,128)(2,1)S(1)} %pad.15.router, s32[8,1,320]{2,1,0:T(1,128)S(1)} %add_select_fusion.2.slots, s32[8,320,2]{2,1,0:T(8,128)S(1)} %bitcast.133, bf16[2,320,1024]{2,1,0:T(8,128)(2,1)S(1)} %bitcast.132, ...), custom_call_target="tpu_custom_call" | custom-call | flops 10000000000 | bytes 30000000 | tf_op jit(solution)/shard_map/compact_rows/pallas_call | solution.py:422
  341.3 27.9 %expert_forward.1.refs_1_ = f32[2560,1024]{1,0:T(8,128)} custom-call(s32[6]{0:T(128)} %concatenate.62.scalars, bf16[2560,1024]{1,0:T(8,128)(2,1)} %get-tuple-element.124.rows, bf16[4,3,352,1024]{3,2,1,0:T(8,128)(2,1)} %get-tuple-element.125.theirs, bf16[3,352,1024]{2,1,0:T(8,128)(2,1)} %fusion.18.own.refs_0_, ...), custom_call_target="tpu_custom_call" | custom-call | flops 44291850240 | bytes 17301504 | tf_op jit(solution)/shard_map/expert_forward/pallas_call | solution.py:615
  369.2 14.1 %expand.2 = (bf16[320,1024]{1,0:T(8,128)(2,1)}, bf16[320,1024]{1,0:T(8,128)(2,1)}, bf16[320,1024]{1,0:T(8,128)(2,1)}, bf16[320,1024]{1,0:T(8,128)(2,1)}, bf16[32...) custom-call(s32[10]{0:T(128)} %copy-done.5, ...), custom_call_target="tpu_custom_call" | custom-call | flops 10000000000 | bytes 30000000 | tf_op jit(solution)/shard_map/expand/pallas_call | solution.py:422
  383.3 22.2 %collective-permute-start.40 = (bf16[320,1024]{1,0:T(8,128)(2,1)}, bf16[320,1024]{1,0:T(8,128)(2,1)S(1)}, u32[]{:S(2)}, u32[]{:S(2)}) collective-permute-start(bf16[320,1024]{1,0:T(8,128)(2,1)} %get-tuple-element.133), channel_id=1, source_target_pairs={{0,16},{8,24},{16,0},{24,8},{1,17},{9,25},{17,1},{25,9},{2,18},{10... | collective-permute-start | bytes 1966088 | tf_op jit(solution)/shard_map/ppermute | solution.py:742
  407.7 13.5 %collective-permute-done.40 = bf16[320,1024]{1,0:T(8,128)(2,1)S(1)} collective-permute-done((bf16[320,1024]{1,0:T(8,128)(2,1)}, bf16[320,1024]{1,0:T(8,128)(2,1)S(1)}, u32[]{:S(2)}, u32[]{:S(2)}) %collective-permute-start.40) | collective-permute-done | bytes 655392 | tf_op jit(solution)/shard_map/ppermute | solution.py:742
  432.2 21.4 %collective-permute-done.44 = s32[8,128]{1,0:T(8,128)S(1)} collective-permute-done((s32[8,128]{1,0:T(8,128)S(1)}, s32[8,128]{1,0:T(8,128)S(1)}, u32[]{:S(2)}, u32[]{:S(2)}) %collective-permute-start.44) | collective-permute-done | bytes 4128 | tf_op jit(solution)/shard_map/ppermute | solution.py:742
  468.4 13.6 %collective-permute-done.46 = bf16[320,1024]{1,0:T(8,128)(2,1)S(1)} collective-permute-done((bf16[320,1024]{1,0:T(8,128)(2,1)S(1)}, bf16[320,1024]{1,0:T(8,128)(2,1)S(1)}, u32[]{:S(2)}, u32[]{:S(2)}) %collective-permute-start.46) | collective-permute-done | bytes 655392 | tf_op jit(solution)/shard_map/ppermute | solution.py:742
  485.8 10.3 collective-permute-done.47
  497.8 11.2 %collective-permute-done.50 = bf16[320,1024]{1,0:T(8,128)(2,1)S(1)} collective-permute-done((bf16[320,1024]{1,0:T(8,128)(2,1)S(1)}, bf16[320,1024]{1,0:T(8,128)(2,1)S(1)}, u32[]{:S(2)}, u32[]{:S(2)}) %collective-permute-start.50) | collective-permute-done | bytes 655392 | tf_op jit(solution)/shard_map/ppermute | solution.py:742
  510.1 14.3 %compact_grads.1 = (bf16[2560,1024]{1,0:T(8,128)(2,1)}, f32[8,320,1]{2,1,0:T(8,128)}) custom-call(s32[10]{0:T(128)} %copy-done.5, s32[8,1,320]{2,1,0:T(1,128)} %copy-done.2, f32[8,320,1]{2,1,0:T(8,128)} %copy-done.7, bf16[8,320,1024]{2,1,0:T(8,128)(2,1)} %get-tuple-element.135.produced, bf16[1,320,1024]{2,1,0:T(8,128)(2,1)} %get-tuple-element.285.refs_0_, ...), custom_call_target="tpu_custom_call" | custom-call | flops 10000000000 | bytes 30000000 | tf_op jit(solution)/shard_map/compact_grads/pallas_call | solution.py:422
  524.4 59.7 %expert_backward.1 = (bf16[4,3,352,1024]{3,2,1,0:T(8,128)(2,1)}, bf16[4,3,352,1024]{3,2,1,0:T(8,128)(2,1)}, f32[2560,1024]{1,0:T(8,128)}) custom-call(s32[6]{0:T(128)} %concatenate.62.scalars, bf16[2560,1024]{1,0:T(8,128)(2,1)} %get-tuple-element.124.rows, bf16[2560,1024]{1,0:T(8,128)(2,1)} %get-tuple-element.137.grads, ...), custom_call_target="tpu_custom_call" | custom-call | flops 118111600640 | bytes 17301504 | tf_op jit(solution)/shard_map/expert_backward/pallas_call | solution.py:680
  584.2 11.0 %expand.3 = (bf16[320,1024]{1,0:T(8,128)(2,1)}, bf16[320,1024]{1,0:T(8,128)(2,1)}, bf16[320,1024]{1,0:T(8,128)(2,1)}, bf16[320,1024]{1,0:T(8,128)(2,1)}, bf16[32...) custom-call(s32[10]{0:T(128)} %copy-done.5, ...), custom_call_target="tpu_custom_call" | custom-call | flops 10000000000 | bytes 30000000 | tf_op jit(solution)/shard_map/expand/pallas_call | solution.py:422
  597.9 47.2 %collective-permute-start.54 = (f32[640]{0:T(1024)S(1)}, f32[640]{0:T(1024)S(1)}, u32[]{:S(2)}, u32[]{:S(2)}) collective-permute-start(f32[640]{0:T(1024)S(1)} %squeeze.41), channel_id=1, source_target_pairs={{0,24},{8,16},{16,8},{24,0},{1,25},{9,17},{17,9},{25,1},{2,26},{10... | collective-permute-start | bytes 7688 | tf_op jit(solution)/shard_map/ppermute | solution.py:742
  652.9 25.8 %collective-permute-done.58 = bf16[320,1024]{1,0:T(8,128)(2,1)} collective-permute-done((bf16[320,1024]{1,0:T(8,128)(2,1)}, bf16[320,1024]{1,0:T(8,128)(2,1)}, u32[]{:S(2)}, u32[]{:S(2)}) %collective-permute-start.58) | collective-permute-done | bytes 655392 | tf_op jit(solution)/shard_map/ppermute | solution.py:742
  686.1 10.1 collective-permute-done.59
  697.6 9.2 add.844
  710.2 7.0 multiply_reduce_fusion.1
  732.2 31.7 %collective-permute-done.62 = bf16[640,256]{1,0:T(8,128)(2,1)S(1)} collective-permute-done((bf16[640,256]{1,0:T(8,128)(2,1)S(1)}, bf16[640,256]{1,0:T(8,128)(2,1)S(1)}, u32[]{:S(2)}, u32[]{:S(2)}) %collective-permute-start.62) | collective-permute-done | bytes 327712 | tf_op jit(solution)/shard_map/ppermute | solution.py:833
  763.9 27.9 %collective-permute-done.63 = bf16[640,256]{1,0:T(8,128)(2,1)S(1)} collective-permute-done((bf16[640,256]{1,0:T(8,128)(2,1)S(1)}, bf16[640,256]{1,0:T(8,128)(2,1)S(1)}, u32[]{:S(2)}, u32[]{:S(2)}) %collective-permute-start.63) | collective-permute-done | bytes 327712 | tf_op jit(solution)/shard_map/ppermute | solution.py:833
  793.0 53.1 %attention_backward.1 = (bf16[256,2560]{1,0:T(8,128)(2,1)}, bf16[2560,256]{1,0:T(8,128)(2,1)}, bf16[2560,256]{1,0:T(8,128)(2,1)}, f32[18,1,512]{2,1,0:T(1,128)}, f32[18,1,512]{2,1,0:T(1,128)}) custom-call(s32[64]{0:T(128)} %copy-done.3, f32[4,128]{1,0:T(4,128)} %copy-done.6, bf16[2560,256]{1,0:T(8,128)(2,1)} %get-tuple-element.113.q, ...), custom_call_target="tpu_custom_call" | custom-call | flops 60000002048 | bytes 10000000 | tf_op jit(solution)/shard_map/attention_backward/pallas_call | solution.py:295
  854.5 8.7 fusion.129
  865.5 3.7 copy.133
  882.3 5.6 collective-permute-done.66
  898.9 3.6 broadcast_select_fusion.2
  904.7 22.3 %collective-permute-start.68 = (f32[8,1024]{1,0:T(8,128)S(1)}, f32[8,1024]{1,0:T(8,128)S(1)}, u32[]{:S(2)}, u32[]{:S(2)}) collective-permute-start(f32[8,1024]{1,0:T(8,128)S(1)} %add.817), channel_id=1, source_target_pairs={{0,2},{2,0},{4,6},{6,4},{1,3},{3,1},{5,7},{7,5},{8,10},{10,8},{12,... | collective-permute-start | bytes 98312 | tf_op jit(solution)/shard_map/ppermute | solution.py:742
  931.2 3.8 collective-permute-start.86
  941.1 13.9 %collective-permute-done.69 = f32[8,1024]{1,0:T(8,128)S(1)} collective-permute-done((f32[8,1024]{1,0:T(8,128)S(1)}, f32[8,1024]{1,0:T(8,128)S(1)}, u32[]{:S(2)}, u32[]{:S(2)}) %collective-permute-start.69) | collective-permute-done | bytes 32800 | tf_op jit(solution)/shard_map/ppermute | solution.py:742
  964.7 4.3 add_select_fusion
  969.1 4.6 collective-permute-start.75
  996.8 3.6 collective-permute-start.76
  1014.8 4.0 fusion.6
  1018.8 5.1 fusion.10
  1025.4 3.7 fusion.119
  (574 shorter events, 251.4 us)
Async XLA Ops:
  7.2 1000.7 %reduce-scatter.2.cloned.1.call-start = ((), (), s32[]{:S(2)}) async-start(), calls=%async_computation.1 | async-start | bytes 10813440 | tf_op jit(solution)/shard_map/reduce_scatter | solution.py:1226
  8.6 61.8 %collective-permute-start.34 = (s32[2,640]{1,0:T(2,128)S(1)}, s32[2,640]{1,0:T(2,128)S(1)}, u32[]{:S(2)}, u32[]{:S(2)}) collective-permute-start(s32[2,640]{1,0:T(2,128)S(1)} %get-tuple-element.307), channel_id=1, source_target_pairs={{0,24},{8,16},{16,8},{24,0},{1,25},{9,17},{17,9},{25,1},{2,26},{10... | collective-permute-start | bytes 15368 | tf_op jit(solution)/shard_map/ppermute | solution.py:742
  12.5 58.0 %collective-permute-start.33 = (s32[2,640]{1,0:T(2,128)S(1)}, s32[2,640]{1,0:T(2,128)S(1)}, u32[]{:S(2)}, u32[]{:S(2)}) collective-permute-start(s32[2,640]{1,0:T(2,128)S(1)} %get-tuple-element.307), channel_id=1, source_target_pairs={{0,16},{8,24},{16,0},{24,8},{1,17},{9,25},{17,1},{25,9},{2,18},{10... | collective-permute-start | bytes 15368 | tf_op jit(solution)/shard_map/ppermute | solution.py:742
  13.0 59.8 %collective-permute-start.32 = (s32[2,640]{1,0:T(2,128)S(1)}, s32[2,640]{1,0:T(2,128)S(1)}, u32[]{:S(2)}, u32[]{:S(2)}) collective-permute-start(s32[2,640]{1,0:T(2,128)S(1)} %get-tuple-element.307), channel_id=1, source_target_pairs={{0,8},{8,0},{16,24},{24,16},{1,9},{9,1},{17,25},{25,17},{2,10},{10... | collective-permute-start | bytes 15368 | tf_op jit(solution)/shard_map/ppermute | solution.py:742
  18.1 30.0 %collective-permute-start.18 = (bf16[640,1024]{1,0:T(8,128)(2,1)}, bf16[640,1024]{1,0:T(8,128)(2,1)}, u32[]{:S(2)}, u32[]{:S(2)}) collective-permute-start(bf16[640,1024]{1,0:T(8,128)(2,1)} %fusion.5.refs_0_), channel_id=1, source_target_pairs={{2,0},{4,2},{6,4},{5,7},{3,5},{1,3},{10,8},{12,10},{14,12},{13,15}... | collective-permute-start | bytes 3932168 | tf_op jit(solution)/shard_map/ppermute | solution.py:833
  22.8 30.1 %collective-permute-start = (s32[64]{0:T(128)S(1)}, s32[64]{0:T(128)S(1)}, u32[]{:S(2)}, u32[]{:S(2)}) collective-permute-start(s32[64]{0:T(128)S(1)} %constant_dynamic-update-slice_fusion.38), channel_id=1, source_target_pairs={{0,1},{1,0},{2,3},{3,2},{4,5},{5,4},{6,7},{7,6},{8,9},{9,8},{10,11... | collective-permute-start | bytes 776 | tf_op jit(solution)/shard_map/ppermute | solution.py:742
  48.2 36.1 %collective-permute-start.19 = (bf16[640,1024]{1,0:T(8,128)(2,1)}, bf16[640,1024]{1,0:T(8,128)(2,1)}, u32[]{:S(2)}, u32[]{:S(2)}) collective-permute-start(bf16[640,1024]{1,0:T(8,128)(2,1)} %collective-permute-done.18.refs_1_), channel_id=1, source_target_pairs={{2,0},{4,2},{5,7},{3,5},{10,8},{12,10},{13,15},{11,13},{18,16},{20... | collective-permute-start | bytes 3932168 | tf_op jit(solution)/shard_map/ppermute | solution.py:833
  53.6 26.3 %collective-permute-start.9 = (bf16[64,1024]{1,0:T(8,128)(2,1)S(1)}, bf16[64,1024]{1,0:T(8,128)(2,1)S(1)}, u32[]{:S(2)}, u32[]{:S(2)}) collective-permute-start(bf16[64,1024]{1,0:T(8,128)(2,1)S(1)} %get-tuple-element.260), channel_id=1, source_target_pairs={{0,2},{2,0},{4,6},{6,4},{1,3},{3,1},{5,7},{7,5},{8,10},{10,8},{12,... | collective-permute-start | bytes 393224 | tf_op jit(solution)/shard_map/ppermute | solution.py:742
  107.1 37.5 %collective-permute-start.22 = (bf16[640,1024]{1,0:T(8,128)(2,1)}, bf16[640,1024]{1,0:T(8,128)(2,1)S(1)}, u32[]{:S(2)}, u32[]{:S(2)}) collective-permute-start(bf16[640,1024]{1,0:T(8,128)(2,1)} %fusion.5.refs_0_), channel_id=1, source_target_pairs={{0,1},{1,0},{2,3},{3,2},{4,5},{5,4},{6,7},{7,6},{8,9},{9,8},{10,11... | collective-permute-start | bytes 3932168 | tf_op jit(solution)/shard_map/ppermute | solution.py:742
  107.2 39.2 %collective-permute-start.23 = (bf16[640,1024]{1,0:T(8,128)(2,1)}, bf16[640,1024]{1,0:T(8,128)(2,1)S(1)}, u32[]{:S(2)}, u32[]{:S(2)}) collective-permute-start(bf16[640,1024]{1,0:T(8,128)(2,1)} %collective-permute-done.18.refs_1_), channel_id=1, source_target_pairs={{0,1},{1,0},{2,3},{3,2},{4,5},{5,4},{6,7},{7,6},{8,9},{9,8},{10,11... | collective-permute-start | bytes 3932168 | tf_op jit(solution)/shard_map/ppermute | solution.py:742
  108.7 38.9 %collective-permute-start.24 = (bf16[640,1024]{1,0:T(8,128)(2,1)}, bf16[640,1024]{1,0:T(8,128)(2,1)S(1)}, u32[]{:S(2)}, u32[]{:S(2)}) collective-permute-start(bf16[640,1024]{1,0:T(8,128)(2,1)} %collective-permute-done.19.refs_2_), channel_id=1, source_target_pairs={{0,1},{1,0},{2,3},{3,2},{4,5},{5,4},{6,7},{7,6},{8,9},{9,8},{10,11... | collective-permute-start | bytes 3932168 | tf_op jit(solution)/shard_map/ppermute | solution.py:742
  108.7 39.8 %collective-permute-start.25 = (bf16[640,1024]{1,0:T(8,128)(2,1)S(1)}, bf16[640,1024]{1,0:T(8,128)(2,1)}, u32[]{:S(2)}, u32[]{:S(2)}) collective-permute-start(bf16[640,1024]{1,0:T(8,128)(2,1)S(1)} %broadcast_select_fusion.3.refs_3_), channel_id=1, source_target_pairs={{0,1},{1,0},{2,3},{3,2},{4,5},{5,4},{6,7},{7,6},{8,9},{9,8},{10,11... | collective-permute-start | bytes 3932168 | tf_op jit(solution)/shard_map/ppermute | solution.py:742
  135.5 56.2 %collective-permute-start.26 = (bf16[3,352,1024]{2,1,0:T(8,128)(2,1)S(1)}, bf16[3,352,1024]{2,1,0:T(8,128)(2,1)}, u32[]{:S(2)}, u32[]{:S(2)}) collective-permute-start(bf16[3,352,1024]{2,1,0:T(8,128)(2,1)S(1)} %copy-done.41), channel_id=1, source_target_pairs={{0,2},{2,4},{4,6},{1,3},{3,5},{5,7},{8,10},{10,12},{12,14},{9,11},... | collective-permute-start | bytes 6488072 | tf_op jit(solution)/shard_map/ppermute | solution.py:918
  144.6 47.2 %collective-permute-start.27 = (bf16[3,352,1024]{2,1,0:T(8,128)(2,1)S(1)}, bf16[3,352,1024]{2,1,0:T(8,128)(2,1)}, u32[]{:S(2)}, u32[]{:S(2)}) collective-permute-start(bf16[3,352,1024]{2,1,0:T(8,128)(2,1)S(1)} %copy-done.41), channel_id=1, source_target_pairs={{2,0},{4,2},{6,4},{3,1},{5,3},{7,5},{10,8},{12,10},{14,12},{11,9},... | collective-permute-start | bytes 6488072 | tf_op jit(solution)/shard_map/ppermute | solution.py:918
  191.8 77.1 %collective-permute-start.35 = (bf16[3,352,1024]{2,1,0:T(8,128)(2,1)}, bf16[3,352,1024]{2,1,0:T(8,128)(2,1)}, u32[]{:S(2)}, u32[]{:S(2)}) collective-permute-start(bf16[3,352,1024]{2,1,0:T(8,128)(2,1)} %collective-permute-done.26.up_one.refs_1_), channel_id=1, source_target_pairs={{2,4},{4,6},{3,5},{5,7},{10,12},{12,14},{11,13},{13,15},{18,20},{2... | collective-permute-start | bytes 6488072 | tf_op jit(solution)/shard_map/ppermute | solution.py:918
  194.0 74.9 %collective-permute-start.36 = (bf16[3,352,1024]{2,1,0:T(8,128)(2,1)}, bf16[3,352,1024]{2,1,0:T(8,128)(2,1)}, u32[]{:S(2)}, u32[]{:S(2)}) collective-permute-start(bf16[3,352,1024]{2,1,0:T(8,128)(2,1)} %collective-permute-done.27.down_one.refs_2_), channel_id=1, source_target_pairs={{4,2},{2,0},{5,3},{3,1},{12,10},{10,8},{13,11},{11,9},{20,18},{18,... | collective-permute-start | bytes 6488072 | tf_op jit(solution)/shard_map/ppermute | solution.py:918
  196.8 59.4 %collective-permute-start.29 = (bf16[256,640]{1,0:T(8,128)(2,1)S(1)}, bf16[256,640]{1,0:T(8,128)(2,1)S(1)}, u32[]{:S(2)}, u32[]{:S(2)}) collective-permute-start(bf16[256,640]{1,0:T(8,128)(2,1)S(1)} %get-tuple-element.290), channel_id=1, source_target_pairs={{0,2},{4,3},{1,4},{5,5},{2,6},{6,7},{3,0},{7,1},{8,10},{12,11},{9,... | collective-permute-start | bytes 983048 | tf_op jit(solution)/shard_map/ppermute | solution.py:833
  209.0 47.3 %collective-permute-start.30 = (bf16[256,640]{1,0:T(8,128)(2,1)S(1)}, bf16[256,640]{1,0:T(8,128)(2,1)S(1)}, u32[]{:S(2)}, u32[]{:S(2)}) collective-permute-start(bf16[256,640]{1,0:T(8,128)(2,1)S(1)} %get-tuple-element.289), channel_id=1, source_target_pairs={{0,4},{4,5},{1,6},{5,7},{2,0},{6,1},{3,2},{7,3},{8,12},{12,13},{9,... | collective-permute-start | bytes 983048 | tf_op jit(solution)/shard_map/ppermute | solution.py:833
  209.1 54.5 %collective-permute-start.31 = (bf16[256,640]{1,0:T(8,128)(2,1)S(1)}, bf16[256,640]{1,0:T(8,128)(2,1)S(1)}, u32[]{:S(2)}, u32[]{:S(2)}) collective-permute-start(bf16[256,640]{1,0:T(8,128)(2,1)S(1)} %get-tuple-element.288), channel_id=1, source_target_pairs={{0,6},{4,7},{1,0},{5,1},{2,2},{6,3},{3,4},{7,5},{8,14},{12,15},{9,... | collective-permute-start | bytes 983048 | tf_op jit(solution)/shard_map/ppermute | solution.py:833
  383.3 37.9 %collective-permute-start.40 = (bf16[320,1024]{1,0:T(8,128)(2,1)}, bf16[320,1024]{1,0:T(8,128)(2,1)S(1)}, u32[]{:S(2)}, u32[]{:S(2)}) collective-permute-start(bf16[320,1024]{1,0:T(8,128)(2,1)} %get-tuple-element.133), channel_id=1, source_target_pairs={{0,16},{8,24},{16,0},{24,8},{1,17},{9,25},{17,1},{25,9},{2,18},{10... | collective-permute-start | bytes 1966088 | tf_op jit(solution)/shard_map/ppermute | solution.py:742
  406.4 52.9 %collective-permute-start.42 = (bf16[320,1024]{1,0:T(8,128)(2,1)}, bf16[320,1024]{1,0:T(8,128)(2,1)S(1)}, u32[]{:S(2)}, u32[]{:S(2)}) collective-permute-start(bf16[320,1024]{1,0:T(8,128)(2,1)} %get-tuple-element.134), channel_id=1, source_target_pairs={{0,16},{8,24},{16,0},{24,8},{1,17},{9,25},{17,1},{25,9},{2,18},{10... | collective-permute-start | bytes 1966088 | tf_op jit(solution)/shard_map/ppermute | solution.py:742
  423.4 36.0 %collective-permute-start.41 = (bf16[320,1024]{1,0:T(8,128)(2,1)}, bf16[320,1024]{1,0:T(8,128)(2,1)S(1)}, u32[]{:S(2)}, u32[]{:S(2)}) collective-permute-start(bf16[320,1024]{1,0:T(8,128)(2,1)} %add.774), channel_id=1, source_target_pairs={{0,8},{8,0},{16,24},{24,16},{1,9},{9,1},{17,25},{25,17},{2,10},{10... | collective-permute-start | bytes 1966088 | tf_op jit(solution)/shard_map/ppermute | solution.py:742
  427.1 32.7 %collective-permute-start.37 = (bf16[320,1024]{1,0:T(8,128)(2,1)}, bf16[320,1024]{1,0:T(8,128)(2,1)S(1)}, u32[]{:S(2)}, u32[]{:S(2)}) collective-permute-start(bf16[320,1024]{1,0:T(8,128)(2,1)} %get-tuple-element.128), channel_id=1, source_target_pairs={{0,8},{8,0},{16,24},{24,16},{1,9},{9,1},{17,25},{25,17},{2,10},{10... | collective-permute-start | bytes 1966088 | tf_op jit(solution)/shard_map/ppermute | solution.py:742
  428.7 31.1 %collective-permute-start.39 = (bf16[320,1024]{1,0:T(8,128)(2,1)S(1)}, bf16[320,1024]{1,0:T(8,128)(2,1)S(1)}, u32[]{:S(2)}, u32[]{:S(2)}) collective-permute-start(bf16[320,1024]{1,0:T(8,128)(2,1)S(1)} %add.772), channel_id=1, source_target_pairs={{0,16},{8,24},{16,0},{24,8},{1,17},{9,25},{17,1},{25,9},{2,18},{10... | collective-permute-start | bytes 1966088 | tf_op jit(solution)/shard_map/ppermute | solution.py:742
  468.1 28.0 %collective-permute-start.47 = (bf16[320,1024]{1,0:T(8,128)(2,1)S(1)}, bf16[320,1024]{1,0:T(8,128)(2,1)S(1)}, u32[]{:S(2)}, u32[]{:S(2)}) collective-permute-start(bf16[320,1024]{1,0:T(8,128)(2,1)S(1)} %get-tuple-element.284), channel_id=1, source_target_pairs={{0,8},{8,0},{16,24},{24,16},{1,9},{9,1},{17,25},{25,17},{2,10},{10... | collective-permute-start | bytes 1966088 | tf_op jit(solution)/shard_map/ppermute | solution.py:742
  468.4 29.4 %collective-permute-start.48 = (bf16[320,1024]{1,0:T(8,128)(2,1)S(1)}, bf16[320,1024]{1,0:T(8,128)(2,1)S(1)}, u32[]{:S(2)}, u32[]{:S(2)}) collective-permute-start(bf16[320,1024]{1,0:T(8,128)(2,1)S(1)} %get-tuple-element.287), channel_id=1, source_target_pairs={{0,16},{8,24},{16,0},{24,8},{1,17},{9,25},{17,1},{25,9},{2,18},{10... | collective-permute-start | bytes 1966088 | tf_op jit(solution)/shard_map/ppermute | solution.py:742
  482.0 27.0 %collective-permute-start.50 = (bf16[320,1024]{1,0:T(8,128)(2,1)S(1)}, bf16[320,1024]{1,0:T(8,128)(2,1)S(1)}, u32[]{:S(2)}, u32[]{:S(2)}) collective-permute-start(bf16[320,1024]{1,0:T(8,128)(2,1)S(1)} %collective-permute-done.46), channel_id=1, source_target_pairs={{0,16},{8,24},{16,0},{24,8},{1,17},{9,25},{17,1},{25,9},{2,18},{10... | collective-permute-start | bytes 1966088 | tf_op jit(solution)/shard_map/ppermute | solution.py:742
  484.0 25.0 %collective-permute-start.51 = (bf16[320,1024]{1,0:T(8,128)(2,1)S(1)}, bf16[320,1024]{1,0:T(8,128)(2,1)S(1)}, u32[]{:S(2)}, u32[]{:S(2)}) collective-permute-start(bf16[320,1024]{1,0:T(8,128)(2,1)S(1)} %collective-permute-done.49), channel_id=1, source_target_pairs={{0,8},{8,0},{16,24},{24,16},{1,9},{9,1},{17,25},{25,17},{2,10},{10... | collective-permute-start | bytes 1966088 | tf_op jit(solution)/shard_map/ppermute | solution.py:742
  595.1 102.4 %collective-permute-start.94 = (bf16[4,3,352,1024]{3,2,1,0:T(8,128)(2,1)}, bf16[4,3,352,1024]{3,2,1,0:T(8,128)(2,1)}, u32[]{:S(2)}, u32[]{:S(2)}) collective-permute-start(bf16[4,3,352,1024]{3,2,1,0:T(8,128)(2,1)} %get-tuple-element.167), channel_id=1, source_target_pairs={{0,1},{1,0},{2,3},{3,2},{4,5},{5,4},{6,7},{7,6},{8,9},{9,8},{10,11... | collective-permute-start | bytes 25952264 | tf_op jit(solution)/shard_map/ppermute | solution.py:742
  597.9 52.0 %collective-permute-start.54 = (f32[640]{0:T(1024)S(1)}, f32[640]{0:T(1024)S(1)}, u32[]{:S(2)}, u32[]{:S(2)}) collective-permute-start(f32[640]{0:T(1024)S(1)} %squeeze.41), channel_id=1, source_target_pairs={{0,24},{8,16},{16,8},{24,0},{1,25},{9,17},{17,9},{25,1},{2,26},{10... | collective-permute-start | bytes 7688 | tf_op jit(solution)/shard_map/ppermute | solution.py:742
  647.8 38.3 %collective-permute-start.60 = (bf16[320,1024]{1,0:T(8,128)(2,1)}, bf16[320,1024]{1,0:T(8,128)(2,1)S(1)}, u32[]{:S(2)}, u32[]{:S(2)}) collective-permute-start(bf16[320,1024]{1,0:T(8,128)(2,1)} %get-tuple-element.156), channel_id=1, source_target_pairs={{0,16},{8,24},{16,0},{24,8},{1,17},{9,25},{17,1},{25,9},{2,18},{10... | collective-permute-start | bytes 1966088 | tf_op jit(solution)/shard_map/ppermute | solution.py:742
  649.9 28.9 %collective-permute-start.58 = (bf16[320,1024]{1,0:T(8,128)(2,1)}, bf16[320,1024]{1,0:T(8,128)(2,1)}, u32[]{:S(2)}, u32[]{:S(2)}) collective-permute-start(bf16[320,1024]{1,0:T(8,128)(2,1)} %get-tuple-element.155), channel_id=1, source_target_pairs={{0,16},{8,24},{16,0},{24,8},{1,17},{9,25},{17,1},{25,9},{2,18},{10... | collective-permute-start | bytes 1966088 | tf_op jit(solution)/shard_map/ppermute | solution.py:742
  650.6 30.5 %collective-permute-start.56 = (bf16[320,1024]{1,0:T(8,128)(2,1)}, bf16[320,1024]{1,0:T(8,128)(2,1)S(1)}, u32[]{:S(2)}, u32[]{:S(2)}) collective-permute-start(bf16[320,1024]{1,0:T(8,128)(2,1)} %get-tuple-element.152), channel_id=1, source_target_pairs={{0,8},{8,0},{16,24},{24,16},{1,9},{9,1},{17,25},{25,17},{2,10},{10... | collective-permute-start | bytes 1966088 | tf_op jit(solution)/shard_map/ppermute | solution.py:742
  651.3 55.7 %collective-permute-start.55 = (bf16[320,1024]{1,0:T(8,128)(2,1)}, bf16[320,1024]{1,0:T(8,128)(2,1)}, u32[]{:S(2)}, u32[]{:S(2)}) collective-permute-start(bf16[320,1024]{1,0:T(8,128)(2,1)} %get-tuple-element.150), channel_id=1, source_target_pairs={{0,8},{8,0},{16,24},{24,16},{1,9},{9,1},{17,25},{25,17},{2,10},{10... | collective-permute-start | bytes 1966088 | tf_op jit(solution)/shard_map/ppermute | solution.py:742
  722.5 41.4 %collective-permute-start.62 = (bf16[640,256]{1,0:T(8,128)(2,1)S(1)}, bf16[640,256]{1,0:T(8,128)(2,1)S(1)}, u32[]{:S(2)}, u32[]{:S(2)}) collective-permute-start(bf16[640,256]{1,0:T(8,128)(2,1)S(1)} %get-tuple-element.282), channel_id=1, source_target_pairs={{2,0},{3,4},{4,1},{5,5},{6,2},{7,6},{0,3},{1,7},{10,8},{11,12},{12... | collective-permute-start | bytes 983048 | tf_op jit(solution)/shard_map/ppermute | solution.py:833
  724.4 67.4 %collective-permute-start.63 = (bf16[640,256]{1,0:T(8,128)(2,1)S(1)}, bf16[640,256]{1,0:T(8,128)(2,1)S(1)}, u32[]{:S(2)}, u32[]{:S(2)}) collective-permute-start(bf16[640,256]{1,0:T(8,128)(2,1)S(1)} %get-tuple-element.281), channel_id=1, source_target_pairs={{4,0},{5,4},{6,1},{7,5},{0,2},{1,6},{2,3},{3,7},{12,8},{13,12},{14... | collective-permute-start | bytes 983048 | tf_op jit(solution)/shard_map/ppermute | solution.py:833
  728.3 63.6 %collective-permute-start.64 = (bf16[640,256]{1,0:T(8,128)(2,1)S(1)}, bf16[640,256]{1,0:T(8,128)(2,1)S(1)}, u32[]{:S(2)}, u32[]{:S(2)}) collective-permute-start(bf16[640,256]{1,0:T(8,128)(2,1)S(1)} %get-tuple-element.280), channel_id=1, source_target_pairs={{6,0},{7,4},{0,1},{1,5},{2,2},{3,6},{4,3},{5,7},{14,8},{15,12},{8,... | collective-permute-start | bytes 983048 | tf_op jit(solution)/shard_map/ppermute | solution.py:833
  852.2 42.5 %collective-permute-start.70 = (bf16[640,1024]{1,0:T(8,128)(2,1)S(1)}, bf16[640,1024]{1,0:T(8,128)(2,1)}, u32[]{:S(2)}, u32[]{:S(2)}) collective-permute-start(bf16[640,1024]{1,0:T(8,128)(2,1)S(1)} %convolution_convert_fusion.4), channel_id=1, source_target_pairs={{0,1},{1,0},{2,3},{3,2},{4,5},{5,4},{6,7},{7,6},{8,9},{9,8},{10,11... | collective-permute-start | bytes 3932168 | tf_op jit(solution)/shard_map/ppermute | solution.py:742
  869.3 29.6 %collective-permute-start.71 = (bf16[640,1024]{1,0:T(8,128)(2,1)}, bf16[640,1024]{1,0:T(8,128)(2,1)}, u32[]{:S(2)}, u32[]{:S(2)}) collective-permute-start(bf16[640,1024]{1,0:T(8,128)(2,1)} %convolution_convert_fusion.3), channel_id=1, source_target_pairs={{0,1},{1,0},{2,3},{3,2},{4,5},{5,4},{6,7},{7,6},{8,9},{9,8},{10,11... | collective-permute-start | bytes 3932168 | tf_op jit(solution)/shard_map/ppermute | solution.py:742
  891.8 35.3 %collective-permute-start.77 = (bf16[128,1792]{1,0:T(8,128)(2,1)S(1)}, bf16[128,1792]{1,0:T(8,128)(2,1)S(1)}, u32[]{:S(2)}, u32[]{:S(2)}) collective-permute-start(bf16[128,1792]{1,0:T(8,128)(2,1)S(1)} %get-tuple-element.271), channel_id=1, source_target_pairs={{0,8},{8,0},{16,24},{24,16},{1,9},{9,1},{17,25},{25,17},{2,10},{10... | collective-permute-start | bytes 1376264 | tf_op jit(solution)/shard_map/ppermute | solution.py:742
  893.1 35.9 %collective-permute-start.82 = (bf16[128,1792]{1,0:T(8,128)(2,1)S(1)}, bf16[128,1792]{1,0:T(8,128)(2,1)S(1)}, u32[]{:S(2)}, u32[]{:S(2)}) collective-permute-start(bf16[128,1792]{1,0:T(8,128)(2,1)S(1)} %get-tuple-element.274), channel_id=1, source_target_pairs={{0,16},{8,24},{16,0},{24,8},{1,17},{9,25},{17,1},{25,9},{2,18},{10... | collective-permute-start | bytes 1376264 | tf_op jit(solution)/shard_map/ppermute | solution.py:742
  894.7 34.4 %collective-permute-start.81 = (bf16[128,1792]{1,0:T(8,128)(2,1)S(1)}, bf16[128,1792]{1,0:T(8,128)(2,1)S(1)}, u32[]{:S(2)}, u32[]{:S(2)}) collective-permute-start(bf16[128,1792]{1,0:T(8,128)(2,1)S(1)} %get-tuple-element.273), channel_id=1, source_target_pairs={{0,8},{8,0},{16,24},{24,16},{1,9},{9,1},{17,25},{25,17},{2,10},{10... | collective-permute-start | bytes 1376264 | tf_op jit(solution)/shard_map/ppermute | solution.py:742
  898.9 65.8 %collective-permute-start.74 = (bf16[640,1024]{1,0:T(8,128)(2,1)}, bf16[640,1024]{1,0:T(8,128)(2,1)}, u32[]{:S(2)}, u32[]{:S(2)}) collective-permute-start(bf16[640,1024]{1,0:T(8,128)(2,1)} %convolution_convert_fusion.1), channel_id=1, source_target_pairs={{0,1},{1,0},{2,3},{3,2},{4,5},{5,4},{6,7},{7,6},{8,9},{9,8},{10,11... | collective-permute-start | bytes 3932168 | tf_op jit(solution)/shard_map/ppermute | solution.py:742
  904.7 30.3 %collective-permute-start.68 = (f32[8,1024]{1,0:T(8,128)S(1)}, f32[8,1024]{1,0:T(8,128)S(1)}, u32[]{:S(2)}, u32[]{:S(2)}) collective-permute-start(f32[8,1024]{1,0:T(8,128)S(1)} %add.817), channel_id=1, source_target_pairs={{0,2},{2,0},{4,6},{6,4},{1,3},{3,1},{5,7},{7,5},{8,10},{10,8},{12,... | collective-permute-start | bytes 98312 | tf_op jit(solution)/shard_map/ppermute | solution.py:742
  927.1 37.6 %collective-permute-start.72 = (bf16[640,1024]{1,0:T(8,128)(2,1)}, bf16[640,1024]{1,0:T(8,128)(2,1)}, u32[]{:S(2)}, u32[]{:S(2)}) collective-permute-start(bf16[640,1024]{1,0:T(8,128)(2,1)} %get-tuple-element.253), channel_id=1, source_target_pairs={{0,2},{2,0},{7,5},{5,7},{8,10},{10,8},{15,13},{13,15},{16,18},{18,... | collective-permute-start | bytes 3932168 | tf_op jit(solution)/shard_map/ppermute | solution.py:833
  931.2 27.1 %collective-permute-start.86 = (bf16[64,1024]{1,0:T(8,128)(2,1)S(1)}, bf16[64,1024]{1,0:T(8,128)(2,1)S(1)}, u32[]{:S(2)}, u32[]{:S(2)}) collective-permute-start(bf16[64,1024]{1,0:T(8,128)(2,1)S(1)} %get-tuple-element.294), channel_id=1, source_target_pairs={{0,6},{2,4},{4,2},{6,0},{1,7},{3,5},{5,3},{7,1},{8,14},{10,12},{12... | collective-permute-start | bytes 393224 | tf_op jit(solution)/shard_map/ppermute | solution.py:742
  961.5 32.3 %collective-permute-start.73 = (bf16[640,1024]{1,0:T(8,128)(2,1)S(1)}, bf16[640,1024]{1,0:T(8,128)(2,1)}, u32[]{:S(2)}, u32[]{:S(2)}) collective-permute-start(bf16[640,1024]{1,0:T(8,128)(2,1)S(1)} %convolution_convert_fusion.2), channel_id=1, source_target_pairs={{0,1},{1,0},{2,3},{3,2},{4,5},{5,4},{6,7},{7,6},{8,9},{9,8},{10,11... | collective-permute-start | bytes 3932168 | tf_op jit(solution)/shard_map/ppermute | solution.py:742
  969.1 24.7 %collective-permute-start.75 = (bf16[640,1024]{1,0:T(8,128)(2,1)}, bf16[640,1024]{1,0:T(8,128)(2,1)}, u32[]{:S(2)}, u32[]{:S(2)}) collective-permute-start(bf16[640,1024]{1,0:T(8,128)(2,1)} %get-tuple-element.251), channel_id=1, source_target_pairs={{0,2},{2,4},{7,5},{5,3},{8,10},{10,12},{15,13},{13,11},{16,18},{18... | collective-permute-start | bytes 3932168 | tf_op jit(solution)/shard_map/ppermute | solution.py:833
  (156 other events, 2108.3 us)
Sparse Core Ops, SparseCore 0:
  706.9 167.4 reduce-scatter.1

commit v3 on v2

--- a/solution.py
+++ b/solution.py
@@ -15,7 +15,7 @@
 MASKED = -1e30
 DIAG, SUB, FAR, NONE, BRANCH_NEAR, LEAF_NEAR, LEAF_BRANCH = 0, 1, 2, 3, 4, 6, 14
 CLASSES = 18
-LIMIT_AT, OFFSET_AT = 0, 32
+LIMIT_AT, OFFSET_AT, INFO_SIZE = 0, 32, 64
 
 
 def head_rows(block, heads):
@@ -353,7 +353,7 @@
             branch,
         ]
     )
-    info = jnp.zeros((64,), jnp.int32)
+    info = jnp.zeros((INFO_SIZE,), jnp.int32)
     info = info.at[:20].set(limits).at[20].set(last).at[OFFSET_AT : OFFSET_AT + CLASSES].set(offsets)
     return info
 
@@ -474,37 +474,33 @@
 
 def expand_kernel(scalars, slots, *refs, blocks, gated):
     gate = refs[0] if gated else None
-    rows, outs = (refs[1], refs[2:]) if gated else (refs[0], refs[1:])
+    rows, out = refs[1:3] if gated else refs
+    count = out.shape[1]
     for b in range(blocks):
-        out = outs[b]
-        count = out.shape[0]
-        out[...] = jnp.zeros_like(out)
+        out[b] = jnp.zeros(out.shape[1:], out.dtype)
 
         def one(tile, carry):
             at = pl.ds(pl.multiple_of(tile * SLOT_TILE, SLOT_TILE), SLOT_TILE)
             pick = slot_pick(slots[b], tile, count, 1)
             part = jnp.dot(pick, rows[at, :].astype(jnp.bfloat16), preferred_element_type=jnp.float32)
-            out[...] += part.astype(jnp.bfloat16)
+            out[b] += part.astype(jnp.bfloat16)
             return carry
 
         lax.fori_loop(scalars[b] // SLOT_TILE, pl.cdiv(scalars[b + 1], SLOT_TILE), one, 0)
         if gated:
-            outs[blocks][b] = out[...]
-            out[...] = (gate[b] * out[...].astype(jnp.float32)).astype(jnp.bfloat16)
+            refs[3][b] = out[b]
+            out[b] = (gate[b] * out[b].astype(jnp.float32)).astype(jnp.bfloat16)
 
 
 def expand(scalars, slots, rows, gate=None):
     blocks, count = slots.shape
-    width = rows.shape[1]
-    shapes = [jax.ShapeDtypeStruct((count, width), jnp.bfloat16)] * blocks
-    if gate is not None:
-        shapes = shapes + [jax.ShapeDtypeStruct((blocks, count, width), jnp.bfloat16)]
+    shape = jax.ShapeDtypeStruct((blocks, count, rows.shape[1]), jnp.bfloat16)
     operands = (scalars, slots.reshape(blocks, count, 1)) + (() if gate is None else (gate,)) + (rows,)
     outs = whole_calls(
         functools.partial(expand_kernel, blocks=blocks, gated=gate is not None),
-        operands, shapes, "expand", 56,
-    )
-    return outs if gate is None else (outs[:blocks], outs[blocks])
+        operands, [shape] * (1 if gate is None else 2), "expand", 56,
+    )
+    return outs[0] if gate is None else outs
 
 
 GELU_IN = math.sqrt(2.0 / math.pi)
@@ -523,19 +519,27 @@
 
 
 def weight_sources(sources, z):
+    theirs, sources = sources[0], sources[1:]
     if len(sources) == 1:
-        return [[(None, sources[0].at[number])] for number in range(sources[0].shape[0])]
-    own, up_one, down_one, up_two, down_two, far = sources
+        mine = [[(None, sources[0].at[number])] for number in range(sources[0].shape[0])]
+        return mine, [[(None, theirs.at[number])] for number in range(theirs.shape[0])]
+    own, up_one, down_one, up_two, down_two = sources[:5]
     low, high = z == 0, z == 3
-    return [
+    mine = [
         [(None, own)],
         [(z < 3, down_one), (high, up_one)],
         [(low, down_two), ((z == 1) | (z == 2), up_one), (high, up_two)],
-        [(low | high, far), (z == 1, down_two), (z == 2, up_two)],
+        [(z == 1, down_two), (z == 2, up_two)],
     ]
-
-
-def weight_copies(step, sources, theirs, room, sem, act):
+    others = [[(None, theirs.at[number])] for number in range(3)]
+    others.append([((z == 1) | (z == 2), theirs.at[3])])
+    if len(sources) == 7:
+        mine[3].append((low | high, sources[5]))
+        others[3].append((low | high, sources[6]))
+    return mine, others
+
+
+def weight_copies(step, sources, room, sem, act):
     def copy(slot, half, view):
         rows = view.shape[1]
         for matrix in range(3):
@@ -547,32 +551,35 @@
                 )
             )
 
-    for number, choices in enumerate(sources):
-        for condition, view in choices:
-            here = step == number if condition is None else (step == number) & condition
-            pl.when(here)(functools.partial(copy, number % 2, 0, view))
-        pl.when(step == number)(functools.partial(copy, number % 2, 1, theirs.at[number]))
-
-
-def next_weights(sources, theirs, room, sem):
-    step, steps = pl.program_id(0), len(sources)
-
-    @pl.when(step == 0)
-    def _():
-        weight_copies(step, sources, theirs, room, sem, lambda copy: copy.start())
-
-    @pl.when(step + 1 < steps)
-    def _():
-        weight_copies(step + 1, sources, theirs, room, sem, lambda copy: copy.start())
-
-    weight_copies(step, sources, theirs, room, sem, lambda copy: copy.wait())
+    for half, places in enumerate(sources):
+        for number, choices in enumerate(places):
+            for condition, view in choices:
+                here = step == number if condition is None else (step == number) & condition
+                pl.when(here)(functools.partial(copy, number % 2, half, view))
+
+
+def next_weights(first, sources, room, sem):
+    number, steps = pl.program_id(0), pl.num_programs(0)
+    step = first + number
+
+    @pl.when(number == 0)
+    def _():
+        weight_copies(step, sources, room, sem, lambda copy: copy.start())
+
+    @pl.when(number + 1 < steps)
+    def _():
+        weight_copies(step + 1, sources, room, sem, lambda copy: copy.start())
+
+    weight_copies(step, sources, room, sem, lambda copy: copy.wait())
     return step % 2
 
 
-def expert_forward_kernel(scalars, rows, theirs, *refs):
-    mine, (total, room, sem) = refs[:-3], refs[-3:]
+def expert_forward_kernel(scalars, rows, *refs, first, sources, aliased):
+    weights, refs = refs[:sources], refs[sources:]
+    before, refs = (refs[0], refs[1:]) if aliased else (None, refs)
+    total, room, sem = refs
     step = pl.program_id(0)
-    slot = next_weights(weight_sources(mine, scalars[1]), theirs, room, sem)
+    slot = next_weights(first, weight_sources(weights, scalars[1]), room, sem)
 
     def one(tile, carry):
         at = pl.ds(pl.multiple_of(tile * SLOT_TILE, SLOT_TILE), SLOT_TILE)
@@ -584,7 +591,7 @@
 
         @pl.when(step == 0)
         def _():
-            total[at, :] = part
+            total[at, :] = part if before is None else part + before[at, :]
 
         @pl.when(step > 0)
         def _():
@@ -608,31 +615,35 @@
     return [pltpu.VMEM((2, 3, 2 * half, width), jnp.bfloat16), pltpu.SemaphoreType.DMA((2, 6))]
 
 
-def expert_forward(scalars, rows, mine, theirs):
+def expert_forward(scalars, rows, weights, first, steps, before=None):
     padded, width = rows.shape
-    shards = theirs.shape[0]
+    theirs = weights[0]
     whole = pl.BlockSpec((padded, width), lambda s, scalars: (0, 0), pipeline_mode=pl.Buffered(1))
+    extra = () if before is None else (before,)
     return pl.pallas_call(
-        expert_forward_kernel,
+        functools.partial(
+            expert_forward_kernel, first=first, sources=len(weights), aliased=before is not None
+        ),
         grid_spec=pltpu.PrefetchScalarGridSpec(
             num_scalar_prefetch=1,
-            grid=(shards,),
-            in_specs=[whole] + [pl.BlockSpec(memory_space=pl.ANY)] * (1 + len(mine)),
+            grid=(steps,),
+            in_specs=[whole] + [pl.BlockSpec(memory_space=pl.ANY)] * len(weights) + [whole] * len(extra),
             out_specs=whole,
             scratch_shapes=expert_scratch(theirs),
         ),
         out_shape=jax.ShapeDtypeStruct((padded, width), jnp.float32),
-        compiler_params=pltpu.CompilerParams(vmem_limit_bytes=56 << 20),
-        cost_estimate=expert_cost(padded, theirs, shards, 3),
+        compiler_params=pltpu.CompilerParams(vmem_limit_bytes=60 << 20),
+        cost_estimate=expert_cost(padded, theirs, steps, 3),
         name="expert_forward",
-    )(scalars, rows, theirs, *mine)
-
-
-def expert_backward_kernel(scalars, rows, grads, theirs, *refs):
-    mine, rest = refs[:-8], refs[-8:]
-    mine_out, theirs_out, total, gate_total, up_total, down_total, room, sem = rest
+    )(scalars, rows, *weights, *extra)
+
+
+def expert_backward_kernel(scalars, rows, grads, *refs):
+    weights, rest = refs[:-10], refs[-10:]
+    mine_gate, theirs_gate, mine_rest, theirs_rest, total = rest[:5]
+    gate_total, up_total, down_total, room, sem = rest[5:]
     step = pl.program_id(0)
-    slot = next_weights(weight_sources(mine, scalars[1]), theirs, room, sem)
+    slot = next_weights(0, weight_sources(weights, scalars[1]), room, sem)
     gate_total[...] = jnp.zeros_like(gate_total)
     up_total[...] = jnp.zeros_like(up_total)
     down_total[...] = jnp.zeros_like(down_total)
@@ -665,64 +676,72 @@
         return carry
 
     lax.fori_loop(0, pl.cdiv(scalars[0], SLOT_TILE), one, 0)
-    half = mine_out.shape[2]
-    for number, sums in enumerate((gate_total, up_total, down_total)):
-        mine_out[0, number] = sums[:half].astype(jnp.bfloat16)
-        theirs_out[0, number] = sums[half:].astype(jnp.bfloat16)
-
-
-def expert_backward(scalars, rows, grads, mine, theirs):
+    half = mine_gate.shape[2]
+    for sums, mine, theirs, number in (
+        (gate_total, mine_gate, theirs_gate, 0),
+        (up_total, mine_rest, theirs_rest, 0),
+        (down_total, mine_rest, theirs_rest, 1),
+    ):
+        mine[0, number] = sums[:half].astype(jnp.bfloat16)
+        theirs[0, number] = sums[half:].astype(jnp.bfloat16)
+
+
+def expert_backward(scalars, rows, grads, weights):
     padded, width = rows.shape
+    theirs = weights[0]
     shards, _, half, _ = theirs.shape
     whole = pl.BlockSpec((padded, width), lambda s, scalars: (0, 0), pipeline_mode=pl.Buffered(1))
-    out = pl.BlockSpec((1, 3, half, width), lambda s, scalars: (scalars[2 + s], 0, 0, 0))
-    shape = jax.ShapeDtypeStruct((shards, 3, half, width), jnp.bfloat16)
+    out = lambda count: pl.BlockSpec(
+        (1, count, half, width), lambda s, scalars: (scalars[2 + s], 0, 0, 0)
+    )
+    shape = lambda count: jax.ShapeDtypeStruct((shards, count, half, width), jnp.bfloat16)
     return pl.pallas_call(
         expert_backward_kernel,
         grid_spec=pltpu.PrefetchScalarGridSpec(
             num_scalar_prefetch=1,
             grid=(shards,),
-            in_specs=[whole, whole] + [pl.BlockSpec(memory_space=pl.ANY)] * (1 + len(mine)),
-            out_specs=[out, out, whole],
+            in_specs=[whole, whole] + [pl.BlockSpec(memory_space=pl.ANY)] * len(weights),
+            out_specs=[out(1), out(1), out(2), out(2), whole],
             scratch_shapes=[pltpu.VMEM((2 * half, width), jnp.float32)] * 3 + expert_scratch(theirs),
         ),
-        out_shape=[shape, shape, jax.ShapeDtypeStruct((padded, width), jnp.float32)],
+        out_shape=[shape(1), shape(1), shape(2), shape(2), jax.ShapeDtypeStruct((padded, width), jnp.float32)],
         compiler_params=pltpu.CompilerParams(vmem_limit_bytes=60 << 20),
         cost_estimate=expert_cost(padded, theirs, shards, 8),
         name="expert_backward",
-    )(scalars, rows, grads, theirs, *mine)
-
-
-def project_kernel(scalars, weights, *refs, parts):
-    mine, others = refs[:parts], refs[parts : 2 * parts]
-    rows_out, q, k, k_t, v, v_t = refs[2 * parts :]
-    count = mine[0].shape[0]
+    )(scalars, rows, grads, *weights)
+
+
+def project_kernel(weights, rows, q, k, k_t, v, v_t):
     columns = q.shape[1]
-    active = scalars[parts] > 0
-    for part in range(parts):
-        at = pl.ds(pl.multiple_of(scalars[part] * count, count), count)
-        rows = jnp.where(active, mine[part][...], others[part][...])
-        rows_out[at, :] = rows
-        low = jnp.dot(rows, weights[...], preferred_element_type=jnp.float32).astype(jnp.bfloat16)
-        q[at, :] = low[:, :columns]
-        k[at, :] = low[:, columns : 2 * columns]
-        v[at, :] = low[:, 2 * columns :]
-        k_t[:, at] = jnp.transpose(low[:, columns : 2 * columns])
-        v_t[:, at] = jnp.transpose(low[:, 2 * columns :])
-
-
-def project(scalars, weights, mine, others):
-    parts, (count, width) = len(mine), mine[0].shape
-    length, columns = parts * count, weights.shape[1] // 3
-    tall = jax.ShapeDtypeStruct((length, columns), jnp.bfloat16)
-    wide = jax.ShapeDtypeStruct((columns, length), jnp.bfloat16)
-    return whole_calls(
-        functools.partial(project_kernel, parts=parts),
-        (scalars, weights, *mine, *others),
-        [jax.ShapeDtypeStruct((length, width), jnp.bfloat16), tall, tall, wide, tall, wide],
-        "project",
-        56,
-    )
+    low = jnp.dot(rows[...], weights[...], preferred_element_type=jnp.float32).astype(jnp.bfloat16)
+    q[...] = low[:, :columns]
+    k[...] = low[:, columns : 2 * columns]
+    v[...] = low[:, 2 * columns :]
+    k_t[...] = jnp.transpose(low[:, columns : 2 * columns])
+    v_t[...] = jnp.transpose(low[:, 2 * columns :])
+
+
+def project(weights, rows):
+    length, width = rows.shape
+    columns = weights.shape[1] // 3
+    count = 2 * TILE
+    tall = pl.BlockSpec((count, columns), lambda i: (i, 0))
+    wide = pl.BlockSpec((columns, count), lambda i: (0, i))
+    tall_shape = jax.ShapeDtypeStruct((length, columns), jnp.bfloat16)
+    wide_shape = jax.ShapeDtypeStruct((columns, length), jnp.bfloat16)
+    return pl.pallas_call(
+        project_kernel,
+        grid=(length // count,),
+        in_specs=[
+            pl.BlockSpec(weights.shape, lambda i: (0, 0)),
+            pl.BlockSpec((count, width), lambda i: (i, 0)),
+        ],
+        out_specs=[tall, tall, wide, tall, wide],
+        out_shape=[tall_shape, tall_shape, wide_shape, tall_shape, wide_shape],
+        compiler_params=pltpu.CompilerParams(vmem_limit_bytes=40 << 20),
+        cost_estimate=pl.CostEstimate(flops=10**10, bytes_accessed=2 * 10**7, transcendentals=0),
+        name="project",
+    )(weights, rows)
 
 
 def split_float(values):
@@ -774,18 +793,34 @@
 
 def layer_scatter(parts):
     if not ring_layer():
-        return lax.psum_scatter(
-            jnp.stack(parts), "expert", scatter_dimension=0, tiled=False
-        ).astype(jnp.float32)
-    top, bottom, x_top, x_bottom, y_top, y_bottom, far_top, far_bottom = parts
-    far_top, far_bottom = swap(far_top, "expert", 1), swap(far_bottom, "expert", 2)
-    x_top, y_bottom = swap(x_top, "expert", 1), swap(y_bottom, "expert", 2)
-    y_top = swap(y_top + far_top, "expert", 2)
-    x_bottom = swap(x_bottom + far_bottom, "expert", 1)
-    wide = lambda array: array.astype(jnp.float32)
-    return jnp.concatenate(
-        [wide(top) + wide(x_top) + wide(y_top), wide(bottom) + wide(x_bottom) + wide(y_bottom)], axis=0
-    )
+        return lax.psum_scatter(parts, "expert", scatter_dimension=0, tiled=False).astype(jnp.float32)
+    _, half, width = parts.shape
+    block = jax.ShapeDtypeStruct((half, width), jnp.float32)
+    low, high = pl.pallas_call(
+        scatter_kernel,
+        in_specs=[pl.BlockSpec(memory_space=pltpu.VMEM)],
+        out_specs=[pl.BlockSpec(memory_space=pltpu.VMEM)] * 2,
+        out_shape=[block, block],
+        scratch_shapes=[pltpu.VMEM((6, half, width), jnp.bfloat16), pltpu.SemaphoreType.DMA((2, 6))],
+        compiler_params=pltpu.CompilerParams(
+            collective_id=6, has_side_effects=True, vmem_limit_bytes=40 << 20
+        ),
+        cost_estimate=pl.CostEstimate(flops=5 * 10**10, bytes_accessed=10**7, transcendentals=0),
+        name="layer_scatter",
+    )(parts)
+    return jnp.concatenate([low, high], axis=0)
+
+
+def scatter_kernel(parts, low_out, high_out, room, sems):
+    column = lax.axis_index("expert")
+    greet([{"expert": column ^ 1}, {"expert": column ^ 2}])
+    halves = lambda ref, owner, side: ref.at[2 * (owner ^ column) + side]
+    onward, terms, finish = ring_scatter(parts, halves, room, sems, 0)
+    onward()
+    low, high = terms()
+    low_out[...] = sum(block[...].astype(jnp.float32) for block in low)
+    high_out[...] = sum(block[...].astype(jnp.float32) for block in high)
+    finish()
 
 
 def layer_small(array):
@@ -801,45 +836,8 @@
     return jnp.stack([array[0]] + [swap(array[n], "expert", n) for n in range(1, array.shape[0])])
 
 
-def layer_blocks(array, rows):
-    half = rows // 2
-    return [
-        lax.dynamic_slice_in_dim(array, layer_member(number) * rows + side * half, half, 0)
-        for number in range(array.shape[0] // rows)
-        for side in range(2)
-    ]
-
-
-def layer_place(pieces):
-    if not ring_layer():
-        return jnp.concatenate(pieces, axis=0)
-    half = pieces[0].shape[0]
-    out = jnp.zeros((half * len(pieces),) + pieces[0].shape[1:], pieces[0].dtype)
-    for place, piece in enumerate(pieces):
-        at = layer_member(place // 2) * 2 * half + (place % 2) * half
-        out = lax.dynamic_update_slice_in_dim(out, piece, at, 0)
-    return out
-
-
-PLACE = ("shard", "dp")
-
-
 def split_trees():
     return lax.axis_size("shard") == 4 and lax.axis_size("dp") == 2 and ring_layer()
-
-
-def move(array, pairs):
-    index = lambda place: place[0] * 2 + place[1]
-    return lax.ppermute(array, PLACE, [(index(a), index(b)) for a, b in pairs])
-
-
-def mirrored(pairs):
-    flip = lambda place: (3 - place[0], 1 - place[1])
-    return pairs + [(flip(a), flip(b)) for a, b in pairs]
-
-
-def heads_place(group, tree):
-    return (2 * tree + group // 2, group % 2)
 
 
 def my_place():
@@ -847,71 +845,11 @@
     return z, core, z // 2, 2 * (z % 2) + core
 
 
-WEIGHT_PAIRS = [((group, tree), heads_place(group, tree)) for group in range(4) for tree in range(2)]
-
-
-def weights_to_groups(array):
-    return move(array, WEIGHT_PAIRS)
-
-
-def groups_to_weights(array):
-    return move(array, [(b, a) for a, b in WEIGHT_PAIRS])
-
-
-def of_tree(array):
-    z, core, tree, group = my_place()
-    return jnp.where(core == tree, array, swap(array, "dp", 1))
-
-
-def tree_gather(own):
-    z, core, tree, group = my_place()
-    first = move(own, mirrored([((1, 0), (0, 0)), ((2, 0), (1, 0)), ((3, 0), (2, 0))]))
-    back = move(own, mirrored([((0, 0), (1, 0))]))
-    second = move(first, mirrored([((1, 0), (0, 0)), ((2, 0), (1, 0))]))
-    third = move(second, mirrored([((1, 0), (0, 0))]))
-    end = (z == 0) | (z == 3)
-    step = jnp.where(tree == 0, 1, -1)
-    blocks = [own, first, second, jnp.where(end, third, back)]
-    places = [z, z + step, z + 2 * step, jnp.where(end, z + 3 * step, z - step)]
-    scalars = jnp.stack(places + [core == tree]).astype(jnp.int32)
-    return scalars, blocks, [swap(block, "dp", 1) for block in blocks]
-
-
-def tree_scatter(rows_of):
-    z, core, tree, group = my_place()
-    active, end = core == tree, (z == 0) | (z == 3)
-
-    def chip_sum(place):
-        part = rows_of(jnp.where(tree == 0, place, 3 - place))
-        return part + swap(part, "dp", 1)
-
-    far, next_far, next_near, near = chip_sum(3), chip_sum(2), chip_sum(1), chip_sum(0)
-    one = move(jnp.where(end, far, near), mirrored([((0, 0), (1, 0)), ((1, 0), (0, 0))]))
-    two = move(
-        jnp.where(end, next_far, far + one), mirrored([((0, 0), (1, 0)), ((1, 0), (2, 0))])
-    )
-    three = move(
-        jnp.where(active, jnp.where(end, next_near, next_far + two), two),
-        mirrored([((0, 0), (1, 0)), ((1, 0), (2, 0)), ((2, 0), (3, 0))]),
-    )
-    wide = lambda array: array.astype(jnp.float32)
-    at_end, in_middle = wide(near) + wide(one), wide(next_near) + wide(three)
-    return jnp.where(active, jnp.where(end, at_end, in_middle), wide(three))
-
-
-def gather_out_weight(weight):
-    if not (split_trees()):
-        return lax.all_gather(weight, "shard", axis=0, tiled=True)
-    z = lax.axis_index("shard")
-    rows, width = weight.shape
-    quarter = rows // 4
-    mine = lax.dynamic_slice_in_dim(weight, lax.axis_index("expert") * quarter, quarter, 0)
-    stack = jnp.zeros((rows, width), weight.dtype)
-    for number in range(4):
-        piece = swap(mine, "shard", number) if number else mine
-        stack = lax.dynamic_update_slice_in_dim(stack, piece, (z ^ number) * quarter, 0)
-    stack = layer_place(layer_gather(stack)).reshape(4, 4, quarter, width)
-    return stack.transpose(1, 0, 2, 3).reshape(4 * rows, width)
+def rows_to_heads(grads, shards):
+    rows, width = grads.shape
+    pieces = grads.reshape(rows, shards, width // shards).transpose(1, 0, 2)
+    pieces = lax.all_to_all(pieces, "shard", split_axis=0, concat_axis=0, tiled=True)
+    return pieces.reshape(shards * rows, width // shards)
 
 
 def hop(array, pairs):
@@ -924,10 +862,9 @@
     return hop(own, [(0, 1), (1, 2), (2, 3)]), hop(own, [(1, 0), (2, 1), (3, 2)])
 
 
-def weight_hop_two(arrays):
-    if not split_trees():
-        return arrays
-    return hop(arrays[0], [(1, 2), (2, 3)]), hop(arrays[1], [(2, 1), (1, 0)])
+def weight_last_hop(two):
+    z = lax.axis_index("shard")
+    return hop(jnp.where(z == 1, two[1], two[0]), [(1, 0), (2, 3)])
 
 
 def weight_shards():
@@ -961,11 +898,729 @@
     )
 
 
-def meet_kernel(rows, own, up_one, down_one, up_two, down_two, layer, theirs, far, sems):
+def other_places():
+    column, z, core = (lax.axis_index(name) for name in ("expert", "shard", "dp"))
+    others = [
+        {"shard": z ^ number, "dp": core ^ side} for number in range(4) for side in range(2) if number + side
+    ]
+    return others + [{"expert": column ^ 1}, {"expert": column ^ 2}]
+
+
+def chip_role():
+    z = lax.axis_index("shard")
+    tree = z // 2
+    at_end = (z == 0) | (z == 3)
+    partner = z ^ 1
+    across = 3 - z
+    return z, tree, at_end, partner, across, lambda number: jnp.where(tree == 0, number, 3 - number)
+
+
+PIECES = 2
+
+
+def gather_kernel(
+    own, three, out, pack,
+    rows, three_all, out_all, packs, three_mine, out_mine, passing, lent, here, sems,
+):
+    column, core = lax.axis_index("expert"), lax.axis_index("dp")
+    z, tree, at_end, partner, across, seat = chip_role()
+    in_middle = jnp.logical_not(at_end)
+    beside, above, twin = {"expert": column ^ 1}, {"expert": column ^ 2}, {"dp": core ^ 1}
+    to_partner, to_across = {"shard": partner}, {"shard": across}
+    greet(near_places())
+    keeps = core == tree
+    lend = send_to(own.at[core ^ 1], lent, sems, 4, twin)
+    lend.start()
+
+    group = 2 * (z % 2) + core
+    stays = (group == z) & keeps
+    group_place = {"shard": 2 * core + z // 2, "dp": z % 2}
+    local_three = pltpu.make_async_copy(three, three_mine, here.at[0])
+    sent_three = send_to(three, three_mine, sems, 12, group_place)
+    pl.when(stays)(local_three.start)
+    pl.when(jnp.logical_not(stays))(sent_three.start)
+    local_packs = [pltpu.make_async_copy(pack, packs.at[8 * n], here.at[5 + n]) for n in range(2)]
+    pack_on = send_to(pack, packs.at[8], sems, 43, group_place)
+    spread = [
+        send_to(
+            pack, packs.at[2 * n + side], sems, 35 + 2 * n + side,
+            {"expert": column ^ n, "dp": core ^ side},
+        )
+        for n in range(4)
+        for side in range(2)
+        if n + side
+    ]
+    for copy in spread:
+        copy.start()
+    local_packs[0].start()
+    pl.when(stays)(local_packs[1].start)
+    pl.when(jnp.logical_not(stays))(pack_on.start)
+
+    height = lent.shape[0] // PIECES
+    piece = lambda ref, k: ref.at[pl.ds(k * height, height)]
+    mine = lambda place, k: rows.at[place, core, pl.ds(k * height, height)]
+    each = range(PIECES)
+
+    def along(source, target, number, k, device, arrival=None):
+        at = lambda n: 44 + PIECES * n + k
+        return pltpu.make_async_remote_copy(
+            src_ref=source,
+            dst_ref=target,
+            send_sem=sems.at[0, at(number)],
+            recv_sem=sems.at[1, at(number if arrival is None else arrival)],
+            device_id=device,
+            device_id_type=pl.DeviceIdType.MESH,
+        )
+
+    def start_both(tree_rows, other_rows):
+        @pl.when(at_end)
+        def _():
+            others = [along(piece(other_rows, k), piece(passing, k), 5, k, to_partner) for k in each]
+            for copy in others:
+                copy.start()
+            for copy in others:
+                copy.wait_send()
+            for k in each:
+                along(piece(tree_rows, k), mine(z, k), 0, k, to_partner).start()
+
+        @pl.when(in_middle)
+        def _():
+            for k in each:
+                along(piece(tree_rows, k), mine(z, k), 1, k, to_partner).start()
+                along(piece(other_rows, k), mine(z, k), 2, k, to_across).start()
+
+    lend.wait_recv()
+
+    @pl.when(keeps)
+    def _():
+        start_both(own.at[core], lent)
+
+    @pl.when(jnp.logical_not(keeps))
+    def _():
+        start_both(lent, own.at[core])
+
+    whole_block = pltpu.make_async_copy(own, rows.at[z], here.at[1])
+    block_to_twin = send_to(own, rows.at[z], sems, 11, twin)
+
+    @pl.when(keeps)
+    def _():
+        whole_block.start()
+        block_to_twin.start()
+
+    keep = pltpu.make_async_copy(out, out_mine.at[z], here.at[3])
+    keep.start()
+    pieces = [send_to(out, out_mine.at[z], sems, 12 + n, {"shard": z ^ n}) for n in range(1, 4)]
+    for copy in pieces:
+        copy.start()
+
+    pl.when(stays)(local_three.wait)
+    pl.when(jnp.logical_not(stays))(sent_three.wait)
+    quarter = three_mine.shape[0]
+    half = quarter // 2
+
+    def three_half(owner, side):
+        return three_all.at[pl.ds(pl.multiple_of(owner * quarter + side * half, half), half)]
+
+    top, bottom = three_mine.at[pl.ds(0, half)], three_mine.at[pl.ds(half, half)]
+    first = [
+        send_to(top, three_half(column, 0), sems, 16, beside),
+        send_to(bottom, three_half(column, 1), sems, 17, above),
+        send_to(bottom, three_half(column, 1), sems, 18, beside),
+        send_to(top, three_half(column, 0), sems, 19, above),
+    ]
+    for copy in first:
+        copy.start()
+    local_all = pltpu.make_async_copy(
+        three_mine, three_all.at[pl.ds(pl.multiple_of(column * quarter, quarter), quarter)], here.at[2]
+    )
+    local_all.start()
+
+    def arrive(number, k):
+        block = mine(seat(number), k)
+        along(piece(lent, k), block, number, k, to_partner).wait_recv()
+        along(block, block, 8 + number, k, twin).start()
+        return block
+
+    @pl.when(in_middle)
+    def _():
+        for k in each:
+            along(piece(lent, k), piece(passing, k), 5, k, to_partner).wait_recv()
+            along(piece(passing, k), mine(partner, k), 3, k, to_across).start()
+            block = arrive(2, k)
+            along(block, block, 6, k, to_partner, 2).start()
+
+    @pl.when(at_end)
+    def _():
+        for k in each:
+            arrive(1, k)
+
+    keep.wait()
+    for copy in pieces:
+        copy.wait()
+    halves = [out_mine.at[pl.ds(0, 2)], out_mine.at[pl.ds(2, 2)]]
+    place = lambda owner, side, owner_core: out_all.at[pl.ds(2 * side, 2), owner, owner_core]
+    third = [
+        send_to(halves[0], place(column, 0, core), sems, 20, beside),
+        send_to(halves[1], place(column, 1, core), sems, 21, above),
+        send_to(halves[1], place(column, 1, core), sems, 22, beside),
+        send_to(halves[0], place(column, 0, core), sems, 23, above),
+    ]
+    for copy in third:
+        copy.start()
+    whole = lambda owner, owner_core: out_all.at[:, owner, owner_core]
+    keep_all = pltpu.make_async_copy(out_mine, whole(column, core), here.at[4])
+    keep_all.start()
+    to_twin = [send_to(out_mine, whole(column, core), sems, 31, twin)]
+    to_twin[0].start()
+    first[0].wait_recv()
+    first[1].wait_recv()
+    second = [
+        send_to(three_half(column ^ 1, 0), three_half(column ^ 1, 0), sems, 24, above),
+        send_to(three_half(column ^ 2, 1), three_half(column ^ 2, 1), sems, 25, beside),
+    ]
+    for copy in second:
+        copy.start()
+
+    @pl.when(in_middle)
+    def _():
+        for k in each:
+            block = arrive(3, k)
+            along(block, block, 7, k, to_partner, 3).start()
+        for k in each:
+            arrive(0, k)
+
+    third[0].wait_recv()
+    third[1].wait_recv()
+    fourth = [
+        send_to(place(column ^ 1, 0, core), place(column ^ 1, 0, core), sems, 26, above),
+        send_to(place(column ^ 2, 1, core), place(column ^ 2, 1, core), sems, 27, beside),
+    ]
+    for copy in fourth:
+        copy.start()
+
+    @pl.when(at_end)
+    def _():
+        for k in each:
+            arrive(2, k)
+
+    third[2].wait_recv()
+    third[3].wait_recv()
+    for copy in fourth:
+        copy.wait_recv()
+    for number in range(1, 4):
+        block = whole(column ^ number, core)
+        to_twin.append(send_to(block, block, sems, 31 + number, twin))
+        to_twin[number].start()
+    local_all.wait()
+    keep_all.wait()
+    for copy in (first[2], first[3], second[0], second[1]):
+        copy.wait_recv()
+    for copy in first + second + third + fourth:
+        copy.wait_send()
+    for copy in to_twin:
+        copy.wait()
+
+    @pl.when(at_end)
+    def _():
+        for k in each:
+            arrive(3, k)
+
+    lend.wait_send()
+    for copy in spread:
+        copy.wait()
+    local_packs[0].wait()
+    pl.when(stays)(local_packs[1].wait)
+    pl.when(jnp.logical_not(stays))(pack_on.wait)
+
+    def settle(sent, traded):
+        for k in each:
+            for number in sent:
+                along(piece(lent, k), mine(z, k), number, k, to_partner).wait_send()
+            for number in traded:
+                along(piece(lent, k), mine(z, k), 8 + number, k, twin).wait()
+
+    pl.when(at_end)(functools.partial(settle, (0,), (1, 2, 3)))
+    pl.when(in_middle)(functools.partial(settle, (1, 2, 3, 6, 7), (0, 2, 3)))
+
+    @pl.when(keeps)
+    def _():
+        whole_block.wait()
+        block_to_twin.wait_send()
+
+    @pl.when(jnp.logical_not(keeps))
+    def _():
+        block_to_twin.wait_recv()
+
+
+def exchange_call(kernel, operands, out_shape, sems, scratch, number, name, cost=5 * 10**10):
+    anywhere = pl.BlockSpec(memory_space=pl.ANY)
+    return pl.pallas_call(
+        kernel,
+        in_specs=[anywhere] * len(operands),
+        out_specs=[anywhere] * len(out_shape),
+        out_shape=[
+            shape if hasattr(shape, "dtype") else jax.ShapeDtypeStruct(shape, jnp.bfloat16)
+            for shape in out_shape
+        ],
+        scratch_shapes=list(scratch) + [pltpu.SemaphoreType.DMA((2, sems))],
+        compiler_params=pltpu.CompilerParams(
+            collective_id=number, has_side_effects=True, vmem_limit_bytes=48 << 20
+        ),
+        cost_estimate=pl.CostEstimate(flops=cost, bytes_accessed=10**6, transcendentals=0),
+        name=name,
+    )(*operands)
+
+
+def gather_tree(own, three, out, pack):
+    part, width = out.shape
+    half = own.shape[0] // 2
+    own = own.reshape(2, half, width)
+    rows, three_all, out_all, packs, _, _, _, _ = exchange_call(
+        gather_kernel,
+        (own, three, out, pack),
+        [
+            (4, 2, half, width),
+            (4 * three.shape[0], three.shape[1]),
+            (4, 4, 2, part, width),
+            jax.ShapeDtypeStruct((9,) + pack.shape, pack.dtype),
+            three.shape,
+            (4, part, width),
+            (half, width),
+            (half, width),
+        ],
+        44 + 12 * PIECES,
+        [pltpu.SemaphoreType.DMA((7,))],
+        2,
+        "gather_tree",
+    )
+    return rows.reshape(-1, width), three_all, out_all.reshape(-1, width), packs
+
+
+SLICES = 4
+
+
+def heads_kernel(attended, heads, here, sems):
+    z, core = lax.axis_index("shard"), lax.axis_index("dp")
+    greet(other_places())
+    tree, group = z // 2, 2 * (z % 2) + core
+    rows = heads.shape[2]
+
+    height = heads.shape[1] // SLICES
+
+    def copies(turn, slice_number):
+        place = (group + turn) % 4
+        features = pl.ds(slice_number * height, height)
+        piece = attended.at[features, pl.ds(pl.multiple_of(place * rows, TILE), rows)]
+        target = heads.at[group, features]
+        local = pltpu.make_async_copy(piece, target, here.at[slice_number])
+        sent = send_to(piece, target, sems, turn * SLICES + slice_number, {"shard": place, "dp": tree})
+        return local, sent, (place == z) & (tree == core)
+
+    steps = [(turn, number) for turn in range(4) for number in range(SLICES)]
+    for step in steps:
+        local, sent, stays = copies(*step)
+        pl.when(stays)(local.start)
+        pl.when(jnp.logical_not(stays))(sent.start)
+    for step in steps:
+        local, sent, stays = copies(*step)
+        pl.when(stays)(local.wait)
+        pl.when(jnp.logical_not(stays))(sent.wait_send)
+        from_me = ((z - step[0]) % 4 == group) & (tree == core)
+        pl.when(jnp.logical_not(from_me))(sent.wait_recv)
+
+
+def trade_heads(attended_t):
+    columns, length = attended_t.shape
+    (heads,) = exchange_call(
+        heads_kernel,
+        (attended_t,),
+        [(4, columns, length // 4)],
+        4 * SLICES,
+        [pltpu.SemaphoreType.DMA((SLICES,))],
+        3,
+        "trade_heads",
+    )
+    return heads.reshape(4 * columns, length // 4)
+
+
+def add_low(*blocks):
+    return sum(block.astype(jnp.float32) for block in blocks).astype(jnp.bfloat16)
+
+
+def near_places():
+    column, core = lax.axis_index("expert"), lax.axis_index("dp")
+    layer = [{"expert": column ^ n, "dp": core ^ side} for n in range(1, 4) for side in range(2)]
+    return other_places()[:7] + layer
+
+
+def ring_scatter(sums, halves, room, sems, base):
+    column = lax.axis_index("expert")
+    beside, above = {"expert": column ^ 1}, {"expert": column ^ 2}
+    first = [
+        send_to(halves(sums, column ^ 3, 0), room.at[0], sems, base, beside),
+        send_to(halves(sums, column ^ 3, 1), room.at[1], sems, base + 1, above),
+        send_to(halves(sums, column ^ 1, 0), room.at[2], sems, base + 2, beside),
+        send_to(halves(sums, column ^ 2, 1), room.at[3], sems, base + 3, above),
+    ]
+    for copy in first:
+        copy.start()
+    second = [
+        send_to(room.at[0], room.at[4], sems, base + 4, above),
+        send_to(room.at[1], room.at[5], sems, base + 5, beside),
+    ]
+
+    def onward():
+        for number, (owner, side) in enumerate(((column ^ 2, 0), (column ^ 1, 1))):
+            first[number].wait_recv()
+            room[number] = add_low(halves(sums, owner, side)[...], room[number])
+            second[number].start()
+
+    def terms():
+        for copy in (first[2], first[3], second[0], second[1]):
+            copy.wait_recv()
+        low = (halves(sums, column, 0)[...], room[2], room[4])
+        high = (halves(sums, column, 1)[...], room[3], room[5])
+        return low, high
+
+    def finish():
+        for copy in first + second:
+            copy.wait_send()
+
+    return onward, terms, finish
+
+
+def back_kernel(
+    grads, out, heads, out_sum, lent, sums, room, quarter, pieces, total, here, sems
+):
+    column, core = lax.axis_index("expert"), lax.axis_index("dp")
+    z, tree, at_end, partner, across, seat = chip_role()
+    twin = {"dp": core ^ 1}
+    greet(near_places())
+    group = 2 * (z % 2) + core
+    columns = heads.shape[2]
+    part = lent.shape[2]
+    lend = send_to(out.at[:, :, pl.ds((core ^ 1) * part, part)], lent, sems, 4, twin)
+    lend.start()
+
+    height = heads.shape[1] // SLICES
+
+    def turn_copies(turn, k):
+        to_group = (z - turn) % 4
+        rows = pl.ds(k * height, height)
+        piece = grads.at[rows, pl.ds(pl.multiple_of(to_group * columns, TILE), columns)]
+        place, side = 2 * core + to_group // 2, to_group % 2
+        target = heads.at[z, rows]
+        local = pltpu.make_async_copy(piece, target, here.at[3 + k])
+        sent = send_to(piece, target, sems, 21 + turn * SLICES + k, {"shard": place, "dp": side})
+        return local, sent, (place == z) & (side == core)
+
+    steps = [(turn, k) for turn in range(4) for k in range(SLICES)]
+    for step in steps:
+        local, sent, stays = turn_copies(*step)
+        pl.when(stays)(local.start)
+        pl.when(jnp.logical_not(stays))(sent.start)
+
+    mine = pltpu.make_async_copy(out.at[:, :, pl.ds(core * part, part)], sums, here.at[1])
+    mine.start()
+    mine.wait()
+    lend.wait_recv()
+    sums[...] = add_low(sums[...], lent[...])
+
+    def halves(ref, owner, side):
+        return ref.at[pl.ds(2 * side, 2), owner]
+
+    onward, terms, finish = ring_scatter(sums, halves, room, sems, 5)
+    onward()
+    low, high = terms()
+    quarter[:2] = add_low(*low)
+    quarter[2:] = add_low(*high)
+    copies = [
+        send_to(quarter.at[z ^ n], pieces.at[n - 1], sems, 10 + n, {"shard": z ^ n}) for n in range(1, 4)
+    ]
+    for copy in copies:
+        copy.start()
+    for copy in copies:
+        copy.wait()
+    total[...] = add_low(quarter[z], pieces[0], pieces[1], pieces[2])
+    spread = [
+        send_to(
+            total, out_sum.at[column, core], sems, 13 + 2 * n + side,
+            {"expert": column ^ n, "dp": core ^ side},
+        )
+        for n in range(4)
+        for side in range(2)
+        if n + side
+    ]
+    for copy in spread:
+        copy.start()
+    keep = pltpu.make_async_copy(total, out_sum.at[column, core], here.at[2])
+    keep.start()
+    keep.wait()
+    for copy in spread:
+        copy.wait()
+    finish()
+    lend.wait_send()
+    for step in steps:
+        local, sent, stays = turn_copies(*step)
+        pl.when(stays)(local.wait)
+        pl.when(jnp.logical_not(stays))(sent.wait_send)
+        from_me = ((group + step[0]) % 4 == z) & (tree == core)
+        pl.when(jnp.logical_not(from_me))(sent.wait_recv)
+
+
+def trade_back(grads, out):
+    rows, width = grads.shape
+    part = width // 32
+    low = jnp.bfloat16
+    heads, out_sum = exchange_call(
+        back_kernel,
+        (grads, out.reshape(4, 4, 2 * part, width)),
+        [(4, rows, width // 4), (4, 2, part, width)],
+        21 + 4 * SLICES,
+        [
+            pltpu.VMEM((4, 4, part, width), low),
+            pltpu.VMEM((4, 4, part, width), low),
+            pltpu.VMEM((6, 2, part, width), low),
+            pltpu.VMEM((4, part, width), low),
+            pltpu.VMEM((3, part, width), low),
+            pltpu.VMEM((part, width), low),
+            pltpu.SemaphoreType.DMA((3 + SLICES,)),
+        ],
+        4,
+        "trade_back",
+        10**6,
+    )
+    return heads.reshape(4 * rows, width // 4), out_sum.reshape(-1, width)
+
+
+def last_kernel(
+    parts, three, small, total, three_all, small_all,
+    lent, forth, arrived, leave, room, quarter, moved, other, mine_half, small_room, here, sems,
+):
+    column, core = lax.axis_index("expert"), lax.axis_index("dp")
+    z, tree, at_end, partner, across, seat = chip_role()
+    in_middle = jnp.logical_not(at_end)
+    twin, to_partner, to_across = {"dp": core ^ 1}, {"shard": partner}, {"shard": across}
+    greet(near_places())
+    keeps = core == tree
+
+    def lend(turn):
+        block = seat(jnp.where(at_end, 3 - turn, (4 - turn) % 4))
+        return block, send_to(parts.at[block, core ^ 1], lent.at[block], sems, turn, twin)
+
+    height = lent.shape[1] // PIECES
+    each = range(PIECES)
+    piece = lambda ref, k: ref.at[pl.ds(k * height, height)]
+
+    def along(source, target, number, device, arrival=None):
+        at = lambda n, k: 33 + PIECES * n + k
+        return [
+            pltpu.make_async_remote_copy(
+                src_ref=piece(source, k),
+                dst_ref=piece(target, k),
+                send_sem=sems.at[0, at(number, k)],
+                recv_sem=sems.at[1, at(number if arrival is None else arrival, k)],
+                device_id=device,
+                device_id_type=pl.DeviceIdType.MESH,
+            )
+            for k in each
+        ]
+
+    def start_all(copies):
+        for copy in copies:
+            copy.start()
+
+    for turn in range(4):
+        lend(turn)[1].start()
+    rows = three.shape[1] // 2
+
+    def halves(ref, owner, side):
+        return ref.at[owner, pl.ds(side * rows, rows)]
+
+    onward, terms, finish = ring_scatter(three, halves, room, sems, 4)
+    partners = [
+        twin, {"expert": column ^ 1}, {"expert": column ^ 2}, {"shard": z ^ 1}, {"shard": z ^ 2}
+    ]
+    small_all[...] = small[...]
+
+    def small_copy(stage):
+        return send_to(small_room.at[stage], small_room.at[5 + stage], sems, 20 + stage, partners[stage])
+
+    def small_start(stage):
+        small_room[stage] = small_all[...]
+        small_copy(stage).start()
+
+    def small_end(stage):
+        small_copy(stage).wait()
+        small_all[...] += small_room[5 + stage]
+
+    small_start(0)
+
+    def chip_sum(turn):
+        block, copy = lend(turn)
+        copy.wait_recv()
+        lent[block] = add_low(parts[block, core], lent[block])
+        return lent.at[block]
+
+    def end_send(turn):
+        start_all(along(chip_sum(turn), forth.at[turn], turn, to_partner))
+
+    pl.when(at_end)(functools.partial(end_send, 0))
+
+    @pl.when(in_middle)
+    def _():
+        start_all(along(chip_sum(0), forth.at[0], 0, to_partner))
+
+    small_end(0)
+    small_start(1)
+    onward()
+    pl.when(at_end)(functools.partial(end_send, 1))
+    small_end(1)
+    small_start(2)
+
+    def middle_sum(turn, onwards=None):
+        block = chip_sum(turn)
+        copies = None if onwards is None else onwards(block)
+        for k, arrival in enumerate(along(forth.at[0], forth.at[turn - 1], turn - 1, to_partner)):
+            arrival.wait_recv()
+            at = pl.ds(k * height, height)
+            block[at] = add_low(block[at], forth[turn - 1, at])
+            if copies is not None:
+                copies[k].start()
+
+    @pl.when(in_middle)
+    def _():
+        middle_sum(1, lambda block: along(block, arrived, 3, {"shard": across ^ 1}))
+
+    low, high = terms()
+    quarter[:rows] = add_low(*low)
+    quarter[rows:] = add_low(*high)
+    group = 2 * (z % 2) + core
+    stays = (group == z) & keeps
+    keep = pltpu.make_async_copy(quarter, moved, here.at[0])
+    move_on = send_to(quarter, moved, sems, 14, {"shard": group, "dp": tree})
+    pl.when(stays)(keep.start)
+    pl.when(jnp.logical_not(stays))(move_on.start)
+    pl.when(at_end)(functools.partial(end_send, 2))
+
+    small_end(2)
+    small_start(3)
+
+    @pl.when(in_middle)
+    def _():
+        middle_sum(2, lambda block: along(block, arrived, 4, to_across, 3))
+
+    pl.when(stays)(keep.wait)
+    pl.when(jnp.logical_not(stays))(move_on.wait)
+    swapped = send_to(moved, other, sems, 16, twin)
+    swapped.start()
+    small_end(3)
+    small_start(4)
+    swapped.wait()
+    at = pl.ds(pl.multiple_of(core * rows, 8), rows)
+    mine_half[...] = add_low(moved[at], other[at])
+    target = three_all.at[column, core]
+    spread = [
+        send_to(mine_half, target, sems, 25 + 2 * n + side, {"expert": column ^ n, "dp": core ^ side})
+        for n in range(4)
+        for side in range(2)
+        if n + side
+    ]
+    for copy in spread:
+        copy.start()
+    keep_half = pltpu.make_async_copy(mine_half, target, here.at[1])
+    keep_half.start()
+    small_end(4)
+
+    @pl.when(at_end)
+    def _():
+        block = chip_sum(3)
+        for copy in along(forth.at[0], forth.at[0], 0, to_partner):
+            copy.wait_recv()
+        block[...] = add_low(block[...], forth[0])
+
+    @pl.when(in_middle)
+    def _():
+        middle_sum(3)
+
+    mine = lent.at[z]
+    for copy in along(forth.at[0], arrived, 3, to_partner):
+        copy.wait_recv()
+
+    @pl.when(keeps)
+    def _():
+        total[core] = mine[...]
+        leave[...] = arrived[...]
+
+    @pl.when(jnp.logical_not(keeps))
+    def _():
+        total[core] = arrived[...]
+        leave[...] = mine[...]
+
+    last = send_to(leave, total.at[core], sems, 17, twin)
+    last.start()
+
+    keep_half.wait()
+    for copy in spread:
+        copy.wait()
+    finish()
+    for turn in range(4):
+        lend(turn)[1].wait_send()
+
+    def settle(numbers):
+        for number in numbers:
+            for copy in along(forth.at[0], forth.at[1], number, to_partner):
+                copy.wait_send()
+
+    pl.when(at_end)(functools.partial(settle, (0, 1, 2)))
+    pl.when(in_middle)(functools.partial(settle, (0, 3, 4)))
+    last.wait()
+
+
+def reduce_last(parts, three, small):
+    blocks, rows, width = parts.shape
+    columns = three.shape[1]
+    half, quarter = rows // 2, width // 4
+    low = jnp.bfloat16
+    vmem = pl.BlockSpec(memory_space=pltpu.VMEM)
+    block = pltpu.VMEM((half, width), low)
+    total, three_all, small_all = pl.pallas_call(
+        last_kernel,
+        in_specs=[vmem] * 3,
+        out_specs=[vmem] * 3,
+        out_shape=[
+            jax.ShapeDtypeStruct((2, half, width), low),
+            jax.ShapeDtypeStruct((4, 2, quarter // 2, columns), low),
+            jax.ShapeDtypeStruct(small.shape, jnp.float32),
+        ],
+        scratch_shapes=[
+            pltpu.VMEM((4, half, width), low),
+            pltpu.VMEM((3, half, width), low),
+            block,
+            block,
+            pltpu.VMEM((6, quarter // 2, columns), low),
+            pltpu.VMEM((quarter, columns), low),
+            pltpu.VMEM((quarter, columns), low),
+            pltpu.VMEM((quarter, columns), low),
+            pltpu.VMEM((quarter // 2, columns), low),
+            pltpu.VMEM((10,) + small.shape, jnp.float32),
+            pltpu.SemaphoreType.DMA((2,)),
+            pltpu.SemaphoreType.DMA((2, 33 + 5 * PIECES)),
+        ],
+        compiler_params=pltpu.CompilerParams(
+            collective_id=5, has_side_effects=True, vmem_limit_bytes=48 << 20
+        ),
+        cost_estimate=pl.CostEstimate(flops=5 * 10**10, bytes_accessed=10**7, transcendentals=0),
+        name="reduce_last",
+    )(parts.reshape(blocks, 2, half, width), three.reshape(4, quarter, columns), small)
+    return total.reshape(rows, width), three_all.reshape(width, columns), small_all
+
+
+def meet_kernel(rows, own, up_one, down_one, layer, theirs, up_two, down_two, sems):
     column, z = lax.axis_index("expert"), lax.axis_index("shard")
     beside, above = {"expert": column ^ 1}, {"expert": column ^ 2}
-    next_z, twin = {"shard": z ^ 1}, {"dp": lax.axis_index("dp") ^ 1}
-    greet([beside, above, next_z, twin])
+    twin = {"dp": lax.axis_index("dp") ^ 1}
+    greet(other_places())
     x_top = send_to(rows.at[0], layer.at[0], sems, 0, beside)
     y_bottom = send_to(rows.at[1], layer.at[3], sems, 1, above)
     x_bottom = send_to(rows.at[1], layer.at[1], sems, 2, beside)
@@ -973,21 +1628,24 @@
     for copy in (x_top, y_bottom, x_bottom, y_top):
         copy.start()
 
-    hop_down = send_to(down_two, far, sems, 6, next_z)
-    hop_up = send_to(up_two, far, sems, 6, next_z)
-    pl.when(z == 1)(hop_down.start)
-    pl.when(z == 2)(hop_up.start)
-    places = weight_sources((own, up_one, down_one, up_two, down_two, far), z)
-    ends = (z == 0) | (z == 3)
-    for place, choices in enumerate(places):
-        for condition, view in choices:
-            if view is far:
-                continue
-            copy = send_to(view, theirs.at[place], sems, 7 + place, twin)
-            if condition is None:
-                copy.start()
-            else:
-                pl.when(condition)(copy.start)
+    between = (z == 1) | (z == 2)
+    hop_up = [send_to(up_one.at[m], up_two.at[m], sems, 12 + m, {"shard": z + 1}) for m in range(3)]
+    hop_down = [send_to(down_one.at[m], down_two.at[m], sems, 15 + m, {"shard": z - 1}) for m in range(3)]
+
+    @pl.when(between)
+    def _():
+        for copy in hop_up + hop_down:
+            copy.start()
+
+    low, high = z == 0, z == 3
+
+    def to_twin(view, place):
+        return send_to(view, theirs.at[place], sems, 8 + place, twin)
+
+    to_twin(own, 0).start()
+    pl.when(z < 3)(to_twin(down_one, 1).start)
+    pl.when(high)(to_twin(up_one, 1).start)
+    pl.when(between)(to_twin(up_one, 2).start)
 
     x_top.wait_recv()
     far_top = send_to(layer.at[0], layer.at[4], sems, 4, above)
@@ -995,109 +1653,57 @@
     y_bottom.wait_recv()
     far_bottom = send_to(layer.at[3], layer.at[5], sems, 5, beside)
     far_bottom.start()
-    last = send_to(far, theirs.at[3], sems, 10, twin)
-
-    @pl.when(ends)
-    def _():
-        hop_down.wait_recv()
-        last.start()
-
-    @pl.when(jnp.logical_not(ends))
-    def _():
-        hop_down.wait_send()
 
     for copy in (x_top, y_bottom):
         copy.wait_send()
     for copy in (x_bottom, y_top, far_top, far_bottom):
         copy.wait()
-    for place in range(4):
-        send_to(own, theirs.at[place], sems, 7 + place, twin).wait()
-
-
-def meet(rows, own, one, two):
+
+    @pl.when(z >= 2)
+    def _():
+        for copy in hop_up:
+            copy.wait_recv()
+
+    @pl.when(z <= 1)
+    def _():
+        for copy in hop_down:
+            copy.wait_recv()
+
+    pl.when(low)(to_twin(down_two, 2).start)
+    pl.when(high)(to_twin(up_two, 2).start)
+    pl.when(z == 1)(to_twin(down_two, 3).start)
+    pl.when(z == 2)(to_twin(up_two, 3).start)
+
+    @pl.when(between)
+    def _():
+        for copy in hop_up + hop_down:
+            copy.wait_send()
+        to_twin(own, 3).wait()
+
+    for place in range(3):
+        to_twin(own, place).wait()
+
+
+def meet(rows, own, one):
     half = rows.shape[0] // 2
     halves = rows.reshape(2, half, rows.shape[1])
-    anywhere = pl.BlockSpec(memory_space=pl.ANY)
-    layer, theirs, far = pl.pallas_call(
+    layer, theirs, up_two, down_two = exchange_call(
         meet_kernel,
-        in_specs=[anywhere] * 6,
-        out_specs=[anywhere] * 3,
-        out_shape=[
-            jax.ShapeDtypeStruct((6,) + halves.shape[1:], rows.dtype),
-            jax.ShapeDtypeStruct((4,) + own.shape, own.dtype),
-            jax.ShapeDtypeStruct(own.shape, own.dtype),
-        ],
-        scratch_shapes=[pltpu.SemaphoreType.DMA((2, 11))],
-        compiler_params=pltpu.CompilerParams(collective_id=1, has_side_effects=True),
-        cost_estimate=pl.CostEstimate(flops=5 * 10**10, bytes_accessed=10**7, transcendentals=0),
-        name="meet",
-    )(halves, own, *one, *two)
-    return [halves, layer], theirs, (own, *one, *two, far)
-
-
-def reduce_attention_grads(three, out):
-    width = out.shape[1]
-    if not (split_trees()):
-        if split_trees():
-            three = groups_to_weights(three)
-        out = lax.psum_scatter(out, "shard", scatter_dimension=0, tiled=True)
-        three = lax.psum(three, ("expert", "dp"))
-        return three.astype(jnp.float32), lax.psum(out, ("expert", "dp")).astype(jnp.float32)
-    z = lax.axis_index("shard")
-    quarter = width // 4
-    part = quarter // 4
-    columns = three.shape[1]
-    out = out.reshape(4, 4, part, width).transpose(1, 0, 2, 3).reshape(width, width)
-    both = jnp.concatenate([three, out], axis=1)
-    both = layer_scatter(layer_blocks(both, quarter)).astype(jnp.bfloat16)
-    three = groups_to_weights(both[:, :columns])
-    out = both[:, columns:]
-    pieces = [lax.dynamic_slice_in_dim(out, (z ^ number) * part, part, 0) for number in range(4)]
-    pieces = [pieces[0]] + [swap(pieces[number], "shard", number) for number in range(1, 4)]
-    out = sum(piece.astype(jnp.float32) for piece in pieces).astype(jnp.bfloat16)
-    both = jnp.concatenate([three, out.reshape(quarter, width // 4)], axis=1)
-    both = both + swap(both, "dp", 1)
-    both = layer_place(layer_gather(both))
-    out = both[:, columns:].reshape(4 * part, width)
-    return both[:, :columns].astype(jnp.float32), out.astype(jnp.float32)
-
-
-def trade_pairs(turn):
-    return [
-        (heads_place(group, tree), ((group + turn) % 4, tree)) for group in range(4) for tree in range(2)
-    ]
+        (halves, own, *one),
+        [(6,) + halves.shape[1:], (4,) + own.shape, own.shape, own.shape],
+        18,
+        [],
+        1,
+        "meet",
+    )
+    return [halves, layer], theirs, (up_two, down_two)
 
 
 def heads_to_rows(attended_t, shards):
     columns, length = attended_t.shape
-    rows = length // shards
-    if not split_trees():
-        pieces = attended_t.reshape(columns, shards, rows).transpose(1, 0, 2)
-        pieces = lax.all_to_all(pieces, "shard", split_axis=0, concat_axis=0, tiled=True)
-        return pieces.reshape(shards * columns, rows)
-    z, core, tree, group = my_place()
-    out = jnp.zeros((shards * columns, rows), attended_t.dtype)
-    for turn in range(4):
-        piece = lax.dynamic_slice_in_dim(attended_t, (group + turn) % 4 * rows, rows, 1)
-        piece = move(piece, trade_pairs(turn))
-        out = lax.dynamic_update_slice_in_dim(out, piece, (z - turn) % 4 * columns, 0)
-    return out
-
-
-def rows_to_heads(grads, shards):
-    rows, width = grads.shape
-    columns = width // shards
-    if not split_trees():
-        pieces = grads.reshape(rows, shards, columns).transpose(1, 0, 2)
-        pieces = lax.all_to_all(pieces, "shard", split_axis=0, concat_axis=0, tiled=True)
-        return pieces.reshape(shards * rows, columns)
-    z, core, tree, group = my_place()
-    out = jnp.zeros((shards * rows, columns), grads.dtype)
-    for turn in range(4):
-        piece = lax.dynamic_slice_in_dim(grads, (z - turn) % 4 * columns, columns, 1)
-        piece = move(piece, [(b, a) for a, b in trade_pairs(turn)])
-        out = lax.dynamic_update_slice_in_dim(out, piece, (group + turn) % 4 * rows, 0)
-    return out
+    pieces = attended_t.reshape(columns, shards, length // shards).transpose(1, 0, 2)
+    pieces = lax.all_to_all(pieces, "shard", split_axis=0, concat_axis=0, tiled=True)
+    return pieces.reshape(shards * columns, length // shards)
 
 
 def on_device(
@@ -1126,37 +1732,43 @@
     expert_w = jnp.stack([w_gate[0].T, w_up[0].T, w_down[0]])
     half = expert_w.shape[1] // lax.axis_size("dp")
     expert_w = lax.dynamic_slice_in_dim(expert_w, lax.axis_index("dp") * half, half, 1)
-    out_all = gather_out_weight(w_out)
-    info = attention_info(validity)
     weights = jnp.concatenate([w_query, w_key, w_value], axis=1)
-    bias_here = rel_bias
+    info, bias_here = attention_info(validity), rel_bias
+    top_count = route_local.shape[1]
     if split_trees():
-        info, bias_here = of_tree(info), weights_to_groups(rel_bias)
-        if ring_layer():
-            quarter = width // columns
-            mine = lax.dynamic_slice_in_dim(weights, expert_index * quarter, quarter, 0)
-            mine, normed_one = lax.optimization_barrier((weights_to_groups(mine), normed_one))
-            weights = layer_place(layer_gather(mine))
-        else:
-            weights = weights_to_groups(weights)
-        places, mine, others = tree_gather(normed_one)
-        mine[3], expert_w = lax.optimization_barrier((mine[3], expert_w))
-        weights_one = weight_hop_one(expert_w)
-        weights, out_all = lax.optimization_barrier((weights, out_all))
-        normed_all, query_rows, key_rows, key_t, value_rows, value_t = project(
-            places, weights, mine, others
+        quarter, part = width // 4, w_out.shape[0] // 8
+        info_row = jnp.pad(info.at[INFO_SIZE - 1].set(jnp.sum(validity)), (0, TILE - INFO_SIZE))
+        rows_of = lambda values: values.astype(jnp.float32).reshape(-1, TILE)
+        pack = jnp.concatenate([rows_of(info_row), rows_of(rel_bias), rows_of(route_local.T)], axis=0)
+        pack = jnp.pad(pack, ((0, -pack.shape[0] % 8), (0, 0)))
+        normed_all, weights, out_all, packs = gather_tree(
+            normed_one,
+            lax.dynamic_slice_in_dim(weights, expert_index * quarter, quarter, 0),
+            lax.dynamic_slice_in_dim(
+                w_out, (expert_index * 2 + lax.axis_index("dp")) * part, part, 0
+            ),
+            pack,
         )
+        expert_w, packs = lax.optimization_barrier((expert_w, packs))
+        tree_rows = packs[:, 0, :INFO_SIZE].astype(jnp.int32)
+        z, core, tree, group = my_place()
+        info = jnp.where(core == tree, tree_rows[0], tree_rows[1])
+        valid_total = jnp.sum(tree_rows[:8, INFO_SIZE - 1]).astype(jnp.float32)
+        bias_rows = rel_bias.size // TILE
+        bias_here = packs[8, 1 : 1 + bias_rows].reshape(rel_bias.shape)
+        route_rows = route_local.size // TILE
+        route_layer = packs[0:8:2, 1 + bias_rows : 1 + bias_rows + route_rows]
+        route_layer = route_layer.reshape(columns, top_count, local_rows).astype(jnp.int32)
     else:
         normed_all = lax.all_gather(normed_one, "shard", axis=0, tiled=True)
-        projected = jnp.dot(normed_all, weights, preferred_element_type=jnp.float32).astype(jnp.bfloat16)
-        query_rows, key_rows, value_rows = jnp.split(projected, 3, axis=1)
-        key_t, value_t = key_rows.T, value_rows.T
-        weights_one = weight_hop_one(expert_w)
-    tree_count = sum_over(jnp.broadcast_to(jnp.sum(validity), (8, 128)), ("dp", "expert"))
-    valid_total = tree_count[0, 0].astype(jnp.float32)
-
-    top_count = route_local.shape[1]
-    route_layer = layer_small(route_local.T)
+        out_all = lax.all_gather(w_out, "shard", axis=0, tiled=True)
+        normed_all, expert_w = lax.optimization_barrier((normed_all, expert_w))
+        tree_count = sum_over(jnp.broadcast_to(jnp.sum(validity), (8, 128)), ("dp", "expert"))
+        valid_total = tree_count[0, 0].astype(jnp.float32)
+        route_layer = layer_small(route_local.T)
+    weights_one = weight_hop_one(expert_w)
+    query_rows, key_rows, key_t, value_rows, value_t = project(weights, normed_all)
+
     taken = jnp.any(route_layer == expert_index, axis=1)
     order = jnp.cumsum(taken.reshape(-1).astype(jnp.int32))
     slots = jnp.where(taken, order.reshape(taken.shape) - 1, -1)
@@ -1171,9 +1783,10 @@
     table = bias_table(bias_here)
     attended_t, log_totals = attention_forward(info, table, query_rows, key_rows, value_t)
 
-    attended_t, *weights_one = lax.optimization_barrier((attended_t, *weights_one))
-    attended_here = heads_to_rows(attended_t, shards)
-    weights_two = weight_hop_two(weights_one)
+    if split_trees():
+        attended_here = trade_heads(attended_t)
+    else:
+        attended_here = heads_to_rows(attended_t, shards)
     update = lax.dot_general(
         attended_here, out_all, (((0,), (0,)), ((), ())), preferred_element_type=jnp.float32
     )
@@ -1194,17 +1807,24 @@
 
     gates, route_match = gates_of(normed_two, route_local)
     if split_trees():
-        normed_layer, theirs_w, mine_w = meet(normed_two, expert_w, weights_one, weights_two)
+        normed_layer, theirs_w, weights_two = meet(normed_two, expert_w, weights_one)
+        weights_near = (theirs_w, expert_w, *weights_one, *weights_two)
+        far = weight_last_hop(weights_two)
     else:
         normed_layer = [block[None] for block in layer_gather(normed_two)]
-        mine_w = weights_one
-        theirs_w = swap(weights_one[0], "dp", 1)
+        weights_all = (swap(weights_one[0], "dp", 1), weights_one[0])
     expert_scalars = jnp.concatenate(
         [order[-1:], shard_index[None].astype(jnp.int32), weight_shards()]
     )
     router_wide = jnp.pad(router_pieces, ((0, 0), (0, TILE - router_pieces.shape[1])))
     expert_rows, gate_here = compact_rows(scalars, router_wide, slots, named, normed_layer, experts)
-    produced = expert_forward(expert_scalars, expert_rows, mine_w, theirs_w)
+    if split_trees():
+        produced = expert_forward(expert_scalars, expert_rows, weights_near, 0, 3)
+        produced, far = lax.optimization_barrier((produced, far))
+        weights_all = weights_near + (far, swap(far, "dp", 1))
+        produced = expert_forward(expert_scalars, expert_rows, weights_all, 3, 1, produced)
+    else:
+        produced = expert_forward(expert_scalars, expert_rows, weights_all, 0, shards)
     shares, produced_layer = expand(scalars, slots, produced, gate_here)
     combined = layer_scatter(shares)
 
@@ -1216,14 +1836,17 @@
     grad_layer = [block[None] for block in layer_gather(grad_output.astype(jnp.bfloat16))]
     grad_rows, gate_grads = compact_grads(scalars, slots, gate_here, produced_layer, grad_layer)
     gate_grads = layer_trade(gate_grads.reshape(columns, local_rows))
-    mine_part, theirs_part, rows_grad = expert_backward(
-        expert_scalars, expert_rows, grad_rows, mine_w, theirs_w
-    )
-    expanded = expand(scalars, slots, rows_grad)
-    *expanded, mine_part, theirs_part = lax.optimization_barrier((*expanded, mine_part, theirs_part))
-    expert_back = layer_scatter(expanded)
-    weight_part = mine_part + swap(theirs_part, "dp", 1)
-    weight_part = lax.psum_scatter(weight_part, "shard", scatter_dimension=0, tiled=False)
+    mine_gate, theirs_gate, mine_rest, theirs_rest, rows_grad = expert_backward(
+        expert_scalars, expert_rows, grad_rows, weights_all
+    )
+    theirs_gate = swap(theirs_gate, "dp", 1)
+    rows_grad, theirs_gate = lax.optimization_barrier(
+        (expand(scalars, slots, rows_grad), theirs_gate)
+    )
+    rows_grad, gate_part = lax.optimization_barrier((rows_grad, mine_gate + theirs_gate))
+    gate_part = lax.psum_scatter(gate_part, "shard", scatter_dimension=0, tiled=False)
+    theirs_rest = swap(theirs_rest, "dp", 1)
+    expert_back = layer_scatter(rows_grad)
 
     members = jnp.stack([jnp.asarray(layer_member(number), jnp.int32) for number in range(columns)])
     grad_gates = jnp.sum(
@@ -1252,7 +1875,18 @@
     grad_heads = lax.dot_general(
         grad_update, out_all, (((1,), (1,)), ((), ())), preferred_element_type=jnp.float32
     ).astype(jnp.bfloat16)
-    grad_attended = rows_to_heads(grad_heads, shards)
+    out_grad = out_grad.astype(jnp.bfloat16)
+    if split_trees():
+        grad_attended, out_grad = trade_back(grad_heads, out_grad)
+    else:
+        grad_attended = rows_to_heads(grad_heads, shards)
+        out_grad = lax.psum_scatter(out_grad, "shard", scatter_dimension=0, tiled=True)
+        out_grad = lax.psum(out_grad, ("expert", "dp"))
+    out_grad = out_grad.astype(jnp.float32)
+    rest_part, grad_attended, gate_part = lax.optimization_barrier(
+        (mine_rest + theirs_rest, grad_attended, gate_part)
+    )
+    rest_part = lax.psum_scatter(rest_part, "shard", scatter_dimension=0, tiled=False)
 
     grad_queries_t, grad_keys, grad_values, ahead, behind = attention_backward(
         info, table, query_rows, key_rows, key_t, value_rows, grad_attended, attended_t, log_totals
@@ -1262,28 +1896,11 @@
     grad_three = jnp.concatenate([grad_queries_t.T, grad_keys, grad_values], axis=1)
     three_wgrad = lax.dot_general(normed_all, grad_three, across, preferred_element_type=jnp.float32)
     norm1_grad = jnp.sum(three_wgrad * weights.astype(jnp.float32), axis=1) / norm1_gain
-    def normed_part(block):
-        part = lax.dynamic_slice_in_dim(grad_three, block * local_rows, local_rows, 0)
-        part = lax.dot_general(
-            part, weights, (((1,), (1,)), ((), ())), preferred_element_type=jnp.float32
-        )
-        return part.astype(jnp.bfloat16)
-
-    if split_trees():
-        grad_normed_one = tree_scatter(normed_part)
-    else:
-        grad_normed_all = jnp.concatenate([normed_part(block) for block in range(shards)], axis=0)
-        grad_normed_one = lax.psum_scatter(
-            grad_normed_all, "shard", scatter_dimension=0, tiled=True
-        ).astype(jnp.float32)
-    grad_base_one = grad_normed_one * norm1_gain
-    grad_tokens = grad_hidden + scale_one * (
-        grad_base_one - base_one * jnp.mean(grad_base_one * base_one, axis=1, keepdims=True)
-    )
-    three_wgrad, out_grad = reduce_attention_grads(
-        three_wgrad.astype(jnp.bfloat16), out_grad.astype(jnp.bfloat16)
-    )
-    query_wgrad, key_wgrad, value_wgrad = jnp.split(three_wgrad, 3, axis=1)
+    grad_normed_all = lax.dot_general(
+        grad_three, weights, (((1,), (1,)), ((), ())), preferred_element_type=jnp.float32
+    ).astype(jnp.bfloat16)
+    three_wgrad = three_wgrad.astype(jnp.bfloat16)
+
     heads_here = bias_grad.shape[1]
     group = my_place()[3] if split_trees() else shard_index
     bias_all = lax.dynamic_update_slice_in_dim(
@@ -1294,20 +1911,36 @@
         [router_grad.T, norm2_grad[None], norm1_grad[None], bias_line[None], jnp.full((1, width), error_sum)],
         axis=0,
     )
-    small = sum_over(small, ("dp", "expert", "shard"))
+    if split_trees():
+        grad_normed_one, three_wgrad, small = reduce_last(
+            grad_normed_all.reshape(shards, local_rows, width), three_wgrad, small
+        )
+    else:
+        grad_normed_one = lax.psum_scatter(grad_normed_all, "shard", scatter_dimension=0, tiled=True)
+        three_wgrad = lax.psum(three_wgrad, ("expert", "dp"))
+        small = sum_over(small, ("dp", "expert", "shard"))
+    three_wgrad = three_wgrad.astype(jnp.float32)
+    query_wgrad, key_wgrad, value_wgrad = jnp.split(three_wgrad, 3, axis=1)
     router_grad, norm2_grad, norm1_grad = small[:experts].T, small[experts], small[experts + 1]
     bias_all = small[experts + 2, : bias_all.size].reshape(bias_all.shape)
     bias_grad = lax.dynamic_slice_in_dim(bias_all, shard_index * heads_here, heads_here, 1)
     error_total = small[experts + 3, 0]
+    grad_normed_one = grad_normed_one.astype(jnp.float32)
+    grad_base_one = grad_normed_one * norm1_gain
+    grad_tokens = grad_hidden + scale_one * (
+        grad_base_one - base_one * jnp.mean(grad_base_one * base_one, axis=1, keepdims=True)
+    )
     loss = error_total / (width * valid_total)
 
-    other_part = swap(weight_part, "dp", 1)
     first_core = lax.axis_index("dp") == 0
-    weight_grad = jnp.concatenate(
-        [jnp.where(first_core, weight_part, other_part), jnp.where(first_core, other_part, weight_part)],
-        axis=1,
-    ).astype(jnp.float32)
-    gate_grad, up_grad, down_grad = weight_grad[0].T[None], weight_grad[1].T[None], weight_grad[2][None]
+
+    def both_halves(mine):
+        other = swap(mine, "dp", 1)
+        halves = [jnp.where(first_core, mine, other), jnp.where(first_core, other, mine)]
+        return jnp.concatenate(halves, axis=1).astype(jnp.float32)
+
+    gate_grad, rest_grad = both_halves(gate_part)[0].T[None], both_halves(rest_part)
+    up_grad, down_grad = rest_grad[0].T[None], rest_grad[1][None]
     return (
         output_rows.astype(jnp.bfloat16)[None],
         loss,

time: 1050 us -> 905 us (0.86); the launches traced: 1040 us -> 905 us
  Pallas kernels: 292 us -> 712 us
  starting transfers between devices: 293 us -> 15.9 us
  waiting for transfers between devices: 250 us -> 36.6 us
  other arithmetic: 84.4 us -> 51.9 us
  local copies, waits for them, and re-layouts: 70.8 us -> 44.4 us
    pallas_call x2 -> x10, Pallas kernels: 86.4 us -> 469 us  [the longest x4 222 us: exchange_call(): pl.pallas_call(kernel, in_specs=[anywhere] * len(operands), out_specs=[an...]
    ppermute x74 -> x14, starting transfers between devices: 193 us -> 10.6 us  [swap(): return lax.ppermute(array, axis, [(i, i ^ bit) for i in range(size)])]
    ppermute x74 -> x14, waiting for transfers between devices: 165 us -> 36.5 us  [swap(): return lax.ppermute(array, axis, [(i, i ^ bit) for i in range(size)])]
    ppermute x18 -> x0, starting transfers between devices: 85.7 us -> none  [move(): return lax.ppermute(array, PLACE, [(index(a), index(b)) for a, b in pairs])]
    ppermute x18 -> x0, waiting for transfers between devices: 84.6 us -> none  [move(): return lax.ppermute(array, PLACE, [(index(a), index(b)) for a, b in pairs])]
    pallas_call x1, Pallas kernels: 59.7 us -> 103 us  [expert_backward(): pl.pallas_call(expert_backward_kernel, grid_spec=pltpu.PrefetchScalarGrid...]
    select_n x6 -> x4, other arithmetic: 12.7 us -> 1.77 us  [the longest x1 1.57 us: weight_last_hop(): return hop(jnp.where(z == 1, two[1], two[0]), [(1, 0), (2, 3)])]
    add x18 -> x3, other arithmetic: 24.1 us -> 16 us  [the longest x1 8.13 us: on_device(): mine_rest + theirs_rest]
  transfers between devices with their start and end apart: 97 -> 19, of which waited for: 32 -> 4; matrix products, arithmetic and copies ran while one was open for 15% -> 9% of each run, Pallas kernels for 9% -> 42%
where the time goes in v3:
time: 905 us
  Pallas kernels  712 us (79%)
  other arithmetic  51.9 us (6%)
  local copies, waits for them, and re-layouts  44.4 us (5%)
  waiting for transfers between devices  36.6 us (4%)
  matrix products  24.8 us (3%)
  between operations  19.5 us (2%)
  starting transfers between devices  15.9 us (2%)
    pallas_call x4, Pallas kernels, exchange_call(): pl.pallas_call(kernel, in_specs=[anywhere] * len(operands), out_specs=[an...  222 us
    pallas_call x1, Pallas kernels, expert_backward(): pl.pallas_call(expert_backward_kernel, grid_spec=pltpu.PrefetchScalarGrid...  103 us
    pallas_call x2, Pallas kernels, layer_scatter(): pl.pallas_call(scatter_kernel, in_specs=[pl.BlockSpec(memory_space=pltpu....  91.2 us
    pallas_call x1, Pallas kernels, reduce_last(): pl.pallas_call(last_kernel, in_specs=[vmem] * 3, out_specs=[vmem] * 3, ou...  90.4 us
    pallas_call x2, Pallas kernels, expert_forward(): pl.pallas_call(functools.partial(expert_forward_kernel, first=first, sour...  57.9 us
    pallas_call x4, Pallas kernels, whole_calls(): pl.pallas_call(kernel, in_specs=specs, out_specs=jax.tree.map(lambda _: p...  57.9 us
    pallas_call x1, Pallas kernels, attention_backward(): pl.pallas_call(functools.partial(backward_kernel, heads=heads, tiles=tile...  52.9 us
    ppermute x14, waiting for transfers between devices, swap(): return lax.ppermute(array, axis, [(i, i ^ bit) for i in range(size)])  36.5 us
  transfers between devices with their start and end apart: 19, of which 4 were waited for; matrix products, arithmetic and copies ran while one was open for 9% of the time, Pallas kernels for 42%

profile of v3, /device:TPU:0, one launch (start us, length us, event | category | flops | bytes accessed | tf_op | source)
XLA Modules:
  0.0 905.1 jit_solution(12951266642156985587)
XLA Ops:
  12.4 1.6 fusion.7
  18.6 3.3 multiply_convert_fusion.1
  22.0 1.6 fusion.11.own.refs_1_
  24.0 63.7 %gather_tree.1 = (bf16[4,2,320,1024]{3,2,1,0:T(8,128)(2,1)}, bf16[1024,768]{1,0:T(8,128)(2,1)S(1)}, bf16[4,4,2,32,1024]{4,3,2,1,0:T(8,128)(2,1)}, f32[9,16,128]{...) custom-call(bf16[2,320,1024]{2,1,0:T(8,128)(2,1)S(1)} %get-tuple-ele, ...), custom_call_target="tpu_custom_call" | custom-call | flops 49999998976 | bytes 1000000 | tf_op jit(solution)/shard_map/gather_tree/pallas_call | solution.py:1157
  87.6 2.7 collective-permute-start
  92.2 2.5 copy-done.14
  94.7 6.7 project.1
  102.7 29.2 %attention_forward.1 = (bf16[256,2560]{1,0:T(8,128)(2,1)S(1)}, f32[20,1,512]{2,1,0:T(1,128)S(1)}) custom-call(s32[64]{0:T(128)S(1)} %fusion.103.info, f32[4,128]{1,0:T(4,128)S(1)} %fusion.21.table, bf16[2560,256]{1,0:T(8,128)(2,1)S(1)} %get-tuple-element.117.q, bf16[2560,256]{1,0:T(8,128)(2,1)S(1)} %get-tuple-element.118.k, bf16[256,2560]{1,0:T(8,128)(2,1)} %copy-done.28), custom_call_target="tpu_custom_call" | custom-call | flops 40000000000 | bytes 10000000 | tf_op jit(solution)/shard_map/attention_forward/pallas_call | solution.py:163
  132.0 28.8 %trade_heads.1 = bf16[4,256,640]{2,1,0:T(8,128)(2,1)S(1)} custom-call(bf16[256,2560]{1,0:T(8,128)(2,1)S(1)} %get-tuple-element.120.attended.attended_t), custom_call_target="tpu_custom_call" | custom-call | flops 49999998976 | bytes 1000000 | tf_op jit(solution)/shard_map/trade_heads/pallas_call | solution.py:1157
  163.0 1.5 copy.101
  166.5 3.3 multiply_reduce_fusion.4
  171.4 63.5 %meet.1 = (bf16[6,320,1024]{2,1,0:T(8,128)(2,1)}, bf16[4,3,352,1024]{3,2,1,0:T(8,128)(2,1)}, bf16[3,352,1024]{2,1,0:T(8,128)(2,1)S(1)}, bf16[3,352,1024]{2,1,0:T(8,128)(2,1)S(1)}) custom-call(bf16[2,320,1024]{2,1,0:T(8,128)(2,1)S(1)} %bitcast.151, bf16[3,352,1024]{2,1,0:T(8,128)(2,1)} %fusion.11.own.refs_1_, ...), custom_call_target="tpu_custom_call" | custom-call | flops 49999998976 | bytes 1000000 | tf_op jit(solution)/shard_map/meet/pallas_call | solution.py:1157
  235.0 1.6 broadcast_select_fusion
  239.0 14.2 %compact_rows.1 = (bf16[2560,1024]{1,0:T(8,128)(2,1)}, f32[8,320,1]{2,1,0:T(8,128)S(1)}) custom-call(s32[10]{0:T(128)S(1)} %pad_add_fusion.1.scalars, bf16[1024,128]{1,0:T(8,128)(2,1)S(1)} %copy-done.9, s32[8,1,320]{2,1,0:T(1,128)S(1)} %add_select_fusion.1.slots, s32[8,320,2]{2,1,0:T(8,128)S(1)} %bitcast.154, bf16[2,320,1024]{2,1,0:T(8,128)(2,1)S(1)} %bitcast.152, ...), custom_call_target="tpu_custom_call" | custom-call | flops 10000000000 | bytes 30000000 | tf_op jit(solution)/shard_map/compact_rows/pallas_call | solution.py:422
  254.2 36.9 %expert_forward.2.refs_8_ = f32[2560,1024]{1,0:T(8,128)} custom-call(s32[6]{0:T(128)} %concatenate.68.scalars, bf16[2560,1024]{1,0:T(8,128)(2,1)} %get-tuple-element.125.rows, bf16[4,3,352,1024]{3,2,1,0:T(8,128)(2,1)} %get-tuple-element.126.refs_0_, bf16[3,352,1024]{2,1,0:T(8,128)(2,1)} %fusion.11.own.refs_1_, ...), custom_call_target="tpu_custom_call" | custom-call | flops 33218887680 | bytes 17301504 | tf_op jit(solution)/shard_map/expert_forward/pallas_call | solution.py:623
  294.0 2.2 reshape.647
  298.4 2.6 add_select_fusion.slots
  301.0 21.0 %expert_forward.3.refs_1_ = f32[2560,1024]{1,0:T(8,128)} custom-call(s32[6]{0:T(128)} %concatenate.68.scalars, bf16[2560,1024]{1,0:T(8,128)(2,1)} %get-tuple-element.125.rows, bf16[4,3,352,1024]{3,2,1,0:T(8,128)(2,1)} %get-tuple-element.126.refs_0_, bf16[3,352,1024]{2,1,0:T(8,128)(2,1)} %fusion.11.own.refs_1_, ...), custom_call_target="tpu_custom_call" | custom-call | flops 11072962560 | bytes 17301504 | tf_op jit(solution)/shard_map/expert_forward/pallas_call | solution.py:623
  322.0 15.7 %expand.2 = (bf16[8,320,1024]{2,1,0:T(8,128)(2,1)}, bf16[8,320,1024]{2,1,0:T(8,128)(2,1)}) custom-call(s32[10]{0:T(128)} %copy-done.12, s32[8,320,1]{2,1,0:T(8,128)} %add_select_fusion.slots, f32[8,320,1]{2,1,0:T(8,128)} %copy-done.23, f32[2560,1024]{1,0:T(8,128)} %expert_forward.3.refs_1_), custom_call_target="tpu_custom_call" | custom-call | flops 10000000000 | bytes 30000000 | tf_op jit(solution)/shard_map/expand/pallas_call | solution.py:422
  337.8 2.5 copy-done.20
  340.3 45.4 %layer_scatter.2 = (f32[320,1024]{1,0:T(8,128)S(1)}, f32[320,1024]{1,0:T(8,128)S(1)}) custom-call(bf16[8,320,1024]{2,1,0:T(8,128)(2,1)S(1)} %copy-done.20), custom_call_target="tpu_custom_call" | custom-call | flops 49999998976 | bytes 10000000 | tf_op jit(solution)/shard_map/layer_scatter/pallas_call | solution.py:799
  387.3 1.4 fusion.89
  393.7 12.8 %collective-permute-done.4 = bf16[320,1024]{1,0:T(8,128)(2,1)} collective-permute-done((bf16[320,1024]{1,0:T(8,128)(2,1)S(1)}, bf16[320,1024]{1,0:T(8,128)(2,1)}, u32[]{:S(2)}, u32[]{:S(2)}) %collective-permute-start.4) | collective-permute-done | bytes 655392 | tf_op jit(solution)/shard_map/ppermute | solution.py:761
  409.6 10.8 %collective-permute-done.5 = bf16[320,1024]{1,0:T(8,128)(2,1)S(1)} collective-permute-done((bf16[320,1024]{1,0:T(8,128)(2,1)S(1)}, bf16[320,1024]{1,0:T(8,128)(2,1)S(1)}, u32[]{:S(2)}, u32[]{:S(2)}) %collective-permute-start.5) | collective-permute-done | bytes 655392 | tf_op jit(solution)/shard_map/ppermute | solution.py:761
  421.3 12.1 %collective-permute-done.8 = bf16[320,1024]{1,0:T(8,128)(2,1)S(1)} collective-permute-done((bf16[320,1024]{1,0:T(8,128)(2,1)}, bf16[320,1024]{1,0:T(8,128)(2,1)S(1)}, u32[]{:S(2)}, u32[]{:S(2)}) %collective-permute-start.8) | collective-permute-done | bytes 655392 | tf_op jit(solution)/shard_map/ppermute | solution.py:761
  434.4 15.9 %compact_grads.1 = (bf16[2560,1024]{1,0:T(8,128)(2,1)}, f32[8,320,1]{2,1,0:T(8,128)}) custom-call(s32[10]{0:T(128)} %copy-done.12, s32[8,1,320]{2,1,0:T(1,128)} %copy-done.10, f32[8,320,1]{2,1,0:T(8,128)} %copy-done.23, bf16[8,320,1024]{2,1,0:T(8,128)(2,1)} %get-tuple-element.136.produced, bf16[1,320,1024]{2,1,0:T(8,128)(2,1)} %get-tuple-element.254.refs_0_, ...), custom_call_target="tpu_custom_call" | custom-call | flops 10000000000 | bytes 30000000 | tf_op jit(solution)/shard_map/compact_grads/pallas_call | solution.py:422
  450.3 103.5 %expert_backward.1 = (bf16[4,1,352,1024]{3,2,1,0:T(8,128)(2,1)}, bf16[4,1,352,1024]{3,2,1,0:T(8,128)(2,1)}, bf16[4,2,352,1024]{3,2,1,0:T(8,128)(2,1)}, bf16[4,2,352,1024]{3,2,1,0:T(8,128)(2,1)}, f32[2560,1024]{1,0:T(8,128)}) custom-call(s32[6]{0:T(128)} %concatenate.68.scalars, bf16[2560,1024]{1,0:T(8,128)(2,1)} %get-tuple-element.125.rows, ...), custom_call_target="tpu_custom_call" | custom-call | flops 118111600640 | bytes 17301504 | tf_op jit(solution)/shard_map/expert_backward/pallas_call | solution.py:698
  554.5 1.5 collective-permute-start.14
  558.2 12.0 %expand.3.parts = bf16[8,320,1024]{2,1,0:T(8,128)(2,1)} custom-call(s32[10]{0:T(128)} %copy-done.12, s32[8,320,1]{2,1,0:T(8,128)} %add_select_fusion.slots, f32[2560,1024]{1,0:T(8,128)} %get-tuple-element.140.refs_0_), custom_call_target="tpu_custom_call" | custom-call | flops 10000000000 | bytes 30000000 | tf_op jit(solution)/shard_map/expand/pallas_call | solution.py:422
  571.6 5.7 add.432
  577.4 2.6 copy-done.19
  580.1 45.8 %layer_scatter.3 = (f32[320,1024]{1,0:T(8,128)S(1)}, f32[320,1024]{1,0:T(8,128)S(1)}) custom-call(bf16[8,320,1024]{2,1,0:T(8,128)(2,1)S(1)} %copy-done.19), custom_call_target="tpu_custom_call" | custom-call | flops 49999998976 | bytes 10000000 | tf_op jit(solution)/shard_map/layer_scatter/pallas_call | solution.py:799
  626.0 5.0 multiply_reduce_fusion.2
  631.0 2.7 multiply_add_fusion
  633.8 1.8 convolution_convert_fusion.1
  636.3 1.6 convolution_convert_fusion.2.grads
  637.9 66.4 %trade_back.1 = (bf16[4,640,256]{2,1,0:T(8,128)(2,1)S(1)}, bf16[4,2,32,1024]{3,2,1,0:T(8,128)(2,1)S(1)}) custom-call(bf16[640,1024]{1,0:T(8,128)(2,1)S(1)} %convolution_convert_fusion.2.grads, bf16[4,4,64,1024]{3,2,1,0:T(8,128)(2,1)S(1)} %bitcast.153), custom_call_target="tpu_custom_call" | custom-call | flops 1000000 | bytes 1000000 | tf_op jit(solution)/shard_map/trade_back/pallas_call | solution.py:1157
  705.7 8.1 add.431
  713.8 52.9 %attention_backward.1 = (bf16[256,2560]{1,0:T(8,128)(2,1)}, bf16[2560,256]{1,0:T(8,128)(2,1)}, bf16[2560,256]{1,0:T(8,128)(2,1)}, f32[18,1,512]{2,1,0:T(1,128)}, f32[18,1,512]{2,1,0:T(1,128)}) custom-call(s32[64]{0:T(128)} %copy-done.11, f32[4,128]{1,0:T(4,128)} %copy-done.18, bf16[2560,256]{1,0:T(8,128)(2,1)} %copy-done.24, bf16[2560,256]{1,0:T(8,128)(2,1)} %copy-done.25, ...), custom_call_target="tpu_custom_call" | custom-call | flops 60000002048 | bytes 10000000 | tf_op jit(solution)/shard_map/attention_backward/pallas_call | solution.py:295
  766.8 1.9 copy.102
  768.8 8.8 multiply_reduce_fusion
  779.1 7.9 convolution_convert_fusion
  787.0 90.4 %reduce_last.1 = (bf16[2,320,1024]{2,1,0:T(8,128)(2,1)S(1)}, bf16[4,2,128,768]{3,2,1,0:T(8,128)(2,1)S(1)}, f32[8,1024]{1,0:T(8,128)S(1)}) custom-call(bf16[4,2,320,1024]{3,2,1,0:T(8,128)(2,1)} %bitcast.191, bf16[4,256,768]{2,1,0:T(8,128)(2,1)S(1)} %bitcast.158, f32[8,1024]{1,0:T(8,128)S(1)} %concatenate.73.small), custom_call_target="tpu_custom_call" | custom-call | flops 49999998976 | bytes 10000000 | tf_op jit(solution)/shard_map/reduce_last/pallas_call | solution.py:1587
  880.7 2.0 bitcast_convert_fusion
  883.8 3.8 fusion.88
  887.6 2.2 fusion.6
  891.0 1.9 convert_bitcast_fusion
  893.9 3.0 fusion.87
  (321 shorter events, 50.4 us)
Async XLA Ops:
  7.2 706.6 %reduce-scatter.3.cloned.1.call-start = ((), (), s32[]{:S(2)}) async-start(), calls=%async_computation.2 | async-start | bytes 3604480 | tf_op jit(solution)/shard_map/reduce_scatter | solution.py:1847
  87.6 82.6 %collective-permute-start = (bf16[3,352,1024]{2,1,0:T(8,128)(2,1)}, bf16[3,352,1024]{2,1,0:T(8,128)(2,1)}, u32[]{:S(2)}, u32[]{:S(2)}) collective-permute-start(bf16[3,352,1024]{2,1,0:T(8,128)(2,1)} %fusion.11.own.refs_1_), channel_id=1, source_target_pairs={{0,2},{2,4},{4,6},{1,3},{3,5},{5,7},{8,10},{10,12},{12,14},{9,11},... | collective-permute-start | bytes 6488072 | tf_op jit(solution)/shard_map/ppermute | solution.py:856
  90.3 80.0 %collective-permute-start.1 = (bf16[3,352,1024]{2,1,0:T(8,128)(2,1)}, bf16[3,352,1024]{2,1,0:T(8,128)(2,1)}, u32[]{:S(2)}, u32[]{:S(2)}) collective-permute-start(bf16[3,352,1024]{2,1,0:T(8,128)(2,1)} %fusion.11.own.refs_1_), channel_id=1, source_target_pairs={{2,0},{4,2},{6,4},{3,1},{5,3},{7,5},{10,8},{12,10},{14,12},{11,9},... | collective-permute-start | bytes 6488072 | tf_op jit(solution)/shard_map/ppermute | solution.py:856
  102.5 29.4 %copy-start.24 = (bf16[2560,256]{1,0:T(8,128)(2,1)}, bf16[2560,256]{1,0:T(8,128)(2,1)S(1)}, u32[]{:S(2)}) copy-start(bf16[2560,256]{1,0:T(8,128)(2,1)S(1)} %get-tuple-element.117.q) | copy-start | bytes 3932164
  102.5 29.5 %copy-start.25 = (bf16[2560,256]{1,0:T(8,128)(2,1)}, bf16[2560,256]{1,0:T(8,128)(2,1)S(1)}, u32[]{:S(2)}) copy-start(bf16[2560,256]{1,0:T(8,128)(2,1)S(1)} %get-tuple-element.118.k) | copy-start | bytes 3932164
  102.5 29.5 %copy-start.26 = (bf16[256,2560]{1,0:T(8,128)(2,1)}, bf16[256,2560]{1,0:T(8,128)(2,1)S(1)}, u32[]{:S(2)}) copy-start(bf16[256,2560]{1,0:T(8,128)(2,1)S(1)} %get-tuple-element.134.k_t) | copy-start | bytes 3932164
  102.5 29.5 %copy-start.27 = (bf16[2560,256]{1,0:T(8,128)(2,1)}, bf16[2560,256]{1,0:T(8,128)(2,1)S(1)}, u32[]{:S(2)}) copy-start(bf16[2560,256]{1,0:T(8,128)(2,1)S(1)} %get-tuple-element.135.v) | copy-start | bytes 3932164
  102.7 29.3 %copy-start.18 = (f32[4,128]{1,0:T(4,128)}, f32[4,128]{1,0:T(4,128)S(1)}, u32[]{:S(2)}) copy-start(f32[4,128]{1,0:T(4,128)S(1)} %fusion.21.table) | copy-start | bytes 6148
  132.0 28.9 %copy-start.29 = (bf16[256,2560]{1,0:T(8,128)(2,1)}, bf16[256,2560]{1,0:T(8,128)(2,1)S(1)}, u32[]{:S(2)}) copy-start(bf16[256,2560]{1,0:T(8,128)(2,1)S(1)} %get-tuple-element.120.attended.attended_t) | copy-start | bytes 3932164
  132.0 30.7 %copy-start.61 = (f32[1024,4]{0,1:T(4,128)S(1)}, f32[1024,4]{0,1:T(4,128)}, u32[]{:S(2)}) copy-start(f32[1024,4]{0,1:T(4,128)} %param.38) | copy-start | bytes 49156
  166.5 72.4 %copy-start.12 = (s32[10]{0:T(128)}, s32[10]{0:T(128)S(1)}, u32[]{:S(2)}) copy-start(s32[10]{0:T(128)S(1)} %pad_add_fusion.1.scalars) | copy-start | bytes 124
  169.9 65.0 %copy-start.58 = (f32[640]{0:T(1024)}, f32[640]{0:T(1024)S(1)}, u32[]{:S(2)}) copy-start(f32[640]{0:T(1024)S(1)} %add_rsqrt_fusion) | copy-start | bytes 7684
  170.0 69.0 %copy-start.10 = (s32[8,1,320]{2,1,0:T(1,128)}, s32[8,1,320]{2,1,0:T(1,128)S(1)}, u32[]{:S(2)}) copy-start(s32[8,1,320]{2,1,0:T(1,128)S(1)} %add_select_fusion.1.slots) | copy-start | bytes 30724
  237.6 53.5 %collective-permute-start.2 = (bf16[3,352,1024]{2,1,0:T(8,128)(2,1)}, bf16[3,352,1024]{2,1,0:T(8,128)(2,1)}, u32[]{:S(2)}, u32[]{:S(2)}) collective-permute-start(bf16[3,352,1024]{2,1,0:T(8,128)(2,1)} %broadcast_select_fusion), channel_id=1, source_target_pairs={{2,0},{4,6},{3,1},{5,7},{10,8},{12,14},{11,9},{13,15},{18,16},{20,... | collective-permute-start | bytes 6488072 | tf_op jit(solution)/shard_map/ppermute | solution.py:856
  291.1 9.9 %collective-permute-start.3 = (bf16[3,352,1024]{2,1,0:T(8,128)(2,1)}, bf16[3,352,1024]{2,1,0:T(8,128)(2,1)}, u32[]{:S(2)}, u32[]{:S(2)}) collective-permute-start(bf16[3,352,1024]{2,1,0:T(8,128)(2,1)} %collective-permute-done.2.refs_6_), channel_id=1, source_target_pairs={{0,1},{1,0},{2,3},{3,2},{4,5},{5,4},{6,7},{7,6},{8,9},{9,8},{10,11... | collective-permute-start | bytes 6488072 | tf_op jit(solution)/shard_map/ppermute | solution.py:761
  298.4 87.3 %copy-start.56 = (f32[640]{0:T(1024)}, f32[640]{0:T(1024)S(1)}, u32[]{:S(2)}) copy-start(f32[640]{0:T(1024)S(1)} %convert_reduce_fusion) | copy-start | bytes 7684
  340.3 45.4 %copy-start.32 = (f32[640,1024]{1,0:T(8,128)S(1)}, f32[640,1024]{1,0:T(8,128)}, u32[]{:S(2)}) copy-start(f32[640,1024]{1,0:T(8,128)} %copy-done.31) | copy-start | bytes 7864324
  340.3 45.5 %copy-start.34 = (bf16[1,640,1024]{2,1,0:T(8,128)(2,1)S(1)}, bf16[1,640,1024]{2,1,0:T(8,128)(2,1)}, u32[]{:S(2)}) copy-start(bf16[1,640,1024]{2,1,0:T(8,128)(2,1)} %param.28) | copy-start | bytes 3932164
  388.7 17.8 %collective-permute-start.4 = (bf16[320,1024]{1,0:T(8,128)(2,1)S(1)}, bf16[320,1024]{1,0:T(8,128)(2,1)}, u32[]{:S(2)}, u32[]{:S(2)}) collective-permute-start(bf16[320,1024]{1,0:T(8,128)(2,1)S(1)} %get-tuple-element.256), channel_id=1, source_target_pairs={{0,8},{8,0},{16,24},{24,16},{1,9},{9,1},{17,25},{25,17},{2,10},{10... | collective-permute-start | bytes 1966088 | tf_op jit(solution)/shard_map/ppermute | solution.py:761
  389.5 17.8 %collective-permute-start.7 = (bf16[320,1024]{1,0:T(8,128)(2,1)S(1)}, bf16[320,1024]{1,0:T(8,128)(2,1)}, u32[]{:S(2)}, u32[]{:S(2)}) collective-permute-start(bf16[320,1024]{1,0:T(8,128)(2,1)S(1)} %get-tuple-element.253), channel_id=1, source_target_pairs={{0,16},{8,24},{16,0},{24,8},{1,17},{9,25},{17,1},{25,9},{2,18},{10... | collective-permute-start | bytes 1966088 | tf_op jit(solution)/shard_map/ppermute | solution.py:761
  391.6 28.8 %collective-permute-start.5 = (bf16[320,1024]{1,0:T(8,128)(2,1)S(1)}, bf16[320,1024]{1,0:T(8,128)(2,1)S(1)}, u32[]{:S(2)}, u32[]{:S(2)}) collective-permute-start(bf16[320,1024]{1,0:T(8,128)(2,1)S(1)} %get-tuple-element.253), channel_id=1, source_target_pairs={{0,8},{8,0},{16,24},{24,16},{1,9},{9,1},{17,25},{25,17},{2,10},{10... | collective-permute-start | bytes 1966088 | tf_op jit(solution)/shard_map/ppermute | solution.py:761
  392.5 28.8 %collective-permute-start.6 = (bf16[320,1024]{1,0:T(8,128)(2,1)S(1)}, bf16[320,1024]{1,0:T(8,128)(2,1)S(1)}, u32[]{:S(2)}, u32[]{:S(2)}) collective-permute-start(bf16[320,1024]{1,0:T(8,128)(2,1)S(1)} %get-tuple-element.256), channel_id=1, source_target_pairs={{0,16},{8,24},{16,0},{24,8},{1,17},{9,25},{17,1},{25,9},{2,18},{10... | collective-permute-start | bytes 1966088 | tf_op jit(solution)/shard_map/ppermute | solution.py:761
  406.5 26.8 %collective-permute-start.8 = (bf16[320,1024]{1,0:T(8,128)(2,1)}, bf16[320,1024]{1,0:T(8,128)(2,1)S(1)}, u32[]{:S(2)}, u32[]{:S(2)}) collective-permute-start(bf16[320,1024]{1,0:T(8,128)(2,1)} %collective-permute-done.4), channel_id=1, source_target_pairs={{0,16},{8,24},{16,0},{24,8},{1,17},{9,25},{17,1},{25,9},{2,18},{10... | collective-permute-start | bytes 1966088 | tf_op jit(solution)/shard_map/ppermute | solution.py:761
  407.3 26.0 %collective-permute-start.9 = (bf16[320,1024]{1,0:T(8,128)(2,1)}, bf16[320,1024]{1,0:T(8,128)(2,1)S(1)}, u32[]{:S(2)}, u32[]{:S(2)}) collective-permute-start(bf16[320,1024]{1,0:T(8,128)(2,1)} %collective-permute-done.7), channel_id=1, source_target_pairs={{0,8},{8,0},{16,24},{24,16},{1,9},{9,1},{17,25},{25,17},{2,10},{10... | collective-permute-start | bytes 1966088 | tf_op jit(solution)/shard_map/ppermute | solution.py:761
  450.3 103.7 %copy-start.45 = (f32[8,320,1]{2,1,0:T(8,128)S(1)}, f32[8,320,1]{2,1,0:T(8,128)}, u32[]{:S(2)}) copy-start(f32[8,320,1]{2,1,0:T(8,128)} %get-tuple-element.148) | copy-start | bytes 30724
  553.8 17.8 %collective-permute-start.11 = (bf16[4,1,352,1024]{3,2,1,0:T(8,128)(2,1)}, bf16[4,1,352,1024]{3,2,1,0:T(8,128)(2,1)}, u32[]{:S(2)}, u32[]{:S(2)}) collective-permute-start(bf16[4,1,352,1024]{3,2,1,0:T(8,128)(2,1)} %get-tuple-element.141), channel_id=1, source_target_pairs={{0,1},{1,0},{2,3},{3,2},{4,5},{5,4},{6,7},{7,6},{8,9},{9,8},{10,11... | collective-permute-start | bytes 8650760 | tf_op jit(solution)/shard_map/ppermute | solution.py:761
  554.5 15.8 %collective-permute-start.14 = (f32[640]{0:T(1024)S(1)}, f32[640]{0:T(1024)S(1)}, u32[]{:S(2)}, u32[]{:S(2)}) collective-permute-start(f32[640]{0:T(1024)S(1)} %squeeze.44), channel_id=1, source_target_pairs={{0,24},{8,16},{16,8},{24,0},{1,25},{9,17},{17,9},{25,1},{2,26},{10... | collective-permute-start | bytes 7688 | tf_op jit(solution)/shard_map/ppermute | solution.py:761
  556.1 14.3 %collective-permute-start.13 = (f32[640]{0:T(1024)S(1)}, f32[640]{0:T(1024)S(1)}, u32[]{:S(2)}, u32[]{:S(2)}) collective-permute-start(f32[640]{0:T(1024)S(1)} %squeeze.43), channel_id=1, source_target_pairs={{0,16},{8,24},{16,0},{24,8},{1,17},{9,25},{17,1},{25,9},{2,18},{10... | collective-permute-start | bytes 7688 | tf_op jit(solution)/shard_map/ppermute | solution.py:761
  557.3 13.0 %collective-permute-start.12 = (f32[640]{0:T(1024)S(1)}, f32[640]{0:T(1024)S(1)}, u32[]{:S(2)}, u32[]{:S(2)}) collective-permute-start(f32[640]{0:T(1024)S(1)} %squeeze.42), channel_id=1, source_target_pairs={{0,8},{8,0},{16,24},{24,16},{1,9},{9,1},{17,25},{25,17},{2,10},{10... | collective-permute-start | bytes 7688 | tf_op jit(solution)/shard_map/ppermute | solution.py:761
  570.3 135.4 %collective-permute-start.10 = (bf16[4,2,352,1024]{3,2,1,0:T(8,128)(2,1)}, bf16[4,2,352,1024]{3,2,1,0:T(8,128)(2,1)}, u32[]{:S(2)}, u32[]{:S(2)}) collective-permute-start(bf16[4,2,352,1024]{3,2,1,0:T(8,128)(2,1)} %get-tuple-element.139), channel_id=1, source_target_pairs={{0,1},{1,0},{2,3},{3,2},{4,5},{5,4},{6,7},{7,6},{8,9},{9,8},{10,11... | collective-permute-start | bytes 17301512 | tf_op jit(solution)/shard_map/ppermute | solution.py:761
  577.3 48.6 %copy-start.3 = (f32[320,1024]{1,0:T(8,128)S(1)}, f32[320,1024]{1,0:T(8,128)}, u32[]{:S(2)}) copy-start(f32[320,1024]{1,0:T(8,128)} %copy-done.2) | copy-start | bytes 3932164
  577.3 48.6 %copy-start.5 = (f32[320,1024]{1,0:T(8,128)S(1)}, f32[320,1024]{1,0:T(8,128)}, u32[]{:S(2)}) copy-start(f32[320,1024]{1,0:T(8,128)} %copy-done.4) | copy-start | bytes 3932164
  577.3 305.4 %reduce-scatter.5.cloned.1.call-start = ((), (), s32[]{:S(2)}) async-start(), calls=%async_computation.3 | async-start | bytes 7208960 | tf_op jit(solution)/shard_map/reduce_scatter | solution.py:1889
  580.0 45.9 %copy-start.33 = (f32[640,1024]{1,0:T(8,128)S(1)}, f32[640,1024]{1,0:T(8,128)}, u32[]{:S(2)}) copy-start(f32[640,1024]{1,0:T(8,128)} %copy-done.31) | copy-start | bytes 7864324
  580.0 45.9 %copy-start.35 = (bf16[1,640,1024]{2,1,0:T(8,128)(2,1)S(1)}, bf16[1,640,1024]{2,1,0:T(8,128)(2,1)}, u32[]{:S(2)}) copy-start(bf16[1,640,1024]{2,1,0:T(8,128)(2,1)} %param.28) | copy-start | bytes 3932164
  580.0 45.9 %copy-start.57 = (f32[640]{0:T(1024)S(1)}, f32[640]{0:T(1024)}, u32[]{:S(2)}) copy-start(f32[640]{0:T(1024)} %copy-done.56) | copy-start | bytes 7684
  580.0 45.9 %copy-start.59 = (f32[640]{0:T(1024)S(1)}, f32[640]{0:T(1024)}, u32[]{:S(2)}) copy-start(f32[640]{0:T(1024)} %copy-done.58) | copy-start | bytes 7684
  580.0 45.9 %copy-start.65 = (f32[1024,1]{0,1:T(1,128)S(1)}, f32[1024,1]{0,1:T(1,128)}, u32[]{:S(2)}) copy-start(f32[1024,1]{0,1:T(1,128)} %get-tuple-element.259) | copy-start | bytes 12292
  580.0 45.9 %copy-start.66 = (f32[1024,1]{0,1:T(1,128)S(1)}, f32[1024,1]{0,1:T(1,128)}, u32[]{:S(2)}) copy-start(f32[1024,1]{0,1:T(1,128)} %get-tuple-element.260) | copy-start | bytes 12292
  580.0 45.9 %copy-start.67 = (f32[1024,1]{0,1:T(1,128)S(1)}, f32[1024,1]{0,1:T(1,128)}, u32[]{:S(2)}) copy-start(f32[1024,1]{0,1:T(1,128)} %get-tuple-element.261) | copy-start | bytes 12292
  580.1 45.9 %copy-start.68 = (f32[1024,1]{0,1:T(1,128)S(1)}, f32[1024,1]{0,1:T(1,128)}, u32[]{:S(2)}) copy-start(f32[1024,1]{0,1:T(1,128)} %get-tuple-element.262) | copy-start | bytes 12292
  580.1 45.9 %copy-start.70 = (f32[1024]{0:T(1024)S(1)}, f32[1024]{0:T(1024)}, u32[]{:S(2)}) copy-start(f32[1024]{0:T(1024)} %param.37) | copy-start | bytes 12292
  633.7 71.9 %slice-start = ((s8[5767168]{0:T(1024)(128)(4,1)}), s8[4194304]{0:T(1024)(128)(4,1)S(1)}, s32[]{:S(2)}) async-start(s8[5767168]{0:T(1024)(128)(4,1)} %bitcast.162), calls=%async_computation.4 | async-start | bytes 8388608
  636.3 69.4 %slice-start.1 = ((s8[5767168]{0:T(1024)(128)(4,1)}), s8[1572864]{0:T(1024)(128)(4,1)S(1)}, s32[]{:S(2)}) async-start(s8[5767168]{0:T(1024)(128)(4,1)} %bitcast.162), calls=%async_computation.5 | async-start | bytes 3145728
  787.0 90.9 %copy-start.38 = (f32[2,320,1024]{2,1,0:T(8,128)S(1)}, f32[2,320,1024]{2,1,0:T(8,128)}, u32[]{:S(2)}) copy-start(f32[2,320,1024]{2,1,0:T(8,128)} %get-tuple-element.240) | copy-start | bytes 7864324
  787.0 90.9 %copy-start.74 = (f32[2,320]{1,0:T(2,128)S(1)}, f32[2,320]{1,0:T(2,128)}, u32[]{:S(2)}) copy-start(f32[2,320]{1,0:T(2,128)} %copy-done.73) | copy-start | bytes 7684
  879.4 10.4 %collective-permute-start.15 = (bf16[1,352,1024]{2,1,0:T(8,128)(2,1)}, bf16[1,352,1024]{2,1,0:T(8,128)(2,1)}, u32[]{:S(2)}, u32[]{:S(2)}) collective-permute-start(bf16[1,352,1024]{2,1,0:T(8,128)(2,1)} %bitcast.170), channel_id=1, source_target_pairs={{0,1},{1,0},{2,3},{3,2},{4,5},{5,4},{6,7},{7,6},{8,9},{9,8},{10,11... | collective-permute-start | bytes 2162696 | tf_op jit(solution)/shard_map/ppermute | solution.py:761
  882.7 10.3 %collective-permute-start.16 = (bf16[2,352,1024]{2,1,0:T(8,128)(2,1)}, bf16[2,352,1024]{2,1,0:T(8,128)(2,1)S(1)}, u32[]{:S(2)}, u32[]{:S(2)}) collective-permute-start(bf16[2,352,1024]{2,1,0:T(8,128)(2,1)} %bitcast.167), channel_id=1, source_target_pairs={{0,1},{1,0},{2,3},{3,2},{4,5},{5,4},{6,7},{7,6},{8,9},{9,8},{10,11... | collective-permute-start | bytes 4325384 | tf_op jit(solution)/shard_map/ppermute | solution.py:761
  (58 other events, 368.2 us)
Sparse Core Ops, SparseCore 0:
  577.4 77.3 reduce-scatter.2
  713.9 128.0 reduce-scatter.4

commit v4 on v3

--- a/solution.py
+++ b/solution.py
@@ -353,8 +353,13 @@
             branch,
         ]
     )
-    info = jnp.zeros((INFO_SIZE,), jnp.int32)
-    info = info.at[:20].set(limits).at[20].set(last).at[OFFSET_AT : OFFSET_AT + CLASSES].set(offsets)
+    gap = lambda count: jnp.zeros((count,), jnp.int32)
+    info = jnp.concatenate(
+        [
+            limits, last[None], gap(OFFSET_AT - 21), offsets,
+            gap(INFO_SIZE - 1 - OFFSET_AT - CLASSES), (trunk + jnp.sum(lengths))[None],
+        ]
+    )
     return info
 
 
@@ -472,10 +477,14 @@
     )
 
 
-def expand_kernel(scalars, slots, *refs, blocks, gated):
-    gate = refs[0] if gated else None
-    rows, out = refs[1:3] if gated else refs
-    count = out.shape[1]
+def expand_kernel(scalars, slots, *refs, gated):
+    gate, (rows, *outs) = (refs[0], refs[1:]) if gated else (None, refs)
+    expand_blocks(scalars, 0, slots, rows, outs, gate)
+
+
+def expand_blocks(scalars, first, slots, rows, outs, gate=None):
+    out = outs[0]
+    blocks, count = out.shape[:2]
     for b in range(blocks):
         out[b] = jnp.zeros(out.shape[1:], out.dtype)
 
@@ -486,9 +495,10 @@
             out[b] += part.astype(jnp.bfloat16)
             return carry
 
-        lax.fori_loop(scalars[b] // SLOT_TILE, pl.cdiv(scalars[b + 1], SLOT_TILE), one, 0)
-        if gated:
-            refs[3][b] = out[b]
+        start, stop = scalars[first + b], scalars[first + b + 1]
+        lax.fori_loop(start // SLOT_TILE, pl.cdiv(stop, SLOT_TILE), one, 0)
+        if gate is not None:
+            outs[1][b] = out[b]
             out[b] = (gate[b] * out[b].astype(jnp.float32)).astype(jnp.bfloat16)
 
 
@@ -497,7 +507,7 @@
     shape = jax.ShapeDtypeStruct((blocks, count, rows.shape[1]), jnp.bfloat16)
     operands = (scalars, slots.reshape(blocks, count, 1)) + (() if gate is None else (gate,)) + (rows,)
     outs = whole_calls(
-        functools.partial(expand_kernel, blocks=blocks, gated=gate is not None),
+        functools.partial(expand_kernel, gated=gate is not None),
         operands, [shape] * (1 if gate is None else 2), "expand", 56,
     )
     return outs[0] if gate is None else outs
@@ -574,15 +584,35 @@
     return step % 2
 
 
-def expert_forward_kernel(scalars, rows, *refs, first, sources, aliased):
+def over_tiles(count, room, body):
+    large = 2 * SLOT_TILE if room <= 10 * SLOT_TILE else SLOT_TILE
+    rest = count % large
+    tiles = count // large + jnp.where(rest > SLOT_TILE if large > SLOT_TILE else rest > 0, 1, 0)
+
+    def one(tile, carry):
+        body(pl.multiple_of(tile * large, large), large)
+        return carry
+
+    lax.fori_loop(0, tiles, one, 0)
+    if large > SLOT_TILE:
+
+        @pl.when((rest > 0) & (rest <= SLOT_TILE))
+        def _():
+            body(pl.multiple_of(tiles * large, large), SLOT_TILE)
+
+
+def expert_forward_kernel(scalars, rows, *refs, first, sources, aliased, blocks):
     weights, refs = refs[:sources], refs[sources:]
     before, refs = (refs[0], refs[1:]) if aliased else (None, refs)
-    total, room, sem = refs
+    if blocks:
+        slots, gate, out, plain, total, room, sem = refs
+    else:
+        total, room, sem = refs
     step = pl.program_id(0)
     slot = next_weights(first, weight_sources(weights, scalars[1]), room, sem)
 
-    def one(tile, carry):
-        at = pl.ds(pl.multiple_of(tile * SLOT_TILE, SLOT_TILE), SLOT_TILE)
+    def body(start, size):
+        at = pl.ds(start, size)
         values = rows[at, :]
         gate_pre = lax.dot_general(values, room[slot, 0], LAST, preferred_element_type=jnp.float32)
         up_pre = lax.dot_general(values, room[slot, 1], LAST, preferred_element_type=jnp.float32)
@@ -597,9 +627,9 @@
         def _():
             total[at, :] += part
 
-        return carry
-
-    lax.fori_loop(0, pl.cdiv(scalars[0], SLOT_TILE), one, 0)
+    over_tiles(scalars[0], rows.shape[0], body)
+    if blocks:
+        expand_blocks(scalars, scalars.shape[0] - blocks - 1, slots, total, (out, plain), gate)
 
 
 def expert_cost(rows, weights, shards, units):
@@ -615,55 +645,72 @@
     return [pltpu.VMEM((2, 3, 2 * half, width), jnp.bfloat16), pltpu.SemaphoreType.DMA((2, 6))]
 
 
-def expert_forward(scalars, rows, weights, first, steps, before=None):
+def expert_forward(scalars, rows, weights, first, steps, before=None, bounds=None, slots=None, gate=None):
     padded, width = rows.shape
     theirs = weights[0]
     whole = pl.BlockSpec((padded, width), lambda s, scalars: (0, 0), pipeline_mode=pl.Buffered(1))
     extra = () if before is None else (before,)
+    extra_specs = [whole] * len(extra)
+    blocks = 0
+    out_specs, scratch = whole, []
+    out_shape = jax.ShapeDtypeStruct((padded, width), jnp.float32)
+    if slots is not None:
+        blocks, count = slots.shape
+        scalars = jnp.concatenate([scalars, bounds[: blocks + 1]])
+        extra += (slots.reshape(blocks, count, 1), gate)
+        extra_specs += [block_spec((blocks, count, 1))] * 2
+        out_specs = [block_spec((blocks, count, width))] * 2
+        out_shape = [jax.ShapeDtypeStruct((blocks, count, width), jnp.bfloat16)] * 2
+        scratch = [pltpu.VMEM((padded, width), jnp.float32)]
     return pl.pallas_call(
         functools.partial(
-            expert_forward_kernel, first=first, sources=len(weights), aliased=before is not None
+            expert_forward_kernel,
+            first=first, sources=len(weights), aliased=before is not None, blocks=blocks,
         ),
         grid_spec=pltpu.PrefetchScalarGridSpec(
             num_scalar_prefetch=1,
             grid=(steps,),
-            in_specs=[whole] + [pl.BlockSpec(memory_space=pl.ANY)] * len(weights) + [whole] * len(extra),
-            out_specs=whole,
-            scratch_shapes=expert_scratch(theirs),
+            in_specs=[whole] + [pl.BlockSpec(memory_space=pl.ANY)] * len(weights) + extra_specs,
+            out_specs=out_specs,
+            scratch_shapes=scratch + expert_scratch(theirs),
         ),
-        out_shape=jax.ShapeDtypeStruct((padded, width), jnp.float32),
+        out_shape=out_shape,
         compiler_params=pltpu.CompilerParams(vmem_limit_bytes=60 << 20),
         cost_estimate=expert_cost(padded, theirs, steps, 3),
         name="expert_forward",
     )(scalars, rows, *weights, *extra)
 
 
-def expert_backward_kernel(scalars, rows, grads, *refs):
-    weights, rest = refs[:-10], refs[-10:]
+def block_spec(shape):
+    return pl.BlockSpec(shape, lambda s, scalars: (0,) * len(shape), pipeline_mode=pl.Buffered(1))
+
+
+def expert_backward_kernel(scalars, rows, grads, *refs, sources):
+    weights, rest = refs[:sources], refs[sources:]
     mine_gate, theirs_gate, mine_rest, theirs_rest, total = rest[:5]
-    gate_total, up_total, down_total, room, sem = rest[5:]
+    gate_total, up_total, down_total, room, sem = rest[-5:]
     step = pl.program_id(0)
     slot = next_weights(0, weight_sources(weights, scalars[1]), room, sem)
     gate_total[...] = jnp.zeros_like(gate_total)
     up_total[...] = jnp.zeros_like(up_total)
     down_total[...] = jnp.zeros_like(down_total)
 
-    def one(tile, carry):
-        at = pl.ds(pl.multiple_of(tile * SLOT_TILE, SLOT_TILE), SLOT_TILE)
+    def body(start, size):
+        at = pl.ds(start, size)
         values, upstream = rows[at, :], grads[at, :]
-        gate_pre = lax.dot_general(values, room[slot, 0], LAST, preferred_element_type=jnp.float32)
-        up_pre = lax.dot_general(values, room[slot, 1], LAST, preferred_element_type=jnp.float32)
-        grad_inner = lax.dot_general(upstream, room[slot, 2], LAST, preferred_element_type=jnp.float32)
+        gate_pre = lax.dot_general(room[slot, 0], values, LAST, preferred_element_type=jnp.float32)
+        up_pre = lax.dot_general(room[slot, 1], values, LAST, preferred_element_type=jnp.float32)
+        grad_inner = lax.dot_general(room[slot, 2], upstream, LAST, preferred_element_type=jnp.float32)
         active, half, bent, square = gelu_parts(gate_pre)
         slope = half + (0.5 * GELU_IN) * gate_pre * (1.0 - bent * bent) * (1.0 + 3.0 * GELU_CUBE * square)
         inner = (active * up_pre).astype(jnp.bfloat16)
         grad_gate = (grad_inner * up_pre * slope).astype(jnp.bfloat16)
         grad_up = (grad_inner * active).astype(jnp.bfloat16)
-        down_total[...] += lax.dot_general(inner, upstream, FIRST, preferred_element_type=jnp.float32)
-        gate_total[...] += lax.dot_general(grad_gate, values, FIRST, preferred_element_type=jnp.float32)
-        up_total[...] += lax.dot_general(grad_up, values, FIRST, preferred_element_type=jnp.float32)
-        part = jnp.dot(grad_gate, room[slot, 0], preferred_element_type=jnp.float32)
-        part = part + jnp.dot(grad_up, room[slot, 1], preferred_element_type=jnp.float32)
+        down_total[...] += jnp.dot(inner, upstream, preferred_element_type=jnp.float32)
+        gate_total[...] += jnp.dot(grad_gate, values, preferred_element_type=jnp.float32)
+        up_total[...] += jnp.dot(grad_up, values, preferred_element_type=jnp.float32)
+        part = lax.dot_general(grad_gate, room[slot, 0], FIRST, preferred_element_type=jnp.float32)
+        part = part + lax.dot_general(grad_up, room[slot, 1], FIRST, preferred_element_type=jnp.float32)
 
         @pl.when(step == 0)
         def _():
@@ -673,9 +720,7 @@
         def _():
             total[at, :] += part
 
-        return carry
-
-    lax.fori_loop(0, pl.cdiv(scalars[0], SLOT_TILE), one, 0)
+    over_tiles(scalars[0], rows.shape[0], body)
     half = mine_gate.shape[2]
     for sums, mine, theirs, number in (
         (gate_total, mine_gate, theirs_gate, 0),
@@ -696,7 +741,7 @@
     )
     shape = lambda count: jax.ShapeDtypeStruct((shards, count, half, width), jnp.bfloat16)
     return pl.pallas_call(
-        expert_backward_kernel,
+        functools.partial(expert_backward_kernel, sources=len(weights)),
         grid_spec=pltpu.PrefetchScalarGridSpec(
             num_scalar_prefetch=1,
             grid=(shards,),
@@ -705,7 +750,7 @@
             scratch_shapes=[pltpu.VMEM((2 * half, width), jnp.float32)] * 3 + expert_scratch(theirs),
         ),
         out_shape=[shape(1), shape(1), shape(2), shape(2), jax.ShapeDtypeStruct((padded, width), jnp.float32)],
-        compiler_params=pltpu.CompilerParams(vmem_limit_bytes=60 << 20),
+        compiler_params=pltpu.CompilerParams(vmem_limit_bytes=63 << 20),
         cost_estimate=expert_cost(padded, theirs, shards, 8),
         name="expert_backward",
     )(scalars, rows, grads, *weights)
@@ -742,6 +787,54 @@
         cost_estimate=pl.CostEstimate(flops=10**10, bytes_accessed=2 * 10**7, transcendentals=0),
         name="project",
     )(weights, rows)
+
+
+def products_kernel(rows, weights, q_t, k, v, parts, three, norm, total):
+    step = pl.program_id(0)
+    grads = jnp.concatenate([jnp.transpose(q_t[...]), k[...], v[...]], axis=1)
+    values = rows[...]
+    part = lax.dot_general(grads, weights[...], LAST, preferred_element_type=jnp.float32)
+    parts[...] = part.astype(jnp.bfloat16)
+    product = lax.dot_general(values, grads, FIRST, preferred_element_type=jnp.float32)
+    column = jnp.sum(part * values.astype(jnp.float32), axis=0, keepdims=True)
+
+    @pl.when(step == 0)
+    def _():
+        total[...] = product
+        norm[...] = column
+
+    @pl.when(step > 0)
+    def _():
+        total[...] += product
+        norm[...] += column
+
+    @pl.when(step == pl.num_programs(0) - 1)
+    def _():
+        three[...] = total[...].astype(jnp.bfloat16)
+
+
+def last_products(rows, weights, q_t, k, v):
+    length, width = rows.shape
+    columns = k.shape[1]
+    count = 4 * TILE
+    whole = lambda shape: pl.BlockSpec(shape, lambda i: (0, 0))
+    tall = pl.BlockSpec((count, columns), lambda i: (i, 0))
+    wide = pl.BlockSpec((count, width), lambda i: (i, 0))
+    return pl.pallas_call(
+        products_kernel,
+        grid=(length // count,),
+        in_specs=[wide, whole(weights.shape), pl.BlockSpec((columns, count), lambda i: (0, i)), tall, tall],
+        out_specs=[wide, whole(weights.shape), whole((1, width))],
+        out_shape=[
+            jax.ShapeDtypeStruct((length, width), jnp.bfloat16),
+            jax.ShapeDtypeStruct(weights.shape, jnp.bfloat16),
+            jax.ShapeDtypeStruct((1, width), jnp.float32),
+        ],
+        scratch_shapes=[pltpu.VMEM(weights.shape, jnp.float32)],
+        compiler_params=pltpu.CompilerParams(vmem_limit_bytes=48 << 20),
+        cost_estimate=pl.CostEstimate(flops=10**10, bytes_accessed=2 * 10**7, transcendentals=0),
+        name="last_products",
+    )(rows, weights, q_t, k, v)
 
 
 def split_float(values):
@@ -1737,7 +1830,7 @@
     top_count = route_local.shape[1]
     if split_trees():
         quarter, part = width // 4, w_out.shape[0] // 8
-        info_row = jnp.pad(info.at[INFO_SIZE - 1].set(jnp.sum(validity)), (0, TILE - INFO_SIZE))
+        info_row = jnp.pad(info, (0, TILE - INFO_SIZE))
         rows_of = lambda values: values.astype(jnp.float32).reshape(-1, TILE)
         pack = jnp.concatenate([rows_of(info_row), rows_of(rel_bias), rows_of(route_local.T)], axis=0)
         pack = jnp.pad(pack, ((0, -pack.shape[0] % 8), (0, 0)))
@@ -1822,10 +1915,12 @@
         produced = expert_forward(expert_scalars, expert_rows, weights_near, 0, 3)
         produced, far = lax.optimization_barrier((produced, far))
         weights_all = weights_near + (far, swap(far, "dp", 1))
-        produced = expert_forward(expert_scalars, expert_rows, weights_all, 3, 1, produced)
+        shares, produced_layer = expert_forward(
+            expert_scalars, expert_rows, weights_all, 3, 1, produced, scalars, slots, gate_here
+        )
     else:
         produced = expert_forward(expert_scalars, expert_rows, weights_all, 0, shards)
-    shares, produced_layer = expand(scalars, slots, produced, gate_here)
+        shares, produced_layer = expand(scalars, slots, produced, gate_here)
     combined = layer_scatter(shares)
 
     output_rows = hidden + combined
@@ -1892,14 +1987,10 @@
         info, table, query_rows, key_rows, key_t, value_rows, grad_attended, attended_t, log_totals
     )
     bias_grad = bias_gradient(ahead, behind, info[OFFSET_AT : OFFSET_AT + CLASSES], bucket_count)
-    across = (((0,), (0,)), ((), ()))
-    grad_three = jnp.concatenate([grad_queries_t.T, grad_keys, grad_values], axis=1)
-    three_wgrad = lax.dot_general(normed_all, grad_three, across, preferred_element_type=jnp.float32)
-    norm1_grad = jnp.sum(three_wgrad * weights.astype(jnp.float32), axis=1) / norm1_gain
-    grad_normed_all = lax.dot_general(
-        grad_three, weights, (((1,), (1,)), ((), ())), preferred_element_type=jnp.float32
-    ).astype(jnp.bfloat16)
-    three_wgrad = three_wgrad.astype(jnp.bfloat16)
+    grad_normed_all, three_wgrad, norm1_grad = last_products(
+        normed_all, weights, grad_queries_t, grad_keys, grad_values
+    )
+    norm1_grad = norm1_grad[0] / norm1_gain
 
     heads_here = bias_grad.shape[1]
     group = my_place()[3] if split_trees() else shard_index

time: 905 us -> 898 us (level); the launches traced: 905 us -> 884 us
  matrix products: 24.8 us -> 8.03 us
  Pallas kernels: 712 us -> 702 us
    pallas_call x4, Pallas kernels: 222 us -> 203 us  [exchange_call(): pl.pallas_call(kernel, in_specs=[anywhere] * len(operands), out_specs=[an...]
    dot_general x2 -> x0, matrix products: 16.7 us -> none  [the longest x1 8.79 us: on_device(): lax.dot_general(normed_all, grad_three, across, preferred_element_type=jn...]
    pallas_call x1 -> x2, Pallas kernels: 103 us -> 112 us  [the longest x1 98.2 us: expert_backward(): pl.pallas_call(functools.partial(expert_backward_kernel, sources=len(weig...]
    unnamed x177 -> x183, local copies, waits for them, and re-layouts: 17.2 us -> 23.8 us
    pallas_call x4 -> x3, Pallas kernels: 57.9 us -> 54.1 us  [whole_calls(): pl.pallas_call(kernel, in_specs=specs, out_specs=jax.tree.map(lambda _: p...]
  transfers between devices with their start and end apart: 19 -> 19, of which waited for: 4 -> 4; matrix products, arithmetic and copies ran while one was open for 9% -> 7% of each run, Pallas kernels for 42% -> 44%
where the time goes in v4:
time: 898 us; the launch traced here: 884 us
  Pallas kernels  702 us (78%)
  other arithmetic  51.1 us (6%)
  local copies, waits for them, and re-layouts  50.1 us (6%)
  waiting for transfers between devices  36.6 us (4%)
  between operations  20.8 us (2%)
  starting transfers between devices  15.9 us (2%)
    pallas_call x4, Pallas kernels, exchange_call(): pl.pallas_call(kernel, in_specs=[anywhere] * len(operands), out_specs=[an...  203 us
    pallas_call x1, Pallas kernels, expert_backward(): pl.pallas_call(functools.partial(expert_backward_kernel, sources=len(weig...  98.2 us
    pallas_call x2, Pallas kernels, layer_scatter(): pl.pallas_call(scatter_kernel, in_specs=[pl.BlockSpec(memory_space=pltpu....  91.2 us
    pallas_call x1, Pallas kernels, reduce_last(): pl.pallas_call(last_kernel, in_specs=[vmem] * 3, out_specs=[vmem] * 3, ou...  88.7 us
    pallas_call x2, Pallas kernels, expert_forward(): pl.pallas_call(functools.partial(expert_forward_kernel, first=first, sour...  63.3 us
    pallas_call x3, Pallas kernels, whole_calls(): pl.pallas_call(kernel, in_specs=specs, out_specs=jax.tree.map(lambda _: p...  54.1 us
    pallas_call x1, Pallas kernels, attention_backward(): pl.pallas_call(functools.partial(backward_kernel, heads=heads, tiles=tile...  52.9 us
    ppermute x14, waiting for transfers between devices, swap(): return lax.ppermute(array, axis, [(i, i ^ bit) for i in range(size)])  36.5 us
  transfers between devices with their start and end apart: 19, of which 4 were waited for; matrix products, arithmetic and copies ran while one was open for 7% of the time, Pallas kernels for 44%

profile of v4, /device:TPU:0, one launch (start us, length us, event | category | flops | bytes accessed | tf_op | source)
XLA Modules:
  0.0 883.9 jit_solution(4303272767661599230)
XLA Ops:
  11.6 1.7 fusion.7
  18.4 3.3 multiply_convert_fusion.1
  21.8 1.5 fusion.11.own.refs_1_
  23.7 63.7 %gather_tree.1 = (bf16[4,2,320,1024]{3,2,1,0:T(8,128)(2,1)}, bf16[1024,768]{1,0:T(8,128)(2,1)S(1)}, bf16[4,4,2,32,1024]{4,3,2,1,0:T(8,128)(2,1)}, f32[9,16,128]{...) custom-call(bf16[2,320,1024]{2,1,0:T(8,128)(2,1)S(1)} %get-tuple-ele, ...), custom_call_target="tpu_custom_call" | custom-call | flops 49999998976 | bytes 1000000 | tf_op jit(solution)/shard_map/gather_tree/pallas_call | solution.py:1250
  87.4 2.6 collective-permute-start
  92.0 2.5 copy-done.18
  94.4 6.7 project.1
  102.4 29.2 %attention_forward.1 = (bf16[256,2560]{1,0:T(8,128)(2,1)S(1)}, f32[20,1,512]{2,1,0:T(1,128)S(1)}) custom-call(s32[64]{0:T(128)S(1)} %fusion.98.info, f32[4,128]{1,0:T(4,128)S(1)} %fusion.20.table, bf16[2560,256]{1,0:T(8,128)(2,1)S(1)} %get-tuple-element.72.q, bf16[2560,256]{1,0:T(8,128)(2,1)S(1)} %get-tuple-element.73.k, bf16[256,2560]{1,0:T(8,128)(2,1)} %copy-done.33), custom_call_target="tpu_custom_call" | custom-call | flops 40000000000 | bytes 10000000 | tf_op jit(solution)/shard_map/attention_forward/pallas_call | solution.py:163
  131.7 28.8 %trade_heads.1 = bf16[4,256,640]{2,1,0:T(8,128)(2,1)S(1)} custom-call(bf16[256,2560]{1,0:T(8,128)(2,1)S(1)} %get-tuple-element.75.attended.attended_t), custom_call_target="tpu_custom_call" | custom-call | flops 49999998976 | bytes 1000000 | tf_op jit(solution)/shard_map/trade_heads/pallas_call | solution.py:1250
  162.7 1.5 copy.94
  166.3 3.3 multiply_reduce_fusion.3
  171.1 63.6 %meet.1 = (bf16[6,320,1024]{2,1,0:T(8,128)(2,1)}, bf16[4,3,352,1024]{3,2,1,0:T(8,128)(2,1)}, bf16[3,352,1024]{2,1,0:T(8,128)(2,1)S(1)}, bf16[3,352,1024]{2,1,0:T(8,128)(2,1)S(1)}) custom-call(bf16[2,320,1024]{2,1,0:T(8,128)(2,1)S(1)} %bitcast.149, bf16[3,352,1024]{2,1,0:T(8,128)(2,1)} %fusion.11.own.refs_1_, ...), custom_call_target="tpu_custom_call" | custom-call | flops 49999998976 | bytes 1000000 | tf_op jit(solution)/shard_map/meet/pallas_call | solution.py:1250
  234.8 1.6 broadcast_select_fusion
  238.8 25.9 %compact_rows.1 = (bf16[2560,1024]{1,0:T(8,128)(2,1)}, f32[8,320,1]{2,1,0:T(8,128)S(1)}) custom-call(s32[10]{0:T(128)S(1)} %pad_add_fusion.scalars, bf16[1024,128]{1,0:T(8,128)(2,1)S(1)} %copy-done.12, s32[8,1,320]{2,1,0:T(1,128)S(1)} %add_select_fusion.1.slots, s32[8,320,2]{2,1,0:T(8,128)S(1)} %bitcast.152, bf16[2,320,1024]{2,1,0:T(8,128)(2,1)S(1)} %bitcast.150, ...), custom_call_target="tpu_custom_call" | custom-call | flops 10000000000 | bytes 30000000 | tf_op jit(solution)/shard_map/compact_rows/pallas_call | solution.py:427
  265.8 35.2 %expert_forward.2.refs_8_ = f32[2560,1024]{1,0:T(8,128)} custom-call(s32[6]{0:T(128)} %concatenate.60.scalars, bf16[2560,1024]{1,0:T(8,128)(2,1)} %get-tuple-element.79.rows, bf16[4,3,352,1024]{3,2,1,0:T(8,128)(2,1)} %get-tuple-element.80.refs_0_, bf16[3,352,1024]{2,1,0:T(8,128)(2,1)} %fusion.11.own.refs_1_, ...), custom_call_target="tpu_custom_call" | custom-call | flops 33218887680 | bytes 17301504 | tf_op jit(solution)/shard_map/expert_forward/pallas_call | solution.py:665
  305.1 2.2 reshape.560
  309.4 2.6 add_select_fusion.refs_9_.slots
  312.1 28.1 %expert_forward.3 = (bf16[8,320,1024]{2,1,0:T(8,128)(2,1)}, bf16[8,320,1024]{2,1,0:T(8,128)(2,1)}) custom-call(s32[15]{0:T(128)} %concatenate.57.scalars, bf16[2560,1024]{1,0:T(8,128)(2,1)} %get-tuple-element.79.rows, bf16[4,3,352,1024]{3,2,1,0:T(8,128)(2,1)} %get-tuple-element.80.refs_0_, bf16[3,352,1024]{2,1,0:T(8,128)(2,1)} %fusion.11.own.refs_1_, ...), custom_call_target="tpu_custom_call" | custom-call | flops 11072962560 | bytes 17301504 | tf_op jit(solution)/shard_map/expert_forward/pallas_call | solution.py:665
  340.2 2.5 copy-done.16
  342.7 45.4 %layer_scatter.2 = (f32[320,1024]{1,0:T(8,128)S(1)}, f32[320,1024]{1,0:T(8,128)S(1)}) custom-call(bf16[8,320,1024]{2,1,0:T(8,128)(2,1)S(1)} %copy-done.16), custom_call_target="tpu_custom_call" | custom-call | flops 49999998976 | bytes 10000000 | tf_op jit(solution)/shard_map/layer_scatter/pallas_call | solution.py:892
  389.6 1.4 fusion.86
  396.0 12.8 %collective-permute-done.4 = bf16[320,1024]{1,0:T(8,128)(2,1)} collective-permute-done((bf16[320,1024]{1,0:T(8,128)(2,1)S(1)}, bf16[320,1024]{1,0:T(8,128)(2,1)}, u32[]{:S(2)}, u32[]{:S(2)}) %collective-permute-start.4) | collective-permute-done | bytes 655392 | tf_op jit(solution)/shard_map/ppermute | solution.py:854
  412.0 10.8 %collective-permute-done.5 = bf16[320,1024]{1,0:T(8,128)(2,1)S(1)} collective-permute-done((bf16[320,1024]{1,0:T(8,128)(2,1)S(1)}, bf16[320,1024]{1,0:T(8,128)(2,1)S(1)}, u32[]{:S(2)}, u32[]{:S(2)}) %collective-permute-start.5) | collective-permute-done | bytes 655392 | tf_op jit(solution)/shard_map/ppermute | solution.py:854
  423.6 12.1 %collective-permute-done.8 = bf16[320,1024]{1,0:T(8,128)(2,1)S(1)} collective-permute-done((bf16[320,1024]{1,0:T(8,128)(2,1)}, bf16[320,1024]{1,0:T(8,128)(2,1)S(1)}, u32[]{:S(2)}, u32[]{:S(2)}) %collective-permute-start.8) | collective-permute-done | bytes 655392 | tf_op jit(solution)/shard_map/ppermute | solution.py:854
  436.7 15.9 %compact_grads.1 = (bf16[2560,1024]{1,0:T(8,128)(2,1)}, f32[8,320,1]{2,1,0:T(8,128)}) custom-call(s32[10]{0:T(128)} %copy-done.15, s32[8,1,320]{2,1,0:T(1,128)} %copy-done.13, f32[8,320,1]{2,1,0:T(8,128)} %copy-done.10, bf16[8,320,1024]{2,1,0:T(8,128)(2,1)} %get-tuple-element.91.produced, bf16[1,320,1024]{2,1,0:T(8,128)(2,1)} %get-tuple-element.212.refs_0_, ...), custom_call_target="tpu_custom_call" | custom-call | flops 10000000000 | bytes 30000000 | tf_op jit(solution)/shard_map/compact_grads/pallas_call | solution.py:427
  452.6 98.2 %expert_backward.1 = (bf16[4,1,352,1024]{3,2,1,0:T(8,128)(2,1)}, bf16[4,1,352,1024]{3,2,1,0:T(8,128)(2,1)}, bf16[4,2,352,1024]{3,2,1,0:T(8,128)(2,1)}, bf16[4,2,352,1024]{3,2,1,0:T(8,128)(2,1)}, f32[2560,1024]{1,0:T(8,128)}) custom-call(s32[6]{0:T(128)} %concatenate.60.scalars, bf16[2560,1024]{1,0:T(8,128)(2,1)} %get-tuple-element.79.rows, ...), custom_call_target="tpu_custom_call" | custom-call | flops 118111600640 | bytes 17301504 | tf_op jit(solution)/shard_map/expert_backward/pallas_call | solution.py:743
  551.0 1.8 slice_reduce_fusion.3
  552.8 1.5 collective-permute-start.14
  554.4 2.0 collective-permute-start.12
  556.5 12.2 %expand.1.parts = bf16[8,320,1024]{2,1,0:T(8,128)(2,1)} custom-call(s32[10]{0:T(128)} %copy-done.15, s32[8,320,1]{2,1,0:T(8,128)} %add_select_fusion.refs_9_.slots, f32[2560,1024]{1,0:T(8,128)} %get-tuple-element.95.refs_0_), custom_call_target="tpu_custom_call" | custom-call | flops 10000000000 | bytes 30000000 | tf_op jit(solution)/shard_map/expand/pallas_call | solution.py:427
  569.5 5.7 add.426
  575.3 2.6 copy-done.24
  578.0 45.8 %layer_scatter.3 = (f32[320,1024]{1,0:T(8,128)S(1)}, f32[320,1024]{1,0:T(8,128)S(1)}) custom-call(bf16[8,320,1024]{2,1,0:T(8,128)(2,1)S(1)} %copy-done.24), custom_call_target="tpu_custom_call" | custom-call | flops 49999998976 | bytes 10000000 | tf_op jit(solution)/shard_map/layer_scatter/pallas_call | solution.py:892
  623.9 5.0 multiply_reduce_fusion.1
  628.9 2.7 multiply_add_fusion
  631.6 1.8 convolution_convert_fusion
  634.2 1.6 convolution_convert_fusion.1.grads
  635.8 47.3 %trade_back.1 = (bf16[4,640,256]{2,1,0:T(8,128)(2,1)S(1)}, bf16[4,2,32,1024]{3,2,1,0:T(8,128)(2,1)S(1)}) custom-call(bf16[640,1024]{1,0:T(8,128)(2,1)S(1)} %convolution_convert_fusion.1.grads, bf16[4,4,64,1024]{3,2,1,0:T(8,128)(2,1)S(1)} %bitcast.151), custom_call_target="tpu_custom_call" | custom-call | flops 1000000 | bytes 1000000 | tf_op jit(solution)/shard_map/trade_back/pallas_call | solution.py:1250
  684.5 8.1 add.425
  692.6 52.9 %attention_backward.1 = (bf16[256,2560]{1,0:T(8,128)(2,1)}, bf16[2560,256]{1,0:T(8,128)(2,1)}, bf16[2560,256]{1,0:T(8,128)(2,1)}, f32[18,1,512]{2,1,0:T(1,128)}, f32[18,1,512]{2,1,0:T(1,128)}) custom-call(s32[64]{0:T(128)} %copy-done.14, f32[4,128]{1,0:T(4,128)} %copy-done.23, bf16[2560,256]{1,0:T(8,128)(2,1)} %copy-done.29, bf16[2560,256]{1,0:T(8,128)(2,1)} %copy-done.30, ...), custom_call_target="tpu_custom_call" | custom-call | flops 60000002048 | bytes 10000000 | tf_op jit(solution)/shard_map/attention_backward/pallas_call | solution.py:295
  749.6 13.9 %last_products.1 = (bf16[2560,1024]{1,0:T(8,128)(2,1)}, bf16[1024,768]{1,0:T(8,128)(2,1)S(1)}, f32[1,1024]{1,0:T(1,128)S(1)}) custom-call(bf16[2560,1024]{1,0:T(8,128)(2,1)} %bitcast.155, bf16[1024,768]{1,0:T(8,128)(2,1)} %copy-done.25, bf16[256,2560]{1,0:T(8,128)(2,1)S(1)} %copy-done.26, bf16[2560,256]{1,0:T(8,128)(2,1)S(1)} %copy-done.27, ...), custom_call_target="tpu_custom_call" | custom-call | flops 10000000000 | bytes 20000000 | tf_op jit(solution)/shard_map/last_products/pallas_call | solution.py:823
  766.1 1.4 copy-done.20
  767.5 88.7 %reduce_last.1 = (bf16[2,320,1024]{2,1,0:T(8,128)(2,1)S(1)}, bf16[4,2,128,768]{3,2,1,0:T(8,128)(2,1)S(1)}, f32[8,1024]{1,0:T(8,128)S(1)}) custom-call(bf16[4,2,320,1024]{3,2,1,0:T(8,128)(2,1)} %bitcast.188, bf16[4,256,768]{2,1,0:T(8,128)(2,1)S(1)} %bitcast.157, f32[8,1024]{1,0:T(8,128)S(1)} %concatenate.64.small), custom_call_target="tpu_custom_call" | custom-call | flops 49999998976 | bytes 10000000 | tf_op jit(solution)/shard_map/reduce_last/pallas_call | solution.py:1680
  859.5 2.0 bitcast_convert_fusion
  862.7 3.8 fusion.85
  866.4 2.2 fusion.6
  869.9 1.9 convert_bitcast_fusion
  872.7 3.0 fusion.84
  (321 shorter events, 52.1 us)
Async XLA Ops:
  7.2 685.4 %reduce-scatter.3.cloned.1.call-start = ((), (), s32[]{:S(2)}) async-start(), calls=%async_computation.2 | async-start | bytes 3604480 | tf_op jit(solution)/shard_map/reduce_scatter | solution.py:1942
  87.4 82.6 %collective-permute-start = (bf16[3,352,1024]{2,1,0:T(8,128)(2,1)}, bf16[3,352,1024]{2,1,0:T(8,128)(2,1)}, u32[]{:S(2)}, u32[]{:S(2)}) collective-permute-start(bf16[3,352,1024]{2,1,0:T(8,128)(2,1)} %fusion.11.own.refs_1_), channel_id=1, source_target_pairs={{0,2},{2,4},{4,6},{1,3},{3,5},{5,7},{8,10},{10,12},{12,14},{9,11},... | collective-permute-start | bytes 6488072 | tf_op jit(solution)/shard_map/ppermute | solution.py:949
  90.0 80.0 %collective-permute-start.1 = (bf16[3,352,1024]{2,1,0:T(8,128)(2,1)}, bf16[3,352,1024]{2,1,0:T(8,128)(2,1)}, u32[]{:S(2)}, u32[]{:S(2)}) collective-permute-start(bf16[3,352,1024]{2,1,0:T(8,128)(2,1)} %fusion.11.own.refs_1_), channel_id=1, source_target_pairs={{2,0},{4,2},{6,4},{3,1},{5,3},{7,5},{10,8},{12,10},{14,12},{11,9},... | collective-permute-start | bytes 6488072 | tf_op jit(solution)/shard_map/ppermute | solution.py:949
  102.2 29.4 %copy-start.29 = (bf16[2560,256]{1,0:T(8,128)(2,1)}, bf16[2560,256]{1,0:T(8,128)(2,1)S(1)}, u32[]{:S(2)}) copy-start(bf16[2560,256]{1,0:T(8,128)(2,1)S(1)} %get-tuple-element.72.q) | copy-start | bytes 3932164
  102.2 29.5 %copy-start.30 = (bf16[2560,256]{1,0:T(8,128)(2,1)}, bf16[2560,256]{1,0:T(8,128)(2,1)S(1)}, u32[]{:S(2)}) copy-start(bf16[2560,256]{1,0:T(8,128)(2,1)S(1)} %get-tuple-element.73.k) | copy-start | bytes 3932164
  102.2 29.5 %copy-start.31 = (bf16[256,2560]{1,0:T(8,128)(2,1)}, bf16[256,2560]{1,0:T(8,128)(2,1)S(1)}, u32[]{:S(2)}) copy-start(bf16[256,2560]{1,0:T(8,128)(2,1)S(1)} %get-tuple-element.89.k_t) | copy-start | bytes 3932164
  102.2 29.5 %copy-start.32 = (bf16[2560,256]{1,0:T(8,128)(2,1)}, bf16[2560,256]{1,0:T(8,128)(2,1)S(1)}, u32[]{:S(2)}) copy-start(bf16[2560,256]{1,0:T(8,128)(2,1)S(1)} %get-tuple-element.90.v) | copy-start | bytes 3932164
  102.4 29.3 %copy-start.23 = (f32[4,128]{1,0:T(4,128)}, f32[4,128]{1,0:T(4,128)S(1)}, u32[]{:S(2)}) copy-start(f32[4,128]{1,0:T(4,128)S(1)} %fusion.20.table) | copy-start | bytes 6148
  131.7 28.9 %copy-start.34 = (bf16[256,2560]{1,0:T(8,128)(2,1)}, bf16[256,2560]{1,0:T(8,128)(2,1)S(1)}, u32[]{:S(2)}) copy-start(bf16[256,2560]{1,0:T(8,128)(2,1)S(1)} %get-tuple-element.75.attended.attended_t) | copy-start | bytes 3932164
  131.7 30.7 %copy-start.65 = (f32[1024,4]{0,1:T(4,128)S(1)}, f32[1024,4]{0,1:T(4,128)}, u32[]{:S(2)}) copy-start(f32[1024,4]{0,1:T(4,128)} %param.30) | copy-start | bytes 49156
  166.3 72.5 %copy-start.15 = (s32[10]{0:T(128)}, s32[10]{0:T(128)S(1)}, u32[]{:S(2)}) copy-start(s32[10]{0:T(128)S(1)} %pad_add_fusion.scalars) | copy-start | bytes 124
  169.7 65.1 %copy-start.62 = (f32[640]{0:T(1024)}, f32[640]{0:T(1024)S(1)}, u32[]{:S(2)}) copy-start(f32[640]{0:T(1024)S(1)} %add_rsqrt_fusion) | copy-start | bytes 7684
  169.7 69.0 %copy-start.13 = (s32[8,1,320]{2,1,0:T(1,128)}, s32[8,1,320]{2,1,0:T(1,128)S(1)}, u32[]{:S(2)}) copy-start(s32[8,1,320]{2,1,0:T(1,128)S(1)} %add_select_fusion.1.slots) | copy-start | bytes 30724
  170.0 240.8 %copy-start.6 = (bf16[640,1024]{1,0:T(8,128)(2,1)}, bf16[640,1024]{1,0:T(8,128)(2,1)S(1)}, u32[]{:S(2)}) copy-start(bf16[640,1024]{1,0:T(8,128)(2,1)S(1)} %multiply_convert_fusion) | copy-start | bytes 3932164
  237.4 63.5 %collective-permute-start.2 = (bf16[3,352,1024]{2,1,0:T(8,128)(2,1)}, bf16[3,352,1024]{2,1,0:T(8,128)(2,1)}, u32[]{:S(2)}, u32[]{:S(2)}) collective-permute-start(bf16[3,352,1024]{2,1,0:T(8,128)(2,1)} %broadcast_select_fusion), channel_id=1, source_target_pairs={{2,0},{4,6},{3,1},{5,7},{10,8},{12,14},{11,9},{13,15},{18,16},{20,... | collective-permute-start | bytes 6488072 | tf_op jit(solution)/shard_map/ppermute | solution.py:949
  301.0 11.1 %collective-permute-start.3 = (bf16[3,352,1024]{2,1,0:T(8,128)(2,1)}, bf16[3,352,1024]{2,1,0:T(8,128)(2,1)}, u32[]{:S(2)}, u32[]{:S(2)}) collective-permute-start(bf16[3,352,1024]{2,1,0:T(8,128)(2,1)} %collective-permute-done.2.refs_6_), channel_id=1, source_target_pairs={{0,1},{1,0},{2,3},{3,2},{4,5},{5,4},{6,7},{7,6},{8,9},{9,8},{10,11... | collective-permute-start | bytes 6488072 | tf_op jit(solution)/shard_map/ppermute | solution.py:854
  309.4 78.7 %copy-start.60 = (f32[640]{0:T(1024)}, f32[640]{0:T(1024)S(1)}, u32[]{:S(2)}) copy-start(f32[640]{0:T(1024)S(1)} %convert_reduce_fusion) | copy-start | bytes 7684
  342.7 45.5 %copy-start.37 = (f32[640,1024]{1,0:T(8,128)S(1)}, f32[640,1024]{1,0:T(8,128)}, u32[]{:S(2)}) copy-start(f32[640,1024]{1,0:T(8,128)} %copy-done.36) | copy-start | bytes 7864324
  342.7 45.5 %copy-start.39 = (bf16[1,640,1024]{2,1,0:T(8,128)(2,1)S(1)}, bf16[1,640,1024]{2,1,0:T(8,128)(2,1)}, u32[]{:S(2)}) copy-start(bf16[1,640,1024]{2,1,0:T(8,128)(2,1)} %param.20) | copy-start | bytes 3932164
  391.0 17.8 %collective-permute-start.4 = (bf16[320,1024]{1,0:T(8,128)(2,1)S(1)}, bf16[320,1024]{1,0:T(8,128)(2,1)}, u32[]{:S(2)}, u32[]{:S(2)}) collective-permute-start(bf16[320,1024]{1,0:T(8,128)(2,1)S(1)} %get-tuple-element.214), channel_id=1, source_target_pairs={{0,8},{8,0},{16,24},{24,16},{1,9},{9,1},{17,25},{25,17},{2,10},{10... | collective-permute-start | bytes 1966088 | tf_op jit(solution)/shard_map/ppermute | solution.py:854
  391.9 17.8 %collective-permute-start.7 = (bf16[320,1024]{1,0:T(8,128)(2,1)S(1)}, bf16[320,1024]{1,0:T(8,128)(2,1)}, u32[]{:S(2)}, u32[]{:S(2)}) collective-permute-start(bf16[320,1024]{1,0:T(8,128)(2,1)S(1)} %get-tuple-element.211), channel_id=1, source_target_pairs={{0,16},{8,24},{16,0},{24,8},{1,17},{9,25},{17,1},{25,9},{2,18},{10... | collective-permute-start | bytes 1966088 | tf_op jit(solution)/shard_map/ppermute | solution.py:854
  394.0 28.8 %collective-permute-start.5 = (bf16[320,1024]{1,0:T(8,128)(2,1)S(1)}, bf16[320,1024]{1,0:T(8,128)(2,1)S(1)}, u32[]{:S(2)}, u32[]{:S(2)}) collective-permute-start(bf16[320,1024]{1,0:T(8,128)(2,1)S(1)} %get-tuple-element.211), channel_id=1, source_target_pairs={{0,8},{8,0},{16,24},{24,16},{1,9},{9,1},{17,25},{25,17},{2,10},{10... | collective-permute-start | bytes 1966088 | tf_op jit(solution)/shard_map/ppermute | solution.py:854
  394.8 28.8 %collective-permute-start.6 = (bf16[320,1024]{1,0:T(8,128)(2,1)S(1)}, bf16[320,1024]{1,0:T(8,128)(2,1)S(1)}, u32[]{:S(2)}, u32[]{:S(2)}) collective-permute-start(bf16[320,1024]{1,0:T(8,128)(2,1)S(1)} %get-tuple-element.214), channel_id=1, source_target_pairs={{0,16},{8,24},{16,0},{24,8},{1,17},{9,25},{17,1},{25,9},{2,18},{10... | collective-permute-start | bytes 1966088 | tf_op jit(solution)/shard_map/ppermute | solution.py:854
  408.8 26.9 %collective-permute-start.8 = (bf16[320,1024]{1,0:T(8,128)(2,1)}, bf16[320,1024]{1,0:T(8,128)(2,1)S(1)}, u32[]{:S(2)}, u32[]{:S(2)}) collective-permute-start(bf16[320,1024]{1,0:T(8,128)(2,1)} %collective-permute-done.4), channel_id=1, source_target_pairs={{0,16},{8,24},{16,0},{24,8},{1,17},{9,25},{17,1},{25,9},{2,18},{10... | collective-permute-start | bytes 1966088 | tf_op jit(solution)/shard_map/ppermute | solution.py:854
  409.7 26.0 %collective-permute-start.9 = (bf16[320,1024]{1,0:T(8,128)(2,1)}, bf16[320,1024]{1,0:T(8,128)(2,1)S(1)}, u32[]{:S(2)}, u32[]{:S(2)}) collective-permute-start(bf16[320,1024]{1,0:T(8,128)(2,1)} %collective-permute-done.7), channel_id=1, source_target_pairs={{0,8},{8,0},{16,24},{24,16},{1,9},{9,1},{17,25},{25,17},{2,10},{10... | collective-permute-start | bytes 1966088 | tf_op jit(solution)/shard_map/ppermute | solution.py:854
  550.8 18.6 %collective-permute-start.11 = (bf16[4,1,352,1024]{3,2,1,0:T(8,128)(2,1)}, bf16[4,1,352,1024]{3,2,1,0:T(8,128)(2,1)}, u32[]{:S(2)}, u32[]{:S(2)}) collective-permute-start(bf16[4,1,352,1024]{3,2,1,0:T(8,128)(2,1)} %get-tuple-element.96), channel_id=1, source_target_pairs={{0,1},{1,0},{2,3},{3,2},{4,5},{5,4},{6,7},{7,6},{8,9},{9,8},{10,11... | collective-permute-start | bytes 8650760 | tf_op jit(solution)/shard_map/ppermute | solution.py:854
  552.8 15.9 %collective-permute-start.14 = (f32[640]{0:T(1024)S(1)}, f32[640]{0:T(1024)S(1)}, u32[]{:S(2)}, u32[]{:S(2)}) collective-permute-start(f32[640]{0:T(1024)S(1)} %squeeze.47), channel_id=1, source_target_pairs={{0,24},{8,16},{16,8},{24,0},{1,25},{9,17},{17,9},{25,1},{2,26},{10... | collective-permute-start | bytes 7688 | tf_op jit(solution)/shard_map/ppermute | solution.py:854
  554.4 14.4 %collective-permute-start.13 = (f32[640]{0:T(1024)S(1)}, f32[640]{0:T(1024)S(1)}, u32[]{:S(2)}, u32[]{:S(2)}) collective-permute-start(f32[640]{0:T(1024)S(1)} %squeeze.46), channel_id=1, source_target_pairs={{0,16},{8,24},{16,0},{24,8},{1,17},{9,25},{17,1},{25,9},{2,18},{10... | collective-permute-start | bytes 7688 | tf_op jit(solution)/shard_map/ppermute | solution.py:854
  554.4 14.4 %collective-permute-start.12 = (f32[640]{0:T(1024)S(1)}, f32[640]{0:T(1024)S(1)}, u32[]{:S(2)}, u32[]{:S(2)}) collective-permute-start(f32[640]{0:T(1024)S(1)} %squeeze.45), channel_id=1, source_target_pairs={{0,8},{8,0},{16,24},{24,16},{1,9},{9,1},{17,25},{25,17},{2,10},{10... | collective-permute-start | bytes 7688 | tf_op jit(solution)/shard_map/ppermute | solution.py:854
  568.8 115.7 %collective-permute-start.10 = (bf16[4,2,352,1024]{3,2,1,0:T(8,128)(2,1)}, bf16[4,2,352,1024]{3,2,1,0:T(8,128)(2,1)}, u32[]{:S(2)}, u32[]{:S(2)}) collective-permute-start(bf16[4,2,352,1024]{3,2,1,0:T(8,128)(2,1)} %get-tuple-element.94), channel_id=1, source_target_pairs={{0,1},{1,0},{2,3},{3,2},{4,5},{5,4},{6,7},{7,6},{8,9},{9,8},{10,11... | collective-permute-start | bytes 17301512 | tf_op jit(solution)/shard_map/ppermute | solution.py:854
  575.2 48.6 %copy-start.3 = (f32[320,1024]{1,0:T(8,128)S(1)}, f32[320,1024]{1,0:T(8,128)}, u32[]{:S(2)}) copy-start(f32[320,1024]{1,0:T(8,128)} %copy-done.2) | copy-start | bytes 3932164
  575.2 48.6 %copy-start.5 = (f32[320,1024]{1,0:T(8,128)S(1)}, f32[320,1024]{1,0:T(8,128)}, u32[]{:S(2)}) copy-start(f32[320,1024]{1,0:T(8,128)} %copy-done.4) | copy-start | bytes 3932164
  575.2 286.3 %reduce-scatter.5.cloned.1.call-start = ((), (), s32[]{:S(2)}) async-start(), calls=%async_computation.3 | async-start | bytes 7208960 | tf_op jit(solution)/shard_map/reduce_scatter | solution.py:1984
  577.9 45.9 %copy-start.38 = (f32[640,1024]{1,0:T(8,128)S(1)}, f32[640,1024]{1,0:T(8,128)}, u32[]{:S(2)}) copy-start(f32[640,1024]{1,0:T(8,128)} %copy-done.36) | copy-start | bytes 7864324
  577.9 45.9 %copy-start.40 = (bf16[1,640,1024]{2,1,0:T(8,128)(2,1)S(1)}, bf16[1,640,1024]{2,1,0:T(8,128)(2,1)}, u32[]{:S(2)}) copy-start(bf16[1,640,1024]{2,1,0:T(8,128)(2,1)} %param.20) | copy-start | bytes 3932164
  577.9 45.9 %copy-start.61 = (f32[640]{0:T(1024)S(1)}, f32[640]{0:T(1024)}, u32[]{:S(2)}) copy-start(f32[640]{0:T(1024)} %copy-done.60) | copy-start | bytes 7684
  577.9 45.9 %copy-start.63 = (f32[640]{0:T(1024)S(1)}, f32[640]{0:T(1024)}, u32[]{:S(2)}) copy-start(f32[640]{0:T(1024)} %copy-done.62) | copy-start | bytes 7684
  577.9 45.9 %copy-start.68 = (f32[1024,1]{0,1:T(1,128)S(1)}, f32[1024,1]{0,1:T(1,128)}, u32[]{:S(2)}) copy-start(f32[1024,1]{0,1:T(1,128)} %get-tuple-element.217) | copy-start | bytes 12292
  577.9 45.9 %copy-start.69 = (f32[1024,1]{0,1:T(1,128)S(1)}, f32[1024,1]{0,1:T(1,128)}, u32[]{:S(2)}) copy-start(f32[1024,1]{0,1:T(1,128)} %get-tuple-element.218) | copy-start | bytes 12292
  577.9 45.9 %copy-start.70 = (f32[1024,1]{0,1:T(1,128)S(1)}, f32[1024,1]{0,1:T(1,128)}, u32[]{:S(2)}) copy-start(f32[1024,1]{0,1:T(1,128)} %get-tuple-element.219) | copy-start | bytes 12292
  577.9 45.9 %copy-start.71 = (f32[1024,1]{0,1:T(1,128)S(1)}, f32[1024,1]{0,1:T(1,128)}, u32[]{:S(2)}) copy-start(f32[1024,1]{0,1:T(1,128)} %get-tuple-element.220) | copy-start | bytes 12292
  577.9 45.9 %copy-start.73 = (f32[1024]{0:T(1024)S(1)}, f32[1024]{0:T(1024)}, u32[]{:S(2)}) copy-start(f32[1024]{0:T(1024)} %param.29) | copy-start | bytes 12292
  631.6 52.8 %slice-start = ((s8[5767168]{0:T(1024)(128)(4,1)}), s8[4194304]{0:T(1024)(128)(4,1)S(1)}, s32[]{:S(2)}) async-start(s8[5767168]{0:T(1024)(128)(4,1)} %bitcast.161), calls=%async_computation.4 | async-start | bytes 8388608
  634.2 50.3 %slice-start.1 = ((s8[5767168]{0:T(1024)(128)(4,1)}), s8[1572864]{0:T(1024)(128)(4,1)S(1)}, s32[]{:S(2)}) async-start(s8[5767168]{0:T(1024)(128)(4,1)} %bitcast.161), calls=%async_computation.5 | async-start | bytes 3145728
  767.5 89.3 %copy-start.43 = (f32[2,320,1024]{2,1,0:T(8,128)S(1)}, f32[2,320,1024]{2,1,0:T(8,128)}, u32[]{:S(2)}) copy-start(f32[2,320,1024]{2,1,0:T(8,128)} %get-tuple-element.200) | copy-start | bytes 7864324
  767.5 89.3 %copy-start.77 = (f32[2,320]{1,0:T(2,128)S(1)}, f32[2,320]{1,0:T(2,128)}, u32[]{:S(2)}) copy-start(f32[2,320]{1,0:T(2,128)} %copy-done.76) | copy-start | bytes 7684
  858.2 10.4 %collective-permute-start.15 = (bf16[1,352,1024]{2,1,0:T(8,128)(2,1)}, bf16[1,352,1024]{2,1,0:T(8,128)(2,1)}, u32[]{:S(2)}, u32[]{:S(2)}) collective-permute-start(bf16[1,352,1024]{2,1,0:T(8,128)(2,1)} %bitcast.167), channel_id=1, source_target_pairs={{0,1},{1,0},{2,3},{3,2},{4,5},{5,4},{6,7},{7,6},{8,9},{9,8},{10,11... | collective-permute-start | bytes 2162696 | tf_op jit(solution)/shard_map/ppermute | solution.py:854
  861.5 10.3 %collective-permute-start.16 = (bf16[2,352,1024]{2,1,0:T(8,128)(2,1)}, bf16[2,352,1024]{2,1,0:T(8,128)(2,1)S(1)}, u32[]{:S(2)}, u32[]{:S(2)}) collective-permute-start(bf16[2,352,1024]{2,1,0:T(8,128)(2,1)} %bitcast.166), channel_id=1, source_target_pairs={{0,1},{1,0},{2,3},{3,2},{4,5},{5,4},{6,7},{7,6},{8,9},{9,8},{10,11... | collective-permute-start | bytes 4325384 | tf_op jit(solution)/shard_map/ppermute | solution.py:854
  (61 other events, 393.6 us)
Sparse Core Ops, SparseCore 0:
  575.3 58.2 reduce-scatter.2
  692.7 125.2 reduce-scatter.4
